TPU v7x, 512 devices: a whole 4x4x16 slice. The times are simulated.
512 devices in a mesh: row: 32 (over z_lo, y, core), col: 4 (over z_hi), rep: 4 (over x).
Axes of the slice: x: 4, y: 4, z: 16 (z_hi: 4, z_lo: 4; z = z_hi * 4 + z_lo), core: 2. Of those that a mesh axis runs over, the one named last changes fastest.
Arguments:
- images: bfloat16 [4, 96, 512, 512], P('rep', None, 'row', 'col'), may hold values from -6 to 6
- gain_first: float32 [96], replicated, may hold values from 0.1 to 1.9
- filter_first: float32 [2, 96, 512, 512], P(None, 'row', 'col'), may hold values from -6 to 6
- reduce_weight: bfloat16 [192, 384], replicated, may hold values from -0.3125 to 0.3125
- gain_second: float32 [192], replicated, may hold values from 0.1 to 1.9
- filter_second: float32 [2, 192, 256, 256], P(None, 'row', 'col'), may hold values from -6 to 6
- grad_out: bfloat16 [4, 192, 256, 256], P('rep', None, 'row', 'col'), may hold values from -6 to 6
Outputs:
- grad_images: bfloat16 [4, 96, 512, 512], P('rep', None, 'row', 'col')
- grad_filter_first: float32 [2, 96, 512, 512], P(None, 'row', 'col', 'rep')
- grad_filter_second: float32 [2, 192, 256, 256], P(None, 'row', 'col', 'rep')
All inputs are finite; a program needn't handle non-finite values.
Results may differ from a plain program's by a relative error of at most 0.022.
Values may be sent and summed in bfloat16 or wider, within the bound.
No kernel may reach another device: no remote copies, remote signals or barrier semaphores. Data moves between devices by JAX's collectives and lax.ppermute only.
A program may use at most 64 MiB of HBM per device.

v0:
```python
import math

import jax
import jax.numpy as jnp
from jax import lax
from jax.sharding import PartitionSpec as P

H1 = 512
W1 = 512
H2 = 256
W2 = 256


epsilon = 1e-06


def tables(length):
    indices = jnp.arange(length, dtype=jnp.int32)
    product = indices[:, None] * indices[None, :] % length
    angles = product.astype(jnp.float32) * (2.0 * math.pi / length)
    factor = 1.0 / math.sqrt(length)
    return (
        (jnp.cos(angles) * factor).astype(jnp.bfloat16),
        (jnp.sin(angles) * factor).astype(jnp.bfloat16),
    )


def contract(pattern, first_op, second_op):
    return jnp.einsum(pattern, first_op, second_op, preferred_element_type=jnp.float32)


def layer_normalize(entry_values, gains):
    center = entry_values - jnp.mean(entry_values, axis=1, keepdims=True)
    spread = jnp.mean(center * center, axis=1, keepdims=True)
    return center * lax.rsqrt(spread + epsilon) * gains[None, :, None, None]


def norm_pullback_step(entry_values, gains, upstream):
    _, pullback = jax.vjp(lambda inner_vals: layer_normalize(inner_vals, gains), entry_values)
    return pullback(upstream.astype(jnp.float32))[0]


def spectrum(entry_values, row_tab, col_tab):
    row_cos, row_sin = row_tab
    col_cos, col_sin = col_tab
    columns = lax.all_to_all(entry_values, "row", split_axis=1, concat_axis=2, tiled=True)
    half_real = contract("kh,bchw->bckw", row_cos, columns).astype(jnp.bfloat16)
    half_imag = (-contract("kh,bchw->bckw", row_sin, columns)).astype(jnp.bfloat16)
    half_real, half_imag = (
        lax.all_to_all(half_real, "col", split_axis=2, concat_axis=3, tiled=True),
        lax.all_to_all(half_imag, "col", split_axis=2, concat_axis=3, tiled=True),
    )
    spec_real = contract("bchw,wk->bchk", half_real, col_cos) + contract(
        "bchw,wk->bchk", half_imag, col_sin
    )
    spec_imag = contract("bchw,wk->bchk", half_imag, col_cos) - contract(
        "bchw,wk->bchk", half_real, col_sin
    )
    return (spec_real, spec_imag)


def inverse(real_part, imag_part, row_tab, col_tab):
    row_cos, row_sin = row_tab
    col_cos, col_sin = col_tab
    rot_real = (
        contract("bchk,kw->bchw", real_part, col_cos)
        - contract("bchk,kw->bchw", imag_part, col_sin)
    ).astype(jnp.bfloat16)
    rot_imag = (
        contract("bchk,kw->bchw", imag_part, col_cos)
        + contract("bchk,kw->bchw", real_part, col_sin)
    ).astype(jnp.bfloat16)
    rot_real, rot_imag = (
        lax.all_to_all(rot_real, "col", split_axis=3, concat_axis=2, tiled=True),
        lax.all_to_all(rot_imag, "col", split_axis=3, concat_axis=2, tiled=True),
    )
    result = contract("hk,bckw->bchw", row_cos, rot_real) - contract(
        "hk,bckw->bchw", row_sin, rot_imag
    )
    return lax.all_to_all(
        result.astype(jnp.bfloat16), "row", split_axis=2, concat_axis=1, tiled=True
    )


def filtered(weights, spec_real, spec_imag):
    return (
        (weights[0] * spec_real - weights[1] * spec_imag).astype(jnp.bfloat16),
        (weights[0] * spec_imag + weights[1] * spec_real).astype(jnp.bfloat16),
    )


def filtered_back(weights, grad_real, grad_imag):
    return (
        (weights[0] * grad_real + weights[1] * grad_imag).astype(jnp.bfloat16),
        (weights[0] * grad_imag - weights[1] * grad_real).astype(jnp.bfloat16),
    )


def filter_grad(grad_real, grad_imag, spec_real, spec_imag):
    first_part = jnp.sum(grad_real * spec_real + grad_imag * spec_imag, axis=0)
    second_part = jnp.sum(grad_imag * spec_real - grad_real * spec_imag, axis=0)
    return jnp.stack([first_part, second_part])


def offset_table(cols_dev):
    half_cols = cols_dev // 2
    target = jnp.arange(2 * cols_dev, dtype=jnp.int32)
    row_off = target // cols_dev
    rest = target % cols_dev
    col_off = rest // half_cols
    inner = rest % half_cols
    source = row_off * cols_dev + 2 * inner + col_off
    place = jnp.arange(2 * cols_dev, dtype=jnp.int32)
    return (place[:, None] == source[None, :]).astype(jnp.float32)


def strided_reduce(entry_values, weight_matrix):
    images_dev, channels, rows_dev, cols_dev = entry_values.shape
    outputs = weight_matrix.shape[0]
    merged = entry_values.reshape(images_dev, channels, rows_dev // 2, 2 * cols_dev)
    placed = jnp.einsum(
        "bcis,st->bcit",
        merged,
        offset_table(cols_dev).astype(jnp.bfloat16),
        preferred_element_type=jnp.float32,
    ).astype(jnp.bfloat16)
    placed = placed.reshape(images_dev, channels, rows_dev // 2, 4, cols_dev // 2)
    kernel = weight_matrix.reshape(outputs, 4, channels)
    return jnp.einsum("oqc,bciqj->boij", kernel, placed, preferred_element_type=jnp.float32).astype(
        jnp.bfloat16
    )


def upsample(upstream, weight_matrix):
    images_dev, outputs, rows_half, cols_half = upstream.shape
    channels = weight_matrix.shape[1] // 4
    kernel = weight_matrix.reshape(outputs, 4, channels)
    patches = jnp.einsum("oqc,boij->bciqj", kernel, upstream, preferred_element_type=jnp.float32)
    patches = patches.reshape(images_dev, channels, rows_half, 8 * cols_half // 2)
    spread_back = jnp.einsum(
        "bcit,st->bcis", patches, offset_table(2 * cols_half), precision=lax.Precision.HIGHEST
    )
    return spread_back.reshape(images_dev, channels, 2 * rows_half, 2 * cols_half).astype(
        jnp.bfloat16
    )


def shards(images, gain_first, filter_first, reduce_weight, gain_second, filter_second, grad_out):
    rows_one = tables(H1)
    cols_one = tables(W1)
    rows_two = tables(H2)
    cols_two = tables(W2)
    pixels_wide = images.astype(jnp.float32)
    norm_one = layer_normalize(pixels_wide, gain_first).astype(jnp.bfloat16)
    spec_one_r, spec_one_i = spectrum(norm_one, rows_one, cols_one)
    mixed_r, mixed_i = filtered(filter_first, spec_one_r, spec_one_i)
    mixed_one = inverse(mixed_r, mixed_i, rows_one, cols_one)
    first_filter_section = (pixels_wide + mixed_one.astype(jnp.float32)).astype(jnp.bfloat16)
    reduced_grid = strided_reduce(first_filter_section, reduce_weight)
    down_wide = reduced_grid.astype(jnp.float32)
    norm_two = layer_normalize(down_wide, gain_second).astype(jnp.bfloat16)
    spec_two_r, spec_two_i = spectrum(norm_two, rows_two, cols_two)
    grad_two_r, grad_two_i = spectrum(grad_out, rows_two, cols_two)
    term_two = filter_grad(grad_two_r, grad_two_i, spec_two_r, spec_two_i)
    dspec_r, dspec_i = filtered_back(filter_second, grad_two_r, grad_two_i)
    grad_norm_two = inverse(dspec_r, dspec_i, rows_two, cols_two)
    grad_down = (
        grad_out.astype(jnp.float32) + norm_pullback_step(down_wide, gain_second, grad_norm_two)
    ).astype(jnp.bfloat16)
    grad_section = upsample(grad_down, reduce_weight)
    grad_one_r, grad_one_i = spectrum(grad_section, rows_one, cols_one)
    term_one = filter_grad(grad_one_r, grad_one_i, spec_one_r, spec_one_i)
    dspec_one_r, dspec_one_i = filtered_back(filter_first, grad_one_r, grad_one_i)
    grad_norm_one = inverse(dspec_one_r, dspec_one_i, rows_one, cols_one)
    grad_images = (
        grad_section.astype(jnp.float32)
        + norm_pullback_step(pixels_wide, gain_first, grad_norm_one)
    ).astype(jnp.bfloat16)
    grad_first, grad_second = (
        lax.psum_scatter(
            term_one.astype(jnp.bfloat16), "rep", scatter_dimension=3, tiled=True
        ).astype(jnp.float32),
        lax.psum_scatter(
            term_two.astype(jnp.bfloat16), "rep", scatter_dimension=3, tiled=True
        ).astype(jnp.float32),
    )
    return (grad_images, grad_first, grad_second)


def solution(mesh):
    placed = (
        P("rep", None, "row", "col"),
        P(),
        P(None, "row", "col", None),
        P(),
        P(),
        P(None, "row", "col", None),
        P("rep", None, "row", "col"),
    )
    return jax.shard_map(
        shards,
        mesh=mesh,
        in_specs=placed,
        out_specs=(
            P("rep", None, "row", "col"),
            P(None, "row", "col", "rep"),
            P(None, "row", "col", "rep"),
        ),
        check_vma=False,
    )
```

profile of v0, /device:TPU:16, one launch (start us, length us, event | category | flops | bytes accessed | tf_op | source)
XLA Modules:
  0.0 613.1 jit_solution(10867213268537306109)
XLA Ops:
  9.4 9.2 %all-to-all-start = ((bf16[32,2,1536]{2,1,0:T(2,128)(2,1)}), bf16[32,2,1536]{2,1,0:T(2,128)(2,1)S(1)}, u32[]{:S(2)}, u32[]{:S(2)}) async-start(bf16[32,2,1536]{2,1,0:T(2,128)(2,1)} %reshape.564), calls=%async_computation | async-start | bytes 393216 | tf_op jit(solution)/shard_map/all_to_all | solution.py:46
  18.7 7.6 %all-to-all-done = bf16[32,2,1536]{2,1,0:T(2,128)(2,1)S(1)} async-done(((bf16[32,2,1536]{2,1,0:T(2,128)(2,1)}), bf16[32,2,1536]{2,1,0:T(2,128)(2,1)S(1)}, u32[]{:S(2)}, u32[]{:S(2)}) %all-to-all-start) | async-done | bytes 196640 | tf_op jit(solution)/shard_map/all_to_all | solution.py:46
  29.5 12.1 %all-to-all-start.1 = ((bf16[4,2,12288]{2,1,0:T(2,128)(2,1)}), bf16[4,2,12288]{2,1,0:T(2,128)(2,1)S(1)}, u32[]{:S(2)}, u32[]{:S(2)}) async-start(bf16[4,2,12288]{2,1,0:T(2,128)(2,1)} %reshape.568), calls=%async_computation.1 | async-start | bytes 393216 | tf_op jit(solution)/shard_map/all_to_all | solution.py:50
  42.6 15.6 %all-to-all-done.1 = bf16[4,2,12288]{2,1,0:T(2,128)(2,1)S(1)} async-done(((bf16[4,2,12288]{2,1,0:T(2,128)(2,1)}), bf16[4,2,12288]{2,1,0:T(2,128)(2,1)S(1)}, u32[]{:S(2)}, u32[]{:S(2)}) %all-to-all-start.1) | async-done | bytes 196640 | tf_op jit(solution)/shard_map/all_to_all | solution.py:50
  58.2 7.3 %all-to-all-start.6 = ((bf16[1,96,16,128]{3,2,0,1:T(8,128)(2,1)}), bf16[1,96,16,128]{3,2,0,1:T(8,128)(2,1)S(1)}, u32[]{:S(2)}, u32[]{:S(2)}) async-start(bf16[1,96,16,128]{3,2,0,1:T(8,128)(2,1)} %fusion.96), calls=%async_computation.6 | async-start | bytes 786432 | tf_op jit(solution)/shard_map/all_to_all | solution.py:46
  68.1 9.3 %all-to-all-done.6 = bf16[1,96,16,128]{3,2,0,1:T(8,128)(2,1)S(1)} async-done(((bf16[1,96,16,128]{3,2,0,1:T(8,128)(2,1)}), bf16[1,96,16,128]{3,2,0,1:T(8,128)(2,1)S(1)}, u32[]{:S(2)}, u32[]{:S(2)}) %all-to-all-start.6) | async-done | bytes 393248 | tf_op jit(solution)/shard_map/all_to_all | solution.py:46
  81.1 4.9 fusion.15
  87.1 10.2 %all-to-all-done.2 = bf16[4,2,12288]{2,1,0:T(2,128)(2,1)S(1)} async-done(((bf16[4,2,12288]{2,1,0:T(2,128)(2,1)}), bf16[4,2,12288]{2,1,0:T(2,128)(2,1)S(1)}, u32[]{:S(2)}, u32[]{:S(2)}) %all-to-all-start.2) | async-done | bytes 196640 | tf_op jit(solution)/shard_map/all_to_all | solution.py:51
  106.3 4.9 fusion.18
  112.3 15.4 %all-to-all-done.7 = bf16[1,3,512,128]{3,1,0,2:T(4,128)(2,1)S(1)} async-done(((bf16[1,3,512,128]{3,1,0,2:T(4,128)(2,1)}), bf16[1,3,512,128]{3,1,0,2:T(4,128)(2,1)S(1)}, u32[]{:S(2)}, u32[]{:S(2)}) %all-to-all-start.7) | async-done | bytes 393248 | tf_op jit(solution)/shard_map/all_to_all | solution.py:50
  127.8 6.8 %all-to-all-start.8 = ((bf16[1,3,512,128]{3,1,0,2:T(4,128)(2,1)}), bf16[1,3,512,128]{3,1,0,2:T(4,128)(2,1)S(1)}, u32[]{:S(2)}, u32[]{:S(2)}) async-start(bf16[1,3,512,128]{3,1,0,2:T(4,128)(2,1)} %copy.131), calls=%async_computation.8 | async-start | bytes 1048576 | tf_op jit(solution)/shard_map/all_to_all | solution.py:51
  143.8 14.3 %all-to-all-done.8 = bf16[1,3,512,128]{3,1,0,2:T(4,128)(2,1)S(1)} async-done(((bf16[1,3,512,128]{3,1,0,2:T(4,128)(2,1)}), bf16[1,3,512,128]{3,1,0,2:T(4,128)(2,1)S(1)}, u32[]{:S(2)}, u32[]{:S(2)}) %all-to-all-start.8) | async-done | bytes 393248 | tf_op jit(solution)/shard_map/all_to_all | solution.py:51
  158.1 11.9 %all-to-all-start.3 = ((bf16[4,2,12288]{2,1,0:T(2,128)(2,1)}), bf16[4,2,12288]{2,1,0:T(2,128)(2,1)}, u32[]{:S(2)}, u32[]{:S(2)}) async-start(bf16[4,2,12288]{2,1,0:T(2,128)(2,1)} %reshape.570), calls=%async_computation.3 | async-start | bytes 393216 | tf_op jit(solution)/shard_map/all_to_all | solution.py:74
  175.2 4.6 fusion.87
  179.8 4.8 convolution_subtract_fusion.5
  184.6 4.8 convolution_add_fusion.3
  189.4 12.2 %all-to-all-start.4 = ((bf16[4,2,12288]{2,1,0:T(2,128)(2,1)}), bf16[4,2,12288]{2,1,0:T(2,128)(2,1)}, u32[]{:S(2)}, u32[]{:S(2)}) async-start(bf16[4,2,12288]{2,1,0:T(2,128)(2,1)} %reshape.572), calls=%async_computation.4 | async-start | bytes 393216 | tf_op jit(solution)/shard_map/all_to_all | solution.py:75
  206.8 4.9 fusion.13
  212.8 5.6 all-to-all-done.4
  218.4 6.4 %all-to-all-start.10 = ((bf16[1,3,128,512]{2,1,0,3:T(4,128)(2,1)}), bf16[1,3,128,512]{2,1,0,3:T(4,128)(2,1)S(1)}, u32[]{:S(2)}, u32[]{:S(2)}) async-start(bf16[1,3,128,512]{2,1,0,3:T(4,128)(2,1)} %copy.135), calls=%async_computation.10 | async-start | bytes 1048576 | tf_op jit(solution)/shard_map/all_to_all | solution.py:75
  229.4 4.9 fusion.14
  235.4 10.0 %all-to-all-done.10 = bf16[1,3,128,512]{2,1,0,3:T(4,128)(2,1)S(1)} async-done(((bf16[1,3,128,512]{2,1,0,3:T(4,128)(2,1)}), bf16[1,3,128,512]{2,1,0,3:T(4,128)(2,1)S(1)}, u32[]{:S(2)}, u32[]{:S(2)}) %all-to-all-start.10) | async-done | bytes 393248 | tf_op jit(solution)/shard_map/all_to_all | solution.py:75
  245.4 13.8 %all-to-all-start.9 = ((bf16[1,3,128,512]{2,1,0,3:T(4,128)(2,1)}), bf16[1,3,128,512]{2,1,0,3:T(4,128)(2,1)S(1)}, u32[]{:S(2)}, u32[]{:S(2)}) async-start(bf16[1,3,128,512]{2,1,0,3:T(4,128)(2,1)} %copy.133), calls=%async_computation.9 | async-start | bytes 1048576 | tf_op jit(solution)/shard_map/all_to_all | solution.py:74
  274.5 17.5 %all-to-all-start.5 = ((bf16[32,2,1536]{2,1,0:T(2,128)(2,1)}), bf16[32,2,1536]{2,1,0:T(2,128)(2,1)}, u32[]{:S(2)}, u32[]{:S(2)}) async-start(bf16[32,2,1536]{2,1,0:T(2,128)(2,1)} %reshape.574), calls=%async_computation.5 | async-start | bytes 393216 | tf_op jit(solution)/shard_map/all_to_all | solution.py:80
  298.5 4.9 fusion.12
  304.5 8.1 %all-to-all-start.11 = ((bf16[1,3,512,128]{3,1,0,2:T(4,128)(2,1)}), bf16[1,3,512,128]{3,1,0,2:T(4,128)(2,1)}, u32[]{:S(2)}, u32[]{:S(2)}) async-start(bf16[1,3,512,128]{3,1,0,2:T(4,128)(2,1)} %copy.137), calls=%async_computation.11 | async-start | bytes 1048576 | tf_op jit(solution)/shard_map/all_to_all | solution.py:80
  314.6 12.6 %all-to-all-done.11 = bf16[1,3,512,128]{3,1,0,2:T(4,128)(2,1)} async-done(((bf16[1,3,512,128]{3,1,0,2:T(4,128)(2,1)}), bf16[1,3,512,128]{3,1,0,2:T(4,128)(2,1)}, u32[]{:S(2)}, u32[]{:S(2)}) %all-to-all-start.11) | async-done | bytes 393248 | tf_op jit(solution)/shard_map/all_to_all | solution.py:80
  337.2 5.8 all-to-all-start.12
  344.3 10.7 %all-to-all-done.12 = bf16[1,96,16,128]{3,2,0,1:T(8,128)(2,1)S(1)} async-done(((bf16[1,96,16,128]{3,2,0,1:T(8,128)(2,1)}), bf16[1,96,16,128]{3,2,0,1:T(8,128)(2,1)S(1)}, u32[]{:S(2)}, u32[]{:S(2)}) %all-to-all-start.12) | async-done | bytes 393248 | tf_op jit(solution)/shard_map/all_to_all | solution.py:46
  355.0 5.8 all-to-all-start.18
  360.9 4.9 fusion.16
  372.0 5.4 fusion.17
  378.5 26.1 %all-to-all-done.13 = bf16[1,3,512,128]{3,1,0,2:T(4,128)(2,1)S(1)} async-done(((bf16[1,3,512,128]{3,1,0,2:T(4,128)(2,1)}), bf16[1,3,512,128]{3,1,0,2:T(4,128)(2,1)S(1)}, u32[]{:S(2)}, u32[]{:S(2)}) %all-to-all-start.13) | async-done | bytes 393248 | tf_op jit(solution)/shard_map/all_to_all | solution.py:50
  420.8 10.0 %all-to-all-done.14 = bf16[1,3,512,128]{3,1,0,2:T(4,128)(2,1)S(1)} async-done(((bf16[1,3,512,128]{3,1,0,2:T(4,128)(2,1)}), bf16[1,3,512,128]{3,1,0,2:T(4,128)(2,1)S(1)}, u32[]{:S(2)}, u32[]{:S(2)}) %all-to-all-start.14) | async-done | bytes 393248 | tf_op jit(solution)/shard_map/all_to_all | solution.py:51
  430.8 9.4 %all-to-all-start.19 = ((bf16[4,2,12288]{2,1,0:T(2,128)(2,1)}), bf16[4,2,12288]{2,1,0:T(2,128)(2,1)}, u32[]{:S(2)}, u32[]{:S(2)}) async-start(bf16[4,2,12288]{2,1,0:T(2,128)(2,1)} %reshape.580), calls=%async_computation.19 | async-start | bytes 393216 | tf_op jit(solution)/shard_map/all_to_all | solution.py:50
  450.1 4.8 convolution_subtract_fusion.2
  454.9 4.8 convolution_add_fusion.1
  459.7 12.5 %all-to-all-start.20 = ((bf16[4,2,12288]{2,1,0:T(2,128)(2,1)}), bf16[4,2,12288]{2,1,0:T(2,128)(2,1)}, u32[]{:S(2)}, u32[]{:S(2)}) async-start(bf16[4,2,12288]{2,1,0:T(2,128)(2,1)} %reshape.578), calls=%async_computation.20 | async-start | bytes 393216 | tf_op jit(solution)/shard_map/all_to_all | solution.py:51
  477.4 4.9 fusion.10
  487.7 7.7 %all-to-all-start.16 = ((bf16[1,3,128,512]{2,1,0,3:T(4,128)(2,1)}), bf16[1,3,128,512]{2,1,0,3:T(4,128)(2,1)S(1)}, u32[]{:S(2)}, u32[]{:S(2)}) async-start(bf16[1,3,128,512]{2,1,0,3:T(4,128)(2,1)} %copy.154), calls=%async_computation.16 | async-start | bytes 1048576 | tf_op jit(solution)/shard_map/all_to_all | solution.py:75
  501.4 4.6 fusion.72
  506.1 4.9 fusion.11
  512.1 10.4 %all-to-all-done.16 = bf16[1,3,128,512]{2,1,0,3:T(4,128)(2,1)S(1)} async-done(((bf16[1,3,128,512]{2,1,0,3:T(4,128)(2,1)}), bf16[1,3,128,512]{2,1,0,3:T(4,128)(2,1)S(1)}, u32[]{:S(2)}, u32[]{:S(2)}) %all-to-all-start.16) | async-done | bytes 393248 | tf_op jit(solution)/shard_map/all_to_all | solution.py:75
  522.5 6.6 %all-to-all-start.15 = ((bf16[1,3,128,512]{2,1,0,3:T(4,128)(2,1)}), bf16[1,3,128,512]{2,1,0,3:T(4,128)(2,1)}, u32[]{:S(2)}, u32[]{:S(2)}) async-start(bf16[1,3,128,512]{2,1,0,3:T(4,128)(2,1)} %copy.152), calls=%async_computation.15 | async-start | bytes 1048576 | tf_op jit(solution)/shard_map/all_to_all | solution.py:74
  540.7 12.0 %all-to-all-done.15 = bf16[1,3,128,512]{2,1,0,3:T(4,128)(2,1)} async-done(((bf16[1,3,128,512]{2,1,0,3:T(4,128)(2,1)}), bf16[1,3,128,512]{2,1,0,3:T(4,128)(2,1)}, u32[]{:S(2)}, u32[]{:S(2)}) %all-to-all-start.15) | async-done | bytes 393248 | tf_op jit(solution)/shard_map/all_to_all | solution.py:74
  558.9 4.9 fusion.9
  564.9 8.7 %all-to-all-start.17 = ((bf16[1,3,512,128]{3,1,0,2:T(4,128)(2,1)}), bf16[1,3,512,128]{3,1,0,2:T(4,128)(2,1)S(1)}, u32[]{:S(2)}, u32[]{:S(2)}) async-start(bf16[1,3,512,128]{3,1,0,2:T(4,128)(2,1)} %copy.156), calls=%async_computation.17 | async-start | bytes 1048576 | tf_op jit(solution)/shard_map/all_to_all | solution.py:80
  575.8 25.1 %reduce-scatter.7.cloned.1.call-done = bf16[128,768]{1,0:T(8,128)(2,1)} async-done(((bf16[512,768]{1,0:T(8,128)(2,1)}), bf16[128,768]{1,0:T(8,128)(2,1)}) %reduce-scatter.7.cloned.1.call-update) | async-done | bytes 196624
  (246 shorter events, 162.7 us)
Async XLA Ops:
  7.2 11.4 %copy-start = (bf16[1,96,16,128]{3,2,1,0:T(8,128)(2,1)S(1)}, bf16[1,96,16,128]{3,2,1,0:T(8,128)(2,1)}, u32[]{:S(2)}) copy-start(bf16[1,96,16,128]{3,2,1,0:T(8,128)(2,1)} %param.7) | copy-start | bytes 1179652
  9.4 17.0 %all-to-all-start = ((bf16[32,2,1536]{2,1,0:T(2,128)(2,1)}), bf16[32,2,1536]{2,1,0:T(2,128)(2,1)S(1)}, u32[]{:S(2)}, u32[]{:S(2)}) async-start(bf16[32,2,1536]{2,1,0:T(2,128)(2,1)} %reshape.564), calls=%async_computation | async-start | bytes 393216 | tf_op jit(solution)/shard_map/all_to_all | solution.py:46
  28.1 13.6 %copy-start.37 = (f32[96]{0:T(128)S(1)}, f32[96]{0:T(128)}, u32[]{:S(2)}) copy-start(f32[96]{0:T(128)} %param.8) | copy-start | bytes 1156
  29.5 28.7 %all-to-all-start.1 = ((bf16[4,2,12288]{2,1,0:T(2,128)(2,1)}), bf16[4,2,12288]{2,1,0:T(2,128)(2,1)S(1)}, u32[]{:S(2)}, u32[]{:S(2)}) async-start(bf16[4,2,12288]{2,1,0:T(2,128)(2,1)} %reshape.568), calls=%async_computation.1 | async-start | bytes 393216 | tf_op jit(solution)/shard_map/all_to_all | solution.py:50
  41.7 25.1 %copy-start.33 = (f32[16,128]{1,0:T(8,128)}, f32[16,128]{1,0:T(8,128)S(1)}, u32[]{:S(2)}) copy-start(f32[16,128]{1,0:T(8,128)S(1)} %fusion.41) | copy-start | bytes 24580
  58.2 19.2 %all-to-all-start.6 = ((bf16[1,96,16,128]{3,2,0,1:T(8,128)(2,1)}), bf16[1,96,16,128]{3,2,0,1:T(8,128)(2,1)S(1)}, u32[]{:S(2)}, u32[]{:S(2)}) async-start(bf16[1,96,16,128]{3,2,0,1:T(8,128)(2,1)} %fusion.96), calls=%async_computation.6 | async-start | bytes 786432 | tf_op jit(solution)/shard_map/all_to_all | solution.py:46
  77.4 19.8 %all-to-all-start.2 = ((bf16[4,2,12288]{2,1,0:T(2,128)(2,1)}), bf16[4,2,12288]{2,1,0:T(2,128)(2,1)S(1)}, u32[]{:S(2)}, u32[]{:S(2)}) async-start(bf16[4,2,12288]{2,1,0:T(2,128)(2,1)} %reshape.566), calls=%async_computation.2 | async-start | bytes 393216 | tf_op jit(solution)/shard_map/all_to_all | solution.py:51
  97.3 30.5 %all-to-all-start.7 = ((bf16[1,3,512,128]{3,1,0,2:T(4,128)(2,1)}), bf16[1,3,512,128]{3,1,0,2:T(4,128)(2,1)S(1)}, u32[]{:S(2)}, u32[]{:S(2)}) async-start(bf16[1,3,512,128]{3,1,0,2:T(4,128)(2,1)} %copy.128), calls=%async_computation.7 | async-start | bytes 1048576 | tf_op jit(solution)/shard_map/all_to_all | solution.py:50
  106.3 29.4 %copy-start.10 = (f32[6,64,256]{2,1,0:T(8,128)}, f32[6,64,256]{2,1,0:T(8,128)S(1)}, u32[]{:S(2)}) copy-start(f32[6,64,256]{2,1,0:T(8,128)S(1)} %convolution_subtract_fusion.9) | copy-start | bytes 1179652
  111.3 24.5 %copy-start.16 = (f32[2,6,64,256]{3,2,1,0:T(8,128)S(1)}, f32[2,6,64,256]{3,2,1,0:T(8,128)}, u32[]{:S(2)}) copy-start(f32[2,6,64,256]{3,2,1,0:T(8,128)} %param.12) | copy-start | bytes 2359300
  127.8 30.3 %all-to-all-start.8 = ((bf16[1,3,512,128]{3,1,0,2:T(4,128)(2,1)}), bf16[1,3,512,128]{3,1,0,2:T(4,128)(2,1)S(1)}, u32[]{:S(2)}, u32[]{:S(2)}) async-start(bf16[1,3,512,128]{3,1,0,2:T(4,128)(2,1)} %copy.131), calls=%async_computation.8 | async-start | bytes 1048576 | tf_op jit(solution)/shard_map/all_to_all | solution.py:51
  158.1 31.3 %all-to-all-start.3 = ((bf16[4,2,12288]{2,1,0:T(2,128)(2,1)}), bf16[4,2,12288]{2,1,0:T(2,128)(2,1)}, u32[]{:S(2)}, u32[]{:S(2)}) async-start(bf16[4,2,12288]{2,1,0:T(2,128)(2,1)} %reshape.570), calls=%async_computation.3 | async-start | bytes 393216 | tf_op jit(solution)/shard_map/all_to_all | solution.py:74
  179.8 4.8 copy-start.21
  184.6 17.1 %copy-start.2 = (f32[3,128,512]{2,1,0:T(8,128)}, f32[3,128,512]{2,1,0:T(8,128)S(1)}, u32[]{:S(2)}) copy-start(f32[3,128,512]{2,1,0:T(8,128)S(1)} %convolution_subtract_fusion.5) | copy-start | bytes 2359300
  184.6 17.1 %copy-start.1 = (f32[2,3,128,512]{3,2,1,0:T(8,128)S(1)}, f32[2,3,128,512]{3,2,1,0:T(8,128)}, u32[]{:S(2)}) copy-start(f32[2,3,128,512]{3,2,1,0:T(8,128)} %param.9) | copy-start | bytes 4718596
  189.4 12.7 %copy-start.4 = (f32[3,128,512]{2,1,0:T(8,128)}, f32[3,128,512]{2,1,0:T(8,128)S(1)}, u32[]{:S(2)}) copy-start(f32[3,128,512]{2,1,0:T(8,128)S(1)} %convolution_add_fusion.3) | copy-start | bytes 2359300
  189.4 29.0 %all-to-all-start.4 = ((bf16[4,2,12288]{2,1,0:T(2,128)(2,1)}), bf16[4,2,12288]{2,1,0:T(2,128)(2,1)}, u32[]{:S(2)}, u32[]{:S(2)}) async-start(bf16[4,2,12288]{2,1,0:T(2,128)(2,1)} %reshape.572), calls=%async_computation.4 | async-start | bytes 393216 | tf_op jit(solution)/shard_map/all_to_all | solution.py:75
  202.1 4.7 copy-start.28
  202.1 4.7 copy-start.30
  211.7 13.1 %copy-start.31 = (bf16[3,128,512]{2,1,0:T(8,128)(2,1)S(1)}, bf16[3,128,512]{2,1,0:T(8,128)(2,1)}, u32[]{:S(2)}) copy-start(bf16[3,128,512]{2,1,0:T(8,128)(2,1)} %copy-done.30) | copy-start | bytes 1179652
  218.4 27.0 %all-to-all-start.10 = ((bf16[1,3,128,512]{2,1,0,3:T(4,128)(2,1)}), bf16[1,3,128,512]{2,1,0,3:T(4,128)(2,1)S(1)}, u32[]{:S(2)}, u32[]{:S(2)}) async-start(bf16[1,3,128,512]{2,1,0,3:T(4,128)(2,1)} %copy.135), calls=%async_computation.10 | async-start | bytes 1048576 | tf_op jit(solution)/shard_map/all_to_all | solution.py:75
  245.4 29.1 %all-to-all-start.9 = ((bf16[1,3,128,512]{2,1,0,3:T(4,128)(2,1)}), bf16[1,3,128,512]{2,1,0,3:T(4,128)(2,1)S(1)}, u32[]{:S(2)}, u32[]{:S(2)}) async-start(bf16[1,3,128,512]{2,1,0,3:T(4,128)(2,1)} %copy.133), calls=%async_computation.9 | async-start | bytes 1048576 | tf_op jit(solution)/shard_map/all_to_all | solution.py:74
  274.5 30.0 %all-to-all-start.5 = ((bf16[32,2,1536]{2,1,0:T(2,128)(2,1)}), bf16[32,2,1536]{2,1,0:T(2,128)(2,1)}, u32[]{:S(2)}, u32[]{:S(2)}) async-start(bf16[32,2,1536]{2,1,0:T(2,128)(2,1)} %reshape.574), calls=%async_computation.5 | async-start | bytes 393216 | tf_op jit(solution)/shard_map/all_to_all | solution.py:80
  303.4 9.2 %copy-start.32 = (bf16[192,384]{1,0:T(8,128)(2,1)S(1)}, bf16[192,384]{1,0:T(8,128)(2,1)}, u32[]{:S(2)}) copy-start(bf16[192,384]{1,0:T(8,128)(2,1)} %param.10) | copy-start | bytes 442372
  304.5 22.7 %all-to-all-start.11 = ((bf16[1,3,512,128]{3,1,0,2:T(4,128)(2,1)}), bf16[1,3,512,128]{3,1,0,2:T(4,128)(2,1)}, u32[]{:S(2)}, u32[]{:S(2)}) async-start(bf16[1,3,512,128]{3,1,0,2:T(4,128)(2,1)} %copy.137), calls=%async_computation.11 | async-start | bytes 1048576 | tf_op jit(solution)/shard_map/all_to_all | solution.py:80
  312.8 18.3 %copy-start.8 = (bf16[192,4,96]{2,1,0:T(4,128)(2,1)}, bf16[192,4,96]{2,1,0:T(4,128)(2,1)S(1)}, u32[]{:S(2)}) copy-start(bf16[192,4,96]{2,1,0:T(4,128)(2,1)S(1)} %reshape.526) | copy-start | bytes 442372
  312.8 15.8 %copy-start.39 = (s32[256]{0:T(256)}, s32[256]{0:T(256)S(1)}, u32[]{:S(2)}) copy-start(s32[256]{0:T(256)S(1)} %fusion.163) | copy-start | bytes 3076
  334.6 8.4 %copy-start.15 = (bf16[1,192,8,64]{1,3,2,0:T(8,128)(2,1)S(1)}, bf16[1,192,8,64]{1,3,2,0:T(8,128)(2,1)}, u32[]{:S(2)}) copy-start(bf16[1,192,8,64]{1,3,2,0:T(8,128)(2,1)} %get-tuple-element.15) | copy-start | bytes 589828
  337.2 17.8 %all-to-all-start.12 = ((bf16[1,96,16,128]{3,2,0,1:T(8,128)(2,1)}), bf16[1,96,16,128]{3,2,0,1:T(8,128)(2,1)S(1)}, u32[]{:S(2)}, u32[]{:S(2)}) async-start(bf16[1,96,16,128]{3,2,0,1:T(8,128)(2,1)} %bitcast.81), calls=%async_computation.12 | async-start | bytes 786432 | tf_op jit(solution)/shard_map/all_to_all | solution.py:46
  355.0 13.5 %all-to-all-start.18 = ((bf16[32,2,1536]{2,1,0:T(2,128)(2,1)}), bf16[32,2,1536]{2,1,0:T(2,128)(2,1)S(1)}, u32[]{:S(2)}, u32[]{:S(2)}) async-start(bf16[32,2,1536]{2,1,0:T(2,128)(2,1)} %reshape.576), calls=%async_computation.18 | async-start | bytes 393216 | tf_op jit(solution)/shard_map/all_to_all | solution.py:46
  360.9 4.9 copy-start.18
  368.5 36.0 %all-to-all-start.13 = ((bf16[1,3,512,128]{3,1,0,2:T(4,128)(2,1)}), bf16[1,3,512,128]{3,1,0,2:T(4,128)(2,1)S(1)}, u32[]{:S(2)}, u32[]{:S(2)}) async-start(bf16[1,3,512,128]{3,1,0,2:T(4,128)(2,1)} %copy.147), calls=%async_computation.13 | async-start | bytes 1048576 | tf_op jit(solution)/shard_map/all_to_all | solution.py:50
  404.5 26.3 %all-to-all-start.14 = ((bf16[1,3,512,128]{3,1,0,2:T(4,128)(2,1)}), bf16[1,3,512,128]{3,1,0,2:T(4,128)(2,1)S(1)}, u32[]{:S(2)}, u32[]{:S(2)}) async-start(bf16[1,3,512,128]{3,1,0,2:T(4,128)(2,1)} %copy.150), calls=%async_computation.14 | async-start | bytes 1048576 | tf_op jit(solution)/shard_map/all_to_all | solution.py:51
  430.8 28.9 %all-to-all-start.19 = ((bf16[4,2,12288]{2,1,0:T(2,128)(2,1)}), bf16[4,2,12288]{2,1,0:T(2,128)(2,1)}, u32[]{:S(2)}, u32[]{:S(2)}) async-start(bf16[4,2,12288]{2,1,0:T(2,128)(2,1)} %reshape.580), calls=%async_computation.19 | async-start | bytes 393216 | tf_op jit(solution)/shard_map/all_to_all | solution.py:50
  440.8 4.7 copy-start.22
  440.8 4.7 copy-start.17
  450.1 4.8 copy-start.23
  454.9 17.3 %copy-start.6 = (f32[3,128,512]{2,1,0:T(8,128)}, f32[3,128,512]{2,1,0:T(8,128)S(1)}, u32[]{:S(2)}) copy-start(f32[3,128,512]{2,1,0:T(8,128)S(1)} %convolution_subtract_fusion.2) | copy-start | bytes 2359300
  459.7 13.0 %copy-start.7 = (f32[3,128,512]{2,1,0:T(8,128)}, f32[3,128,512]{2,1,0:T(8,128)S(1)}, u32[]{:S(2)}) copy-start(f32[3,128,512]{2,1,0:T(8,128)S(1)} %convolution_add_fusion.1) | copy-start | bytes 2359300
  459.7 27.9 %all-to-all-start.20 = ((bf16[4,2,12288]{2,1,0:T(2,128)(2,1)}), bf16[4,2,12288]{2,1,0:T(2,128)(2,1)}, u32[]{:S(2)}, u32[]{:S(2)}) async-start(bf16[4,2,12288]{2,1,0:T(2,128)(2,1)} %reshape.578), calls=%async_computation.20 | async-start | bytes 393216 | tf_op jit(solution)/shard_map/all_to_all | solution.py:51
  472.7 4.7 copy-start.24
  487.7 34.8 %all-to-all-start.16 = ((bf16[1,3,128,512]{2,1,0,3:T(4,128)(2,1)}), bf16[1,3,128,512]{2,1,0,3:T(4,128)(2,1)S(1)}, u32[]{:S(2)}, u32[]{:S(2)}) async-start(bf16[1,3,128,512]{2,1,0,3:T(4,128)(2,1)} %copy.154), calls=%async_computation.16 | async-start | bytes 1048576 | tf_op jit(solution)/shard_map/all_to_all | solution.py:75
  511.0 19.5 %copy-start.11 = (f32[6,64,256]{2,1,0:T(8,128)S(1)}, f32[6,64,256]{2,1,0:T(8,128)}, u32[]{:S(2)}) copy-start(f32[6,64,256]{2,1,0:T(8,128)} %copy-done.10) | copy-start | bytes 1179652
  511.0 19.5 %copy-start.13 = (f32[6,64,256]{2,1,0:T(8,128)S(1)}, f32[6,64,256]{2,1,0:T(8,128)}, u32[]{:S(2)}) copy-start(f32[6,64,256]{2,1,0:T(8,128)} %copy-done.12) | copy-start | bytes 1179652
  522.5 30.2 %all-to-all-start.15 = ((bf16[1,3,128,512]{2,1,0,3:T(4,128)(2,1)}), bf16[1,3,128,512]{2,1,0,3:T(4,128)(2,1)}, u32[]{:S(2)}, u32[]{:S(2)}) async-start(bf16[1,3,128,512]{2,1,0,3:T(4,128)(2,1)} %copy.152), calls=%async_computation.15 | async-start | bytes 1048576 | tf_op jit(solution)/shard_map/all_to_all | solution.py:74
  529.1 44.5 %reduce-scatter.9.cloned.1.call-start = ((), (), s32[]{:S(2)}) async-start(), calls=%async_computation.24 | async-start | bytes 491520
  536.0 64.9 %reduce-scatter.7.cloned.1.call-start = ((), (), s32[]{:S(2)}) async-start(), calls=%async_computation.23 | async-start | bytes 983040
  564.9 38.0 %all-to-all-start.17 = ((bf16[1,3,512,128]{3,1,0,2:T(4,128)(2,1)}), bf16[1,3,512,128]{3,1,0,2:T(4,128)(2,1)S(1)}, u32[]{:S(2)}, u32[]{:S(2)}) async-start(bf16[1,3,512,128]{3,1,0,2:T(4,128)(2,1)} %copy.156), calls=%async_computation.17 | async-start | bytes 1048576 | tf_op jit(solution)/shard_map/all_to_all | solution.py:80
  (16 other events, 45.0 us)
Sparse Core Ops, SparseCore 0:
  536.1 31.6 reduce-scatter.8
  570.8 29.9 reduce-scatter.6
where the time goes:
time: 621 us; the launch traced here: 613 us
  waiting for transfers between devices  202 us (33%)
  starting transfers between devices  177 us (29%)
  matrix products  144 us (23%)
  local copies, waits for them, and re-layouts  63.7 us (10%)
  between operations  15.8 us (3%)
  other arithmetic  10.5 us (2%)
    dot_general x40, matrix products, contract(): jnp.einsum(pattern, first_op, second_op, preferred_element_type=jnp.float32)  138 us
    all_to_all x4, waiting for transfers between devices, spectrum(): lax.all_to_all(half_real, 'col', split_axis=2, concat_axis=3, tiled=True)  57.1 us
    all_to_all x4, waiting for transfers between devices, spectrum(): lax.all_to_all(half_imag, 'col', split_axis=2, concat_axis=3, tiled=True)  38.8 us
    all_to_all x3, starting transfers between devices, inverse(): lax.all_to_all(result.astype(jnp.bfloat16), 'row', split_axis=2, concat_a...  34.4 us
    all_to_all x3, starting transfers between devices, inverse(): lax.all_to_all(rot_real, 'col', split_axis=3, concat_axis=2, tiled=True)  32.3 us
    all_to_all x4, waiting for transfers between devices, spectrum(): lax.all_to_all(entry_values, 'row', split_axis=1, concat_axis=2, tiled=True)  29.4 us
    all_to_all x4, starting transfers between devices, spectrum(): lax.all_to_all(half_real, 'col', split_axis=2, concat_axis=3, tiled=True)  28.7 us
    all_to_all x4, starting transfers between devices, spectrum(): lax.all_to_all(entry_values, 'row', split_axis=1, concat_axis=2, tiled=True)  28.3 us
  transfers between devices with their start and end apart: 23, of which 18 were waited for; matrix products, arithmetic and copies ran while one was open for 33% of the time, Pallas kernels for 0%

commit v1 on v0

v1 whole, which is shorter than its diff:
```python
import functools
import math

import jax
import jax.numpy as jnp
import numpy as np
from jax import lax
from jax.experimental import pallas as pl
from jax.experimental.pallas import tpu as pltpu
from jax.sharding import PartitionSpec as P

H1 = 512
H2 = 256
GROUPS = 3
COLS = 4
ROWS = 32
LANES = 128

epsilon = 1e-06

ORDER = (0, 2, 3, 1)
SWAP = ((0, 3), (3, 0), (1, 2), (2, 1))


def cos_sin(n):
    index = np.arange(n)
    angles = (index[:, None] * index[None, :] % n) * (2.0 * math.pi / n)
    factor = 1.0 / math.sqrt(n)
    return np.cos(angles) * factor, np.sin(angles) * factor


def row_table(n):
    cos, sin = cos_sin(n)
    slots = n // 8
    parts = []
    for c in range(COLS):
        k = ORDER[c] * slots + np.arange(slots)
        real, imag = cos[k], -sin[k]
        if c == 0:
            imag[0] = cos[n // 2]
        parts += [real, imag]
    return np.concatenate(parts, axis=0)


def col_tables(n):
    cos, sin = cos_sin(n)
    pair = 512 // n
    width = LANES // pair
    if pair == 1:
        return cos, sin
    out = []
    for table in (cos, sin):
        blocks = table.reshape(COLS, width, COLS, width)
        full = np.zeros((COLS, pair, width, COLS, pair, width))
        for p in range(pair):
            full[:, p, :, :, p, :] = blocks
        out.append(full.reshape(512, 512))
    return tuple(out)


def mirror_matrix(slots):
    matrix = np.zeros((2 * slots, 2 * slots))
    for s in range(slots):
        matrix[s, slots - s] = 1.0
        matrix[slots + s, (2 * slots - s) % (2 * slots)] = 1.0
    return matrix


def constant(values):
    return jnp.asarray(np.asarray(values, np.float32).astype(jnp.bfloat16))


def dot(a, b):
    return jnp.dot(a, b, preferred_element_type=jnp.float32)


def params(flops, traffic):
    return dict(
        compiler_params=pltpu.CompilerParams(vmem_limit_bytes=40 * 1024 * 1024),
        cost_estimate=pl.CostEstimate(flops=flops, bytes_accessed=traffic, transcendentals=0),
    )


def gather_rows(block, rows):
    parts = []
    for g in range(GROUPS):
        part = block[:, g * rows : (g + 1) * rows, :]
        if rows % 16:
            part = part.astype(jnp.float32)
        parts.append(part.reshape(ROWS * rows, LANES).astype(jnp.bfloat16))
    return jnp.concatenate(parts, axis=1)


def forward_rows_kernel(layout, *refs):
    x_ref, tables, out_ref = refs[0], refs[1:-1], refs[-1]
    for (n, first_in, first_out), table in zip(layout, tables):
        rows = n // ROWS
        slots = n // 8
        block = x_ref[:, first_in : first_in + GROUPS * rows, :]
        half = dot(table[...], gather_rows(block, rows)).astype(jnp.bfloat16)
        half = half.reshape(COLS, 2, slots, GROUPS * LANES)
        for part in range(2):
            for g in range(GROUPS):
                at = first_out + (part * GROUPS + g) * slots
                out_ref[:, at : at + slots, :] = half[:, part, :, g * LANES : (g + 1) * LANES]


def forward_rows(entries, sizes):
    layout, first_in, first_out = [], 0, 0
    for n in sizes:
        layout.append((n, first_in, first_out))
        first_in += GROUPS * n // ROWS
        first_out += 2 * GROUPS * n // 8
    flops = sum(2 * n * n * GROUPS * LANES for n in sizes)
    return pl.pallas_call(
        functools.partial(forward_rows_kernel, tuple(layout)),
        out_shape=jax.ShapeDtypeStruct((COLS, first_out, LANES), jnp.bfloat16),
        name="forward_rows_" + "_".join(str(n) for n in sizes),
        **params(flops, 2 << 20),
    )(entries, *[constant(row_table(n)) for n in sizes])


def inverse_rows_kernel(n, x_ref, table, out_ref):
    rows = n // ROWS
    slots = n // 8
    parts = []
    for g in range(GROUPS):
        both = [
            x_ref[:, (part * GROUPS + g) * slots : (part * GROUPS + g + 1) * slots, :].reshape(
                COLS, 1, slots, LANES
            )
            for part in range(2)
        ]
        parts.append(jnp.concatenate(both, axis=1).reshape(n, LANES))
    result = dot(table[...], jnp.concatenate(parts, axis=1))
    pieces = [
        result[:, g * LANES : (g + 1) * LANES].reshape(ROWS, rows, LANES) for g in range(GROUPS)
    ]
    out_ref[...] = jnp.concatenate(pieces, axis=1).astype(jnp.bfloat16)


def inverse_rows(entries, n):
    return pl.pallas_call(
        functools.partial(inverse_rows_kernel, n),
        out_shape=jax.ShapeDtypeStruct((ROWS, GROUPS * n // ROWS, LANES), jnp.bfloat16),
        name="inverse_rows_" + str(n),
        **params(2 * n * n * GROUPS * LANES, 2 << 20),
    )(entries, constant(row_table(n).T))


def wide(ref, first, count):
    return jnp.concatenate([ref[q, first : first + count, :] for q in range(COLS)], axis=1)


def spectrum(ref, first, slots, special, cos, sin):
    count = GROUPS * slots
    real, imag = wide(ref, first, count), wide(ref, first + count, count)
    real_cos, real_sin = dot(real, cos), dot(real, sin)
    imag_cos, imag_sin = dot(imag, cos), dot(imag, sin)
    return (
        jnp.where(special, real_cos, real_cos + imag_sin),
        jnp.where(special, -real_sin, imag_cos - real_sin),
        jnp.where(special, imag_cos, real_cos - imag_sin),
        jnp.where(special, -imag_sin, -imag_cos - real_sin),
    )


def filters(near, kept_ref, recv_ref, first, slots):
    count = GROUPS * slots
    out = []
    for part in range(2):
        kept = wide(kept_ref, first + part * count, count).astype(jnp.float32)
        recv = wide(recv_ref, first + part * count, count).astype(jnp.float32)
        out.append((jnp.where(near, kept, recv), jnp.where(near, recv, kept)))
    return out


def put_inverse(out_ref, slots, special, up, down, cos, sin):
    count = GROUPS * slots
    (up_r, up_i), (down_r, down_i) = up, down
    bf16 = jnp.bfloat16
    sum_r = jnp.where(special, up_r, up_r + down_r).astype(bf16)
    sum_i = jnp.where(special, up_i, up_i + down_i).astype(bf16)
    dif_i = jnp.where(special, down_r, up_i - down_i).astype(bf16)
    dif_r = jnp.where(special, -down_i, up_r - down_r).astype(bf16)
    rot_real = (dot(sum_r, cos) - dot(sum_i, sin)).astype(bf16)
    rot_imag = (dot(dif_i, cos) + dot(dif_r, sin)).astype(bf16)
    for q in range(COLS):
        out_ref[q, :count, :] = rot_real[:, q * LANES : (q + 1) * LANES]
        out_ref[q, count:, :] = rot_imag[:, q * LANES : (q + 1) * LANES]


def masks(col_ref, slots):
    col = col_ref[0]
    row = lax.broadcasted_iota(jnp.int32, (GROUPS * slots, 512), 0)
    return (lax.rem(row, slots) + col * slots) == 0, col < 2


def mix_forward_kernel(n, first_filter, col_ref, x_ref, kept_ref, recv_ref, cos, sin, out_ref):
    slots = n // 8
    special, near = masks(col_ref, slots)
    up_r, up_i, down_r, down_i = spectrum(x_ref, 0, slots, special, cos[...], sin[...])
    real, imag = filters(near, kept_ref, recv_ref, first_filter, slots)
    up = (real[0] * up_r - imag[0] * up_i, real[0] * up_i + imag[0] * up_r)
    down = (real[1] * down_r - imag[1] * down_i, real[1] * down_i + imag[1] * down_r)
    put_inverse(out_ref, slots, special, up, down, cos[...], sin[...])


def mix_back_kernel(
    n, first_filter, first_field, first_grad, col_ref, x_ref, g_ref, kept_ref, recv_ref,
    cos, sin, cos_back, sin_back, out_ref, grad_ref,
):
    slots = n // 8
    count = GROUPS * slots
    special, near = masks(col_ref, slots)
    field = spectrum(x_ref, first_field, slots, special, cos[...], sin[...])
    grad = spectrum(g_ref, first_grad, slots, special, cos[...], sin[...])
    real, imag = filters(near, kept_ref, recv_ref, first_filter, slots)
    sides, terms = [], []
    for side in range(2):
        g_r, g_i = grad[2 * side], grad[2 * side + 1]
        s_r, s_i = field[2 * side], field[2 * side + 1]
        sides.append((real[side] * g_r + imag[side] * g_i, real[side] * g_i - imag[side] * g_r))
        terms.append((g_r * s_r + g_i * s_i, g_i * s_r - g_r * s_i))
    put_inverse(out_ref, slots, special, sides[0], sides[1], cos_back[...], sin_back[...])
    for part in range(2):
        up, down = terms[0][part], terms[1][part]
        kept = jnp.where(near, up, down).astype(jnp.bfloat16)
        sent = jnp.where(near, down, up).astype(jnp.bfloat16)
        for q in range(COLS):
            lanes = slice(q * LANES, (q + 1) * LANES)
            grad_ref[q, part * count : (part + 1) * count, :] = kept[:, lanes]
            grad_ref[q, (2 + part) * count : (3 + part) * count, :] = sent[:, lanes]


def smem():
    return pl.BlockSpec(memory_space=pltpu.SMEM)


def vmem(count):
    return [pl.BlockSpec(memory_space=pltpu.VMEM)] * count


def mix_forward(n, col, entries, kept, recv, first_filter):
    rows = 2 * GROUPS * n // 8
    cos, sin = col_tables(n)
    return pl.pallas_call(
        functools.partial(mix_forward_kernel, n, first_filter),
        out_shape=jax.ShapeDtypeStruct((COLS, rows, LANES), jnp.bfloat16),
        in_specs=[smem()] + vmem(5),
        name="mix_forward_" + str(n),
        **params(8 * rows * 512 * 512, 4 << 20),
    )(col, entries, kept, recv, constant(cos), constant(sin))


def mix_back(n, col, entries, first_field, upstream, first_grad, kept, recv, first_filter):
    rows = 2 * GROUPS * n // 8
    cos, sin = col_tables(n)
    return pl.pallas_call(
        functools.partial(mix_back_kernel, n, first_filter, first_field, first_grad),
        out_shape=(
            jax.ShapeDtypeStruct((COLS, rows, LANES), jnp.bfloat16),
            jax.ShapeDtypeStruct((COLS, 2 * rows, LANES), jnp.bfloat16),
        ),
        in_specs=[smem()] + vmem(8),
        name="mix_back_" + str(n),
        **params(12 * rows * 512 * 512, 6 << 20),
    )(
        col, entries, upstream, kept, recv,
        constant(cos), constant(sin), constant(cos.T), constant(sin.T),
    )


def pair_lanes():
    matrix = np.zeros((2, COLS, 64, COLS, 2, 64))
    for p in range(2):
        for q in range(COLS):
            matrix[p, q, :, q, p, :] = np.eye(64)
    return matrix.reshape(512, 512)


def take_filters_kernel(first_ref, second_ref, pick_first, pick_second, lanes, kept_ref, sent_ref):
    at = 0
    for n, pick in ((H1, pick_first), (H2, pick_second)):
        slots = n // 8
        for part in range(2):
            for g in range(GROUPS):
                if n == H1:
                    rows = first_ref[part, g].astype(jnp.bfloat16)
                else:
                    pair = [second_ref[part, 2 * g + i].astype(jnp.bfloat16) for i in range(2)]
                    rows = dot(jnp.concatenate(pair, axis=1), lanes[...]).astype(jnp.bfloat16)
                rows = dot(pick[...], rows).astype(jnp.bfloat16)
                for q in range(COLS):
                    cut = slice(q * LANES, (q + 1) * LANES)
                    kept_ref[q, at : at + slots, :] = rows[:slots, cut]
                    sent_ref[q, at : at + slots, :] = rows[slots:, cut]
                at += slots


def slot_zero(block, first, slots):
    count = 2 * GROUPS * slots
    return block[first : first + count].reshape(2 * GROUPS, slots, LANES)[:, :1]


def put_slot_zero(block, zero, take, slots):
    shaped = block.reshape(2 * GROUPS, slots, LANES)
    here = (jnp.arange(slots) == 0)[None, :, None] & take
    return jnp.where(here, zero, shaped).reshape(2 * GROUPS * slots, LANES)


def take_filters(filter_first, filter_second, col, pick_first, pick_second):
    rows = 2 * GROUPS * (H1 + H2) // 8
    shape = jax.ShapeDtypeStruct((COLS, rows, LANES), jnp.bfloat16)
    kept, sent = pl.pallas_call(
        take_filters_kernel,
        out_shape=(shape, shape),
        name="take_filters",
        **params(12 * 128 * 128 * 512 * 2, 4 << 20),
    )(filter_first, filter_second, pick_first, pick_second, constant(pair_lanes()))
    quarter = lax.dynamic_index_in_dim(sent, lax.axis_index("rep"), 0, keepdims=False)
    recv = lax.ppermute(quarter, "col", SWAP)
    split = 2 * GROUPS * H1 // 8
    zero = jnp.concatenate(
        [slot_zero(quarter, 0, H1 // 8), slot_zero(quarter, split, H2 // 8)], axis=1
    )
    zero = lax.ppermute(zero, "col", ((2, 0), (3, 1)))
    near = col < 2
    recv = jnp.concatenate(
        [
            put_slot_zero(recv[:split], zero[:, :1], near, H1 // 8),
            put_slot_zero(recv[split:], zero[:, 1:], near, H2 // 8),
        ],
        axis=0,
    )
    return kept, lax.all_gather(recv, "rep", axis=0, tiled=False)


def place_grads_kernel(
    kept_first, recv_first, kept_second, recv_second, pick_first, pick_second, lanes,
    first_ref, second_ref,
):
    for n, pick, kept, recv in (
        (H1, pick_first, kept_first, recv_first),
        (H2, pick_second, kept_second, recv_second),
    ):
        slots = n // 8
        for part in range(2):
            for g in range(GROUPS):
                at = (part * GROUPS + g) * slots
                both = jnp.concatenate([kept[at : at + slots], recv[at : at + slots]], axis=0)
                rows = dot(pick[...], both)
                if n == H1:
                    first_ref[part, g] = rows
                else:
                    rows = rows.astype(jnp.bfloat16)
                    for i in range(2):
                        second_ref[part, 2 * g + i] = dot(rows, lanes[i])


def summed(terms):
    return lax.psum_scatter(terms, "rep", scatter_dimension=0, tiled=False)


def place_grads(sum_first, sum_second, col, pick_first, pick_second):
    count_first, count_second = 2 * GROUPS * H1 // 8, 2 * GROUPS * H2 // 8
    sent = jnp.concatenate([sum_first[count_first:], sum_second[count_second:]], axis=0)
    zero = jnp.concatenate(
        [slot_zero(sent, 0, H1 // 8), slot_zero(sent, count_first, H2 // 8)], axis=1
    )
    recv = lax.ppermute(sent, "col", SWAP)
    zero = lax.ppermute(zero, "col", ((0, 2), (1, 3)))
    far = col >= 2
    recv_first = put_slot_zero(recv[:count_first], zero[:, :1], far, H1 // 8)
    recv_second = put_slot_zero(recv[count_first:], zero[:, 1:], far, H2 // 8)
    lanes = np.zeros((2, 128, 64))
    lanes[0, :64] = np.eye(64)
    lanes[1, 64:] = np.eye(64)
    return pl.pallas_call(
        place_grads_kernel,
        out_shape=(
            jax.ShapeDtypeStruct((2, GROUPS, H1 // 4, LANES), jnp.float32),
            jax.ShapeDtypeStruct((2, 2 * GROUPS, H2 // 4, LANES // 2), jnp.float32),
        ),
        name="place_grads",
        **params(12 * 128 * 128 * 128 * 2, 2 << 20),
    )(
        sum_first[:count_first], recv_first, sum_second[:count_second], recv_second,
        pick_first.T, pick_second.T, constant(lanes),
    )


def layer_normalize(entry_values, gains):
    center = entry_values - jnp.mean(entry_values, axis=1, keepdims=True)
    spread = jnp.mean(center * center, axis=1, keepdims=True)
    return center * lax.rsqrt(spread + epsilon) * gains[None, :, None, None]


def norm_pullback_step(entry_values, gains, upstream):
    _, pullback = jax.vjp(lambda inner_vals: layer_normalize(inner_vals, gains), entry_values)
    return pullback(upstream.astype(jnp.float32))[0]


def offset_table(cols_dev):
    half_cols = cols_dev // 2
    target = np.arange(2 * cols_dev)
    row_off = target // cols_dev
    rest = target % cols_dev
    source = row_off * cols_dev + 2 * (rest % half_cols) + rest // half_cols
    place = np.arange(2 * cols_dev)
    return constant(place[:, None] == source[None, :])


def strided_reduce(entry_values, weight_matrix):
    images_dev, channels, rows_dev, cols_dev = entry_values.shape
    outputs = weight_matrix.shape[0]
    merged = entry_values.reshape(images_dev, channels, rows_dev // 2, 2 * cols_dev)
    placed = jnp.einsum(
        "bcis,st->bcit", merged, offset_table(cols_dev), preferred_element_type=jnp.float32
    ).astype(jnp.bfloat16)
    placed = placed.reshape(images_dev, channels, rows_dev // 2, 4, cols_dev // 2)
    kernel = weight_matrix.reshape(outputs, 4, channels)
    return jnp.einsum("oqc,bciqj->boij", kernel, placed, preferred_element_type=jnp.float32).astype(
        jnp.bfloat16
    )


def upsample(upstream, weight_matrix):
    images_dev, outputs, rows_half, cols_half = upstream.shape
    channels = weight_matrix.shape[1] // 4
    kernel = weight_matrix.reshape(outputs, 4, channels)
    patches = jnp.einsum(
        "oqc,boij->bciqj", kernel, upstream, preferred_element_type=jnp.float32
    ).astype(jnp.bfloat16)
    patches = patches.reshape(images_dev, channels, rows_half, 8 * cols_half // 2)
    spread_back = jnp.einsum(
        "bcit,st->bcis", patches, offset_table(2 * cols_half), preferred_element_type=jnp.float32
    )
    return spread_back.reshape(images_dev, channels, 2 * rows_half, 2 * cols_half).astype(
        jnp.bfloat16
    )


def pack_first(field):
    return field.reshape(ROWS, GROUPS * 16, LANES)


def unpack_first(blocks):
    return blocks.reshape(1, 96, 16, LANES)


def pack_second(field):
    pairs = field.reshape(96, 2, 8, 64).transpose(0, 2, 1, 3)
    return pairs.reshape(ROWS, GROUPS * 8, LANES)


def unpack_second(blocks):
    return blocks.reshape(96, 8, 2, 64).transpose(0, 2, 1, 3).reshape(1, 192, 8, 64)


def exchange(blocks, axis):
    return lax.all_to_all(blocks, axis, split_axis=0, concat_axis=0, tiled=True)


def shards(images, gain_first, filter_first, reduce_weight, gain_second, filter_second, grad_out):
    col = lax.axis_index("col")
    col_word = col.astype(jnp.int32).reshape(1)
    picks = [
        jnp.where(col < 2, constant(np.eye(n // 4)), constant(mirror_matrix(n // 8)))
        for n in (H1, H2)
    ]
    kept, recv = take_filters(filter_first, filter_second, col, *picks)
    second_rows = 2 * GROUPS * H1 // 8

    pixels_wide = images.astype(jnp.float32)
    norm_one = layer_normalize(pixels_wide, gain_first).astype(jnp.bfloat16)
    both = jnp.concatenate([pack_first(norm_one), pack_second(grad_out)], axis=1)
    both = exchange(forward_rows(exchange(both, "row"), (H1, H2)), "col")
    mixed = exchange(mix_forward(H1, col_word, both, kept, recv, 0), "col")
    mixed_one = unpack_first(exchange(inverse_rows(mixed, H1), "row"))

    section_one = (pixels_wide + mixed_one.astype(jnp.float32)).astype(jnp.bfloat16)
    down_wide = strided_reduce(section_one, reduce_weight).astype(jnp.float32)
    norm_two = layer_normalize(down_wide, gain_second).astype(jnp.bfloat16)
    half_two = exchange(forward_rows(exchange(pack_second(norm_two), "row"), (H2,)), "col")
    dspec_two, terms_two = mix_back(
        H2, col_word, half_two, 0, both, second_rows, kept, recv, second_rows
    )
    sum_two = summed(terms_two)
    back_two = inverse_rows(exchange(dspec_two, "col"), H2)
    grad_norm_two = unpack_second(exchange(back_two, "row"))

    grad_down = (
        grad_out.astype(jnp.float32) + norm_pullback_step(down_wide, gain_second, grad_norm_two)
    ).astype(jnp.bfloat16)
    grad_section = upsample(grad_down, reduce_weight)
    half_grad = exchange(forward_rows(exchange(pack_first(grad_section), "row"), (H1,)), "col")
    dspec_one, terms_one = mix_back(H1, col_word, both, 0, half_grad, 0, kept, recv, 0)
    sum_one = summed(terms_one)
    back_one = inverse_rows(exchange(dspec_one, "col"), H1)
    grad_norm_one = unpack_first(exchange(back_one, "row"))
    grad_images = (
        grad_section.astype(jnp.float32)
        + norm_pullback_step(pixels_wide, gain_first, grad_norm_one)
    ).astype(jnp.bfloat16)
    grad_first, grad_second = place_grads(sum_one, sum_two, col, *picks)
    return (grad_images, grad_first, grad_second)


def solution(mesh):
    placed = (
        P("rep", None, "row", "col"),
        P(),
        P(None, "row", "col", None),
        P(),
        P(),
        P(None, "row", "col", None),
        P("rep", None, "row", "col"),
    )
    return jax.shard_map(
        shards,
        mesh=mesh,
        in_specs=placed,
        out_specs=(
            P("rep", None, "row", "col"),
            P(None, "row", "col", "rep"),
            P(None, "row", "col", "rep"),
        ),
        check_vma=False,
    )
```

time: 621 us -> 382 us (0.62)
  the two profiles are of different devices: /device:TPU:16 before, /device:TPU:105 now
where the time goes in v1:
time: 382 us; the launch traced here: 380 us
  blocking collectives  148 us (39%)
  waiting for transfers between devices  93.9 us (25%)
  starting transfers between devices  74 us (19%)
  local copies, waits for them, and re-layouts  24.6 us (6%)
  between operations  14.8 us (4%)
  Pallas kernels  14.7 us (4%)
  other arithmetic  6.58 us (2%)
    all_to_all x7, blocking collectives, exchange(): return lax.all_to_all(blocks, axis, split_axis=0, concat_axis=0, tiled=True)  137 us
    all_to_all x5, starting transfers between devices, exchange(): return lax.all_to_all(blocks, axis, split_axis=0, concat_axis=0, tiled=True)  49.3 us
    all_to_all x5, waiting for transfers between devices, exchange(): return lax.all_to_all(blocks, axis, split_axis=0, concat_axis=0, tiled=True)  47.7 us
    ppermute x1, waiting for transfers between devices, take_filters(): recv = lax.ppermute(quarter, 'col', SWAP)  25.1 us
    ppermute x1, waiting for transfers between devices, place_grads(): recv = lax.ppermute(sent, 'col', SWAP)  18.2 us
    ppermute x1, starting transfers between devices, take_filters(): recv = lax.ppermute(quarter, 'col', SWAP)  13 us
    all_gather x1, blocking collectives, take_filters(): return (kept, lax.all_gather(recv, 'rep', axis=0, tiled=False))  11.5 us
    ppermute x1, starting transfers between devices, place_grads(): zero = lax.ppermute(zero, 'col', ((0, 2), (1, 3)))  8.33 us
  transfers between devices with their start and end apart: 11, of which 6 were waited for; matrix products, arithmetic and copies ran while one was open for 1% of the time, Pallas kernels for 2%

profile of v1, /device:TPU:105, one launch (start us, length us, event | category | flops | bytes accessed | tf_op | source)
XLA Modules:
  0.0 380.0 jit_solution(405549749620359443)
XLA Ops:
  7.2 1.1 convert_reduce_fusion
  8.3 1.2 fusion.8
  9.5 1.2 copy.44
  11.5 22.4 %all_to_all.60.refs_0_ = bf16[32,72,128]{2,1,0:T(8,128)(2,1)S(1)} all-to-all(bf16[32,72,128]{2,1,0:T(8,128)(2,1)S(1)} %pad_maximum_fusion), channel_id=1, replica_groups=mesh['row'=32,'col'=4,'rep'=4] {'row'}, dimensions={0} | all-to-all | bytes 1179648 | tf_op jit(solution)/shard_map/all_to_all | solution.py:462
  34.0 1.3 forward_rows_512_256.1
  35.4 12.2 %all-to-all-start.1 = ((bf16[4,576,128]{2,1,0:T(8,128)(2,1)}), bf16[4,576,128]{2,1,0:T(8,128)(2,1)S(1)}, u32[]{:S(2)}, u32[]{:S(2)}) async-start(bf16[4,576,128]{2,1,0:T(8,128)(2,1)} %forward_rows_512_256.1), calls=%async_computation.1 | async-start | bytes 1179648 | tf_op jit(solution)/shard_map/all_to_all | solution.py:462
  47.9 1.4 copy-done.5
  49.3 1.7 take_filters.1
  51.1 1.4 collective-permute-start
  52.6 13.0 %collective-permute-start.1 = (bf16[576,128]{1,0:T(8,128)(2,1)S(1)}, bf16[576,128]{1,0:T(8,128)(2,1)S(1)}, u32[]{:S(2)}, u32[]{:S(2)}) collective-permute-start(bf16[576,128]{1,0:T(8,128)(2,1)S(1)} %dynamic-slice_bitcast_fusion), channel_id=1, source_target_pairs={{0,12},{12,0},{4,8},{8,4},{1,13},{13,1},{5,9},{9,5},{2,14},{14,2},... | collective-permute-start | bytes 442376 | tf_op jit(solution)/shard_map/ppermute | solution.py:322
  65.8 1.4 collective-permute-done
  67.1 25.1 %collective-permute-done.1 = bf16[576,128]{1,0:T(8,128)(2,1)S(1)} collective-permute-done((bf16[576,128]{1,0:T(8,128)(2,1)S(1)}, bf16[576,128]{1,0:T(8,128)(2,1)S(1)}, u32[]{:S(2)}, u32[]{:S(2)}) %collective-permute-start.1) | collective-permute-done | bytes 147488 | tf_op jit(solution)/shard_map/ppermute | solution.py:322
  92.5 11.5 %all-gather = bf16[2304,128]{1,0:T(8,128)(2,1)S(1)} all-gather(bf16[576,128]{1,0:T(8,128)(2,1)S(1)} %pad_maximum_fusion.1), channel_id=2, replica_groups=mesh['row'=32,'col'=4,'rep'=4] {'rep'}, dimensions={0}, use_global_device_ids=true | all-gather | bytes 737280 | tf_op jit(solution)/shard_map/all_gather | solution.py:336
  104.0 1.0 copy-done.10
  105.1 1.5 mix_forward_512.1
  106.6 26.7 %all_to_all.61.x_ref = bf16[4,384,128]{2,1,0:T(8,128)(2,1)S(1)} all-to-all(bf16[4,384,128]{2,1,0:T(8,128)(2,1)S(1)} %mix_forward_512.1), channel_id=1, replica_groups=mesh['row'=32,'col'=4,'rep'=4] {'col'}, dimensions={0} | all-to-all | bytes 786432 | tf_op jit(solution)/shard_map/all_to_all | solution.py:462
  133.2 1.2 inverse_rows_512.2
  134.4 10.7 %all-to-all-start.3 = ((bf16[32,48,128]{2,1,0:T(8,128)(2,1)}), bf16[32,48,128]{2,1,0:T(8,128)(2,1)S(1)}, u32[]{:S(2)}, u32[]{:S(2)}) async-start(bf16[32,48,128]{2,1,0:T(8,128)(2,1)} %inverse_rows_512.2), calls=%async_computation.3 | async-start | bytes 786432 | tf_op jit(solution)/shard_map/all_to_all | solution.py:462
  145.1 1.8 reshape.327
  146.9 8.8 %all-to-all-done.3 = bf16[32,48,128]{2,1,0:T(8,128)(2,1)S(1)} async-done(((bf16[32,48,128]{2,1,0:T(8,128)(2,1)}), bf16[32,48,128]{2,1,0:T(8,128)(2,1)S(1)}, u32[]{:S(2)}, u32[]{:S(2)}) %all-to-all-start.3) | async-done | bytes 393248 | tf_op jit(solution)/shard_map/all_to_all | solution.py:462
  156.5 1.1 reshape.325
  158.3 1.3 fusion.28
  161.7 2.1 copy.53
  163.8 1.9 reshape.329
  165.7 13.9 %all_to_all.62.refs_0_ = bf16[32,24,128]{2,1,0:T(8,128)(2,1)S(1)} all-to-all(bf16[32,24,128]{2,1,0:T(8,128)(2,1)} %reshape.329), channel_id=1, replica_groups=mesh['row'=32,'col'=4,'rep'=4] {'row'}, dimensions={0} | all-to-all | bytes 393216 | tf_op jit(solution)/shard_map/all_to_all | solution.py:462
  179.9 21.2 %all_to_all.63.x_ref = bf16[4,192,128]{2,1,0:T(8,128)(2,1)S(1)} all-to-all(bf16[4,192,128]{2,1,0:T(8,128)(2,1)S(1)} %forward_rows_256.1), channel_id=1, replica_groups=mesh['row'=32,'col'=4,'rep'=4] {'col'}, dimensions={0} | all-to-all | bytes 393216 | tf_op jit(solution)/shard_map/all_to_all | solution.py:462
  201.1 1.5 mix_back_256.1
  203.4 17.4 %all_to_all.64.x_ref = bf16[4,192,128]{2,1,0:T(8,128)(2,1)S(1)} all-to-all(bf16[4,192,128]{2,1,0:T(8,128)(2,1)S(1)} %get-tuple-element.13), channel_id=1, replica_groups=mesh['row'=32,'col'=4,'rep'=4] {'col'}, dimensions={0} | all-to-all | bytes 393216 | tf_op jit(solution)/shard_map/all_to_all | solution.py:462
  221.1 17.8 %all_to_all.65 = bf16[32,24,128]{2,1,0:T(8,128)(2,1)S(1)} all-to-all(bf16[32,24,128]{2,1,0:T(8,128)(2,1)S(1)} %inverse_rows_256.1), channel_id=1, replica_groups=mesh['row'=32,'col'=4,'rep'=4] {'row'}, dimensions={0} | all-to-all | bytes 393216 | tf_op jit(solution)/shard_map/all_to_all | solution.py:462
  238.9 1.4 reshape.339
  240.3 2.1 copy.54
  242.4 1.5 copy.55
  245.0 1.3 convolution_convert_fusion
  246.3 1.4 copy.57
  248.7 17.2 %all_to_all.66.refs_0_ = bf16[32,48,128]{2,1,0:T(8,128)(2,1)S(1)} all-to-all(bf16[32,48,128]{2,1,0:T(8,128)(2,1)S(1)} %convert_element_type.158), channel_id=1, replica_groups=mesh['row'=32,'col'=4,'rep'=4] {'row'}, dimensions={0} | all-to-all | bytes 786432 | tf_op jit(solution)/shard_map/all_to_all | solution.py:462
  265.9 1.2 forward_rows_512.1
  267.1 3.5 all-to-all-start.9
  271.3 22.6 %all-to-all-done.9.g_ref = bf16[4,384,128]{2,1,0:T(8,128)(2,1)S(1)} async-done(((bf16[4,384,128]{2,1,0:T(8,128)(2,1)}), bf16[4,384,128]{2,1,0:T(8,128)(2,1)S(1)}, u32[]{:S(2)}, u32[]{:S(2)}) %all-to-all-start.9) | async-done | bytes 393248 | tf_op jit(solution)/shard_map/all_to_all | solution.py:462
  293.9 2.9 mix_back_512.1
  297.6 5.4 %all-to-all-start.10 = ((bf16[4,384,128]{2,1,0:T(8,128)(2,1)}), bf16[4,384,128]{2,1,0:T(8,128)(2,1)S(1)}, u32[]{:S(2)}, u32[]{:S(2)}) async-start(bf16[4,384,128]{2,1,0:T(8,128)(2,1)} %copy-done.14), calls=%async_computation.10 | async-start | bytes 786432 | tf_op jit(solution)/shard_map/all_to_all | solution.py:462
  303.8 16.3 %all-to-all-done.10.x_ref = bf16[4,384,128]{2,1,0:T(8,128)(2,1)S(1)} async-done(((bf16[4,384,128]{2,1,0:T(8,128)(2,1)}), bf16[4,384,128]{2,1,0:T(8,128)(2,1)S(1)}, u32[]{:S(2)}, u32[]{:S(2)}) %all-to-all-start.10) | async-done | bytes 393248 | tf_op jit(solution)/shard_map/all_to_all | solution.py:462
  320.1 1.2 inverse_rows_512.3
  321.2 17.5 %all-to-all-start.11 = ((bf16[32,48,128]{2,1,0:T(8,128)(2,1)}), bf16[32,48,128]{2,1,0:T(8,128)(2,1)S(1)}, u32[]{:S(2)}, u32[]{:S(2)}) async-start(bf16[32,48,128]{2,1,0:T(8,128)(2,1)} %inverse_rows_512.3), calls=%async_computation.11 | async-start | bytes 786432 | tf_op jit(solution)/shard_map/all_to_all | solution.py:462
  341.1 8.3 %collective-permute-start.2 = (bf16[6,2,128]{2,0,1:T(8,128)(2,1)S(1)}, bf16[6,2,128]{2,0,1:T(8,128)(2,1)S(1)}, u32[]{:S(2)}, u32[]{:S(2)}) collective-permute-start(bf16[6,2,128]{2,0,1:T(8,128)(2,1)S(1)} %pad_maximum_fusion.4), channel_id=1, source_target_pairs={{0,8},{4,12},{1,9},{5,13},{2,10},{6,14},{3,11},{7,15},{16,24},{20,... | collective-permute-start | bytes 9224 | tf_op jit(solution)/shard_map/ppermute | solution.py:372
  349.4 1.9 collective-permute-start.3
  351.4 18.2 %collective-permute-done.3 = bf16[576,128]{1,0:T(8,128)(2,1)S(1)} collective-permute-done((bf16[576,128]{1,0:T(8,128)(2,1)S(1)}, bf16[576,128]{1,0:T(8,128)(2,1)S(1)}, u32[]{:S(2)}, u32[]{:S(2)}) %collective-permute-start.3) | collective-permute-done | bytes 147488 | tf_op jit(solution)/shard_map/ppermute | solution.py:371
  369.8 1.7 place_grads.1
  372.1 1.1 add_convert_fusion
  (151 shorter events, 13.4 us)
Async XLA Ops:
  8.3 3.0 copy-start.17
  8.3 3.0 copy-start.37
  11.4 22.5 %copy-start.2 = (bf16[512,512]{1,0:T(8,128)(2,1)S(1)}, bf16[512,512]{1,0:T(8,128)(2,1)}, u32[]{:S(2)}) copy-start(bf16[512,512]{1,0:T(8,128)(2,1)} %constant.72.clone.refs_1_) | copy-start | bytes 1572868
  11.4 22.5 %copy-start.7 = (bf16[256,256]{1,0:T(8,128)(2,1)S(1)}, bf16[256,256]{1,0:T(8,128)(2,1)}, u32[]{:S(2)}) copy-start(bf16[256,256]{1,0:T(8,128)(2,1)} %constant.73.clone.refs_2_.refs_1_) | copy-start | bytes 393220
  34.0 13.6 %copy-start.35 = (bf16[64,64]{0,1:T(8,128)(2,1)S(1)}, bf16[64,64]{0,1:T(8,128)(2,1)}, u32[]{:S(2)}) copy-start(bf16[64,64]{0,1:T(8,128)(2,1)} %constant.70.clone) | copy-start | bytes 24580
  34.0 13.6 %copy-start.36 = (bf16[64,64]{0,1:T(8,128)(2,1)S(1)}, bf16[64,64]{0,1:T(8,128)(2,1)}, u32[]{:S(2)}) copy-start(bf16[64,64]{0,1:T(8,128)(2,1)} %constant.69.clone) | copy-start | bytes 24580
  34.0 13.7 %copy-start.30 = (bf16[128,128]{0,1:T(8,128)(2,1)S(1)}, bf16[128,128]{0,1:T(8,128)(2,1)}, u32[]{:S(2)}) copy-start(bf16[128,128]{0,1:T(8,128)(2,1)} %constant.68.clone) | copy-start | bytes 98308
  34.0 13.7 %copy-start.31 = (bf16[128,128]{0,1:T(8,128)(2,1)S(1)}, bf16[128,128]{0,1:T(8,128)(2,1)}, u32[]{:S(2)}) copy-start(bf16[128,128]{0,1:T(8,128)(2,1)} %constant.67.clone) | copy-start | bytes 98308
  35.3 12.5 %copy-start.6 = (f32[2,6,64,256]{3,2,1,0:T(8,128)S(1)}, f32[2,6,64,256]{3,2,1,0:T(8,128)}, u32[]{:S(2)}) copy-start(f32[2,6,64,256]{3,2,1,0:T(8,128)} %second_ref.1) | copy-start | bytes 2359300
  35.4 12.5 %copy-start.12 = (bf16[512,512]{1,0:T(8,128)(2,1)S(1)}, bf16[512,512]{1,0:T(8,128)(2,1)}, u32[]{:S(2)}) copy-start(bf16[512,512]{1,0:T(8,128)(2,1)} %constant.71.clone.lanes) | copy-start | bytes 1572868
  35.4 68.7 %all-to-all-start.1 = ((bf16[4,576,128]{2,1,0:T(8,128)(2,1)}), bf16[4,576,128]{2,1,0:T(8,128)(2,1)S(1)}, u32[]{:S(2)}, u32[]{:S(2)}) async-start(bf16[4,576,128]{2,1,0:T(8,128)(2,1)} %forward_rows_512_256.1), calls=%async_computation.1 | async-start | bytes 1179648 | tf_op jit(solution)/shard_map/all_to_all | solution.py:462
  47.9 1.4 copy-start.5
  51.0 53.0 %copy-start.8 = (bf16[512,512]{1,0:T(8,128)(2,1)S(1)}, bf16[512,512]{1,0:T(8,128)(2,1)}, u32[]{:S(2)}) copy-start(bf16[512,512]{1,0:T(8,128)(2,1)} %constant.75.clone.sin.sin_back) | copy-start | bytes 1572868
  51.1 16.0 %collective-permute-start = (bf16[6,2,128]{2,0,1:T(8,128)(2,1)S(1)}, bf16[6,2,128]{2,0,1:T(8,128)(2,1)S(1)}, u32[]{:S(2)}, u32[]{:S(2)}) collective-permute-start(bf16[6,2,128]{2,0,1:T(8,128)(2,1)S(1)} %pad_maximum_fusion.3), channel_id=1, source_target_pairs={{8,0},{12,4},{9,1},{13,5},{10,2},{14,6},{11,3},{15,7},{24,16},{28,... | collective-permute-start | bytes 9224 | tf_op jit(solution)/shard_map/ppermute | solution.py:327
  52.6 39.7 %collective-permute-start.1 = (bf16[576,128]{1,0:T(8,128)(2,1)S(1)}, bf16[576,128]{1,0:T(8,128)(2,1)S(1)}, u32[]{:S(2)}, u32[]{:S(2)}) collective-permute-start(bf16[576,128]{1,0:T(8,128)(2,1)S(1)} %dynamic-slice_bitcast_fusion), channel_id=1, source_target_pairs={{0,12},{12,0},{4,8},{8,4},{1,13},{13,1},{5,9},{9,5},{2,14},{14,2},... | collective-permute-start | bytes 442376 | tf_op jit(solution)/shard_map/ppermute | solution.py:322
  104.0 1.0 copy-start.10
  105.1 28.2 %copy-start.3 = (bf16[512,512]{1,0:T(8,128)(2,1)S(1)}, bf16[512,512]{1,0:T(8,128)(2,1)}, u32[]{:S(2)}) copy-start(bf16[512,512]{1,0:T(8,128)(2,1)} %constant.76.clone.table) | copy-start | bytes 1572868
  133.2 22.4 %copy-start.18 = (bf16[1,96,16,128]{3,2,1,0:T(8,128)(2,1)S(1)}, bf16[1,96,16,128]{3,2,1,0:T(8,128)(2,1)}, u32[]{:S(2)}) copy-start(bf16[1,96,16,128]{3,2,1,0:T(8,128)(2,1)} %param.32) | copy-start | bytes 1179652
  134.4 21.2 %all-to-all-start.3 = ((bf16[32,48,128]{2,1,0:T(8,128)(2,1)}), bf16[32,48,128]{2,1,0:T(8,128)(2,1)S(1)}, u32[]{:S(2)}, u32[]{:S(2)}) async-start(bf16[32,48,128]{2,1,0:T(8,128)(2,1)} %inverse_rows_512.2), calls=%async_computation.3 | async-start | bytes 786432 | tf_op jit(solution)/shard_map/all_to_all | solution.py:462
  145.1 12.5 %copy-start.26 = (bf16[256,256,1]{1,0,2:T(8,128)(2,1)S(1)}, bf16[256,256,1]{1,0,2:T(8,128)(2,1)}, u32[]{:S(2)}) copy-start(bf16[256,256,1]{1,0,2:T(8,128)(2,1)} %constant.86) | copy-start | bytes 393220
  158.3 2.2 copy-start.32
  159.6 2.1 copy-start.20
  161.7 39.4 %copy-start = (bf16[512,512]{1,0:T(8,128)(2,1)S(1)}, bf16[512,512]{1,0:T(8,128)(2,1)}, u32[]{:S(2)}) copy-start(bf16[512,512]{1,0:T(8,128)(2,1)} %constant.79.clone.sin.sin_back) | copy-start | bytes 1572868
  161.7 39.4 %copy-start.1 = (bf16[512,512]{1,0:T(8,128)(2,1)S(1)}, bf16[512,512]{1,0:T(8,128)(2,1)}, u32[]{:S(2)}) copy-start(bf16[512,512]{1,0:T(8,128)(2,1)} %constant.78.clone.cos.cos_back) | copy-start | bytes 1572868
  201.1 19.7 %copy-start.15 = (bf16[256,256]{1,0:T(8,128)(2,1)S(1)}, bf16[256,256]{1,0:T(8,128)(2,1)}, u32[]{:S(2)}) copy-start(bf16[256,256]{1,0:T(8,128)(2,1)} %constant.80.clone.table) | copy-start | bytes 393220
  202.7 0.8 copy-start.13
  240.3 3.6 copy-start.21
  240.3 3.6 copy-start.33
  242.4 1.8 copy-start.29
  243.9 0.9 copy-start.24
  243.9 1.0 copy-start.25
  243.9 1.0 copy-start.34
  245.0 2.6 copy-start.27
  247.9 0.7 copy-start.22
  265.9 28.0 %copy-start.9 = (bf16[512,512]{1,0:T(8,128)(2,1)S(1)}, bf16[512,512]{1,0:T(8,128)(2,1)}, u32[]{:S(2)}) copy-start(bf16[512,512]{1,0:T(8,128)(2,1)} %constant.75.clone.sin.sin_back) | copy-start | bytes 1572868
  265.9 28.0 %copy-start.11 = (bf16[512,512]{1,0:T(8,128)(2,1)S(1)}, bf16[512,512]{1,0:T(8,128)(2,1)}, u32[]{:S(2)}) copy-start(bf16[512,512]{1,0:T(8,128)(2,1)} %constant.74.clone.cos.cos_back) | copy-start | bytes 1572868
  267.1 26.8 %all-to-all-start.9 = ((bf16[4,384,128]{2,1,0:T(8,128)(2,1)}), bf16[4,384,128]{2,1,0:T(8,128)(2,1)S(1)}, u32[]{:S(2)}, u32[]{:S(2)}) async-start(bf16[4,384,128]{2,1,0:T(8,128)(2,1)} %forward_rows_512.1), calls=%async_computation.9 | async-start | bytes 786432 | tf_op jit(solution)/shard_map/all_to_all | solution.py:462
  270.5 68.4 %reduce-scatter.5.cloned.1.call-start = ((), (), s32[]{:S(2)}) async-start(), calls=%async_computation.15 | async-start | bytes 491520 | tf_op jit(solution)/shard_map/reduce_scatter | solution.py:362
  297.6 22.5 %copy-start.4 = (bf16[512,512]{1,0:T(8,128)(2,1)S(1)}, bf16[512,512]{1,0:T(8,128)(2,1)}, u32[]{:S(2)}) copy-start(bf16[512,512]{1,0:T(8,128)(2,1)} %constant.76.clone.table) | copy-start | bytes 1572868
  297.6 22.5 %all-to-all-start.10 = ((bf16[4,384,128]{2,1,0:T(8,128)(2,1)}), bf16[4,384,128]{2,1,0:T(8,128)(2,1)S(1)}, u32[]{:S(2)}, u32[]{:S(2)}) async-start(bf16[4,384,128]{2,1,0:T(8,128)(2,1)} %copy-done.14), calls=%async_computation.10 | async-start | bytes 786432 | tf_op jit(solution)/shard_map/all_to_all | solution.py:462
  303.0 37.0 %reduce-scatter.3.cloned.1.call-start = ((), (), s32[]{:S(2)}) async-start(), calls=%async_computation.14 | async-start | bytes 983040 | tf_op jit(solution)/shard_map/reduce_scatter | solution.py:362
  303.7 36.1 %copy-start.23 = (bf16[96,8,256]{2,1,0:T(8,128)(2,1)S(1)}, bf16[96,8,256]{2,1,0:T(8,128)(2,1)}, u32[]{:S(2)}) copy-start(bf16[96,8,256]{2,1,0:T(8,128)(2,1)} %copy-done.22) | copy-start | bytes 1179652
  321.2 50.3 %all-to-all-start.11 = ((bf16[32,48,128]{2,1,0:T(8,128)(2,1)}), bf16[32,48,128]{2,1,0:T(8,128)(2,1)S(1)}, u32[]{:S(2)}, u32[]{:S(2)}) async-start(bf16[32,48,128]{2,1,0:T(8,128)(2,1)} %inverse_rows_512.3), calls=%async_computation.11 | async-start | bytes 786432 | tf_op jit(solution)/shard_map/all_to_all | solution.py:462
  339.8 30.0 %copy-start.16 = (bf16[2,128,64]{2,1,0:T(8,128)(2,1)S(1)}, bf16[2,128,64]{2,1,0:T(8,128)(2,1)}, u32[]{:S(2)}) copy-start(bf16[2,128,64]{2,1,0:T(8,128)(2,1)} %constant.81.clone.lanes) | copy-start | bytes 98308
  339.9 31.7 %copy-start.19 = (bf16[1,96,16,128]{3,2,1,0:T(8,128)(2,1)S(1)}, bf16[1,96,16,128]{3,2,1,0:T(8,128)(2,1)}, u32[]{:S(2)}) copy-start(bf16[1,96,16,128]{3,2,1,0:T(8,128)(2,1)} %param.32) | copy-start | bytes 1179652
  339.9 31.7 %copy-start.38 = (f32[96]{0:T(128)S(1)}, f32[96]{0:T(128)}, u32[]{:S(2)}) copy-start(f32[96]{0:T(128)} %param.33) | copy-start | bytes 1156
  341.1 10.3 %collective-permute-start.2 = (bf16[6,2,128]{2,0,1:T(8,128)(2,1)S(1)}, bf16[6,2,128]{2,0,1:T(8,128)(2,1)S(1)}, u32[]{:S(2)}, u32[]{:S(2)}) collective-permute-start(bf16[6,2,128]{2,0,1:T(8,128)(2,1)S(1)} %pad_maximum_fusion.4), channel_id=1, source_target_pairs={{0,8},{4,12},{1,9},{5,13},{2,10},{6,14},{3,11},{7,15},{16,24},{20,... | collective-permute-start | bytes 9224 | tf_op jit(solution)/shard_map/ppermute | solution.py:372
  349.4 20.2 %collective-permute-start.3 = (bf16[576,128]{1,0:T(8,128)(2,1)S(1)}, bf16[576,128]{1,0:T(8,128)(2,1)S(1)}, u32[]{:S(2)}, u32[]{:S(2)}) collective-permute-start(bf16[576,128]{1,0:T(8,128)(2,1)S(1)} %pad_maximum_fusion.2), channel_id=1, source_target_pairs={{0,12},{12,0},{4,8},{8,4},{1,13},{13,1},{5,9},{9,5},{2,14},{14,2},... | collective-permute-start | bytes 442376 | tf_op jit(solution)/shard_map/ppermute | solution.py:371
  (2 other events, 1.3 us)
Sparse Core Ops, SparseCore 0:
  274.2 27.9 reduce-scatter.4
  306.9 31.5 reduce-scatter.2

commit v2 on v1

--- a/solution.py
+++ b/solution.py
@@ -309,7 +309,7 @@
     return jnp.where(here, zero, shaped).reshape(2 * GROUPS * slots, LANES)
 
 
-def take_filters(filter_first, filter_second, col, pick_first, pick_second):
+def take_filters(filter_first, filter_second, pick_first, pick_second):
     rows = 2 * GROUPS * (H1 + H2) // 8
     shape = jax.ShapeDtypeStruct((COLS, rows, LANES), jnp.bfloat16)
     kept, sent = pl.pallas_call(
@@ -319,12 +319,19 @@
         **params(12 * 128 * 128 * 512 * 2, 4 << 20),
     )(filter_first, filter_second, pick_first, pick_second, constant(pair_lanes()))
     quarter = lax.dynamic_index_in_dim(sent, lax.axis_index("rep"), 0, keepdims=False)
-    recv = lax.ppermute(quarter, "col", SWAP)
     split = 2 * GROUPS * H1 // 8
     zero = jnp.concatenate(
         [slot_zero(quarter, 0, H1 // 8), slot_zero(quarter, split, H2 // 8)], axis=1
     )
-    zero = lax.ppermute(zero, "col", ((2, 0), (3, 1)))
+    return kept, quarter, zero
+
+
+def swap_filters(quarter, zero):
+    return lax.ppermute(quarter, "col", SWAP), lax.ppermute(zero, "col", ((2, 0), (3, 1)))
+
+
+def patch_filters(recv, zero, col):
+    split = 2 * GROUPS * H1 // 8
     near = col < 2
     recv = jnp.concatenate(
         [
@@ -333,7 +340,7 @@
         ],
         axis=0,
     )
-    return kept, lax.all_gather(recv, "rep", axis=0, tiled=False)
+    return lax.all_gather(recv, "rep", axis=0, tiled=False)
 
 
 def place_grads_kernel(
@@ -362,17 +369,18 @@
     return lax.psum_scatter(terms, "rep", scatter_dimension=0, tiled=False)
 
 
-def place_grads(sum_first, sum_second, col, pick_first, pick_second):
+def swap_grads(total, n):
+    count = 2 * GROUPS * n // 8
+    sent = total[count:]
+    zero = slot_zero(sent, 0, n // 8)
+    return lax.ppermute(sent, "col", SWAP), lax.ppermute(zero, "col", ((0, 2), (1, 3)))
+
+
+def place_grads(sum_first, swap_first, sum_second, swap_second, col, pick_first, pick_second):
     count_first, count_second = 2 * GROUPS * H1 // 8, 2 * GROUPS * H2 // 8
-    sent = jnp.concatenate([sum_first[count_first:], sum_second[count_second:]], axis=0)
-    zero = jnp.concatenate(
-        [slot_zero(sent, 0, H1 // 8), slot_zero(sent, count_first, H2 // 8)], axis=1
-    )
-    recv = lax.ppermute(sent, "col", SWAP)
-    zero = lax.ppermute(zero, "col", ((0, 2), (1, 3)))
     far = col >= 2
-    recv_first = put_slot_zero(recv[:count_first], zero[:, :1], far, H1 // 8)
-    recv_second = put_slot_zero(recv[count_first:], zero[:, 1:], far, H2 // 8)
+    recv_first = put_slot_zero(*swap_first, far, H1 // 8)
+    recv_second = put_slot_zero(*swap_second, far, H2 // 8)
     lanes = np.zeros((2, 128, 64))
     lanes[0, :64] = np.eye(64)
     lanes[1, 64:] = np.eye(64)
@@ -469,13 +477,18 @@
         jnp.where(col < 2, constant(np.eye(n // 4)), constant(mirror_matrix(n // 8)))
         for n in (H1, H2)
     ]
-    kept, recv = take_filters(filter_first, filter_second, col, *picks)
+    kept, quarter, zero = take_filters(filter_first, filter_second, *picks)
     second_rows = 2 * GROUPS * H1 // 8
 
     pixels_wide = images.astype(jnp.float32)
     norm_one = layer_normalize(pixels_wide, gain_first).astype(jnp.bfloat16)
     both = jnp.concatenate([pack_first(norm_one), pack_second(grad_out)], axis=1)
-    both = exchange(forward_rows(exchange(both, "row"), (H1, H2)), "col")
+    both, quarter, zero = lax.optimization_barrier((both, quarter, zero))
+    swapped = swap_filters(quarter, zero)
+    half = forward_rows(exchange(both, "row"), (H1, H2))
+    half, swapped = lax.optimization_barrier((half, swapped))
+    recv = patch_filters(*swapped, col)
+    both = exchange(half, "col")
     mixed = exchange(mix_forward(H1, col_word, both, kept, recv, 0), "col")
     mixed_one = unpack_first(exchange(inverse_rows(mixed, H1), "row"))
 
@@ -487,23 +500,34 @@
         H2, col_word, half_two, 0, both, second_rows, kept, recv, second_rows
     )
     sum_two = summed(terms_two)
-    back_two = inverse_rows(exchange(dspec_two, "col"), H2)
+    rot_two = exchange(dspec_two, "col")
+    back_two = inverse_rows(rot_two, H2)
     grad_norm_two = unpack_second(exchange(back_two, "row"))
 
     grad_down = (
         grad_out.astype(jnp.float32) + norm_pullback_step(down_wide, gain_second, grad_norm_two)
     ).astype(jnp.bfloat16)
     grad_section = upsample(grad_down, reduce_weight)
-    half_grad = exchange(forward_rows(exchange(pack_first(grad_section), "row"), (H1,)), "col")
+    packed = pack_first(grad_section)
+    packed, sum_two = lax.optimization_barrier((packed, sum_two))
+    swap_two = swap_grads(sum_two, H2)
+    half_grad = forward_rows(exchange(packed, "row"), (H1,))
+    half_grad, swap_two = lax.optimization_barrier((half_grad, swap_two))
+    half_grad = exchange(half_grad, "col")
     dspec_one, terms_one = mix_back(H1, col_word, both, 0, half_grad, 0, kept, recv, 0)
     sum_one = summed(terms_one)
-    back_one = inverse_rows(exchange(dspec_one, "col"), H1)
+    rot_one = exchange(dspec_one, "col")
+    rot_one, sum_one = lax.optimization_barrier((rot_one, sum_one))
+    swap_one = swap_grads(sum_one, H1)
+    back_one = inverse_rows(rot_one, H1)
     grad_norm_one = unpack_first(exchange(back_one, "row"))
     grad_images = (
         grad_section.astype(jnp.float32)
         + norm_pullback_step(pixels_wide, gain_first, grad_norm_one)
     ).astype(jnp.bfloat16)
-    grad_first, grad_second = place_grads(sum_one, sum_two, col, *picks)
+    grad_first, grad_second = place_grads(
+        sum_one, swap_one, sum_two, swap_two, col, *picks
+    )
     return (grad_images, grad_first, grad_second)
 
 

time: 382 us -> 378 us (0.990)
  the two profiles are of different devices: /device:TPU:105 before, /device:TPU:97 now
where the time goes in v2:
time: 378 us; the launch traced here: 377 us
  blocking collectives  148 us (39%)
  starting transfers between devices  99.1 us (26%)
  waiting for transfers between devices  63.7 us (17%)
  local copies, waits for them, and re-layouts  26.2 us (7%)
  Pallas kernels  14.9 us (4%)
  between operations  14.7 us (4%)
  other arithmetic  6.83 us (2%)
    all_to_all x6, blocking collectives, exchange(): return lax.all_to_all(blocks, axis, split_axis=0, concat_axis=0, tiled=True)  136 us
    all_to_all x6, starting transfers between devices, exchange(): return lax.all_to_all(blocks, axis, split_axis=0, concat_axis=0, tiled=True)  63.1 us
    all_to_all x6, waiting for transfers between devices, exchange(): return lax.all_to_all(blocks, axis, split_axis=0, concat_axis=0, tiled=True)  44.7 us
    ppermute x2, starting transfers between devices, swap_grads(): lax.ppermute(zero, 'col', ((0, 2), (1, 3)))  17.5 us
    all_gather x1, blocking collectives, patch_filters(): return lax.all_gather(recv, 'rep', axis=0, tiled=False)  12.2 us
    reduce_scatter x2, waiting for transfers between devices, summed(): return lax.psum_scatter(terms, 'rep', scatter_dimension=0, tiled=False)  10.3 us
    ppermute x1, starting transfers between devices, swap_filters(): lax.ppermute(quarter, 'col', SWAP)  9.41 us
    unnamed x75, local copies, waits for them, and re-layouts  8.59 us
  transfers between devices with their start and end apart: 14, of which 10 were waited for; matrix products, arithmetic and copies ran while one was open for 3% of the time, Pallas kernels for 1%

profile of v2, /device:TPU:97, one launch (start us, length us, event | category | flops | bytes accessed | tf_op | source)
XLA Modules:
  0.0 376.6 jit_solution(17964806519834452250)
XLA Ops:
  8.9 1.4 copy-done.5
  10.3 1.1 copy-done.6
  12.5 1.7 take_filters.1
  17.1 8.6 %all-to-all-start = ((bf16[32,72,128]{2,1,0:T(8,128)(2,1)}), bf16[32,72,128]{2,1,0:T(8,128)(2,1)S(1)}, u32[]{:S(2)}, u32[]{:S(2)}) async-start(bf16[32,72,128]{2,1,0:T(8,128)(2,1)} %pad_maximum_fusion), calls=%async_computation | async-start | bytes 1179648 | tf_op jit(solution)/shard_map/all_to_all | solution.py:470
  25.7 9.4 %collective-permute-start = (bf16[576,128]{1,0:T(8,128)(2,1)S(1)}, bf16[576,128]{1,0:T(8,128)(2,1)S(1)}, u32[]{:S(2)}, u32[]{:S(2)}) collective-permute-start(bf16[576,128]{1,0:T(8,128)(2,1)S(1)} %dynamic-slice_bitcast_fusion), channel_id=1, source_target_pairs={{0,12},{12,0},{4,8},{8,4},{1,13},{13,1},{5,9},{9,5},{2,14},{14,2},... | collective-permute-start | bytes 442376 | tf_op jit(solution)/shard_map/ppermute | solution.py:330
  35.1 1.3 collective-permute-start.1
  36.4 9.4 %all-to-all-done.refs_0_ = bf16[32,72,128]{2,1,0:T(8,128)(2,1)S(1)} async-done(((bf16[32,72,128]{2,1,0:T(8,128)(2,1)}), bf16[32,72,128]{2,1,0:T(8,128)(2,1)S(1)}, u32[]{:S(2)}, u32[]{:S(2)}) %all-to-all-start) | async-done | bytes 589856 | tf_op jit(solution)/shard_map/all_to_all | solution.py:470
  45.9 1.3 forward_rows_512_256.1
  47.2 2.3 collective-permute-done.1
  49.5 11.5 %all-to-all-start.1 = ((bf16[4,576,128]{2,1,0:T(8,128)(2,1)}), bf16[4,576,128]{2,1,0:T(8,128)(2,1)S(1)}, u32[]{:S(2)}, u32[]{:S(2)}) async-start(bf16[4,576,128]{2,1,0:T(8,128)(2,1)} %forward_rows_512_256.1), calls=%async_computation.1 | async-start | bytes 1179648 | tf_op jit(solution)/shard_map/all_to_all | solution.py:470
  61.5 12.2 %all-gather = bf16[2304,128]{1,0:T(8,128)(2,1)S(1)} all-gather(bf16[576,128]{1,0:T(8,128)(2,1)S(1)} %pad_maximum_fusion.1), channel_id=2, replica_groups=mesh['row'=32,'col'=4,'rep'=4] {'rep'}, dimensions={0}, use_global_device_ids=true | all-gather | bytes 737280 | tf_op jit(solution)/shard_map/all_gather | solution.py:343
  73.7 18.3 %all-to-all-done.1.x_ref.g_ref = bf16[4,576,128]{2,1,0:T(8,128)(2,1)S(1)} async-done(((bf16[4,576,128]{2,1,0:T(8,128)(2,1)}), bf16[4,576,128]{2,1,0:T(8,128)(2,1)S(1)}, u32[]{:S(2)}, u32[]{:S(2)}) %all-to-all-start.1) | async-done | bytes 589856 | tf_op jit(solution)/shard_map/all_to_all | solution.py:470
  93.0 1.5 mix_forward_512.1
  94.5 28.1 %all_to_all.60.x_ref = bf16[4,384,128]{2,1,0:T(8,128)(2,1)S(1)} all-to-all(bf16[4,384,128]{2,1,0:T(8,128)(2,1)S(1)} %mix_forward_512.1), channel_id=1, replica_groups=mesh['row'=32,'col'=4,'rep'=4] {'col'}, dimensions={0} | all-to-all | bytes 786432 | tf_op jit(solution)/shard_map/all_to_all | solution.py:470
  122.5 1.2 inverse_rows_512.2
  123.7 9.2 %all-to-all-start.3 = ((bf16[32,48,128]{2,1,0:T(8,128)(2,1)}), bf16[32,48,128]{2,1,0:T(8,128)(2,1)S(1)}, u32[]{:S(2)}, u32[]{:S(2)}) async-start(bf16[32,48,128]{2,1,0:T(8,128)(2,1)} %inverse_rows_512.2), calls=%async_computation.3 | async-start | bytes 786432 | tf_op jit(solution)/shard_map/all_to_all | solution.py:470
  133.0 1.8 reshape.321
  134.7 9.9 %all-to-all-done.3 = bf16[32,48,128]{2,1,0:T(8,128)(2,1)S(1)} async-done(((bf16[32,48,128]{2,1,0:T(8,128)(2,1)}), bf16[32,48,128]{2,1,0:T(8,128)(2,1)S(1)}, u32[]{:S(2)}, u32[]{:S(2)}) %all-to-all-start.3) | async-done | bytes 393248 | tf_op jit(solution)/shard_map/all_to_all | solution.py:470
  145.5 1.1 reshape.319
  147.3 1.3 fusion.29
  150.7 2.1 copy.53
  152.9 1.9 reshape.323
  154.8 13.8 %all_to_all.61.refs_0_ = bf16[32,24,128]{2,1,0:T(8,128)(2,1)S(1)} all-to-all(bf16[32,24,128]{2,1,0:T(8,128)(2,1)} %reshape.323), channel_id=1, replica_groups=mesh['row'=32,'col'=4,'rep'=4] {'row'}, dimensions={0} | all-to-all | bytes 393216 | tf_op jit(solution)/shard_map/all_to_all | solution.py:470
  168.8 16.4 %all_to_all.62.x_ref = bf16[4,192,128]{2,1,0:T(8,128)(2,1)S(1)} all-to-all(bf16[4,192,128]{2,1,0:T(8,128)(2,1)S(1)} %forward_rows_256.1), channel_id=1, replica_groups=mesh['row'=32,'col'=4,'rep'=4] {'col'}, dimensions={0} | all-to-all | bytes 393216 | tf_op jit(solution)/shard_map/all_to_all | solution.py:470
  185.2 1.8 mix_back_256.1
  187.0 20.1 %all_to_all.63.x_ref = bf16[4,192,128]{2,1,0:T(8,128)(2,1)S(1)} all-to-all(bf16[4,192,128]{2,1,0:T(8,128)(2,1)S(1)} %get-tuple-element.32), channel_id=1, replica_groups=mesh['row'=32,'col'=4,'rep'=4] {'col'}, dimensions={0} | all-to-all | bytes 393216 | tf_op jit(solution)/shard_map/all_to_all | solution.py:470
  208.0 10.7 %all-to-all-start.7 = ((bf16[32,24,128]{2,1,0:T(8,128)(2,1)}), bf16[32,24,128]{2,1,0:T(8,128)(2,1)S(1)}, u32[]{:S(2)}, u32[]{:S(2)}) async-start(bf16[32,24,128]{2,1,0:T(8,128)(2,1)} %inverse_rows_256.1), calls=%async_computation.7 | async-start | bytes 393216 | tf_op jit(solution)/shard_map/all_to_all | solution.py:470
  219.5 7.0 %all-to-all-done.7 = bf16[32,24,128]{2,1,0:T(8,128)(2,1)S(1)} async-done(((bf16[32,24,128]{2,1,0:T(8,128)(2,1)}), bf16[32,24,128]{2,1,0:T(8,128)(2,1)S(1)}, u32[]{:S(2)}, u32[]{:S(2)}) %all-to-all-start.7) | async-done | bytes 196640 | tf_op jit(solution)/shard_map/all_to_all | solution.py:470
  226.5 1.3 reshape.333
  227.9 2.2 copy.54
  230.0 1.5 copy.55
  232.6 1.3 convolution_convert_fusion
  233.8 1.4 copy.57
  236.4 8.0 %reduce-scatter.3.cloned.1.call-done = bf16[1,384,128]{2,1,0:T(8,128)(2,1)} async-done(((bf16[4,384,128]{2,1,0:T(8,128)(2,1)}), bf16[1,384,128]{2,1,0:T(8,128)(2,1)}) %reduce-scatter.3.cloned.1.call-update) | async-done | bytes 98320 | tf_op jit(solution)/shard_map/reduce_scatter | solution.py:369
  244.5 10.1 %all-to-all-start.8 = ((bf16[32,48,128]{2,1,0:T(8,128)(2,1)}), bf16[32,48,128]{2,1,0:T(8,128)(2,1)S(1)}, u32[]{:S(2)}, u32[]{:S(2)}) async-start(bf16[32,48,128]{2,1,0:T(8,128)(2,1)} %convert_element_type.158), calls=%async_computation.9 | async-start | bytes 786432 | tf_op jit(solution)/shard_map/all_to_all | solution.py:470
  255.4 5.4 %collective-permute-start.2 = (bf16[192,128]{1,0:T(8,128)(2,1)S(1)}, bf16[192,128]{1,0:T(8,128)(2,1)S(1)}, u32[]{:S(2)}, u32[]{:S(2)}) collective-permute-start(bf16[192,128]{1,0:T(8,128)(2,1)S(1)} %get-tuple-element.48), channel_id=1, source_target_pairs={{0,12},{12,0},{4,8},{8,4},{1,13},{13,1},{5,9},{9,5},{2,14},{14,2},... | collective-permute-start | bytes 147464 | tf_op jit(solution)/shard_map/ppermute | solution.py:376
  260.9 9.0 %collective-permute-start.3 = (bf16[6,1,128]{2,0,1:T(8,128)(2,1)S(1)}, bf16[6,1,128]{2,0,1:T(8,128)(2,1)S(1)}, u32[]{:S(2)}, u32[]{:S(2)}) collective-permute-start(bf16[6,1,128]{2,0,1:T(8,128)(2,1)S(1)} %copy.64), channel_id=1, source_target_pairs={{0,8},{4,12},{1,9},{5,13},{2,10},{6,14},{3,11},{7,15},{16,24},{20,... | collective-permute-start | bytes 4616 | tf_op jit(solution)/shard_map/ppermute | solution.py:376
  270.6 33.4 %all_to_all.64.g_ref = bf16[4,384,128]{2,1,0:T(8,128)(2,1)S(1)} all-to-all(bf16[4,384,128]{2,1,0:T(8,128)(2,1)S(1)} %forward_rows_512.1), channel_id=1, replica_groups=mesh['row'=32,'col'=4,'rep'=4] {'col'}, dimensions={0} | all-to-all | bytes 786432 | tf_op jit(solution)/shard_map/all_to_all | solution.py:470
  306.0 2.9 mix_back_512.1
  309.0 24.0 %all_to_all.65.x_ref = bf16[4,384,128]{2,1,0:T(8,128)(2,1)S(1)} all-to-all(bf16[4,384,128]{2,1,0:T(8,128)(2,1)S(1)} %get-tuple-element.37), channel_id=1, replica_groups=mesh['row'=32,'col'=4,'rep'=4] {'col'}, dimensions={0} | all-to-all | bytes 786432 | tf_op jit(solution)/shard_map/all_to_all | solution.py:470
  333.0 2.2 reduce-scatter.5.cloned.1.call-done
  335.3 1.2 inverse_rows_512.3
  336.5 12.9 %all-to-all-start.11 = ((bf16[32,48,128]{2,1,0:T(8,128)(2,1)}), bf16[32,48,128]{2,1,0:T(8,128)(2,1)S(1)}, u32[]{:S(2)}, u32[]{:S(2)}) async-start(bf16[32,48,128]{2,1,0:T(8,128)(2,1)} %inverse_rows_512.3), calls=%async_computation.13 | async-start | bytes 786432 | tf_op jit(solution)/shard_map/all_to_all | solution.py:470
  349.5 2.2 collective-permute-start.5
  351.7 8.6 %collective-permute-start.4 = (bf16[6,1,128]{2,0,1:T(8,128)(2,1)S(1)}, bf16[6,1,128]{2,0,1:T(8,128)(2,1)S(1)}, u32[]{:S(2)}, u32[]{:S(2)}) collective-permute-start(bf16[6,1,128]{2,0,1:T(8,128)(2,1)S(1)} %copy.65), channel_id=1, source_target_pairs={{0,8},{4,12},{1,9},{5,13},{2,10},{6,14},{3,11},{7,15},{16,24},{20,... | collective-permute-start | bytes 4616 | tf_op jit(solution)/shard_map/ppermute | solution.py:376
  361.0 5.3 %collective-permute-done.5 = bf16[384,128]{1,0:T(8,128)(2,1)S(1)} collective-permute-done((bf16[384,128]{1,0:T(8,128)(2,1)S(1)}, bf16[384,128]{1,0:T(8,128)(2,1)S(1)}, u32[]{:S(2)}, u32[]{:S(2)}) %collective-permute-start.5) | collective-permute-done | bytes 98336 | tf_op jit(solution)/shard_map/ppermute | solution.py:376
  366.5 1.7 place_grads.1
  368.7 1.1 add_convert_fusion
  (145 shorter events, 19.6 us)
Async XLA Ops:
  8.9 1.4 copy-start.5
  10.3 1.1 copy-start.6
  11.5 1.0 copy-start.12
  12.5 1.8 copy-start.15
  14.2 1.0 copy-start.23
  14.5 1.5 copy-start.33
  16.2 29.7 %copy-start.2 = (bf16[512,512]{1,0:T(8,128)(2,1)S(1)}, bf16[512,512]{1,0:T(8,128)(2,1)}, u32[]{:S(2)}) copy-start(bf16[512,512]{1,0:T(8,128)(2,1)} %constant.72.clone.refs_1_) | copy-start | bytes 1572868
  16.2 29.7 %copy-start.7 = (bf16[256,256]{1,0:T(8,128)(2,1)S(1)}, bf16[256,256]{1,0:T(8,128)(2,1)}, u32[]{:S(2)}) copy-start(bf16[256,256]{1,0:T(8,128)(2,1)} %constant.73.clone.refs_2_.refs_1_) | copy-start | bytes 393220
  17.1 28.8 %all-to-all-start = ((bf16[32,72,128]{2,1,0:T(8,128)(2,1)}), bf16[32,72,128]{2,1,0:T(8,128)(2,1)S(1)}, u32[]{:S(2)}, u32[]{:S(2)}) async-start(bf16[32,72,128]{2,1,0:T(8,128)(2,1)} %pad_maximum_fusion), calls=%async_computation | async-start | bytes 1179648 | tf_op jit(solution)/shard_map/all_to_all | solution.py:470
  25.7 23.8 %collective-permute-start = (bf16[576,128]{1,0:T(8,128)(2,1)S(1)}, bf16[576,128]{1,0:T(8,128)(2,1)S(1)}, u32[]{:S(2)}, u32[]{:S(2)}) collective-permute-start(bf16[576,128]{1,0:T(8,128)(2,1)S(1)} %dynamic-slice_bitcast_fusion), channel_id=1, source_target_pairs={{0,12},{12,0},{4,8},{8,4},{1,13},{13,1},{5,9},{9,5},{2,14},{14,2},... | collective-permute-start | bytes 442376 | tf_op jit(solution)/shard_map/ppermute | solution.py:330
  35.1 14.4 %collective-permute-start.1 = (bf16[6,2,128]{2,0,1:T(8,128)(2,1)S(1)}, bf16[6,2,128]{2,0,1:T(8,128)(2,1)S(1)}, u32[]{:S(2)}, u32[]{:S(2)}) collective-permute-start(bf16[6,2,128]{2,0,1:T(8,128)(2,1)S(1)} %pad_maximum_fusion.2), channel_id=1, source_target_pairs={{8,0},{12,4},{9,1},{13,5},{10,2},{14,6},{11,3},{15,7},{24,16},{28,... | collective-permute-start | bytes 9224 | tf_op jit(solution)/shard_map/ppermute | solution.py:330
  47.2 44.8 %copy-start.8 = (bf16[512,512]{1,0:T(8,128)(2,1)S(1)}, bf16[512,512]{1,0:T(8,128)(2,1)}, u32[]{:S(2)}) copy-start(bf16[512,512]{1,0:T(8,128)(2,1)} %constant.75.clone.sin.sin_back) | copy-start | bytes 1572868
  49.5 42.4 %all-to-all-start.1 = ((bf16[4,576,128]{2,1,0:T(8,128)(2,1)}), bf16[4,576,128]{2,1,0:T(8,128)(2,1)S(1)}, u32[]{:S(2)}, u32[]{:S(2)}) async-start(bf16[4,576,128]{2,1,0:T(8,128)(2,1)} %forward_rows_512_256.1), calls=%async_computation.1 | async-start | bytes 1179648 | tf_op jit(solution)/shard_map/all_to_all | solution.py:470
  91.9 1.0 copy-start.10
  93.0 29.6 %copy-start.3 = (bf16[512,512]{1,0:T(8,128)(2,1)S(1)}, bf16[512,512]{1,0:T(8,128)(2,1)}, u32[]{:S(2)}) copy-start(bf16[512,512]{1,0:T(8,128)(2,1)} %constant.76.clone.table) | copy-start | bytes 1572868
  123.7 20.9 %copy-start.16 = (bf16[1,96,16,128]{3,2,1,0:T(8,128)(2,1)S(1)}, bf16[1,96,16,128]{3,2,1,0:T(8,128)(2,1)}, u32[]{:S(2)}) copy-start(bf16[1,96,16,128]{3,2,1,0:T(8,128)(2,1)} %param.32) | copy-start | bytes 1179652
  123.7 20.9 %all-to-all-start.3 = ((bf16[32,48,128]{2,1,0:T(8,128)(2,1)}), bf16[32,48,128]{2,1,0:T(8,128)(2,1)S(1)}, u32[]{:S(2)}, u32[]{:S(2)}) async-start(bf16[32,48,128]{2,1,0:T(8,128)(2,1)} %inverse_rows_512.2), calls=%async_computation.3 | async-start | bytes 786432 | tf_op jit(solution)/shard_map/all_to_all | solution.py:470
  133.0 13.7 %copy-start.25 = (bf16[256,256,1]{1,0,2:T(8,128)(2,1)S(1)}, bf16[256,256,1]{1,0,2:T(8,128)(2,1)}, u32[]{:S(2)}) copy-start(bf16[256,256,1]{1,0,2:T(8,128)(2,1)} %constant.86) | copy-start | bytes 393220
  147.3 2.2 copy-start.30
  148.6 2.1 copy-start.18
  150.7 34.5 %copy-start = (bf16[512,512]{1,0:T(8,128)(2,1)S(1)}, bf16[512,512]{1,0:T(8,128)(2,1)}, u32[]{:S(2)}) copy-start(bf16[512,512]{1,0:T(8,128)(2,1)} %constant.79.clone.sin.sin_back) | copy-start | bytes 1572868
  150.7 34.5 %copy-start.1 = (bf16[512,512]{1,0:T(8,128)(2,1)S(1)}, bf16[512,512]{1,0:T(8,128)(2,1)}, u32[]{:S(2)}) copy-start(bf16[512,512]{1,0:T(8,128)(2,1)} %constant.78.clone.cos.cos_back) | copy-start | bytes 1572868
  185.2 21.9 %copy-start.13 = (bf16[256,256]{1,0:T(8,128)(2,1)S(1)}, bf16[256,256]{1,0:T(8,128)(2,1)}, u32[]{:S(2)}) copy-start(bf16[256,256]{1,0:T(8,128)(2,1)} %constant.80.clone.table) | copy-start | bytes 393220
  208.0 18.5 %all-to-all-start.7 = ((bf16[32,24,128]{2,1,0:T(8,128)(2,1)}), bf16[32,24,128]{2,1,0:T(8,128)(2,1)S(1)}, u32[]{:S(2)}, u32[]{:S(2)}) async-start(bf16[32,24,128]{2,1,0:T(8,128)(2,1)} %inverse_rows_256.1), calls=%async_computation.7 | async-start | bytes 393216 | tf_op jit(solution)/shard_map/all_to_all | solution.py:470
  218.8 25.7 %reduce-scatter.3.cloned.1.call-start = ((), (), s32[]{:S(2)}) async-start(), calls=%async_computation.14 | async-start | bytes 491520 | tf_op jit(solution)/shard_map/reduce_scatter | solution.py:369
  227.9 3.6 copy-start.19
  227.9 3.6 copy-start.31
  230.0 1.8 copy-start.29
  231.5 0.9 copy-start.22
  231.5 1.0 copy-start.24
  231.5 1.0 copy-start.32
  232.6 2.6 copy-start.26
  235.5 8.9 %copy-start.20 = (bf16[96,8,256]{2,1,0:T(8,128)(2,1)}, bf16[96,8,256]{2,1,0:T(8,128)(2,1)S(1)}, u32[]{:S(2)}) copy-start(bf16[96,8,256]{2,1,0:T(8,128)(2,1)S(1)} %convolution_convert_fusion.1) | copy-start | bytes 1179652
  244.5 25.4 %all-to-all-start.8 = ((bf16[32,48,128]{2,1,0:T(8,128)(2,1)}), bf16[32,48,128]{2,1,0:T(8,128)(2,1)S(1)}, u32[]{:S(2)}, u32[]{:S(2)}) async-start(bf16[32,48,128]{2,1,0:T(8,128)(2,1)} %convert_element_type.158), calls=%async_computation.9 | async-start | bytes 786432 | tf_op jit(solution)/shard_map/all_to_all | solution.py:470
  254.6 80.7 %reduce-scatter.5.cloned.1.call-start = ((), (), s32[]{:S(2)}) async-start(), calls=%async_computation.15 | async-start | bytes 983040 | tf_op jit(solution)/shard_map/reduce_scatter | solution.py:369
  255.4 15.1 %collective-permute-start.2 = (bf16[192,128]{1,0:T(8,128)(2,1)S(1)}, bf16[192,128]{1,0:T(8,128)(2,1)S(1)}, u32[]{:S(2)}, u32[]{:S(2)}) collective-permute-start(bf16[192,128]{1,0:T(8,128)(2,1)S(1)} %get-tuple-element.48), channel_id=1, source_target_pairs={{0,12},{12,0},{4,8},{8,4},{1,13},{13,1},{5,9},{9,5},{2,14},{14,2},... | collective-permute-start | bytes 147464 | tf_op jit(solution)/shard_map/ppermute | solution.py:376
  260.9 9.7 %collective-permute-start.3 = (bf16[6,1,128]{2,0,1:T(8,128)(2,1)S(1)}, bf16[6,1,128]{2,0,1:T(8,128)(2,1)S(1)}, u32[]{:S(2)}, u32[]{:S(2)}) collective-permute-start(bf16[6,1,128]{2,0,1:T(8,128)(2,1)S(1)} %copy.64), channel_id=1, source_target_pairs={{0,8},{4,12},{1,9},{5,13},{2,10},{6,14},{3,11},{7,15},{16,24},{20,... | collective-permute-start | bytes 4616 | tf_op jit(solution)/shard_map/ppermute | solution.py:376
  304.0 1.0 copy-start.9
  305.0 1.0 copy-start.11
  309.0 26.3 %copy-start.4 = (bf16[512,512]{1,0:T(8,128)(2,1)S(1)}, bf16[512,512]{1,0:T(8,128)(2,1)}, u32[]{:S(2)}) copy-start(bf16[512,512]{1,0:T(8,128)(2,1)} %constant.76.clone.table) | copy-start | bytes 1572868
  335.3 14.2 %copy-start.27 = (bf16[1,768,128]{2,1,0:T(8,128)(2,1)S(1)}, bf16[1,768,128]{2,1,0:T(8,128)(2,1)}, u32[]{:S(2)}) copy-start(bf16[1,768,128]{2,1,0:T(8,128)(2,1)} %reduce-scatter.5.cloned.1.call-done) | copy-start | bytes 589828
  335.3 25.2 %copy-start.21 = (bf16[96,8,256]{2,1,0:T(8,128)(2,1)S(1)}, bf16[96,8,256]{2,1,0:T(8,128)(2,1)}, u32[]{:S(2)}) copy-start(bf16[96,8,256]{2,1,0:T(8,128)(2,1)} %copy-done.20) | copy-start | bytes 1179652
  336.5 30.0 %copy-start.14 = (bf16[2,128,64]{2,1,0:T(8,128)(2,1)S(1)}, bf16[2,128,64]{2,1,0:T(8,128)(2,1)}, u32[]{:S(2)}) copy-start(bf16[2,128,64]{2,1,0:T(8,128)(2,1)} %constant.81.clone.lanes) | copy-start | bytes 98308
  336.5 31.7 %all-to-all-start.11 = ((bf16[32,48,128]{2,1,0:T(8,128)(2,1)}), bf16[32,48,128]{2,1,0:T(8,128)(2,1)S(1)}, u32[]{:S(2)}, u32[]{:S(2)}) async-start(bf16[32,48,128]{2,1,0:T(8,128)(2,1)} %inverse_rows_512.3), calls=%async_computation.13 | async-start | bytes 786432 | tf_op jit(solution)/shard_map/all_to_all | solution.py:470
  349.4 18.8 %copy-start.17 = (bf16[1,96,16,128]{3,2,1,0:T(8,128)(2,1)S(1)}, bf16[1,96,16,128]{3,2,1,0:T(8,128)(2,1)}, u32[]{:S(2)}) copy-start(bf16[1,96,16,128]{3,2,1,0:T(8,128)(2,1)} %param.32) | copy-start | bytes 1179652
  349.4 18.8 %copy-start.34 = (f32[96]{0:T(128)S(1)}, f32[96]{0:T(128)}, u32[]{:S(2)}) copy-start(f32[96]{0:T(128)} %param.33) | copy-start | bytes 1156
  349.5 16.8 %collective-permute-start.5 = (bf16[384,128]{1,0:T(8,128)(2,1)S(1)}, bf16[384,128]{1,0:T(8,128)(2,1)S(1)}, u32[]{:S(2)}, u32[]{:S(2)}) collective-permute-start(bf16[384,128]{1,0:T(8,128)(2,1)S(1)} %get-tuple-element.45), channel_id=1, source_target_pairs={{0,12},{12,0},{4,8},{8,4},{1,13},{13,1},{5,9},{9,5},{2,14},{14,2},... | collective-permute-start | bytes 294920 | tf_op jit(solution)/shard_map/ppermute | solution.py:376
  351.7 9.3 %collective-permute-start.4 = (bf16[6,1,128]{2,0,1:T(8,128)(2,1)S(1)}, bf16[6,1,128]{2,0,1:T(8,128)(2,1)S(1)}, u32[]{:S(2)}, u32[]{:S(2)}) collective-permute-start(bf16[6,1,128]{2,0,1:T(8,128)(2,1)S(1)} %copy.65), channel_id=1, source_target_pairs={{0,8},{4,12},{1,9},{5,13},{2,10},{6,14},{3,11},{7,15},{16,24},{20,... | collective-permute-start | bytes 4616 | tf_op jit(solution)/shard_map/ppermute | solution.py:376
  (1 other events, 0.6 us)
Sparse Core Ops, SparseCore 0:
  223.0 21.4 reduce-scatter.2
  309.1 26.1 reduce-scatter.4

commit v3 on v2

--- a/solution.py
+++ b/solution.py
@@ -409,48 +409,164 @@
     return pullback(upstream.astype(jnp.float32))[0]
 
 
-def offset_table(cols_dev):
-    half_cols = cols_dev // 2
-    target = np.arange(2 * cols_dev)
-    row_off = target // cols_dev
-    rest = target % cols_dev
-    source = row_off * cols_dev + 2 * (rest % half_cols) + rest // half_cols
-    place = np.arange(2 * cols_dev)
-    return constant(place[:, None] == source[None, :])
-
-
-def strided_reduce(entry_values, weight_matrix):
-    images_dev, channels, rows_dev, cols_dev = entry_values.shape
-    outputs = weight_matrix.shape[0]
-    merged = entry_values.reshape(images_dev, channels, rows_dev // 2, 2 * cols_dev)
-    placed = jnp.einsum(
-        "bcis,st->bcit", merged, offset_table(cols_dev), preferred_element_type=jnp.float32
-    ).astype(jnp.bfloat16)
-    placed = placed.reshape(images_dev, channels, rows_dev // 2, 4, cols_dev // 2)
-    kernel = weight_matrix.reshape(outputs, 4, channels)
-    return jnp.einsum("oqc,bciqj->boij", kernel, placed, preferred_element_type=jnp.float32).astype(
-        jnp.bfloat16
-    )
-
-
-def upsample(upstream, weight_matrix):
-    images_dev, outputs, rows_half, cols_half = upstream.shape
-    channels = weight_matrix.shape[1] // 4
-    kernel = weight_matrix.reshape(outputs, 4, channels)
-    patches = jnp.einsum(
-        "oqc,boij->bciqj", kernel, upstream, preferred_element_type=jnp.float32
-    ).astype(jnp.bfloat16)
-    patches = patches.reshape(images_dev, channels, rows_half, 8 * cols_half // 2)
-    spread_back = jnp.einsum(
-        "bcit,st->bcis", patches, offset_table(2 * cols_half), preferred_element_type=jnp.float32
-    )
-    return spread_back.reshape(images_dev, channels, 2 * rows_half, 2 * cols_half).astype(
-        jnp.bfloat16
-    )
-
-
-def pack_first(field):
-    return field.reshape(ROWS, GROUPS * 16, LANES)
+def fold(values):
+    total = jnp.broadcast_to(jnp.sum(values, axis=0, keepdims=True), (8, LANES))
+    return (total + pltpu.roll(total, LANES // 2, 1))[:1]
+
+
+def standardize(values):
+    center = values - fold(values) / 192.0
+    scale = lax.rsqrt(fold(center * center) / 192.0 + epsilon)
+    return center * scale, scale
+
+
+def first_norm_kernel(x_ref, g_ref, gain_ref, pair_ref, out_ref, grad_ref):
+    pixels = x_ref[...].astype(jnp.float32)
+    center = pixels - jnp.sum(pixels, axis=0, keepdims=True) / 96.0
+    scale = lax.rsqrt(jnp.sum(center * center, axis=0) / 96.0 + epsilon)
+    for c in range(96):
+        at = (c % GROUPS) * 16
+        out_ref[c // GROUPS, at : at + 16, :] = (center[c] * scale * gain_ref[c]).astype(
+            jnp.bfloat16
+        )
+    upstream = g_ref[...].astype(jnp.float32).reshape(96, 2, 8, 64)
+    packed = sum(
+        dot(upstream[:, i].reshape(768, 64).astype(jnp.bfloat16), pair_ref[i]) for i in range(2)
+    )
+    packed = packed.reshape(ROWS, GROUPS * 8, LANES).astype(jnp.bfloat16)
+    out_ref[:, GROUPS * 16 :, :] = packed
+    grad_ref[...] = packed
+
+
+def first_norm(images, grad_out, gains):
+    pair = np.zeros((2, 64, 128))
+    pair[0, :, :64] = np.eye(64)
+    pair[1, :, 64:] = np.eye(64)
+    return pl.pallas_call(
+        first_norm_kernel,
+        out_shape=(
+            jax.ShapeDtypeStruct((ROWS, GROUPS * 24, LANES), jnp.bfloat16),
+            jax.ShapeDtypeStruct((ROWS, GROUPS * 8, LANES), jnp.bfloat16),
+        ),
+        in_specs=vmem(2) + [smem()] + vmem(1),
+        name="first_norm",
+        **params(4 * 768 * 64 * 128, 2 << 20),
+    )(images.reshape(96, 16, LANES), grad_out.reshape(192, 8, 64), gains, constant(pair))
+
+
+def spread_columns():
+    matrix = np.zeros((64, 2, 2, 2, 64))
+    for e in range(2):
+        for half in range(2):
+            matrix[:, e, e, half, :] = np.eye(64)
+    return matrix.reshape(128, 256)
+
+
+def merge_columns():
+    matrix = np.zeros((2, 2, 64, 2, 64, 2))
+    for e in range(2):
+        for i in range(2):
+            matrix[e, i, :, i, :, e] = np.eye(64)
+    return matrix.reshape(256, 256)
+
+
+def low_half():
+    return lax.broadcasted_iota(jnp.int32, (96, LANES), 1) < LANES // 2
+
+
+def reduce_kernel(x_ref, m_ref, w_ref, gain_ref, spread_ref, norm_ref, down_ref, s_ref, n_ref):
+    mixed = m_ref[...].astype(jnp.float32).reshape(1536, LANES)
+    section = x_ref[...].astype(jnp.float32).reshape(1536, LANES) + mixed
+    spread = dot(section.astype(jnp.bfloat16), spread_ref[...])
+    for e in range(2):
+        s_ref[e] = spread[:, e * LANES : (e + 1) * LANES]
+    low = low_half()
+    for first in range(0, 8, 2):
+        patches = [
+            jnp.concatenate(
+                [
+                    s_ref[e, pl.ds(2 * i + a, 96, stride=16), :].astype(jnp.bfloat16)
+                    for a in range(2)
+                    for e in range(2)
+                ],
+                axis=0,
+            )
+            for i in (first, first + 1)
+        ]
+        both = dot(w_ref[...], jnp.concatenate(patches, axis=1))
+        for i in range(2):
+            block = both[:, i * LANES : (i + 1) * LANES]
+            down = jnp.where(low, block[:96], block[96:]).astype(jnp.bfloat16)
+            down_ref[first + i] = down
+            normed, _ = standardize(down.astype(jnp.float32))
+            n_ref[pl.ds(first + i, 96, stride=8), :] = normed * gain_ref[...]
+    norm_ref[...] = n_ref[...].reshape(ROWS, GROUPS * 8, LANES).astype(jnp.bfloat16)
+
+
+def reduce_step(images, mixed, weight, gains):
+    return pl.pallas_call(
+        reduce_kernel,
+        out_shape=(
+            jax.ShapeDtypeStruct((ROWS, GROUPS * 8, LANES), jnp.bfloat16),
+            jax.ShapeDtypeStruct((8, 96, LANES), jnp.bfloat16),
+        ),
+        in_specs=vmem(5),
+        scratch_shapes=[
+            pltpu.VMEM((2, 1536, LANES), jnp.float32),
+            pltpu.VMEM((768, LANES), jnp.float32),
+        ],
+        name="reduce_step",
+        **params(4 * 2 * 192 * 384 * 256, 2 << 20),
+    )(images.reshape(96, 16, LANES), mixed, weight, gains, constant(spread_columns()))
+
+
+def expand_kernel(
+    b_ref, down_ref, g_ref, w_ref, gain_ref, merge_ref, out_ref, back_ref, grad_ref, o_ref
+):
+    back_ref[...] = b_ref[...].astype(jnp.float32).reshape(768, LANES)
+    grad_ref[...] = g_ref[...].astype(jnp.float32).reshape(768, LANES)
+    low = low_half()
+    for first in range(0, 8, 2):
+        grads = []
+        for i in (first, first + 1):
+            normed, scale = standardize(down_ref[i].astype(jnp.float32))
+            upstream = back_ref[pl.ds(i, 96, stride=8), :] * gain_ref[...]
+            step = upstream - fold(upstream) / 192.0 - normed * (fold(upstream * normed) / 192.0)
+            total = grad_ref[pl.ds(i, 96, stride=8), :] + scale * step
+            total = total.astype(jnp.bfloat16).astype(jnp.float32)
+            grads.append((total, pltpu.roll(total, LANES // 2, 1)))
+        even = jnp.where(low, grads[0][0], grads[1][1])
+        odd = jnp.where(low, grads[0][1], grads[1][0])
+        both = jnp.concatenate([even, odd], axis=0).astype(jnp.bfloat16)
+        patches = dot(w_ref[...], both).astype(jnp.bfloat16)
+        rows = [
+            jnp.concatenate(
+                [patches[(2 * a + e) * 96 : (2 * a + e + 1) * 96] for e in range(2)], axis=1
+            )
+            for a in range(2)
+        ]
+        merged = dot(jnp.concatenate(rows, axis=0), merge_ref[...])
+        for i in range(2):
+            for a in range(2):
+                o_ref[pl.ds(2 * (first + i) + a, 96, stride=16), :] = merged[
+                    a * 96 : (a + 1) * 96, i * LANES : (i + 1) * LANES
+                ]
+    out_ref[...] = o_ref[...].reshape(ROWS, GROUPS * 16, LANES).astype(jnp.bfloat16)
+
+
+def expand_step(back, down, upstream, weight, gains):
+    return pl.pallas_call(
+        expand_kernel,
+        out_shape=jax.ShapeDtypeStruct((ROWS, GROUPS * 16, LANES), jnp.bfloat16),
+        in_specs=vmem(6),
+        scratch_shapes=[
+            pltpu.VMEM((768, LANES), jnp.float32),
+            pltpu.VMEM((768, LANES), jnp.float32),
+            pltpu.VMEM((1536, LANES), jnp.float32),
+        ],
+        name="expand_step",
+        **params(4 * 2 * 192 * 384 * 256, 2 << 20),
+    )(back, down, upstream, weight, gains, constant(merge_columns()))
 
 
 def unpack_first(blocks):
@@ -460,10 +576,6 @@
 def pack_second(field):
     pairs = field.reshape(96, 2, 8, 64).transpose(0, 2, 1, 3)
     return pairs.reshape(ROWS, GROUPS * 8, LANES)
-
-
-def unpack_second(blocks):
-    return blocks.reshape(96, 8, 2, 64).transpose(0, 2, 1, 3).reshape(1, 192, 8, 64)
 
 
 def exchange(blocks, axis):
@@ -480,50 +592,41 @@
     kept, quarter, zero = take_filters(filter_first, filter_second, *picks)
     second_rows = 2 * GROUPS * H1 // 8
 
-    pixels_wide = images.astype(jnp.float32)
-    norm_one = layer_normalize(pixels_wide, gain_first).astype(jnp.bfloat16)
-    both = jnp.concatenate([pack_first(norm_one), pack_second(grad_out)], axis=1)
-    both, quarter, zero = lax.optimization_barrier((both, quarter, zero))
+    weight = reduce_weight.reshape(96, 2, 384).transpose(1, 0, 2).reshape(192, 384)
+    gains = jnp.repeat(gain_second.reshape(96, 2), 64, axis=1)
+
+    both, packed_out = first_norm(images, grad_out, gain_first)
     swapped = swap_filters(quarter, zero)
     half = forward_rows(exchange(both, "row"), (H1, H2))
     half, swapped = lax.optimization_barrier((half, swapped))
     recv = patch_filters(*swapped, col)
     both = exchange(half, "col")
     mixed = exchange(mix_forward(H1, col_word, both, kept, recv, 0), "col")
-    mixed_one = unpack_first(exchange(inverse_rows(mixed, H1), "row"))
-
-    section_one = (pixels_wide + mixed_one.astype(jnp.float32)).astype(jnp.bfloat16)
-    down_wide = strided_reduce(section_one, reduce_weight).astype(jnp.float32)
-    norm_two = layer_normalize(down_wide, gain_second).astype(jnp.bfloat16)
-    half_two = exchange(forward_rows(exchange(pack_second(norm_two), "row"), (H2,)), "col")
+    mixed_one = exchange(inverse_rows(mixed, H1), "row")
+
+    norm_two, down = reduce_step(images, mixed_one, weight, gains)
+    half_two = exchange(forward_rows(exchange(norm_two, "row"), (H2,)), "col")
     dspec_two, terms_two = mix_back(
         H2, col_word, half_two, 0, both, second_rows, kept, recv, second_rows
     )
     sum_two = summed(terms_two)
     rot_two = exchange(dspec_two, "col")
-    back_two = inverse_rows(rot_two, H2)
-    grad_norm_two = unpack_second(exchange(back_two, "row"))
-
-    grad_down = (
-        grad_out.astype(jnp.float32) + norm_pullback_step(down_wide, gain_second, grad_norm_two)
-    ).astype(jnp.bfloat16)
-    grad_section = upsample(grad_down, reduce_weight)
-    packed = pack_first(grad_section)
-    packed, sum_two = lax.optimization_barrier((packed, sum_two))
+    rot_two, sum_two = lax.optimization_barrier((rot_two, sum_two))
     swap_two = swap_grads(sum_two, H2)
-    half_grad = forward_rows(exchange(packed, "row"), (H1,))
-    half_grad, swap_two = lax.optimization_barrier((half_grad, swap_two))
-    half_grad = exchange(half_grad, "col")
+    back_two = exchange(inverse_rows(rot_two, H2), "row")
+    back_two, swap_two = lax.optimization_barrier((back_two, swap_two))
+
+    grad_section = expand_step(back_two, down, packed_out, weight.T, gains)
+    half_grad = exchange(forward_rows(exchange(grad_section, "row"), (H1,)), "col")
     dspec_one, terms_one = mix_back(H1, col_word, both, 0, half_grad, 0, kept, recv, 0)
     sum_one = summed(terms_one)
     rot_one = exchange(dspec_one, "col")
     rot_one, sum_one = lax.optimization_barrier((rot_one, sum_one))
     swap_one = swap_grads(sum_one, H1)
-    back_one = inverse_rows(rot_one, H1)
-    grad_norm_one = unpack_first(exchange(back_one, "row"))
+    grad_norm_one = unpack_first(exchange(inverse_rows(rot_one, H1), "row"))
     grad_images = (
-        grad_section.astype(jnp.float32)
-        + norm_pullback_step(pixels_wide, gain_first, grad_norm_one)
+        unpack_first(grad_section).astype(jnp.float32)
+        + norm_pullback_step(images.astype(jnp.float32), gain_first, grad_norm_one)
     ).astype(jnp.bfloat16)
     grad_first, grad_second = place_grads(
         sum_one, swap_one, sum_two, swap_two, col, *picks

time: 378 us -> 361 us (0.955)
  the two profiles are of different devices: /device:TPU:97 before, /device:TPU:105 now
where the time goes in v3:
time: 361 us; the launch traced here: 359 us
  blocking collectives  162 us (45%)
  starting transfers between devices  89.3 us (25%)
  waiting for transfers between devices  47.4 us (13%)
  local copies, waits for them, and re-layouts  22 us (6%)
  Pallas kernels  20.5 us (6%)
  between operations  14.7 us (4%)
    all_to_all x7, blocking collectives, exchange(): return lax.all_to_all(blocks, axis, split_axis=0, concat_axis=0, tiled=True)  150 us
    all_to_all x5, starting transfers between devices, exchange(): return lax.all_to_all(blocks, axis, split_axis=0, concat_axis=0, tiled=True)  54.4 us
    all_to_all x5, waiting for transfers between devices, exchange(): return lax.all_to_all(blocks, axis, split_axis=0, concat_axis=0, tiled=True)  25.2 us
    ppermute x2, starting transfers between devices, swap_grads(): lax.ppermute(zero, 'col', ((0, 2), (1, 3)))  15.3 us
    unnamed x87, local copies, waits for them, and re-layouts  13.7 us
    all_gather x1, blocking collectives, patch_filters(): return lax.all_gather(recv, 'rep', axis=0, tiled=False)  11.9 us
    ppermute x1, waiting for transfers between devices, swap_filters(): lax.ppermute(zero, 'col', ((2, 0), (3, 1)))  10.4 us
    ppermute x1, starting transfers between devices, swap_filters(): lax.ppermute(quarter, 'col', SWAP)  9.41 us
  transfers between devices with their start and end apart: 13, of which 7 were waited for; matrix products, arithmetic and copies ran while one was open for 3% of the time, Pallas kernels for 2%

profile of v3, /device:TPU:105, one launch (start us, length us, event | category | flops | bytes accessed | tf_op | source)
XLA Modules:
  0.0 358.8 jit_solution(13518420206245027505)
XLA Ops:
  7.2 1.2 copy.52
  8.5 1.0 copy-done
  10.9 1.8 first_norm.1
  13.4 8.5 %all-to-all-start = ((bf16[32,72,128]{2,1,0:T(8,128)(2,1)}), bf16[32,72,128]{2,1,0:T(8,128)(2,1)S(1)}, u32[]{:S(2)}, u32[]{:S(2)}) async-start(bf16[32,72,128]{2,1,0:T(8,128)(2,1)} %get-tuple-element.25), calls=%async_computation | async-start | bytes 1179648 | tf_op jit(solution)/shard_map/all_to_all | solution.py:582
  22.8 1.4 copy-done.8
  24.2 2.5 take_filters.1
  26.8 0.9 dynamic-slice_bitcast_fusion
  27.7 9.4 %collective-permute-start = (bf16[576,128]{1,0:T(8,128)(2,1)S(1)}, bf16[576,128]{1,0:T(8,128)(2,1)S(1)}, u32[]{:S(2)}, u32[]{:S(2)}) collective-permute-start(bf16[576,128]{1,0:T(8,128)(2,1)S(1)} %dynamic-slice_bitcast_fusion), channel_id=1, source_target_pairs={{0,12},{12,0},{4,8},{8,4},{1,13},{13,1},{5,9},{9,5},{2,14},{14,2},... | collective-permute-start | bytes 442376 | tf_op jit(solution)/shard_map/ppermute | solution.py:330
  37.1 0.9 constant_dynamic-slice_fusion.1
  38.9 1.3 collective-permute-start.1
  40.2 1.3 forward_rows_512_256.1
  41.5 10.4 %collective-permute-done.1 = bf16[6,2,128]{2,0,1:T(8,128)(2,1)S(1)} collective-permute-done((bf16[6,2,128]{2,0,1:T(8,128)(2,1)S(1)}, bf16[6,2,128]{2,0,1:T(8,128)(2,1)S(1)}, u32[]{:S(2)}, u32[]{:S(2)}) %collective-permute-start.1) | collective-permute-done | bytes 3104 | tf_op jit(solution)/shard_map/ppermute | solution.py:330
  51.9 8.5 %all-to-all-start.1 = ((bf16[4,576,128]{2,1,0:T(8,128)(2,1)}), bf16[4,576,128]{2,1,0:T(8,128)(2,1)S(1)}, u32[]{:S(2)}, u32[]{:S(2)}) async-start(bf16[4,576,128]{2,1,0:T(8,128)(2,1)} %forward_rows_512_256.1), calls=%async_computation.1 | async-start | bytes 1179648 | tf_op jit(solution)/shard_map/all_to_all | solution.py:582
  60.9 11.9 %all-gather = bf16[2304,128]{1,0:T(8,128)(2,1)S(1)} all-gather(bf16[576,128]{1,0:T(8,128)(2,1)S(1)} %pad_maximum_fusion), channel_id=2, replica_groups=mesh['row'=32,'col'=4,'rep'=4] {'rep'}, dimensions={0}, use_global_device_ids=true | all-gather | bytes 737280 | tf_op jit(solution)/shard_map/all_gather | solution.py:343
  72.8 18.1 %all-to-all-done.1.x_ref.g_ref = bf16[4,576,128]{2,1,0:T(8,128)(2,1)S(1)} async-done(((bf16[4,576,128]{2,1,0:T(8,128)(2,1)}), bf16[4,576,128]{2,1,0:T(8,128)(2,1)S(1)}, u32[]{:S(2)}, u32[]{:S(2)}) %all-to-all-start.1) | async-done | bytes 589856 | tf_op jit(solution)/shard_map/all_to_all | solution.py:582
  90.9 1.0 copy-done.14
  92.0 1.5 mix_forward_512.1
  93.5 20.8 %all_to_all.60.x_ref = bf16[4,384,128]{2,1,0:T(8,128)(2,1)S(1)} all-to-all(bf16[4,384,128]{2,1,0:T(8,128)(2,1)S(1)} %mix_forward_512.1), channel_id=1, replica_groups=mesh['row'=32,'col'=4,'rep'=4] {'col'}, dimensions={0} | all-to-all | bytes 786432 | tf_op jit(solution)/shard_map/all_to_all | solution.py:582
  114.3 1.2 inverse_rows_512.2
  115.5 11.8 %all-to-all-start.3 = ((bf16[32,48,128]{2,1,0:T(8,128)(2,1)}), bf16[32,48,128]{2,1,0:T(8,128)(2,1)S(1)}, u32[]{:S(2)}, u32[]{:S(2)}) async-start(bf16[32,48,128]{2,1,0:T(8,128)(2,1)} %inverse_rows_512.2), calls=%async_computation.3 | async-start | bytes 786432 | tf_op jit(solution)/shard_map/all_to_all | solution.py:582
  128.1 0.9 copy.57
  129.9 0.9 copy.59.gain_ref
  130.8 7.0 %all-to-all-done.3.m_ref = bf16[32,48,128]{2,1,0:T(8,128)(2,1)S(1)} async-done(((bf16[32,48,128]{2,1,0:T(8,128)(2,1)}), bf16[32,48,128]{2,1,0:T(8,128)(2,1)S(1)}, u32[]{:S(2)}, u32[]{:S(2)}) %all-to-all-start.3) | async-done | bytes 393248 | tf_op jit(solution)/shard_map/all_to_all | solution.py:582
  137.8 1.5 reduce_step.1
  140.0 13.7 %all_to_all.61.refs_0_ = bf16[32,24,128]{2,1,0:T(8,128)(2,1)S(1)} all-to-all(bf16[32,24,128]{2,1,0:T(8,128)(2,1)S(1)} %get-tuple-element.31), channel_id=1, replica_groups=mesh['row'=32,'col'=4,'rep'=4] {'row'}, dimensions={0} | all-to-all | bytes 393216 | tf_op jit(solution)/shard_map/all_to_all | solution.py:582
  154.0 20.4 %all_to_all.62.x_ref = bf16[4,192,128]{2,1,0:T(8,128)(2,1)S(1)} all-to-all(bf16[4,192,128]{2,1,0:T(8,128)(2,1)S(1)} %forward_rows_256.1), channel_id=1, replica_groups=mesh['row'=32,'col'=4,'rep'=4] {'col'}, dimensions={0} | all-to-all | bytes 393216 | tf_op jit(solution)/shard_map/all_to_all | solution.py:582
  174.4 1.0 copy-done.3
  175.4 1.5 mix_back_256.1
  177.7 17.5 %all_to_all.63.x_ref = bf16[4,192,128]{2,1,0:T(8,128)(2,1)S(1)} all-to-all(bf16[4,192,128]{2,1,0:T(8,128)(2,1)S(1)} %get-tuple-element.32), channel_id=1, replica_groups=mesh['row'=32,'col'=4,'rep'=4] {'col'}, dimensions={0} | all-to-all | bytes 393216 | tf_op jit(solution)/shard_map/all_to_all | solution.py:582
  195.2 4.6 %reduce-scatter.3.cloned.1.call-done = bf16[1,384,128]{2,1,0:T(8,128)(2,1)} async-done(((bf16[4,384,128]{2,1,0:T(8,128)(2,1)}), bf16[1,384,128]{2,1,0:T(8,128)(2,1)}) %reduce-scatter.3.cloned.1.call-update) | async-done | bytes 98320 | tf_op jit(solution)/shard_map/reduce_scatter | solution.py:369
  200.7 10.1 %all-to-all-start.7 = ((bf16[32,24,128]{2,1,0:T(8,128)(2,1)}), bf16[32,24,128]{2,1,0:T(8,128)(2,1)S(1)}, u32[]{:S(2)}, u32[]{:S(2)}) async-start(bf16[32,24,128]{2,1,0:T(8,128)(2,1)} %inverse_rows_256.1), calls=%async_computation.8 | async-start | bytes 393216 | tf_op jit(solution)/shard_map/all_to_all | solution.py:582
  211.7 5.4 %collective-permute-start.2 = (bf16[192,128]{1,0:T(8,128)(2,1)S(1)}, bf16[192,128]{1,0:T(8,128)(2,1)S(1)}, u32[]{:S(2)}, u32[]{:S(2)}) collective-permute-start(bf16[192,128]{1,0:T(8,128)(2,1)S(1)} %get-tuple-element.52), channel_id=1, source_target_pairs={{0,12},{12,0},{4,8},{8,4},{1,13},{13,1},{5,9},{9,5},{2,14},{14,2},... | collective-permute-start | bytes 147464 | tf_op jit(solution)/shard_map/ppermute | solution.py:376
  217.1 8.8 %collective-permute-start.3 = (bf16[6,1,128]{2,0,1:T(8,128)(2,1)S(1)}, bf16[6,1,128]{2,0,1:T(8,128)(2,1)S(1)}, u32[]{:S(2)}, u32[]{:S(2)}) collective-permute-start(bf16[6,1,128]{2,0,1:T(8,128)(2,1)S(1)} %copy.66), channel_id=1, source_target_pairs={{0,8},{4,12},{1,9},{5,13},{2,10},{6,14},{3,11},{7,15},{16,24},{20,... | collective-permute-start | bytes 4616 | tf_op jit(solution)/shard_map/ppermute | solution.py:376
  227.4 0.9 copy-done.10
  228.3 0.9 copy-done.19
  229.3 0.9 copy-done.21
  231.1 1.7 expand_step.1
  232.8 19.2 %all_to_all.64.refs_0_ = bf16[32,48,128]{2,1,0:T(8,128)(2,1)S(1)} all-to-all(bf16[32,48,128]{2,1,0:T(8,128)(2,1)S(1)} %expand_step.1), channel_id=1, replica_groups=mesh['row'=32,'col'=4,'rep'=4] {'row'}, dimensions={0} | all-to-all | bytes 786432 | tf_op jit(solution)/shard_map/all_to_all | solution.py:582
  252.5 33.8 %all_to_all.65.g_ref = bf16[4,384,128]{2,1,0:T(8,128)(2,1)S(1)} all-to-all(bf16[4,384,128]{2,1,0:T(8,128)(2,1)S(1)} %forward_rows_512.1), channel_id=1, replica_groups=mesh['row'=32,'col'=4,'rep'=4] {'col'}, dimensions={0} | all-to-all | bytes 786432 | tf_op jit(solution)/shard_map/all_to_all | solution.py:582
  286.3 3.0 mix_back_512.1
  289.3 24.9 %all_to_all.66.x_ref = bf16[4,384,128]{2,1,0:T(8,128)(2,1)S(1)} all-to-all(bf16[4,384,128]{2,1,0:T(8,128)(2,1)S(1)} %get-tuple-element.39), channel_id=1, replica_groups=mesh['row'=32,'col'=4,'rep'=4] {'col'}, dimensions={0} | all-to-all | bytes 786432 | tf_op jit(solution)/shard_map/all_to_all | solution.py:582
  315.0 1.2 inverse_rows_512.3
  316.2 15.4 %all-to-all-start.11 = ((bf16[32,48,128]{2,1,0:T(8,128)(2,1)}), bf16[32,48,128]{2,1,0:T(8,128)(2,1)S(1)}, u32[]{:S(2)}, u32[]{:S(2)}) async-start(bf16[32,48,128]{2,1,0:T(8,128)(2,1)} %inverse_rows_512.3), calls=%async_computation.13 | async-start | bytes 786432 | tf_op jit(solution)/shard_map/all_to_all | solution.py:582
  331.8 3.5 collective-permute-start.5
  335.3 6.4 %collective-permute-start.4 = (bf16[6,1,128]{2,0,1:T(8,128)(2,1)S(1)}, bf16[6,1,128]{2,0,1:T(8,128)(2,1)S(1)}, u32[]{:S(2)}, u32[]{:S(2)}) collective-permute-start(bf16[6,1,128]{2,0,1:T(8,128)(2,1)S(1)} %copy.67), channel_id=1, source_target_pairs={{0,8},{4,12},{1,9},{5,13},{2,10},{6,14},{3,11},{7,15},{16,24},{20,... | collective-permute-start | bytes 4616 | tf_op jit(solution)/shard_map/ppermute | solution.py:376
  342.5 6.0 %collective-permute-done.5 = bf16[384,128]{1,0:T(8,128)(2,1)S(1)} collective-permute-done((bf16[384,128]{1,0:T(8,128)(2,1)S(1)}, bf16[384,128]{1,0:T(8,128)(2,1)S(1)}, u32[]{:S(2)}, u32[]{:S(2)}) %collective-permute-start.5) | collective-permute-done | bytes 98336 | tf_op jit(solution)/shard_map/ppermute | solution.py:376
  348.6 1.7 place_grads.1
  350.9 1.1 fusion.6
  (135 shorter events, 14.4 us)
Async XLA Ops:
  7.2 14.8 %copy-start.34 = (bf16[128,128]{0,1:T(8,128)(2,1)S(1)}, bf16[128,128]{0,1:T(8,128)(2,1)}, u32[]{:S(2)}) copy-start(bf16[128,128]{0,1:T(8,128)(2,1)} %constant.63.clone) | copy-start | bytes 98308
  7.2 14.8 %copy-start.35 = (bf16[128,128]{0,1:T(8,128)(2,1)S(1)}, bf16[128,128]{0,1:T(8,128)(2,1)}, u32[]{:S(2)}) copy-start(bf16[128,128]{0,1:T(8,128)(2,1)} %constant.64.clone) | copy-start | bytes 98308
  7.2 14.9 %copy-start.36 = (bf16[64,64]{0,1:T(8,128)(2,1)S(1)}, bf16[64,64]{0,1:T(8,128)(2,1)}, u32[]{:S(2)}) copy-start(bf16[64,64]{0,1:T(8,128)(2,1)} %constant.65.clone) | copy-start | bytes 24580
  7.2 14.9 %copy-start.37 = (bf16[64,64]{0,1:T(8,128)(2,1)S(1)}, bf16[64,64]{0,1:T(8,128)(2,1)}, u32[]{:S(2)}) copy-start(bf16[64,64]{0,1:T(8,128)(2,1)} %constant.66.clone) | copy-start | bytes 24580
  7.2 15.6 %copy-start.16 = (bf16[512,512]{1,0:T(8,128)(2,1)S(1)}, bf16[512,512]{1,0:T(8,128)(2,1)}, u32[]{:S(2)}) copy-start(bf16[512,512]{1,0:T(8,128)(2,1)} %constant.67.clone.lanes) | copy-start | bytes 1572868
  8.5 1.0 copy-start
  9.5 0.8 copy-start.27
  10.9 11.9 %copy-start.9 = (f32[2,6,64,256]{3,2,1,0:T(8,128)S(1)}, f32[2,6,64,256]{3,2,1,0:T(8,128)}, u32[]{:S(2)}) copy-start(f32[2,6,64,256]{3,2,1,0:T(8,128)} %second_ref.1) | copy-start | bytes 2359300
  13.4 26.8 %all-to-all-start = ((bf16[32,72,128]{2,1,0:T(8,128)(2,1)}), bf16[32,72,128]{2,1,0:T(8,128)(2,1)S(1)}, u32[]{:S(2)}, u32[]{:S(2)}) async-start(bf16[32,72,128]{2,1,0:T(8,128)(2,1)} %get-tuple-element.25), calls=%async_computation | async-start | bytes 1179648 | tf_op jit(solution)/shard_map/all_to_all | solution.py:582
  22.8 1.4 copy-start.8
  24.2 16.0 %copy-start.4 = (bf16[512,512]{1,0:T(8,128)(2,1)S(1)}, bf16[512,512]{1,0:T(8,128)(2,1)}, u32[]{:S(2)}) copy-start(bf16[512,512]{1,0:T(8,128)(2,1)} %constant.69.clone.refs_1_) | copy-start | bytes 1572868
  24.2 16.0 %copy-start.11 = (bf16[256,256]{1,0:T(8,128)(2,1)S(1)}, bf16[256,256]{1,0:T(8,128)(2,1)}, u32[]{:S(2)}) copy-start(bf16[256,256]{1,0:T(8,128)(2,1)} %constant.70.clone.refs_2_.refs_1_) | copy-start | bytes 393220
  27.7 24.3 %collective-permute-start = (bf16[576,128]{1,0:T(8,128)(2,1)S(1)}, bf16[576,128]{1,0:T(8,128)(2,1)S(1)}, u32[]{:S(2)}, u32[]{:S(2)}) collective-permute-start(bf16[576,128]{1,0:T(8,128)(2,1)S(1)} %dynamic-slice_bitcast_fusion), channel_id=1, source_target_pairs={{0,12},{12,0},{4,8},{8,4},{1,13},{13,1},{5,9},{9,5},{2,14},{14,2},... | collective-permute-start | bytes 442376 | tf_op jit(solution)/shard_map/ppermute | solution.py:330
  38.9 13.1 %collective-permute-start.1 = (bf16[6,2,128]{2,0,1:T(8,128)(2,1)S(1)}, bf16[6,2,128]{2,0,1:T(8,128)(2,1)S(1)}, u32[]{:S(2)}, u32[]{:S(2)}) collective-permute-start(bf16[6,2,128]{2,0,1:T(8,128)(2,1)S(1)} %pad_maximum_fusion.1), channel_id=1, source_target_pairs={{8,0},{12,4},{9,1},{13,5},{10,2},{14,6},{11,3},{15,7},{24,16},{28,... | collective-permute-start | bytes 9224 | tf_op jit(solution)/shard_map/ppermute | solution.py:330
  41.5 49.4 %copy-start.12 = (bf16[512,512]{1,0:T(8,128)(2,1)S(1)}, bf16[512,512]{1,0:T(8,128)(2,1)}, u32[]{:S(2)}) copy-start(bf16[512,512]{1,0:T(8,128)(2,1)} %constant.71.clone.cos.cos_back) | copy-start | bytes 1572868
  51.9 39.0 %all-to-all-start.1 = ((bf16[4,576,128]{2,1,0:T(8,128)(2,1)}), bf16[4,576,128]{2,1,0:T(8,128)(2,1)S(1)}, u32[]{:S(2)}, u32[]{:S(2)}) async-start(bf16[4,576,128]{2,1,0:T(8,128)(2,1)} %forward_rows_512_256.1), calls=%async_computation.1 | async-start | bytes 1179648 | tf_op jit(solution)/shard_map/all_to_all | solution.py:582
  90.9 1.0 copy-start.14
  92.0 22.3 %copy-start.6 = (bf16[512,512]{1,0:T(8,128)(2,1)S(1)}, bf16[512,512]{1,0:T(8,128)(2,1)}, u32[]{:S(2)}) copy-start(bf16[512,512]{1,0:T(8,128)(2,1)} %constant.73.clone.table) | copy-start | bytes 1572868
  93.4 33.9 %copy-start.31 = (bf16[192,384]{1,0:T(8,128)(2,1)S(1)}, bf16[192,384]{1,0:T(8,128)(2,1)}, u32[]{:S(2)}) copy-start(bf16[192,384]{1,0:T(8,128)(2,1)} %param.36) | copy-start | bytes 442372
  93.5 35.5 %copy-start.40 = (f32[192]{0:T(256)S(1)}, f32[192]{0:T(256)}, u32[]{:S(2)}) copy-start(f32[192]{0:T(256)} %param.37) | copy-start | bytes 2308
  114.3 23.5 %copy-start.1 = (bf16[1,96,16,128]{3,2,1,0:T(8,128)(2,1)S(1)}, bf16[1,96,16,128]{3,2,1,0:T(8,128)(2,1)}, u32[]{:S(2)}) copy-start(bf16[1,96,16,128]{3,2,1,0:T(8,128)(2,1)} %param.33) | copy-start | bytes 1179652
  114.3 23.5 %copy-start.25 = (bf16[128,256]{1,0:T(8,128)(2,1)S(1)}, bf16[128,256]{1,0:T(8,128)(2,1)}, u32[]{:S(2)}) copy-start(bf16[128,256]{1,0:T(8,128)(2,1)} %constant.74.clone.spread_ref) | copy-start | bytes 196612
  115.5 22.4 %all-to-all-start.3 = ((bf16[32,48,128]{2,1,0:T(8,128)(2,1)}), bf16[32,48,128]{2,1,0:T(8,128)(2,1)S(1)}, u32[]{:S(2)}, u32[]{:S(2)}) async-start(bf16[32,48,128]{2,1,0:T(8,128)(2,1)} %inverse_rows_512.2), calls=%async_computation.3 | async-start | bytes 786432 | tf_op jit(solution)/shard_map/all_to_all | solution.py:582
  127.3 47.1 %copy-start.2 = (bf16[512,512]{1,0:T(8,128)(2,1)S(1)}, bf16[512,512]{1,0:T(8,128)(2,1)}, u32[]{:S(2)}) copy-start(bf16[512,512]{1,0:T(8,128)(2,1)} %constant.75.clone.cos.cos_back) | copy-start | bytes 1572868
  127.3 72.5 %reduce-scatter.3.cloned.1.call-start = ((), (), s32[]{:S(2)}) async-start(), calls=%async_computation.14 | async-start | bytes 491520 | tf_op jit(solution)/shard_map/reduce_scatter | solution.py:369
  174.4 1.0 copy-start.3
  175.4 24.3 %copy-start.22 = (bf16[256,256]{1,0:T(8,128)(2,1)S(1)}, bf16[256,256]{1,0:T(8,128)(2,1)}, u32[]{:S(2)}) copy-start(bf16[256,256]{1,0:T(8,128)(2,1)} %constant.77.clone.table) | copy-start | bytes 393220
  200.7 51.4 %copy-start.5 = (bf16[512,512]{1,0:T(8,128)(2,1)S(1)}, bf16[512,512]{1,0:T(8,128)(2,1)}, u32[]{:S(2)}) copy-start(bf16[512,512]{1,0:T(8,128)(2,1)} %constant.69.clone.refs_1_) | copy-start | bytes 1572868
  200.7 26.2 %all-to-all-start.7 = ((bf16[32,24,128]{2,1,0:T(8,128)(2,1)}), bf16[32,24,128]{2,1,0:T(8,128)(2,1)S(1)}, u32[]{:S(2)}, u32[]{:S(2)}) async-start(bf16[32,24,128]{2,1,0:T(8,128)(2,1)} %inverse_rows_256.1), calls=%async_computation.8 | async-start | bytes 393216 | tf_op jit(solution)/shard_map/all_to_all | solution.py:582
  210.8 104.2 %reduce-scatter.5.cloned.1.call-start = ((), (), s32[]{:S(2)}) async-start(), calls=%async_computation.15 | async-start | bytes 983040 | tf_op jit(solution)/shard_map/reduce_scatter | solution.py:369
  211.7 15.1 %collective-permute-start.2 = (bf16[192,128]{1,0:T(8,128)(2,1)S(1)}, bf16[192,128]{1,0:T(8,128)(2,1)S(1)}, u32[]{:S(2)}, u32[]{:S(2)}) collective-permute-start(bf16[192,128]{1,0:T(8,128)(2,1)S(1)} %get-tuple-element.52), channel_id=1, source_target_pairs={{0,12},{12,0},{4,8},{8,4},{1,13},{13,1},{5,9},{9,5},{2,14},{14,2},... | collective-permute-start | bytes 147464 | tf_op jit(solution)/shard_map/ppermute | solution.py:376
  217.1 9.7 %collective-permute-start.3 = (bf16[6,1,128]{2,0,1:T(8,128)(2,1)S(1)}, bf16[6,1,128]{2,0,1:T(8,128)(2,1)S(1)}, u32[]{:S(2)}, u32[]{:S(2)}) collective-permute-start(bf16[6,1,128]{2,0,1:T(8,128)(2,1)S(1)} %copy.66), channel_id=1, source_target_pairs={{0,8},{4,12},{1,9},{5,13},{2,10},{6,14},{3,11},{7,15},{16,24},{20,... | collective-permute-start | bytes 4616 | tf_op jit(solution)/shard_map/ppermute | solution.py:376
  227.4 0.9 copy-start.10
  228.3 0.9 copy-start.19
  229.3 0.9 copy-start.21
  230.2 0.9 copy-start.23
  232.8 53.5 %copy-start.13 = (bf16[512,512]{1,0:T(8,128)(2,1)S(1)}, bf16[512,512]{1,0:T(8,128)(2,1)}, u32[]{:S(2)}) copy-start(bf16[512,512]{1,0:T(8,128)(2,1)} %constant.71.clone.cos.cos_back) | copy-start | bytes 1572868
  232.8 53.5 %copy-start.15 = (bf16[512,512]{1,0:T(8,128)(2,1)S(1)}, bf16[512,512]{1,0:T(8,128)(2,1)}, u32[]{:S(2)}) copy-start(bf16[512,512]{1,0:T(8,128)(2,1)} %constant.72.clone.sin.sin_back) | copy-start | bytes 1572868
  289.2 25.8 %copy-start.7 = (bf16[512,512]{1,0:T(8,128)(2,1)S(1)}, bf16[512,512]{1,0:T(8,128)(2,1)}, u32[]{:S(2)}) copy-start(bf16[512,512]{1,0:T(8,128)(2,1)} %constant.73.clone.table) | copy-start | bytes 1572868
  314.2 27.8 %copy-start.33 = (bf16[192,128]{1,0:T(8,128)(2,1)S(1)}, bf16[192,128]{1,0:T(8,128)(2,1)}, u32[]{:S(2)}) copy-start(bf16[192,128]{1,0:T(8,128)(2,1)} %copy-done.32) | copy-start | bytes 147460
  314.2 27.8 %copy-start.39 = (bf16[6,1,128]{2,0,1:T(8,128)(2,1)S(1)}, bf16[6,1,128]{2,0,1:T(8,128)(2,1)}, u32[]{:S(2)}) copy-start(bf16[6,1,128]{2,0,1:T(8,128)(2,1)} %copy-done.38) | copy-start | bytes 4612
  315.0 16.7 %copy-start.30 = (bf16[1,768,128]{2,1,0:T(8,128)(2,1)S(1)}, bf16[1,768,128]{2,1,0:T(8,128)(2,1)}, u32[]{:S(2)}) copy-start(bf16[1,768,128]{2,1,0:T(8,128)(2,1)} %reduce-scatter.5.cloned.1.call-done) | copy-start | bytes 589828
  315.0 33.6 %copy-start.24 = (bf16[2,128,64]{2,1,0:T(8,128)(2,1)S(1)}, bf16[2,128,64]{2,1,0:T(8,128)(2,1)}, u32[]{:S(2)}) copy-start(bf16[2,128,64]{2,1,0:T(8,128)(2,1)} %constant.79.clone.lanes) | copy-start | bytes 98308
  315.0 33.6 %copy-start.26 = (bf16[64,64]{1,0:T(8,128)(2,1)S(1)}, bf16[64,64]{1,0:T(8,128)(2,1)}, u32[]{:S(2)}) copy-start(bf16[64,64]{1,0:T(8,128)(2,1)} %get-tuple-element.55.pick_second) | copy-start | bytes 24580
  315.0 35.3 %copy-start.29 = (f32[96]{0:T(128)S(1)}, f32[96]{0:T(128)}, u32[]{:S(2)}) copy-start(f32[96]{0:T(128)} %gain_ref.1) | copy-start | bytes 1156
  316.2 34.1 %all-to-all-start.11 = ((bf16[32,48,128]{2,1,0:T(8,128)(2,1)}), bf16[32,48,128]{2,1,0:T(8,128)(2,1)S(1)}, u32[]{:S(2)}, u32[]{:S(2)}) async-start(bf16[32,48,128]{2,1,0:T(8,128)(2,1)} %inverse_rows_512.3), calls=%async_computation.13 | async-start | bytes 786432 | tf_op jit(solution)/shard_map/all_to_all | solution.py:582
  331.8 16.7 %collective-permute-start.5 = (bf16[384,128]{1,0:T(8,128)(2,1)S(1)}, bf16[384,128]{1,0:T(8,128)(2,1)S(1)}, u32[]{:S(2)}, u32[]{:S(2)}) collective-permute-start(bf16[384,128]{1,0:T(8,128)(2,1)S(1)} %get-tuple-element.49), channel_id=1, source_target_pairs={{0,12},{12,0},{4,8},{8,4},{1,13},{13,1},{5,9},{9,5},{2,14},{14,2},... | collective-permute-start | bytes 294920 | tf_op jit(solution)/shard_map/ppermute | solution.py:376
  335.3 7.2 %collective-permute-start.4 = (bf16[6,1,128]{2,0,1:T(8,128)(2,1)S(1)}, bf16[6,1,128]{2,0,1:T(8,128)(2,1)S(1)}, u32[]{:S(2)}, u32[]{:S(2)}) collective-permute-start(bf16[6,1,128]{2,0,1:T(8,128)(2,1)S(1)} %copy.67), channel_id=1, source_target_pairs={{0,8},{4,12},{1,9},{5,13},{2,10},{6,14},{3,11},{7,15},{16,24},{20,... | collective-permute-start | bytes 4616 | tf_op jit(solution)/shard_map/ppermute | solution.py:376
  (6 other events, 4.0 us)
Sparse Core Ops, SparseCore 0:
  177.8 21.8 reduce-scatter.2
  289.4 25.5 reduce-scatter.4

commit v4 on v3

--- a/solution.py
+++ b/solution.py
@@ -56,14 +56,6 @@
             full[:, p, :, :, p, :] = blocks
         out.append(full.reshape(512, 512))
     return tuple(out)
-
-
-def mirror_matrix(slots):
-    matrix = np.zeros((2 * slots, 2 * slots))
-    for s in range(slots):
-        matrix[s, slots - s] = 1.0
-        matrix[slots + s, (2 * slots - s) % (2 * slots)] = 1.0
-    return matrix
 
 
 def constant(values):
@@ -190,39 +182,37 @@
         out_ref[q, count:, :] = rot_imag[:, q * LANES : (q + 1) * LANES]
 
 
-def masks(col_ref, slots):
-    col = col_ref[0]
+def masks(place_ref, slots):
+    col = place_ref[0]
     row = lax.broadcasted_iota(jnp.int32, (GROUPS * slots, 512), 0)
     return (lax.rem(row, slots) + col * slots) == 0, col < 2
 
 
-def mix_forward_kernel(n, first_filter, col_ref, x_ref, kept_ref, recv_ref, cos, sin, out_ref):
+def mix_forward_kernel(n, first_filter, place_ref, x_ref, kept_ref, recv_ref, tables, out_ref):
     slots = n // 8
-    special, near = masks(col_ref, slots)
-    up_r, up_i, down_r, down_i = spectrum(x_ref, 0, slots, special, cos[...], sin[...])
+    special, near = masks(place_ref, slots)
+    cos, sin = tables[0], tables[1]
+    up_r, up_i, down_r, down_i = spectrum(x_ref, 0, slots, special, cos, sin)
     real, imag = filters(near, kept_ref, recv_ref, first_filter, slots)
     up = (real[0] * up_r - imag[0] * up_i, real[0] * up_i + imag[0] * up_r)
     down = (real[1] * down_r - imag[1] * down_i, real[1] * down_i + imag[1] * down_r)
-    put_inverse(out_ref, slots, special, up, down, cos[...], sin[...])
+    put_inverse(out_ref, slots, special, up, down, cos, sin)
 
 
 def mix_back_kernel(
-    n, first_filter, first_field, first_grad, col_ref, x_ref, g_ref, kept_ref, recv_ref,
-    cos, sin, cos_back, sin_back, out_ref, grad_ref,
+    n, first_filter, first_field, first_grad, place_ref, x_ref, g_ref, kept_ref, recv_ref,
+    tables, out_ref, total_ref, grad_ref, sem,
 ):
     slots = n // 8
     count = GROUPS * slots
-    special, near = masks(col_ref, slots)
-    field = spectrum(x_ref, first_field, slots, special, cos[...], sin[...])
-    grad = spectrum(g_ref, first_grad, slots, special, cos[...], sin[...])
-    real, imag = filters(near, kept_ref, recv_ref, first_filter, slots)
-    sides, terms = [], []
+    special, near = masks(place_ref, slots)
+    field = spectrum(x_ref, first_field, slots, special, tables[0], tables[1])
+    grad = spectrum(g_ref, first_grad, slots, special, tables[0], tables[1])
+    terms = []
     for side in range(2):
         g_r, g_i = grad[2 * side], grad[2 * side + 1]
         s_r, s_i = field[2 * side], field[2 * side + 1]
-        sides.append((real[side] * g_r + imag[side] * g_i, real[side] * g_i - imag[side] * g_r))
         terms.append((g_r * s_r + g_i * s_i, g_i * s_r - g_r * s_i))
-    put_inverse(out_ref, slots, special, sides[0], sides[1], cos_back[...], sin_back[...])
     for part in range(2):
         up, down = terms[0][part], terms[1][part]
         kept = jnp.where(near, up, down).astype(jnp.bfloat16)
@@ -231,132 +221,221 @@
             lanes = slice(q * LANES, (q + 1) * LANES)
             grad_ref[q, part * count : (part + 1) * count, :] = kept[:, lanes]
             grad_ref[q, (2 + part) * count : (3 + part) * count, :] = sent[:, lanes]
+    copy = pltpu.make_async_copy(grad_ref, total_ref, sem)
+    copy.start()
+    real, imag = filters(near, kept_ref, recv_ref, first_filter, slots)
+    sides = []
+    for side in range(2):
+        g_r, g_i = grad[2 * side], grad[2 * side + 1]
+        sides.append((real[side] * g_r + imag[side] * g_i, real[side] * g_i - imag[side] * g_r))
+    last = tables.shape[0] - 2
+    put_inverse(out_ref, slots, special, sides[0], sides[1], tables[last], tables[last + 1])
+    copy.wait()
 
 
 def smem():
     return pl.BlockSpec(memory_space=pltpu.SMEM)
 
 
+def hbm(count):
+    return [pl.BlockSpec(memory_space=pltpu.HBM)] * count
+
+
 def vmem(count):
     return [pl.BlockSpec(memory_space=pltpu.VMEM)] * count
 
 
-def mix_forward(n, col, entries, kept, recv, first_filter):
+def mix_forward(n, place, entries, kept, recv, first_filter):
     rows = 2 * GROUPS * n // 8
-    cos, sin = col_tables(n)
     return pl.pallas_call(
         functools.partial(mix_forward_kernel, n, first_filter),
         out_shape=jax.ShapeDtypeStruct((COLS, rows, LANES), jnp.bfloat16),
-        in_specs=[smem()] + vmem(5),
+        in_specs=[smem()] + vmem(4),
         name="mix_forward_" + str(n),
         **params(8 * rows * 512 * 512, 4 << 20),
-    )(col, entries, kept, recv, constant(cos), constant(sin))
-
-
-def mix_back(n, col, entries, first_field, upstream, first_grad, kept, recv, first_filter):
+    )(place, entries, kept, recv, constant(np.stack(col_tables(n))))
+
+
+def mix_back(n, place, entries, first_field, upstream, first_grad, kept, recv, first_filter):
     rows = 2 * GROUPS * n // 8
-    cos, sin = col_tables(n)
+    tables = col_tables(n)
+    if n == H2:
+        tables = tables + tuple(table.T for table in tables)
+    total = (COLS, 2 * rows, LANES)
     return pl.pallas_call(
         functools.partial(mix_back_kernel, n, first_filter, first_field, first_grad),
         out_shape=(
             jax.ShapeDtypeStruct((COLS, rows, LANES), jnp.bfloat16),
-            jax.ShapeDtypeStruct((COLS, 2 * rows, LANES), jnp.bfloat16),
+            jax.ShapeDtypeStruct(total, jnp.bfloat16),
         ),
-        in_specs=[smem()] + vmem(8),
+        in_specs=[smem()] + vmem(5),
+        out_specs=tuple(vmem(1) + hbm(1)),
+        scratch_shapes=[pltpu.VMEM(total, jnp.bfloat16), pltpu.SemaphoreType.DMA],
         name="mix_back_" + str(n),
         **params(12 * rows * 512 * 512, 6 << 20),
-    )(
-        col, entries, upstream, kept, recv,
-        constant(cos), constant(sin), constant(cos.T), constant(sin.T),
-    )
-
-
-def pair_lanes():
-    matrix = np.zeros((2, COLS, 64, COLS, 2, 64))
-    for p in range(2):
-        for q in range(COLS):
-            matrix[p, q, :, q, p, :] = np.eye(64)
-    return matrix.reshape(512, 512)
-
-
-def take_filters_kernel(first_ref, second_ref, pick_first, pick_second, lanes, kept_ref, sent_ref):
-    at = 0
-    for n, pick in ((H1, pick_first), (H2, pick_second)):
+    )(place, entries, upstream, kept, recv, constant(np.stack(tables)))
+
+
+def grid_of(rows, columns):
+    shape = (rows, columns)
+    return lax.broadcasted_iota(jnp.int32, shape, 0), lax.broadcasted_iota(jnp.int32, shape, 1)
+
+
+def ones_at(mask):
+    return jnp.where(mask, 1.0, 0.0).astype(jnp.bfloat16)
+
+
+def kept_rows(near, slots):
+    slot, local = grid_of(slots, 2 * slots)
+    return ones_at(local == jnp.where(near, slot, slots - slot))
+
+
+def sent_rows(near, slots):
+    slot, local = grid_of(slots, 2 * slots)
+    return ones_at(local == jnp.where(near, slots + slot, lax.rem(2 * slots - slot, 2 * slots)))
+
+
+def quarter_lanes(quarter):
+    wide_at, narrow_at = grid_of(512, LANES)
+    return ones_at(
+        wide_at == lax.div(narrow_at, 64) * 256 + 64 * quarter + lax.rem(narrow_at, 64)
+    )
+
+
+def second_pair(ref, part, g):
+    pair = [ref[part, 2 * g + i].astype(jnp.bfloat16) for i in range(2)]
+    return jnp.concatenate(pair, axis=1)
+
+
+def send_filters_kernel(
+    place_ref, first_ref, second_ref, sent_ref, zero_ref, first_buf, second_buf, sems
+):
+    quarter = place_ref[1]
+    at = pl.ds(pl.multiple_of(quarter * LANES, LANES), LANES)
+    first_copy = pltpu.make_async_copy(first_ref.at[:, :, :, at], first_buf, sems.at[0])
+    second_copy = pltpu.make_async_copy(second_ref, second_buf, sems.at[1])
+    first_copy.start()
+    second_copy.start()
+    near = place_ref[0] < 2
+    zeros = []
+    for n in (H1, H2):
         slots = n // 8
+        first = 0 if n == H1 else 2 * GROUPS * H1 // 8
+        pick = sent_rows(near, slots)
+        if n == H1:
+            first_copy.wait()
+        else:
+            second_copy.wait()
+            lanes = quarter_lanes(quarter)
+        for part in range(2):
+            for g in range(GROUPS):
+                if n == H1:
+                    rows = first_buf[part, g].astype(jnp.bfloat16)
+                else:
+                    rows = dot(second_pair(second_buf, part, g), lanes).astype(jnp.bfloat16)
+                rows = dot(pick, rows)
+                zeros.append(rows[:1])
+                sent_ref[first : first + slots, :] = rows.astype(jnp.bfloat16)
+                first += slots
+    zeros.append(jnp.zeros((4, LANES), jnp.float32))
+    zero_ref[...] = jnp.concatenate(zeros, axis=0).astype(jnp.bfloat16)
+
+
+def keep_filters_kernel(place_ref, first_ref, second_ref, kept_ref):
+    near = place_ref[0] < 2
+    first = 0
+    lanes = [quarter_lanes(q) for q in range(COLS)]
+    for n in (H1, H2):
+        slots = n // 8
+        pick = kept_rows(near, slots)
         for part in range(2):
             for g in range(GROUPS):
                 if n == H1:
                     rows = first_ref[part, g].astype(jnp.bfloat16)
                 else:
-                    pair = [second_ref[part, 2 * g + i].astype(jnp.bfloat16) for i in range(2)]
-                    rows = dot(jnp.concatenate(pair, axis=1), lanes[...]).astype(jnp.bfloat16)
-                rows = dot(pick[...], rows).astype(jnp.bfloat16)
+                    rows = second_pair(second_ref, part, g)
+                rows = dot(pick, rows).astype(jnp.bfloat16)
                 for q in range(COLS):
-                    cut = slice(q * LANES, (q + 1) * LANES)
-                    kept_ref[q, at : at + slots, :] = rows[:slots, cut]
-                    sent_ref[q, at : at + slots, :] = rows[slots:, cut]
-                at += slots
-
-
-def slot_zero(block, first, slots):
-    count = 2 * GROUPS * slots
-    return block[first : first + count].reshape(2 * GROUPS, slots, LANES)[:, :1]
+                    if n == H1:
+                        cut = rows[:, q * LANES : (q + 1) * LANES]
+                    else:
+                        cut = dot(rows, lanes[q]).astype(jnp.bfloat16)
+                    kept_ref[q, first : first + slots, :] = cut
+                first += slots
+
+
+FILTER_ROWS = 2 * GROUPS * (H1 + H2) // 8
+
+
+def send_filters(place, filter_first, filter_second):
+    return pl.pallas_call(
+        send_filters_kernel,
+        out_shape=(
+            jax.ShapeDtypeStruct((FILTER_ROWS, LANES), jnp.bfloat16),
+            jax.ShapeDtypeStruct((16, LANES), jnp.bfloat16),
+        ),
+        in_specs=[smem()] + hbm(2),
+        scratch_shapes=[
+            pltpu.VMEM((2, GROUPS, H1 // 4, LANES), jnp.float32),
+            pltpu.VMEM((2, 2 * GROUPS, H2 // 4, H2), jnp.float32),
+            pltpu.SemaphoreType.DMA((2,)),
+        ],
+        name="send_filters",
+        **params(12 * 64 * 512 * 128 * 2, 2 << 20),
+    )(place, filter_first, filter_second)
+
+
+def keep_filters(place, filter_first, filter_second):
+    return pl.pallas_call(
+        keep_filters_kernel,
+        out_shape=jax.ShapeDtypeStruct((COLS, FILTER_ROWS, LANES), jnp.bfloat16),
+        in_specs=[smem()] + vmem(2),
+        name="keep_filters",
+        **params(12 * 64 * 512 * 512 * 2, 4 << 20),
+    )(place, filter_first, filter_second)
 
 
 def put_slot_zero(block, zero, take, slots):
     shaped = block.reshape(2 * GROUPS, slots, LANES)
     here = (jnp.arange(slots) == 0)[None, :, None] & take
-    return jnp.where(here, zero, shaped).reshape(2 * GROUPS * slots, LANES)
-
-
-def take_filters(filter_first, filter_second, pick_first, pick_second):
-    rows = 2 * GROUPS * (H1 + H2) // 8
-    shape = jax.ShapeDtypeStruct((COLS, rows, LANES), jnp.bfloat16)
-    kept, sent = pl.pallas_call(
-        take_filters_kernel,
-        out_shape=(shape, shape),
-        name="take_filters",
-        **params(12 * 128 * 128 * 512 * 2, 4 << 20),
-    )(filter_first, filter_second, pick_first, pick_second, constant(pair_lanes()))
-    quarter = lax.dynamic_index_in_dim(sent, lax.axis_index("rep"), 0, keepdims=False)
-    split = 2 * GROUPS * H1 // 8
-    zero = jnp.concatenate(
-        [slot_zero(quarter, 0, H1 // 8), slot_zero(quarter, split, H2 // 8)], axis=1
-    )
-    return kept, quarter, zero
-
-
-def swap_filters(quarter, zero):
-    return lax.ppermute(quarter, "col", SWAP), lax.ppermute(zero, "col", ((2, 0), (3, 1)))
+    return jnp.where(here, zero[:, None, :], shaped).reshape(2 * GROUPS * slots, LANES)
+
+
+def put_slots_zero(block, zero, take):
+    split, groups = 2 * GROUPS * H1 // 8, 2 * GROUPS
+    return (
+        put_slot_zero(block[:split], zero[:groups], take, H1 // 8),
+        put_slot_zero(block[split:], zero[groups : 2 * groups], take, H2 // 8),
+    )
+
+
+def swap_filters(sent, zero):
+    return lax.ppermute(sent, "col", SWAP), lax.ppermute(zero, "col", ((2, 0), (3, 1)))
 
 
 def patch_filters(recv, zero, col):
-    split = 2 * GROUPS * H1 // 8
-    near = col < 2
-    recv = jnp.concatenate(
-        [
-            put_slot_zero(recv[:split], zero[:, :1], near, H1 // 8),
-            put_slot_zero(recv[split:], zero[:, 1:], near, H2 // 8),
-        ],
-        axis=0,
-    )
+    recv = jnp.concatenate(put_slots_zero(recv, zero, col < 2), axis=0)
     return lax.all_gather(recv, "rep", axis=0, tiled=False)
 
 
 def place_grads_kernel(
-    kept_first, recv_first, kept_second, recv_second, pick_first, pick_second, lanes,
-    first_ref, second_ref,
+    place_ref, kept_first, recv_first, kept_second, recv_second, first_ref, second_ref
 ):
-    for n, pick, kept, recv in (
-        (H1, pick_first, kept_first, recv_first),
-        (H2, pick_second, kept_second, recv_second),
-    ):
+    near = place_ref[0] < 2
+    wide_at, narrow_at = grid_of(LANES, LANES // 2)
+    lanes = [ones_at(wide_at == narrow_at + 64 * i) for i in range(2)]
+    for n, kept, recv in ((H1, kept_first, recv_first), (H2, kept_second, recv_second)):
         slots = n // 8
+        local, slot = grid_of(2 * slots, slots)
+        mirror = lax.rem(2 * slots - slot, 2 * slots)
+        pick_kept = ones_at(local == jnp.where(near, slot, slots - slot))
+        pick_recv = ones_at(local == jnp.where(near, slots + slot, mirror))
         for part in range(2):
             for g in range(GROUPS):
                 at = (part * GROUPS + g) * slots
-                both = jnp.concatenate([kept[at : at + slots], recv[at : at + slots]], axis=0)
-                rows = dot(pick[...], both)
+                rows = dot(pick_kept, kept[at : at + slots]) + dot(
+                    pick_recv, recv[at : at + slots]
+                )
                 if n == H1:
                     first_ref[part, g] = rows
                 else:
@@ -369,33 +448,33 @@
     return lax.psum_scatter(terms, "rep", scatter_dimension=0, tiled=False)
 
 
-def swap_grads(total, n):
-    count = 2 * GROUPS * n // 8
-    sent = total[count:]
-    zero = slot_zero(sent, 0, n // 8)
+def swap_grads(sum_first, sum_second):
+    count_first, count_second = 2 * GROUPS * H1 // 8, 2 * GROUPS * H2 // 8
+    sent = jnp.concatenate([sum_first[count_first:], sum_second[count_second:]], axis=0)
+    zero = jnp.concatenate(
+        [
+            sum_first[count_first:].reshape(2 * GROUPS, H1 // 8, LANES)[:, 0],
+            sum_second[count_second:].reshape(2 * GROUPS, H2 // 8, LANES)[:, 0],
+            jnp.zeros((4, LANES), jnp.bfloat16),
+        ],
+        axis=0,
+    )
     return lax.ppermute(sent, "col", SWAP), lax.ppermute(zero, "col", ((0, 2), (1, 3)))
 
 
-def place_grads(sum_first, swap_first, sum_second, swap_second, col, pick_first, pick_second):
+def place_grads(place, sum_first, sum_second, swapped, col):
     count_first, count_second = 2 * GROUPS * H1 // 8, 2 * GROUPS * H2 // 8
-    far = col >= 2
-    recv_first = put_slot_zero(*swap_first, far, H1 // 8)
-    recv_second = put_slot_zero(*swap_second, far, H2 // 8)
-    lanes = np.zeros((2, 128, 64))
-    lanes[0, :64] = np.eye(64)
-    lanes[1, 64:] = np.eye(64)
+    recv_first, recv_second = put_slots_zero(*swapped, col >= 2)
     return pl.pallas_call(
         place_grads_kernel,
         out_shape=(
             jax.ShapeDtypeStruct((2, GROUPS, H1 // 4, LANES), jnp.float32),
             jax.ShapeDtypeStruct((2, 2 * GROUPS, H2 // 4, LANES // 2), jnp.float32),
         ),
+        in_specs=[smem()] + vmem(4),
         name="place_grads",
         **params(12 * 128 * 128 * 128 * 2, 2 << 20),
-    )(
-        sum_first[:count_first], recv_first, sum_second[:count_second], recv_second,
-        pick_first.T, pick_second.T, constant(lanes),
-    )
+    )(place, sum_first[:count_first], recv_first, sum_second[:count_second], recv_second)
 
 
 def layer_normalize(entry_values, gains):
@@ -420,67 +499,78 @@
     return center * scale, scale
 
 
-def first_norm_kernel(x_ref, g_ref, gain_ref, pair_ref, out_ref, grad_ref):
-    pixels = x_ref[...].astype(jnp.float32)
+def pack_pairs(block):
+    fields = block.astype(jnp.float32).reshape(96, 2, 8, 64)
+    at, lane = grid_of(64, LANES)
+    return sum(
+        dot(fields[:, i].reshape(768, 64).astype(jnp.bfloat16), ones_at(lane == at + 64 * i))
+        for i in range(2)
+    )
+
+
+def first_norm_kernel(x_ref, g_ref, gain_ref, out_ref, x_buf, g_buf, gain_buf, sems):
+    copies = [
+        pltpu.make_async_copy(source, target, sems.at[i])
+        for i, (source, target) in enumerate(
+            ((x_ref, x_buf), (gain_ref, gain_buf), (g_ref, g_buf))
+        )
+    ]
+    for copy in copies:
+        copy.start()
+    copies[0].wait()
+    copies[1].wait()
+    pixels = x_buf[...].astype(jnp.float32)
     center = pixels - jnp.sum(pixels, axis=0, keepdims=True) / 96.0
     scale = lax.rsqrt(jnp.sum(center * center, axis=0) / 96.0 + epsilon)
     for c in range(96):
         at = (c % GROUPS) * 16
-        out_ref[c // GROUPS, at : at + 16, :] = (center[c] * scale * gain_ref[c]).astype(
+        out_ref[c // GROUPS, at : at + 16, :] = (center[c] * scale * gain_buf[c]).astype(
             jnp.bfloat16
         )
-    upstream = g_ref[...].astype(jnp.float32).reshape(96, 2, 8, 64)
-    packed = sum(
-        dot(upstream[:, i].reshape(768, 64).astype(jnp.bfloat16), pair_ref[i]) for i in range(2)
-    )
-    packed = packed.reshape(ROWS, GROUPS * 8, LANES).astype(jnp.bfloat16)
-    out_ref[:, GROUPS * 16 :, :] = packed
-    grad_ref[...] = packed
+    copies[2].wait()
+    packed = pack_pairs(g_buf[...]).reshape(ROWS, GROUPS * 8, LANES)
+    out_ref[:, GROUPS * 16 :, :] = packed.astype(jnp.bfloat16)
 
 
 def first_norm(images, grad_out, gains):
-    pair = np.zeros((2, 64, 128))
-    pair[0, :, :64] = np.eye(64)
-    pair[1, :, 64:] = np.eye(64)
     return pl.pallas_call(
         first_norm_kernel,
-        out_shape=(
-            jax.ShapeDtypeStruct((ROWS, GROUPS * 24, LANES), jnp.bfloat16),
-            jax.ShapeDtypeStruct((ROWS, GROUPS * 8, LANES), jnp.bfloat16),
-        ),
-        in_specs=vmem(2) + [smem()] + vmem(1),
+        out_shape=jax.ShapeDtypeStruct((ROWS, GROUPS * 24, LANES), jnp.bfloat16),
+        in_specs=hbm(3),
+        scratch_shapes=[
+            pltpu.VMEM((96, 16, LANES), jnp.bfloat16),
+            pltpu.VMEM((192, 8, 64), jnp.bfloat16),
+            pltpu.SMEM((96,), jnp.float32),
+            pltpu.SemaphoreType.DMA((3,)),
+        ],
         name="first_norm",
         **params(4 * 768 * 64 * 128, 2 << 20),
-    )(images.reshape(96, 16, LANES), grad_out.reshape(192, 8, 64), gains, constant(pair))
-
-
-def spread_columns():
-    matrix = np.zeros((64, 2, 2, 2, 64))
-    for e in range(2):
-        for half in range(2):
-            matrix[:, e, e, half, :] = np.eye(64)
-    return matrix.reshape(128, 256)
-
-
-def merge_columns():
-    matrix = np.zeros((2, 2, 64, 2, 64, 2))
-    for e in range(2):
-        for i in range(2):
-            matrix[e, i, :, i, :, e] = np.eye(64)
-    return matrix.reshape(256, 256)
+    )(images, grad_out, gains)
 
 
 def low_half():
     return lax.broadcasted_iota(jnp.int32, (96, LANES), 1) < LANES // 2
 
 
-def reduce_kernel(x_ref, m_ref, w_ref, gain_ref, spread_ref, norm_ref, down_ref, s_ref, n_ref):
+def reduce_kernel(
+    x_hbm, m_ref, w_hbm, gain_ref, norm_ref, down_hbm, x_ref, w_ref, down_ref, s_ref, n_ref, sems
+):
+    copies = [
+        pltpu.make_async_copy(x_hbm, x_ref, sems.at[0]),
+        pltpu.make_async_copy(w_hbm, w_ref, sems.at[1]),
+    ]
+    for copy in copies:
+        copy.start()
+    at, lane = grid_of(LANES, 2 * LANES)
+    spread_at = ones_at(at == 2 * lax.rem(lane, 64) + lax.div(lane, LANES))
+    copies[0].wait()
     mixed = m_ref[...].astype(jnp.float32).reshape(1536, LANES)
     section = x_ref[...].astype(jnp.float32).reshape(1536, LANES) + mixed
-    spread = dot(section.astype(jnp.bfloat16), spread_ref[...])
+    spread = dot(section.astype(jnp.bfloat16), spread_at)
     for e in range(2):
         s_ref[e] = spread[:, e * LANES : (e + 1) * LANES]
     low = low_half()
+    copies[1].wait()
     for first in range(0, 8, 2):
         patches = [
             jnp.concatenate(
@@ -500,7 +590,10 @@
             down_ref[first + i] = down
             normed, _ = standardize(down.astype(jnp.float32))
             n_ref[pl.ds(first + i, 96, stride=8), :] = normed * gain_ref[...]
+    copy = pltpu.make_async_copy(down_ref, down_hbm, sems.at[2])
+    copy.start()
     norm_ref[...] = n_ref[...].reshape(ROWS, GROUPS * 8, LANES).astype(jnp.bfloat16)
+    copy.wait()
 
 
 def reduce_step(images, mixed, weight, gains):
@@ -510,21 +603,40 @@
             jax.ShapeDtypeStruct((ROWS, GROUPS * 8, LANES), jnp.bfloat16),
             jax.ShapeDtypeStruct((8, 96, LANES), jnp.bfloat16),
         ),
-        in_specs=vmem(5),
+        in_specs=hbm(1) + vmem(1) + hbm(1) + vmem(1),
+        out_specs=tuple(vmem(1) + hbm(1)),
         scratch_shapes=[
+            pltpu.VMEM((96, 16, LANES), jnp.bfloat16),
+            pltpu.VMEM((192, 384), jnp.bfloat16),
+            pltpu.VMEM((8, 96, LANES), jnp.bfloat16),
             pltpu.VMEM((2, 1536, LANES), jnp.float32),
             pltpu.VMEM((768, LANES), jnp.float32),
+            pltpu.SemaphoreType.DMA((3,)),
         ],
         name="reduce_step",
         **params(4 * 2 * 192 * 384 * 256, 2 << 20),
-    )(images.reshape(96, 16, LANES), mixed, weight, gains, constant(spread_columns()))
+    )(images, mixed, weight, gains)
 
 
 def expand_kernel(
-    b_ref, down_ref, g_ref, w_ref, gain_ref, merge_ref, out_ref, back_ref, grad_ref, o_ref
+    b_ref, down_hbm, g_hbm, w_hbm, gain_ref, out_ref,
+    down_ref, g_ref, w_ref, back_ref, grad_ref, o_ref, sems,
 ):
+    copies = [
+        pltpu.make_async_copy(source, target, sems.at[i])
+        for i, (source, target) in enumerate(
+            ((g_hbm, g_ref), (down_hbm, down_ref), (w_hbm, w_ref))
+        )
+    ]
+    for copy in copies:
+        copy.start()
+    at, lane = grid_of(2 * LANES, 2 * LANES)
+    here = LANES * lax.rem(lax.div(at, 64), 2) + 2 * lax.rem(at, 64) + lax.div(at, LANES)
+    merge_at = ones_at(lane == here)
     back_ref[...] = b_ref[...].astype(jnp.float32).reshape(768, LANES)
-    grad_ref[...] = g_ref[...].astype(jnp.float32).reshape(768, LANES)
+    for copy in copies:
+        copy.wait()
+    grad_ref[...] = pack_pairs(g_ref[...])
     low = low_half()
     for first in range(0, 8, 2):
         grads = []
@@ -545,7 +657,7 @@
             )
             for a in range(2)
         ]
-        merged = dot(jnp.concatenate(rows, axis=0), merge_ref[...])
+        merged = dot(jnp.concatenate(rows, axis=0), merge_at)
         for i in range(2):
             for a in range(2):
                 o_ref[pl.ds(2 * (first + i) + a, 96, stride=16), :] = merged[
@@ -554,19 +666,23 @@
     out_ref[...] = o_ref[...].reshape(ROWS, GROUPS * 16, LANES).astype(jnp.bfloat16)
 
 
-def expand_step(back, down, upstream, weight, gains):
+def expand_step(back, down, grad_out, weight, gains):
     return pl.pallas_call(
         expand_kernel,
         out_shape=jax.ShapeDtypeStruct((ROWS, GROUPS * 16, LANES), jnp.bfloat16),
-        in_specs=vmem(6),
+        in_specs=vmem(1) + hbm(3) + vmem(1),
         scratch_shapes=[
+            pltpu.VMEM((8, 96, LANES), jnp.bfloat16),
+            pltpu.VMEM((192, 8, 64), jnp.bfloat16),
+            pltpu.VMEM((384, 192), jnp.bfloat16),
             pltpu.VMEM((768, LANES), jnp.float32),
             pltpu.VMEM((768, LANES), jnp.float32),
             pltpu.VMEM((1536, LANES), jnp.float32),
+            pltpu.SemaphoreType.DMA((3,)),
         ],
         name="expand_step",
         **params(4 * 2 * 192 * 384 * 256, 2 << 20),
-    )(back, down, upstream, weight, gains, constant(merge_columns()))
+    )(back, down, grad_out, weight, gains)
 
 
 def unpack_first(blocks):
@@ -584,53 +700,48 @@
 
 def shards(images, gain_first, filter_first, reduce_weight, gain_second, filter_second, grad_out):
     col = lax.axis_index("col")
-    col_word = col.astype(jnp.int32).reshape(1)
-    picks = [
-        jnp.where(col < 2, constant(np.eye(n // 4)), constant(mirror_matrix(n // 8)))
-        for n in (H1, H2)
-    ]
-    kept, quarter, zero = take_filters(filter_first, filter_second, *picks)
+    place = jnp.stack([col, lax.axis_index("rep")]).astype(jnp.int32)
     second_rows = 2 * GROUPS * H1 // 8
-
+    pixels = images.reshape(96, 16, LANES)
+    upstream = grad_out.reshape(192, 8, 64)
     weight = reduce_weight.reshape(96, 2, 384).transpose(1, 0, 2).reshape(192, 384)
     gains = jnp.repeat(gain_second.reshape(96, 2), 64, axis=1)
 
-    both, packed_out = first_norm(images, grad_out, gain_first)
-    swapped = swap_filters(quarter, zero)
-    half = forward_rows(exchange(both, "row"), (H1, H2))
+    sent, zero = send_filters(place, filter_first, filter_second)
+    swapped = swap_filters(sent, zero)
+    pixels, sent = lax.optimization_barrier((pixels, sent))
+    both = exchange(first_norm(pixels, upstream, gain_first), "row")
+    kept = keep_filters(place, filter_first, filter_second)
+    half = forward_rows(both, (H1, H2))
     half, swapped = lax.optimization_barrier((half, swapped))
     recv = patch_filters(*swapped, col)
     both = exchange(half, "col")
-    mixed = exchange(mix_forward(H1, col_word, both, kept, recv, 0), "col")
+    mixed = exchange(mix_forward(H1, place, both, kept, recv, 0), "col")
     mixed_one = exchange(inverse_rows(mixed, H1), "row")
 
-    norm_two, down = reduce_step(images, mixed_one, weight, gains)
+    norm_two, down = reduce_step(pixels, mixed_one, weight, gains)
     half_two = exchange(forward_rows(exchange(norm_two, "row"), (H2,)), "col")
     dspec_two, terms_two = mix_back(
-        H2, col_word, half_two, 0, both, second_rows, kept, recv, second_rows
+        H2, place, half_two, 0, both, second_rows, kept, recv, second_rows
     )
     sum_two = summed(terms_two)
     rot_two = exchange(dspec_two, "col")
     rot_two, sum_two = lax.optimization_barrier((rot_two, sum_two))
-    swap_two = swap_grads(sum_two, H2)
     back_two = exchange(inverse_rows(rot_two, H2), "row")
-    back_two, swap_two = lax.optimization_barrier((back_two, swap_two))
-
-    grad_section = expand_step(back_two, down, packed_out, weight.T, gains)
+
+    grad_section = expand_step(back_two, down, upstream, weight.T, gains)
     half_grad = exchange(forward_rows(exchange(grad_section, "row"), (H1,)), "col")
-    dspec_one, terms_one = mix_back(H1, col_word, both, 0, half_grad, 0, kept, recv, 0)
+    dspec_one, terms_one = mix_back(H1, place, both, 0, half_grad, 0, kept, recv, 0)
     sum_one = summed(terms_one)
     rot_one = exchange(dspec_one, "col")
     rot_one, sum_one = lax.optimization_barrier((rot_one, sum_one))
-    swap_one = swap_grads(sum_one, H1)
+    swapped = swap_grads(sum_one, sum_two)
     grad_norm_one = unpack_first(exchange(inverse_rows(rot_one, H1), "row"))
     grad_images = (
         unpack_first(grad_section).astype(jnp.float32)
         + norm_pullback_step(images.astype(jnp.float32), gain_first, grad_norm_one)
     ).astype(jnp.bfloat16)
-    grad_first, grad_second = place_grads(
-        sum_one, swap_one, sum_two, swap_two, col, *picks
-    )
+    grad_first, grad_second = place_grads(place, sum_one, sum_two, swapped, col)
     return (grad_images, grad_first, grad_second)
 
 

time: 361 us -> 362 us (level)
  waiting for transfers between devices: 47.4 us -> 81.4 us
  blocking collectives: 162 us -> 138 us
  starting transfers between devices: 89.3 us -> 79.1 us
  Pallas kernels: 20.5 us -> 26.1 us
  local copies, waits for them, and re-layouts: 22 us -> 17.5 us
    all_to_all x5 -> x6, waiting for transfers between devices: 25.2 us -> 54.7 us  [exchange(): return lax.all_to_all(blocks, axis, split_axis=0, concat_axis=0, tiled=True)]
    all_to_all x7 -> x6, blocking collectives: 150 us -> 127 us  [exchange(): return lax.all_to_all(blocks, axis, split_axis=0, concat_axis=0, tiled=True)]
    ppermute x2 -> x1, waiting for transfers between devices: 6.03 us -> 18.4 us  [swap_grads(): lax.ppermute(sent, 'col', SWAP)]
    ppermute x2 -> x1, starting transfers between devices: 15.3 us -> 3.48 us  [swap_grads(): lax.ppermute(zero, 'col', ((0, 2), (1, 3)))]
    all_to_all x5 -> x6, starting transfers between devices: 54.4 us -> 62.8 us  [exchange(): return lax.all_to_all(blocks, axis, split_axis=0, concat_axis=0, tiled=True)]
    ppermute x1, waiting for transfers between devices: 10.4 us -> 3.08 us  [swap_filters(): lax.ppermute(zero, 'col', ((2, 0), (3, 1)))]
    ppermute x2 -> x1, starting transfers between devices: 8.88 us -> 1.92 us  [swap_grads(): lax.ppermute(sent, 'col', SWAP)]
    unnamed x87 -> x61, local copies, waits for them, and re-layouts: 13.7 us -> 13.4 us
  transfers between devices with their start and end apart: 13 -> 12, of which waited for: 7 -> 10; matrix products, arithmetic and copies ran while one was open for 3% -> 2% of each run, Pallas kernels for 2% -> 2%
where the time goes in v4:
time: 362 us; the launch traced here: 361 us
  blocking collectives  138 us (38%)
  waiting for transfers between devices  81.4 us (22%)
  starting transfers between devices  79.1 us (22%)
  Pallas kernels  26.1 us (7%)
  local copies, waits for them, and re-layouts  17.5 us (5%)
  between operations  14.5 us (4%)
  other arithmetic  4.02 us (1%)
    all_to_all x6, blocking collectives, exchange(): return lax.all_to_all(blocks, axis, split_axis=0, concat_axis=0, tiled=True)  127 us
    all_to_all x6, starting transfers between devices, exchange(): return lax.all_to_all(blocks, axis, split_axis=0, concat_axis=0, tiled=True)  62.8 us
    all_to_all x6, waiting for transfers between devices, exchange(): return lax.all_to_all(blocks, axis, split_axis=0, concat_axis=0, tiled=True)  54.7 us
    ppermute x1, waiting for transfers between devices, swap_grads(): lax.ppermute(sent, 'col', SWAP)  18.4 us
    unnamed x61, local copies, waits for them, and re-layouts  13.4 us
    all_gather x1, blocking collectives, patch_filters(): return lax.all_gather(recv, 'rep', axis=0, tiled=False)  11.6 us
    ppermute x1, starting transfers between devices, swap_filters(): lax.ppermute(sent, 'col', SWAP)  9.41 us
  transfers between devices with their start and end apart: 12, of which 10 were waited for; matrix products, arithmetic and copies ran while one was open for 2% of the time, Pallas kernels for 2%

profile of v4, /device:TPU:105, one launch (start us, length us, event | category | flops | bytes accessed | tf_op | source)
XLA Modules:
  0.0 361.1 jit_solution(11435840573791067952)
XLA Ops:
  7.3 1.4 copy-done.1
  8.7 1.1 copy-done.3
  9.8 1.9 send_filters.1
  12.7 2.1 first_norm.1
  14.8 8.6 %all-to-all-start = ((bf16[32,72,128]{2,1,0:T(8,128)(2,1)}), bf16[32,72,128]{2,1,0:T(8,128)(2,1)S(1)}, u32[]{:S(2)}, u32[]{:S(2)}) async-start(bf16[32,72,128]{2,1,0:T(8,128)(2,1)} %first_norm.1), calls=%async_computation | async-start | bytes 1179648 | tf_op jit(solution)/shard_map/all_to_all | solution.py:698
  23.5 9.4 %collective-permute-start = (bf16[576,128]{1,0:T(8,128)(2,1)}, bf16[576,128]{1,0:T(8,128)(2,1)}, u32[]{:S(2)}, u32[]{:S(2)}) collective-permute-start(bf16[576,128]{1,0:T(8,128)(2,1)} %copy-done.24), channel_id=1, source_target_pairs={{0,12},{12,0},{4,8},{8,4},{1,13},{13,1},{5,9},{9,5},{2,14},{14,2},... | collective-permute-start | bytes 442376 | tf_op jit(solution)/shard_map/ppermute | solution.py:413
  32.9 1.3 collective-permute-start.1
  34.2 7.8 %all-to-all-done.refs_0_ = bf16[32,72,128]{2,1,0:T(8,128)(2,1)S(1)} async-done(((bf16[32,72,128]{2,1,0:T(8,128)(2,1)}), bf16[32,72,128]{2,1,0:T(8,128)(2,1)S(1)}, u32[]{:S(2)}, u32[]{:S(2)}) %all-to-all-start) | async-done | bytes 589856 | tf_op jit(solution)/shard_map/all_to_all | solution.py:698
  42.9 1.3 forward_rows_512_256.1
  44.2 3.1 collective-permute-done.1
  47.3 10.9 %all-to-all-start.1 = ((bf16[4,576,128]{2,1,0:T(8,128)(2,1)}), bf16[4,576,128]{2,1,0:T(8,128)(2,1)S(1)}, u32[]{:S(2)}, u32[]{:S(2)}) async-start(bf16[4,576,128]{2,1,0:T(8,128)(2,1)} %forward_rows_512_256.1), calls=%async_computation.1 | async-start | bytes 1179648 | tf_op jit(solution)/shard_map/all_to_all | solution.py:698
  59.0 1.1 copy-done.4
  60.1 2.0 keep_filters.1.kept_ref
  62.1 1.0 bitcast_select_fusion
  64.1 11.6 %all-gather = bf16[2304,128]{1,0:T(8,128)(2,1)S(1)} all-gather(bf16[576,128]{1,0:T(8,128)(2,1)S(1)} %pad_maximum_fusion), channel_id=2, replica_groups=mesh['row'=32,'col'=4,'rep'=4] {'rep'}, dimensions={0}, use_global_device_ids=true | all-gather | bytes 737280 | tf_op jit(solution)/shard_map/all_gather | solution.py:418
  75.7 14.6 %all-to-all-done.1.x_ref.g_ref = bf16[4,576,128]{2,1,0:T(8,128)(2,1)S(1)} async-done(((bf16[4,576,128]{2,1,0:T(8,128)(2,1)}), bf16[4,576,128]{2,1,0:T(8,128)(2,1)S(1)}, u32[]{:S(2)}, u32[]{:S(2)}) %all-to-all-start.1) | async-done | bytes 589856 | tf_op jit(solution)/shard_map/all_to_all | solution.py:698
  90.2 1.2 copy-done.11
  91.4 2.1 mix_forward_512.1
  93.6 27.5 %all_to_all.60.x_ref = bf16[4,384,128]{2,1,0:T(8,128)(2,1)S(1)} all-to-all(bf16[4,384,128]{2,1,0:T(8,128)(2,1)S(1)} %mix_forward_512.1), channel_id=1, replica_groups=mesh['row'=32,'col'=4,'rep'=4] {'col'}, dimensions={0} | all-to-all | bytes 786432 | tf_op jit(solution)/shard_map/all_to_all | solution.py:698
  121.1 1.2 inverse_rows_512.2
  122.3 10.5 %all-to-all-start.3 = ((bf16[32,48,128]{2,1,0:T(8,128)(2,1)}), bf16[32,48,128]{2,1,0:T(8,128)(2,1)S(1)}, u32[]{:S(2)}, u32[]{:S(2)}) async-start(bf16[32,48,128]{2,1,0:T(8,128)(2,1)} %inverse_rows_512.2), calls=%async_computation.3 | async-start | bytes 786432 | tf_op jit(solution)/shard_map/all_to_all | solution.py:698
  132.9 1.0 reshape.168
  134.2 9.1 %all-to-all-done.3.m_ref = bf16[32,48,128]{2,1,0:T(8,128)(2,1)S(1)} async-done(((bf16[32,48,128]{2,1,0:T(8,128)(2,1)}), bf16[32,48,128]{2,1,0:T(8,128)(2,1)S(1)}, u32[]{:S(2)}, u32[]{:S(2)}) %all-to-all-start.3) | async-done | bytes 393248 | tf_op jit(solution)/shard_map/all_to_all | solution.py:698
  143.3 2.1 reduce_step.1
  146.1 13.7 %all_to_all.61.refs_0_ = bf16[32,24,128]{2,1,0:T(8,128)(2,1)S(1)} all-to-all(bf16[32,24,128]{2,1,0:T(8,128)(2,1)S(1)} %get-tuple-element.27), channel_id=1, replica_groups=mesh['row'=32,'col'=4,'rep'=4] {'row'}, dimensions={0} | all-to-all | bytes 393216 | tf_op jit(solution)/shard_map/all_to_all | solution.py:698
  160.1 20.0 %all_to_all.62.x_ref = bf16[4,192,128]{2,1,0:T(8,128)(2,1)S(1)} all-to-all(bf16[4,192,128]{2,1,0:T(8,128)(2,1)S(1)} %forward_rows_256.1), channel_id=1, replica_groups=mesh['row'=32,'col'=4,'rep'=4] {'col'}, dimensions={0} | all-to-all | bytes 393216 | tf_op jit(solution)/shard_map/all_to_all | solution.py:698
  180.0 2.3 mix_back_256.1
  183.2 17.6 %all_to_all.63.x_ref = bf16[4,192,128]{2,1,0:T(8,128)(2,1)S(1)} all-to-all(bf16[4,192,128]{2,1,0:T(8,128)(2,1)S(1)} %get-tuple-element.28), channel_id=1, replica_groups=mesh['row'=32,'col'=4,'rep'=4] {'col'}, dimensions={0} | all-to-all | bytes 393216 | tf_op jit(solution)/shard_map/all_to_all | solution.py:698
  200.7 4.5 %reduce-scatter.3.cloned.1.call-done = bf16[1,384,128]{2,1,0:T(8,128)(2,1)} async-done(((bf16[4,384,128]{2,1,0:T(8,128)(2,1)}), bf16[1,384,128]{2,1,0:T(8,128)(2,1)}) %reduce-scatter.3.cloned.1.call-update) | async-done | bytes 98320 | tf_op jit(solution)/shard_map/reduce_scatter | solution.py:448
  207.0 10.0 %all-to-all-start.7 = ((bf16[32,24,128]{2,1,0:T(8,128)(2,1)}), bf16[32,24,128]{2,1,0:T(8,128)(2,1)S(1)}, u32[]{:S(2)}, u32[]{:S(2)}) async-start(bf16[32,24,128]{2,1,0:T(8,128)(2,1)} %inverse_rows_256.1), calls=%async_computation.8 | async-start | bytes 393216 | tf_op jit(solution)/shard_map/all_to_all | solution.py:698
  217.3 1.7 copy.35
  219.0 4.8 %all-to-all-done.7.b_ref = bf16[32,24,128]{2,1,0:T(8,128)(2,1)S(1)} async-done(((bf16[32,24,128]{2,1,0:T(8,128)(2,1)}), bf16[32,24,128]{2,1,0:T(8,128)(2,1)S(1)}, u32[]{:S(2)}, u32[]{:S(2)}) %all-to-all-start.7) | async-done | bytes 196640 | tf_op jit(solution)/shard_map/all_to_all | solution.py:698
  224.5 0.9 copy-done.15
  225.4 0.9 copy-done.16
  226.3 0.9 copy-done.21
  227.2 2.5 expand_step.1
  229.7 17.2 %all_to_all.64.refs_0_ = bf16[32,48,128]{2,1,0:T(8,128)(2,1)S(1)} all-to-all(bf16[32,48,128]{2,1,0:T(8,128)(2,1)S(1)} %expand_step.1), channel_id=1, replica_groups=mesh['row'=32,'col'=4,'rep'=4] {'row'}, dimensions={0} | all-to-all | bytes 786432 | tf_op jit(solution)/shard_map/all_to_all | solution.py:698
  247.4 30.9 %all_to_all.65.g_ref = bf16[4,384,128]{2,1,0:T(8,128)(2,1)S(1)} all-to-all(bf16[4,384,128]{2,1,0:T(8,128)(2,1)S(1)} %forward_rows_512.1), channel_id=1, replica_groups=mesh['row'=32,'col'=4,'rep'=4] {'col'}, dimensions={0} | all-to-all | bytes 786432 | tf_op jit(solution)/shard_map/all_to_all | solution.py:698
  278.3 3.5 mix_back_512.1
  282.7 7.1 %all-to-all-start.10 = ((bf16[4,384,128]{2,1,0:T(8,128)(2,1)}), bf16[4,384,128]{2,1,0:T(8,128)(2,1)S(1)}, u32[]{:S(2)}, u32[]{:S(2)}) async-start(bf16[4,384,128]{2,1,0:T(8,128)(2,1)} %get-tuple-element.32), calls=%async_computation.11 | async-start | bytes 786432 | tf_op jit(solution)/shard_map/all_to_all | solution.py:698
  289.9 18.5 %all-to-all-done.10.x_ref = bf16[4,384,128]{2,1,0:T(8,128)(2,1)S(1)} async-done(((bf16[4,384,128]{2,1,0:T(8,128)(2,1)}), bf16[4,384,128]{2,1,0:T(8,128)(2,1)S(1)}, u32[]{:S(2)}, u32[]{:S(2)}) %all-to-all-start.10) | async-done | bytes 393248 | tf_op jit(solution)/shard_map/all_to_all | solution.py:698
  308.4 1.2 inverse_rows_512.3
  309.6 15.6 %all-to-all-start.11 = ((bf16[32,48,128]{2,1,0:T(8,128)(2,1)}), bf16[32,48,128]{2,1,0:T(8,128)(2,1)S(1)}, u32[]{:S(2)}, u32[]{:S(2)}) async-start(bf16[32,48,128]{2,1,0:T(8,128)(2,1)} %inverse_rows_512.3), calls=%async_computation.13 | async-start | bytes 786432 | tf_op jit(solution)/shard_map/all_to_all | solution.py:698
  325.7 3.5 collective-permute-start.2
  329.2 1.9 collective-permute-start.3
  331.8 18.4 %collective-permute-done.3 = bf16[576,128]{1,0:T(8,128)(2,1)S(1)} collective-permute-done((bf16[576,128]{1,0:T(8,128)(2,1)S(1)}, bf16[576,128]{1,0:T(8,128)(2,1)S(1)}, u32[]{:S(2)}, u32[]{:S(2)}) %collective-permute-start.3) | collective-permute-done | bytes 147488 | tf_op jit(solution)/shard_map/ppermute | solution.py:462
  350.4 2.3 place_grads.1
  353.2 1.1 fusion.6
  (104 shorter events, 11.6 us)
Async XLA Ops:
  7.2 5.5 %copy-start = (bf16[1,96,16,128]{3,2,1,0:T(8,128)(2,1)S(1)}, bf16[1,96,16,128]{3,2,1,0:T(8,128)(2,1)}, u32[]{:S(2)}) copy-start(bf16[1,96,16,128]{3,2,1,0:T(8,128)(2,1)} %param.17) | copy-start | bytes 1179652
  7.3 1.4 copy-start.1
  8.7 1.1 copy-start.3
  9.8 2.6 copy-start.25
  9.8 2.8 copy-start.23
  11.7 0.7 copy-start.24
  11.8 30.2 %copy-start.5 = (bf16[512,512]{1,0:T(8,128)(2,1)S(1)}, bf16[512,512]{1,0:T(8,128)(2,1)}, u32[]{:S(2)}) copy-start(bf16[512,512]{1,0:T(8,128)(2,1)} %constant.38.clone.refs_1_) | copy-start | bytes 1572868
  14.8 44.2 %copy-start.2 = (f32[2,3,128,512]{3,2,1,0:T(8,128)S(1)}, f32[2,3,128,512]{3,2,1,0:T(8,128)}, u32[]{:S(2)}) copy-start(f32[2,3,128,512]{3,2,1,0:T(8,128)} %first_ref.3) | copy-start | bytes 4718596
  14.8 27.2 %all-to-all-start = ((bf16[32,72,128]{2,1,0:T(8,128)(2,1)}), bf16[32,72,128]{2,1,0:T(8,128)(2,1)S(1)}, u32[]{:S(2)}, u32[]{:S(2)}) async-start(bf16[32,72,128]{2,1,0:T(8,128)(2,1)} %first_norm.1), calls=%async_computation | async-start | bytes 1179648 | tf_op jit(solution)/shard_map/all_to_all | solution.py:698
  23.5 23.8 %collective-permute-start = (bf16[576,128]{1,0:T(8,128)(2,1)}, bf16[576,128]{1,0:T(8,128)(2,1)}, u32[]{:S(2)}, u32[]{:S(2)}) collective-permute-start(bf16[576,128]{1,0:T(8,128)(2,1)} %copy-done.24), channel_id=1, source_target_pairs={{0,12},{12,0},{4,8},{8,4},{1,13},{13,1},{5,9},{9,5},{2,14},{14,2},... | collective-permute-start | bytes 442376 | tf_op jit(solution)/shard_map/ppermute | solution.py:413
  32.9 14.4 %collective-permute-start.1 = (bf16[16,128]{1,0:T(8,128)(2,1)S(1)}, bf16[16,128]{1,0:T(8,128)(2,1)S(1)}, u32[]{:S(2)}, u32[]{:S(2)}) collective-permute-start(bf16[16,128]{1,0:T(8,128)(2,1)S(1)} %get-tuple-element.23), channel_id=1, source_target_pairs={{8,0},{12,4},{9,1},{13,5},{10,2},{14,6},{11,3},{15,7},{24,16},{28,... | collective-permute-start | bytes 12296 | tf_op jit(solution)/shard_map/ppermute | solution.py:413
  42.0 0.9 copy-start.17
  47.3 42.9 %all-to-all-start.1 = ((bf16[4,576,128]{2,1,0:T(8,128)(2,1)}), bf16[4,576,128]{2,1,0:T(8,128)(2,1)S(1)}, u32[]{:S(2)}, u32[]{:S(2)}) async-start(bf16[4,576,128]{2,1,0:T(8,128)(2,1)} %forward_rows_512_256.1), calls=%async_computation.1 | async-start | bytes 1179648 | tf_op jit(solution)/shard_map/all_to_all | solution.py:698
  59.0 1.1 copy-start.4
  60.1 3.0 copy-start.29
  75.7 45.4 %copy-start.8 = (bf16[512,512]{1,0:T(8,128)(2,1)S(1)}, bf16[512,512]{1,0:T(8,128)(2,1)}, u32[]{:S(2)}) copy-start(bf16[512,512]{1,0:T(8,128)(2,1)} %constant.41.clone.table) | copy-start | bytes 1572868
  90.2 1.2 copy-start.11
  93.6 40.3 %copy-start.28 = (f32[192]{0:T(256)S(1)}, f32[192]{0:T(256)}, u32[]{:S(2)}) copy-start(f32[192]{0:T(256)} %param.21) | copy-start | bytes 2308
  122.3 37.6 %copy-start.18 = (bf16[256,256]{1,0:T(8,128)(2,1)S(1)}, bf16[256,256]{1,0:T(8,128)(2,1)}, u32[]{:S(2)}) copy-start(bf16[256,256]{1,0:T(8,128)(2,1)} %constant.39.clone.refs_2_.refs_1_) | copy-start | bytes 393220
  122.3 21.0 %all-to-all-start.3 = ((bf16[32,48,128]{2,1,0:T(8,128)(2,1)}), bf16[32,48,128]{2,1,0:T(8,128)(2,1)S(1)}, u32[]{:S(2)}, u32[]{:S(2)}) async-start(bf16[32,48,128]{2,1,0:T(8,128)(2,1)} %inverse_rows_512.2), calls=%async_computation.3 | async-start | bytes 786432 | tf_op jit(solution)/shard_map/all_to_all | solution.py:698
  132.8 72.4 %reduce-scatter.3.cloned.1.call-start = ((), (), s32[]{:S(2)}) async-start(), calls=%async_computation.14 | async-start | bytes 491520 | tf_op jit(solution)/shard_map/reduce_scatter | solution.py:448
  133.9 49.2 %copy-start.10 = (bf16[2,96,384]{2,1,0:T(8,128)(2,1)}, bf16[2,96,384]{2,1,0:T(8,128)(2,1)S(1)}, u32[]{:S(2)}) copy-start(bf16[2,96,384]{2,1,0:T(8,128)(2,1)S(1)} %copy.32) | copy-start | bytes 442372
  143.3 36.7 %copy-start.7 = (bf16[4,512,512]{2,1,0:T(8,128)(2,1)S(1)}, bf16[4,512,512]{2,1,0:T(8,128)(2,1)}, u32[]{:S(2)}) copy-start(bf16[4,512,512]{2,1,0:T(8,128)(2,1)} %constant.42.clone.tables) | copy-start | bytes 6291460
  145.5 0.7 copy-start.20
  182.4 0.7 copy-start.19
  183.1 63.8 %copy-start.6 = (bf16[512,512]{1,0:T(8,128)(2,1)S(1)}, bf16[512,512]{1,0:T(8,128)(2,1)}, u32[]{:S(2)}) copy-start(bf16[512,512]{1,0:T(8,128)(2,1)} %constant.38.clone.refs_1_) | copy-start | bytes 1572868
  205.2 0.9 copy-start.22
  207.0 16.8 %all-to-all-start.7 = ((bf16[32,24,128]{2,1,0:T(8,128)(2,1)}), bf16[32,24,128]{2,1,0:T(8,128)(2,1)S(1)}, u32[]{:S(2)}, u32[]{:S(2)}) async-start(bf16[32,24,128]{2,1,0:T(8,128)(2,1)} %inverse_rows_256.1), calls=%async_computation.8 | async-start | bytes 393216 | tf_op jit(solution)/shard_map/all_to_all | solution.py:698
  217.0 91.4 %reduce-scatter.5.cloned.1.call-start = ((), (), s32[]{:S(2)}) async-start(), calls=%async_computation.15 | async-start | bytes 983040 | tf_op jit(solution)/shard_map/reduce_scatter | solution.py:448
  223.8 0.7 copy-start.14
  224.4 0.9 copy-start.15
  225.4 0.9 copy-start.16
  226.3 0.9 copy-start.21
  227.2 51.0 %copy-start.12 = (bf16[2,512,512]{2,1,0:T(8,128)(2,1)S(1)}, bf16[2,512,512]{2,1,0:T(8,128)(2,1)}, u32[]{:S(2)}) copy-start(bf16[2,512,512]{2,1,0:T(8,128)(2,1)} %constant.40.clone.tables) | copy-start | bytes 3145732
  281.8 0.9 copy-start.13
  282.7 25.7 %copy-start.9 = (bf16[512,512]{1,0:T(8,128)(2,1)S(1)}, bf16[512,512]{1,0:T(8,128)(2,1)}, u32[]{:S(2)}) copy-start(bf16[512,512]{1,0:T(8,128)(2,1)} %constant.41.clone.table) | copy-start | bytes 1572868
  282.7 42.8 %copy-start.27 = (bf16[1,384,128]{2,1,0:T(8,128)(2,1)S(1)}, bf16[1,384,128]{2,1,0:T(8,128)(2,1)}, u32[]{:S(2)}) copy-start(bf16[1,384,128]{2,1,0:T(8,128)(2,1)} %reduce-scatter.3.cloned.1.call-done) | copy-start | bytes 294916
  282.7 25.6 %all-to-all-start.10 = ((bf16[4,384,128]{2,1,0:T(8,128)(2,1)}), bf16[4,384,128]{2,1,0:T(8,128)(2,1)S(1)}, u32[]{:S(2)}, u32[]{:S(2)}) async-start(bf16[4,384,128]{2,1,0:T(8,128)(2,1)} %get-tuple-element.32), calls=%async_computation.11 | async-start | bytes 786432 | tf_op jit(solution)/shard_map/all_to_all | solution.py:698
  308.4 17.1 %copy-start.26 = (bf16[1,768,128]{2,1,0:T(8,128)(2,1)S(1)}, bf16[1,768,128]{2,1,0:T(8,128)(2,1)}, u32[]{:S(2)}) copy-start(bf16[1,768,128]{2,1,0:T(8,128)(2,1)} %reduce-scatter.5.cloned.1.call-done) | copy-start | bytes 589828
  309.6 43.1 %all-to-all-start.11 = ((bf16[32,48,128]{2,1,0:T(8,128)(2,1)}), bf16[32,48,128]{2,1,0:T(8,128)(2,1)S(1)}, u32[]{:S(2)}, u32[]{:S(2)}) async-start(bf16[32,48,128]{2,1,0:T(8,128)(2,1)} %inverse_rows_512.3), calls=%async_computation.13 | async-start | bytes 786432 | tf_op jit(solution)/shard_map/all_to_all | solution.py:698
  325.7 6.1 %collective-permute-start.2 = (bf16[16,128]{1,0:T(8,128)(2,1)S(1)}, bf16[16,128]{1,0:T(8,128)(2,1)S(1)}, u32[]{:S(2)}, u32[]{:S(2)}) collective-permute-start(bf16[16,128]{1,0:T(8,128)(2,1)S(1)} %maximum_maximum_fusion), channel_id=1, source_target_pairs={{0,8},{4,12},{1,9},{5,13},{2,10},{6,14},{3,11},{7,15},{16,24},{20,... | collective-permute-start | bytes 12296 | tf_op jit(solution)/shard_map/ppermute | solution.py:462
  329.2 21.0 %collective-permute-start.3 = (bf16[576,128]{1,0:T(8,128)(2,1)S(1)}, bf16[576,128]{1,0:T(8,128)(2,1)S(1)}, u32[]{:S(2)}, u32[]{:S(2)}) collective-permute-start(bf16[576,128]{1,0:T(8,128)(2,1)S(1)} %pad_maximum_fusion.1), channel_id=1, source_target_pairs={{0,12},{12,0},{4,8},{8,4},{1,13},{13,1},{5,9},{9,5},{2,14},{14,2},... | collective-permute-start | bytes 442376 | tf_op jit(solution)/shard_map/ppermute | solution.py:462
Sparse Core Ops, SparseCore 0:
  183.3 21.8 reduce-scatter.2
  282.8 25.5 reduce-scatter.4

commit v5 on v4

--- a/solution.py
+++ b/solution.py
@@ -15,6 +15,8 @@
 COLS = 4
 ROWS = 32
 LANES = 128
+SECOND_SLOT = 2 * GROUPS * H1 // 8
+FILTER_ROWS = 2 * GROUPS * (H1 + H2) // 8
 
 epsilon = 1e-06
 
@@ -66,9 +68,9 @@
     return jnp.dot(a, b, preferred_element_type=jnp.float32)
 
 
-def params(flops, traffic):
+def params(flops, traffic, vmem_mib=40):
     return dict(
-        compiler_params=pltpu.CompilerParams(vmem_limit_bytes=40 * 1024 * 1024),
+        compiler_params=pltpu.CompilerParams(vmem_limit_bytes=vmem_mib * 1024 * 1024),
         cost_estimate=pl.CostEstimate(flops=flops, bytes_accessed=traffic, transcendentals=0),
     )
 
@@ -98,46 +100,56 @@
 
 
 def forward_rows(entries, sizes):
-    layout, first_in, first_out = [], 0, 0
-    for n in sizes:
-        layout.append((n, first_in, first_out))
-        first_in += GROUPS * n // ROWS
-        first_out += 2 * GROUPS * n // 8
+    layout, _, slots = layout_of(sizes)
     flops = sum(2 * n * n * GROUPS * LANES for n in sizes)
     return pl.pallas_call(
-        functools.partial(forward_rows_kernel, tuple(layout)),
-        out_shape=jax.ShapeDtypeStruct((COLS, first_out, LANES), jnp.bfloat16),
+        functools.partial(forward_rows_kernel, layout),
+        out_shape=jax.ShapeDtypeStruct((COLS, slots, LANES), jnp.bfloat16),
         name="forward_rows_" + "_".join(str(n) for n in sizes),
         **params(flops, 2 << 20),
     )(entries, *[constant(row_table(n)) for n in sizes])
 
 
-def inverse_rows_kernel(n, x_ref, table, out_ref):
-    rows = n // ROWS
-    slots = n // 8
-    parts = []
-    for g in range(GROUPS):
-        both = [
-            x_ref[:, (part * GROUPS + g) * slots : (part * GROUPS + g + 1) * slots, :].reshape(
-                COLS, 1, slots, LANES
-            )
-            for part in range(2)
+def inverse_rows_kernel(layout, *refs):
+    x_ref, tables, out_ref = refs[0], refs[1:-1], refs[-1]
+    for (n, first_out, first_in), table in zip(layout, tables):
+        rows = n // ROWS
+        slots = n // 8
+        parts = []
+        for g in range(GROUPS):
+            both = []
+            for part in range(2):
+                at = first_in + (part * GROUPS + g) * slots
+                both.append(x_ref[:, at : at + slots, :].reshape(COLS, 1, slots, LANES))
+            parts.append(jnp.concatenate(both, axis=1).reshape(n, LANES))
+        result = dot(table[...], jnp.concatenate(parts, axis=1))
+        pieces = [
+            result[:, g * LANES : (g + 1) * LANES].reshape(ROWS, rows, LANES)
+            for g in range(GROUPS)
         ]
-        parts.append(jnp.concatenate(both, axis=1).reshape(n, LANES))
-    result = dot(table[...], jnp.concatenate(parts, axis=1))
-    pieces = [
-        result[:, g * LANES : (g + 1) * LANES].reshape(ROWS, rows, LANES) for g in range(GROUPS)
-    ]
-    out_ref[...] = jnp.concatenate(pieces, axis=1).astype(jnp.bfloat16)
-
-
-def inverse_rows(entries, n):
-    return pl.pallas_call(
-        functools.partial(inverse_rows_kernel, n),
-        out_shape=jax.ShapeDtypeStruct((ROWS, GROUPS * n // ROWS, LANES), jnp.bfloat16),
-        name="inverse_rows_" + str(n),
-        **params(2 * n * n * GROUPS * LANES, 2 << 20),
-    )(entries, constant(row_table(n).T))
+        out_ref[:, first_out : first_out + GROUPS * rows, :] = jnp.concatenate(
+            pieces, axis=1
+        ).astype(jnp.bfloat16)
+
+
+def layout_of(sizes):
+    layout, first_token, first_slot = [], 0, 0
+    for n in sizes:
+        layout.append((n, first_token, first_slot))
+        first_token += GROUPS * n // ROWS
+        first_slot += 2 * GROUPS * n // 8
+    return tuple(layout), first_token, first_slot
+
+
+def inverse_rows(entries, sizes):
+    layout, tokens, _ = layout_of(sizes)
+    flops = sum(2 * n * n * GROUPS * LANES for n in sizes)
+    return pl.pallas_call(
+        functools.partial(inverse_rows_kernel, layout),
+        out_shape=jax.ShapeDtypeStruct((ROWS, tokens, LANES), jnp.bfloat16),
+        name="inverse_rows_" + "_".join(str(n) for n in sizes),
+        **params(flops, 2 << 20),
+    )(entries, *[constant(row_table(n).T) for n in sizes])
 
 
 def wide(ref, first, count):
@@ -167,7 +179,7 @@
     return out
 
 
-def put_inverse(out_ref, slots, special, up, down, cos, sin):
+def put_inverse(out_ref, first, slots, special, up, down, cos, sin):
     count = GROUPS * slots
     (up_r, up_i), (down_r, down_i) = up, down
     bf16 = jnp.bfloat16
@@ -178,8 +190,9 @@
     rot_real = (dot(sum_r, cos) - dot(sum_i, sin)).astype(bf16)
     rot_imag = (dot(dif_i, cos) + dot(dif_r, sin)).astype(bf16)
     for q in range(COLS):
-        out_ref[q, :count, :] = rot_real[:, q * LANES : (q + 1) * LANES]
-        out_ref[q, count:, :] = rot_imag[:, q * LANES : (q + 1) * LANES]
+        lanes = slice(q * LANES, (q + 1) * LANES)
+        out_ref[q, first : first + count, :] = rot_real[:, lanes]
+        out_ref[q, first + count : first + 2 * count, :] = rot_imag[:, lanes]
 
 
 def masks(place_ref, slots):
@@ -188,26 +201,37 @@
     return (lax.rem(row, slots) + col * slots) == 0, col < 2
 
 
-def mix_forward_kernel(n, first_filter, place_ref, x_ref, kept_ref, recv_ref, tables, out_ref):
-    slots = n // 8
+def apply_back(real, imag, grad):
+    return [
+        (
+            real[side] * grad[2 * side] + imag[side] * grad[2 * side + 1],
+            real[side] * grad[2 * side + 1] - imag[side] * grad[2 * side],
+        )
+        for side in range(2)
+    ]
+
+
+def mix_first_kernel(place_ref, x_ref, kept_ref, recv_ref, first_tables, second_tables, out_ref):
+    slots = H1 // 8
     special, near = masks(place_ref, slots)
-    cos, sin = tables[0], tables[1]
+    cos, sin = first_tables[0], first_tables[1]
     up_r, up_i, down_r, down_i = spectrum(x_ref, 0, slots, special, cos, sin)
-    real, imag = filters(near, kept_ref, recv_ref, first_filter, slots)
+    real, imag = filters(near, kept_ref, recv_ref, 0, slots)
     up = (real[0] * up_r - imag[0] * up_i, real[0] * up_i + imag[0] * up_r)
     down = (real[1] * down_r - imag[1] * down_i, real[1] * down_i + imag[1] * down_r)
-    put_inverse(out_ref, slots, special, up, down, cos, sin)
-
-
-def mix_back_kernel(
-    n, first_filter, first_field, first_grad, place_ref, x_ref, g_ref, kept_ref, recv_ref,
-    tables, out_ref, total_ref, grad_ref, sem,
-):
-    slots = n // 8
+    put_inverse(out_ref, 0, slots, special, up, down, cos, sin)
+
+    first, slots = SECOND_SLOT, H2 // 8
+    special, near = masks(place_ref, slots)
+    cos, sin = second_tables[0], second_tables[1]
+    grad = spectrum(x_ref, first, slots, special, cos, sin)
+    real, imag = filters(near, kept_ref, recv_ref, first, slots)
+    up, down = apply_back(real, imag, grad)
+    put_inverse(out_ref, first, slots, special, up, down, cos, sin)
+
+
+def put_terms(out_ref, first, slots, near, field, grad):
     count = GROUPS * slots
-    special, near = masks(place_ref, slots)
-    field = spectrum(x_ref, first_field, slots, special, tables[0], tables[1])
-    grad = spectrum(g_ref, first_grad, slots, special, tables[0], tables[1])
     terms = []
     for side in range(2):
         g_r, g_i = grad[2 * side], grad[2 * side + 1]
@@ -217,19 +241,34 @@
         up, down = terms[0][part], terms[1][part]
         kept = jnp.where(near, up, down).astype(jnp.bfloat16)
         sent = jnp.where(near, down, up).astype(jnp.bfloat16)
+        at = first + part * count
         for q in range(COLS):
             lanes = slice(q * LANES, (q + 1) * LANES)
-            grad_ref[q, part * count : (part + 1) * count, :] = kept[:, lanes]
-            grad_ref[q, (2 + part) * count : (3 + part) * count, :] = sent[:, lanes]
-    copy = pltpu.make_async_copy(grad_ref, total_ref, sem)
+            out_ref[q, at : at + count, :] = kept[:, lanes]
+            out_ref[q, FILTER_ROWS + at : FILTER_ROWS + at + count, :] = sent[:, lanes]
+
+
+def mix_last_kernel(
+    place_ref, x_ref, y_ref, kept_ref, recv_ref, first_tables, second_tables,
+    out_ref, total_ref, terms_ref, sem,
+):
+    slots = H2 // 8
+    special, near = masks(place_ref, slots)
+    tables = second_tables[0], second_tables[1]
+    grad = spectrum(x_ref, SECOND_SLOT, slots, special, *tables)
+    field = spectrum(y_ref, SECOND_SLOT, slots, special, *tables)
+    put_terms(terms_ref, SECOND_SLOT, slots, near, field, grad)
+    slots = H1 // 8
+    special, near = masks(place_ref, slots)
+    tables = first_tables[0], first_tables[1]
+    field = spectrum(x_ref, 0, slots, special, *tables)
+    grad = spectrum(y_ref, 0, slots, special, *tables)
+    put_terms(terms_ref, 0, slots, near, field, grad)
+    copy = pltpu.make_async_copy(terms_ref, total_ref, sem)
     copy.start()
-    real, imag = filters(near, kept_ref, recv_ref, first_filter, slots)
-    sides = []
-    for side in range(2):
-        g_r, g_i = grad[2 * side], grad[2 * side + 1]
-        sides.append((real[side] * g_r + imag[side] * g_i, real[side] * g_i - imag[side] * g_r))
-    last = tables.shape[0] - 2
-    put_inverse(out_ref, slots, special, sides[0], sides[1], tables[last], tables[last + 1])
+    real, imag = filters(near, kept_ref, recv_ref, 0, slots)
+    up, down = apply_back(real, imag, grad)
+    put_inverse(out_ref, 0, slots, special, up, down, *tables)
     copy.wait()
 
 
@@ -245,35 +284,34 @@
     return [pl.BlockSpec(memory_space=pltpu.VMEM)] * count
 
 
-def mix_forward(n, place, entries, kept, recv, first_filter):
-    rows = 2 * GROUPS * n // 8
-    return pl.pallas_call(
-        functools.partial(mix_forward_kernel, n, first_filter),
-        out_shape=jax.ShapeDtypeStruct((COLS, rows, LANES), jnp.bfloat16),
-        in_specs=[smem()] + vmem(4),
-        name="mix_forward_" + str(n),
-        **params(8 * rows * 512 * 512, 4 << 20),
-    )(place, entries, kept, recv, constant(np.stack(col_tables(n))))
-
-
-def mix_back(n, place, entries, first_field, upstream, first_grad, kept, recv, first_filter):
-    rows = 2 * GROUPS * n // 8
-    tables = col_tables(n)
-    if n == H2:
-        tables = tables + tuple(table.T for table in tables)
-    total = (COLS, 2 * rows, LANES)
-    return pl.pallas_call(
-        functools.partial(mix_back_kernel, n, first_filter, first_field, first_grad),
+def both_tables():
+    return [constant(np.stack(col_tables(n))) for n in (H1, H2)]
+
+
+def mix_first(place, entries, kept, recv):
+    return pl.pallas_call(
+        mix_first_kernel,
+        out_shape=jax.ShapeDtypeStruct((COLS, FILTER_ROWS, LANES), jnp.bfloat16),
+        in_specs=[smem()] + vmem(5),
+        name="mix_first",
+        **params(8 * FILTER_ROWS * 512 * 512, 6 << 20),
+    )(place, entries, kept, recv, *both_tables())
+
+
+def mix_last(place, entries, later, kept, recv):
+    total = (COLS, 2 * FILTER_ROWS, LANES)
+    return pl.pallas_call(
+        mix_last_kernel,
         out_shape=(
-            jax.ShapeDtypeStruct((COLS, rows, LANES), jnp.bfloat16),
+            jax.ShapeDtypeStruct((COLS, SECOND_SLOT, LANES), jnp.bfloat16),
             jax.ShapeDtypeStruct(total, jnp.bfloat16),
         ),
-        in_specs=[smem()] + vmem(5),
+        in_specs=[smem()] + vmem(6),
         out_specs=tuple(vmem(1) + hbm(1)),
         scratch_shapes=[pltpu.VMEM(total, jnp.bfloat16), pltpu.SemaphoreType.DMA],
-        name="mix_back_" + str(n),
-        **params(12 * rows * 512 * 512, 6 << 20),
-    )(place, entries, upstream, kept, recv, constant(np.stack(tables)))
+        name="mix_last",
+        **params(12 * FILTER_ROWS * 512 * 512, 8 << 20),
+    )(place, entries, later, kept, recv, *both_tables())
 
 
 def grid_of(rows, columns):
@@ -364,9 +402,6 @@
                 first += slots
 
 
-FILTER_ROWS = 2 * GROUPS * (H1 + H2) // 8
-
-
 def send_filters(place, filter_first, filter_second):
     return pl.pallas_call(
         send_filters_kernel,
@@ -381,7 +416,7 @@
             pltpu.SemaphoreType.DMA((2,)),
         ],
         name="send_filters",
-        **params(12 * 64 * 512 * 128 * 2, 2 << 20),
+        **params(12 * 64 * 512 * 128 * 2, 2 << 20, 60),
     )(place, filter_first, filter_second)
 
 
@@ -448,13 +483,12 @@
     return lax.psum_scatter(terms, "rep", scatter_dimension=0, tiled=False)
 
 
-def swap_grads(sum_first, sum_second):
-    count_first, count_second = 2 * GROUPS * H1 // 8, 2 * GROUPS * H2 // 8
-    sent = jnp.concatenate([sum_first[count_first:], sum_second[count_second:]], axis=0)
+def swap_grads(sent):
+    groups = 2 * GROUPS
     zero = jnp.concatenate(
         [
-            sum_first[count_first:].reshape(2 * GROUPS, H1 // 8, LANES)[:, 0],
-            sum_second[count_second:].reshape(2 * GROUPS, H2 // 8, LANES)[:, 0],
+            sent[:SECOND_SLOT].reshape(groups, H1 // 8, LANES)[:, 0],
+            sent[SECOND_SLOT:].reshape(groups, H2 // 8, LANES)[:, 0],
             jnp.zeros((4, LANES), jnp.bfloat16),
         ],
         axis=0,
@@ -462,8 +496,7 @@
     return lax.ppermute(sent, "col", SWAP), lax.ppermute(zero, "col", ((0, 2), (1, 3)))
 
 
-def place_grads(place, sum_first, sum_second, swapped, col):
-    count_first, count_second = 2 * GROUPS * H1 // 8, 2 * GROUPS * H2 // 8
+def place_grads(place, kept, swapped, col):
     recv_first, recv_second = put_slots_zero(*swapped, col >= 2)
     return pl.pallas_call(
         place_grads_kernel,
@@ -474,7 +507,7 @@
         in_specs=[smem()] + vmem(4),
         name="place_grads",
         **params(12 * 128 * 128 * 128 * 2, 2 << 20),
-    )(place, sum_first[:count_first], recv_first, sum_second[:count_second], recv_second)
+    )(place, kept[:SECOND_SLOT], recv_first, kept[SECOND_SLOT:], recv_second)
 
 
 def layer_normalize(entry_values, gains):
@@ -544,7 +577,7 @@
             pltpu.SemaphoreType.DMA((3,)),
         ],
         name="first_norm",
-        **params(4 * 768 * 64 * 128, 2 << 20),
+        **params(4 * 768 * 64 * 128, 2 << 20, 60),
     )(images, grad_out, gains)
 
 
@@ -552,25 +585,34 @@
     return lax.broadcasted_iota(jnp.int32, (96, LANES), 1) < LANES // 2
 
 
-def reduce_kernel(
-    x_hbm, m_ref, w_hbm, gain_ref, norm_ref, down_hbm, x_ref, w_ref, down_ref, s_ref, n_ref, sems
+def token_kernel(
+    x_hbm, m_ref, g_hbm, w_hbm, wt_hbm, gain_ref, out_ref,
+    x_ref, g_ref, w_ref, wt_ref, s_ref, n_ref, back_ref, grad_ref, o_ref, sems,
 ):
     copies = [
-        pltpu.make_async_copy(x_hbm, x_ref, sems.at[0]),
-        pltpu.make_async_copy(w_hbm, w_ref, sems.at[1]),
+        pltpu.make_async_copy(source, target, sems.at[i])
+        for i, (source, target) in enumerate(
+            ((x_hbm, x_ref), (w_hbm, w_ref), (g_hbm, g_ref), (wt_hbm, wt_ref))
+        )
     ]
     for copy in copies:
         copy.start()
     at, lane = grid_of(LANES, 2 * LANES)
     spread_at = ones_at(at == 2 * lax.rem(lane, 64) + lax.div(lane, LANES))
+    at, lane = grid_of(2 * LANES, 2 * LANES)
+    here = LANES * lax.rem(lax.div(at, 64), 2) + 2 * lax.rem(at, 64) + lax.div(at, LANES)
+    merge_at = ones_at(lane == here)
+    mixed = m_ref[:, : GROUPS * 16, :].astype(jnp.float32).reshape(1536, LANES)
+    back_ref[...] = m_ref[:, GROUPS * 16 :, :].astype(jnp.float32).reshape(768, LANES)
     copies[0].wait()
-    mixed = m_ref[...].astype(jnp.float32).reshape(1536, LANES)
     section = x_ref[...].astype(jnp.float32).reshape(1536, LANES) + mixed
     spread = dot(section.astype(jnp.bfloat16), spread_at)
     for e in range(2):
         s_ref[e] = spread[:, e * LANES : (e + 1) * LANES]
     low = low_half()
-    copies[1].wait()
+    for copy in copies[1:]:
+        copy.wait()
+    grad_ref[...] = pack_pairs(g_ref[...])
     for first in range(0, 8, 2):
         patches = [
             jnp.concatenate(
@@ -584,73 +626,22 @@
             for i in (first, first + 1)
         ]
         both = dot(w_ref[...], jnp.concatenate(patches, axis=1))
+        grads = []
         for i in range(2):
             block = both[:, i * LANES : (i + 1) * LANES]
             down = jnp.where(low, block[:96], block[96:]).astype(jnp.bfloat16)
-            down_ref[first + i] = down
-            normed, _ = standardize(down.astype(jnp.float32))
-            n_ref[pl.ds(first + i, 96, stride=8), :] = normed * gain_ref[...]
-    copy = pltpu.make_async_copy(down_ref, down_hbm, sems.at[2])
-    copy.start()
-    norm_ref[...] = n_ref[...].reshape(ROWS, GROUPS * 8, LANES).astype(jnp.bfloat16)
-    copy.wait()
-
-
-def reduce_step(images, mixed, weight, gains):
-    return pl.pallas_call(
-        reduce_kernel,
-        out_shape=(
-            jax.ShapeDtypeStruct((ROWS, GROUPS * 8, LANES), jnp.bfloat16),
-            jax.ShapeDtypeStruct((8, 96, LANES), jnp.bfloat16),
-        ),
-        in_specs=hbm(1) + vmem(1) + hbm(1) + vmem(1),
-        out_specs=tuple(vmem(1) + hbm(1)),
-        scratch_shapes=[
-            pltpu.VMEM((96, 16, LANES), jnp.bfloat16),
-            pltpu.VMEM((192, 384), jnp.bfloat16),
-            pltpu.VMEM((8, 96, LANES), jnp.bfloat16),
-            pltpu.VMEM((2, 1536, LANES), jnp.float32),
-            pltpu.VMEM((768, LANES), jnp.float32),
-            pltpu.SemaphoreType.DMA((3,)),
-        ],
-        name="reduce_step",
-        **params(4 * 2 * 192 * 384 * 256, 2 << 20),
-    )(images, mixed, weight, gains)
-
-
-def expand_kernel(
-    b_ref, down_hbm, g_hbm, w_hbm, gain_ref, out_ref,
-    down_ref, g_ref, w_ref, back_ref, grad_ref, o_ref, sems,
-):
-    copies = [
-        pltpu.make_async_copy(source, target, sems.at[i])
-        for i, (source, target) in enumerate(
-            ((g_hbm, g_ref), (down_hbm, down_ref), (w_hbm, w_ref))
-        )
-    ]
-    for copy in copies:
-        copy.start()
-    at, lane = grid_of(2 * LANES, 2 * LANES)
-    here = LANES * lax.rem(lax.div(at, 64), 2) + 2 * lax.rem(at, 64) + lax.div(at, LANES)
-    merge_at = ones_at(lane == here)
-    back_ref[...] = b_ref[...].astype(jnp.float32).reshape(768, LANES)
-    for copy in copies:
-        copy.wait()
-    grad_ref[...] = pack_pairs(g_ref[...])
-    low = low_half()
-    for first in range(0, 8, 2):
-        grads = []
-        for i in (first, first + 1):
-            normed, scale = standardize(down_ref[i].astype(jnp.float32))
-            upstream = back_ref[pl.ds(i, 96, stride=8), :] * gain_ref[...]
+            normed, scale = standardize(down.astype(jnp.float32))
+            rows = pl.ds(first + i, 96, stride=8)
+            n_ref[rows, :] = normed * gain_ref[...]
+            upstream = back_ref[rows, :] * gain_ref[...]
             step = upstream - fold(upstream) / 192.0 - normed * (fold(upstream * normed) / 192.0)
-            total = grad_ref[pl.ds(i, 96, stride=8), :] + scale * step
+            total = grad_ref[rows, :] + scale * step
             total = total.astype(jnp.bfloat16).astype(jnp.float32)
             grads.append((total, pltpu.roll(total, LANES // 2, 1)))
         even = jnp.where(low, grads[0][0], grads[1][1])
         odd = jnp.where(low, grads[0][1], grads[1][0])
         both = jnp.concatenate([even, odd], axis=0).astype(jnp.bfloat16)
-        patches = dot(w_ref[...], both).astype(jnp.bfloat16)
+        patches = dot(wt_ref[...], both).astype(jnp.bfloat16)
         rows = [
             jnp.concatenate(
                 [patches[(2 * a + e) * 96 : (2 * a + e + 1) * 96] for e in range(2)], axis=1
@@ -663,26 +654,34 @@
                 o_ref[pl.ds(2 * (first + i) + a, 96, stride=16), :] = merged[
                     a * 96 : (a + 1) * 96, i * LANES : (i + 1) * LANES
                 ]
-    out_ref[...] = o_ref[...].reshape(ROWS, GROUPS * 16, LANES).astype(jnp.bfloat16)
-
-
-def expand_step(back, down, grad_out, weight, gains):
-    return pl.pallas_call(
-        expand_kernel,
-        out_shape=jax.ShapeDtypeStruct((ROWS, GROUPS * 16, LANES), jnp.bfloat16),
-        in_specs=vmem(1) + hbm(3) + vmem(1),
+    out_ref[:, : GROUPS * 16, :] = (
+        o_ref[...].reshape(ROWS, GROUPS * 16, LANES).astype(jnp.bfloat16)
+    )
+    out_ref[:, GROUPS * 16 :, :] = (
+        n_ref[...].reshape(ROWS, GROUPS * 8, LANES).astype(jnp.bfloat16)
+    )
+
+
+def token_step(images, back, grad_out, weight, gains):
+    return pl.pallas_call(
+        token_kernel,
+        out_shape=jax.ShapeDtypeStruct((ROWS, GROUPS * 24, LANES), jnp.bfloat16),
+        in_specs=hbm(1) + vmem(1) + hbm(3) + vmem(1),
         scratch_shapes=[
-            pltpu.VMEM((8, 96, LANES), jnp.bfloat16),
+            pltpu.VMEM((96, 16, LANES), jnp.bfloat16),
             pltpu.VMEM((192, 8, 64), jnp.bfloat16),
+            pltpu.VMEM((192, 384), jnp.bfloat16),
             pltpu.VMEM((384, 192), jnp.bfloat16),
+            pltpu.VMEM((2, 1536, LANES), jnp.float32),
+            pltpu.VMEM((768, LANES), jnp.float32),
             pltpu.VMEM((768, LANES), jnp.float32),
             pltpu.VMEM((768, LANES), jnp.float32),
             pltpu.VMEM((1536, LANES), jnp.float32),
-            pltpu.SemaphoreType.DMA((3,)),
+            pltpu.SemaphoreType.DMA((4,)),
         ],
-        name="expand_step",
-        **params(4 * 2 * 192 * 384 * 256, 2 << 20),
-    )(back, down, grad_out, weight, gains)
+        name="token_step",
+        **params(8 * 2 * 192 * 384 * 256, 4 << 20),
+    )(images, back, grad_out, weight, weight.T, gains)
 
 
 def unpack_first(blocks):
@@ -701,7 +700,6 @@
 def shards(images, gain_first, filter_first, reduce_weight, gain_second, filter_second, grad_out):
     col = lax.axis_index("col")
     place = jnp.stack([col, lax.axis_index("rep")]).astype(jnp.int32)
-    second_rows = 2 * GROUPS * H1 // 8
     pixels = images.reshape(96, 16, LANES)
     upstream = grad_out.reshape(192, 8, 64)
     weight = reduce_weight.reshape(96, 2, 384).transpose(1, 0, 2).reshape(192, 384)
@@ -709,39 +707,27 @@
 
     sent, zero = send_filters(place, filter_first, filter_second)
     swapped = swap_filters(sent, zero)
-    pixels, sent = lax.optimization_barrier((pixels, sent))
+    kept = keep_filters(place, filter_first, filter_second)
     both = exchange(first_norm(pixels, upstream, gain_first), "row")
-    kept = keep_filters(place, filter_first, filter_second)
     half = forward_rows(both, (H1, H2))
     half, swapped = lax.optimization_barrier((half, swapped))
     recv = patch_filters(*swapped, col)
     both = exchange(half, "col")
-    mixed = exchange(mix_forward(H1, place, both, kept, recv, 0), "col")
-    mixed_one = exchange(inverse_rows(mixed, H1), "row")
-
-    norm_two, down = reduce_step(pixels, mixed_one, weight, gains)
-    half_two = exchange(forward_rows(exchange(norm_two, "row"), (H2,)), "col")
-    dspec_two, terms_two = mix_back(
-        H2, place, half_two, 0, both, second_rows, kept, recv, second_rows
-    )
-    sum_two = summed(terms_two)
-    rot_two = exchange(dspec_two, "col")
-    rot_two, sum_two = lax.optimization_barrier((rot_two, sum_two))
-    back_two = exchange(inverse_rows(rot_two, H2), "row")
-
-    grad_section = expand_step(back_two, down, upstream, weight.T, gains)
-    half_grad = exchange(forward_rows(exchange(grad_section, "row"), (H1,)), "col")
-    dspec_one, terms_one = mix_back(H1, place, both, 0, half_grad, 0, kept, recv, 0)
-    sum_one = summed(terms_one)
+    mixed = exchange(mix_first(place, both, kept, recv), "col")
+    mixed = exchange(inverse_rows(mixed, (H1, H2)), "row")
+    tokens = token_step(pixels, mixed, upstream, weight, gains)
+    later = exchange(forward_rows(exchange(tokens, "row"), (H1, H2)), "col")
+    dspec_one, terms = mix_last(place, both, later, kept, recv)
+    terms = summed(terms)
     rot_one = exchange(dspec_one, "col")
-    rot_one, sum_one = lax.optimization_barrier((rot_one, sum_one))
-    swapped = swap_grads(sum_one, sum_two)
-    grad_norm_one = unpack_first(exchange(inverse_rows(rot_one, H1), "row"))
+    rot_one, terms = lax.optimization_barrier((rot_one, terms))
+    swapped = swap_grads(terms[FILTER_ROWS:])
+    grad_norm_one = unpack_first(exchange(inverse_rows(rot_one, (H1,)), "row"))
     grad_images = (
-        unpack_first(grad_section).astype(jnp.float32)
+        unpack_first(tokens[:, : GROUPS * 16]).astype(jnp.float32)
         + norm_pullback_step(images.astype(jnp.float32), gain_first, grad_norm_one)
     ).astype(jnp.bfloat16)
-    grad_first, grad_second = place_grads(place, sum_one, sum_two, swapped, col)
+    grad_first, grad_second = place_grads(place, terms[:FILTER_ROWS], swapped, col)
     return (grad_images, grad_first, grad_second)
 
 

time: 362 us -> 302 us (0.83)
  blocking collectives: 138 us -> 97.5 us
  starting transfers between devices: 79.1 us -> 66.4 us
  local copies, waits for them, and re-layouts: 17.5 us -> 11.2 us
    all_to_all x6 -> x3, blocking collectives: 127 us -> 85.5 us  [exchange(): return lax.all_to_all(blocks, axis, split_axis=0, concat_axis=0, tiled=True)]
    all_to_all x6 -> x5, starting transfers between devices: 62.8 us -> 46.7 us  [exchange(): return lax.all_to_all(blocks, axis, split_axis=0, concat_axis=0, tiled=True)]
    all_to_all x6 -> x5, waiting for transfers between devices: 54.7 us -> 41.9 us  [exchange(): return lax.all_to_all(blocks, axis, split_axis=0, concat_axis=0, tiled=True)]
    ppermute x1, waiting for transfers between devices: 3.08 us -> 9.79 us  [swap_filters(): lax.ppermute(zero, 'col', ((2, 0), (3, 1)))]
    reduce_scatter x2 -> x1, waiting for transfers between devices: 4.56 us -> 8.49 us  [summed(): return lax.psum_scatter(terms, 'rep', scatter_dimension=0, tiled=False)]
    unnamed x61 -> x57, local copies, waits for them, and re-layouts: 13.4 us -> 10.2 us
    pallas_call x11 -> x7, Pallas kernels: 17.8 us -> 16.5 us  [the longest x1 4.61 us: mix_last(): pl.pallas_call(mix_last_kernel, out_shape=(jax.ShapeDtypeStruct((COLS, SE...]
  transfers between devices with their start and end apart: 12 -> 10, of which waited for: 10 -> 6; matrix products, arithmetic and copies ran while one was open for 2% -> 1% of each run, Pallas kernels for 2% -> 3%
where the time goes in v5:
time: 302 us; the launch traced here: 300 us
  blocking collectives  97.5 us (32%)
  waiting for transfers between devices  79.2 us (26%)
  starting transfers between devices  66.4 us (22%)
  Pallas kernels  26.9 us (9%)
  between operations  14.5 us (5%)
  local copies, waits for them, and re-layouts  11.2 us (4%)
  other arithmetic  4.65 us (2%)
    all_to_all x3, blocking collectives, exchange(): return lax.all_to_all(blocks, axis, split_axis=0, concat_axis=0, tiled=True)  85.5 us
    all_to_all x5, starting transfers between devices, exchange(): return lax.all_to_all(blocks, axis, split_axis=0, concat_axis=0, tiled=True)  46.7 us
    all_to_all x5, waiting for transfers between devices, exchange(): return lax.all_to_all(blocks, axis, split_axis=0, concat_axis=0, tiled=True)  41.9 us
    ppermute x1, waiting for transfers between devices, swap_grads(): lax.ppermute(sent, 'col', SWAP)  19 us
    all_gather x1, blocking collectives, patch_filters(): return lax.all_gather(recv, 'rep', axis=0, tiled=False)  12 us
    unnamed x57, local copies, waits for them, and re-layouts  10.2 us
    ppermute x1, waiting for transfers between devices, swap_filters(): lax.ppermute(zero, 'col', ((2, 0), (3, 1)))  9.79 us
    ppermute x1, starting transfers between devices, swap_filters(): lax.ppermute(sent, 'col', SWAP)  9.54 us
  transfers between devices with their start and end apart: 10, of which 6 were waited for; matrix products, arithmetic and copies ran while one was open for 1% of the time, Pallas kernels for 3%

profile of v5, /device:TPU:105, one launch (start us, length us, event | category | flops | bytes accessed | tf_op | source)
XLA Modules:
  0.0 300.5 jit_solution(4669224493509785336)
XLA Ops:
  7.2 1.9 copy.31
  9.1 2.4 first_norm.1
  11.5 8.6 %all-to-all-start = ((bf16[32,72,128]{2,1,0:T(8,128)(2,1)}), bf16[32,72,128]{2,1,0:T(8,128)(2,1)S(1)}, u32[]{:S(2)}, u32[]{:S(2)}) async-start(bf16[32,72,128]{2,1,0:T(8,128)(2,1)} %first_norm.1), calls=%async_computation | async-start | bytes 1179648 | tf_op jit(solution)/shard_map/all_to_all | solution.py:697
  20.2 0.6 pad_add_fusion.place_ref
  20.8 3.8 %send_filters.1 = (bf16[576,128]{1,0:T(8,128)(2,1)}, bf16[16,128]{1,0:T(8,128)(2,1)}) custom-call(s32[2]{0:T(128)} %pad_add_fusion.place_ref, f32[2,3,128,512]{3,2,1,0:T(8,128)} %first_ref.3, f32[2,6,64,256]{3,2,1,0:T(8,128)} %second_ref.3), custom_call_target="tpu_custom_call" | custom-call | flops 100663296 | bytes 2097152 | tf_op jit(solution)/shard_map/send_filters/pallas_call | solution.py:406
  24.6 9.5 %collective-permute-start = (bf16[576,128]{1,0:T(8,128)(2,1)}, bf16[576,128]{1,0:T(8,128)(2,1)}, u32[]{:S(2)}, u32[]{:S(2)}) collective-permute-start(bf16[576,128]{1,0:T(8,128)(2,1)} %get-tuple-element.14), channel_id=1, source_target_pairs={{0,12},{12,0},{4,8},{8,4},{1,13},{13,1},{5,9},{9,5},{2,14},{14,2},... | collective-permute-start | bytes 442376 | tf_op jit(solution)/shard_map/ppermute | solution.py:448
  34.2 1.3 collective-permute-start.1
  35.5 0.9 copy-done.16
  36.4 1.4 forward_rows_512_256.2
  37.7 9.8 %collective-permute-done.1 = bf16[16,128]{1,0:T(8,128)(2,1)S(1)} collective-permute-done((bf16[16,128]{1,0:T(8,128)(2,1)}, bf16[16,128]{1,0:T(8,128)(2,1)S(1)}, u32[]{:S(2)}, u32[]{:S(2)}) %collective-permute-start.1) | collective-permute-done | bytes 4128 | tf_op jit(solution)/shard_map/ppermute | solution.py:448
  47.5 10.3 %all-to-all-start.1 = ((bf16[4,576,128]{2,1,0:T(8,128)(2,1)}), bf16[4,576,128]{2,1,0:T(8,128)(2,1)S(1)}, u32[]{:S(2)}, u32[]{:S(2)}) async-start(bf16[4,576,128]{2,1,0:T(8,128)(2,1)} %forward_rows_512_256.2), calls=%async_computation.1 | async-start | bytes 1179648 | tf_op jit(solution)/shard_map/all_to_all | solution.py:697
  58.0 2.0 keep_filters.1.kept_ref
  60.0 1.0 bitcast_select_fusion.1
  61.0 1.0 bitcast_select_fusion
  62.1 12.0 %all-gather = bf16[2304,128]{1,0:T(8,128)(2,1)S(1)} all-gather(bf16[576,128]{1,0:T(8,128)(2,1)S(1)} %pad_maximum_fusion), channel_id=2, replica_groups=mesh['row'=32,'col'=4,'rep'=4] {'rep'}, dimensions={0}, use_global_device_ids=true | all-gather | bytes 737280 | tf_op jit(solution)/shard_map/all_gather | solution.py:453
  74.0 14.4 %all-to-all-done.1.x_ref = bf16[4,576,128]{2,1,0:T(8,128)(2,1)S(1)} async-done(((bf16[4,576,128]{2,1,0:T(8,128)(2,1)}), bf16[4,576,128]{2,1,0:T(8,128)(2,1)S(1)}, u32[]{:S(2)}, u32[]{:S(2)}) %all-to-all-start.1) | async-done | bytes 589856 | tf_op jit(solution)/shard_map/all_to_all | solution.py:697
  88.4 0.9 copy-done.8
  89.3 1.1 copy-done.9
  90.3 1.1 copy-done.14
  91.4 1.2 copy-done.20
  92.6 1.2 copy-done.22
  93.9 3.0 %mix_first.1 = bf16[4,576,128]{2,1,0:T(8,128)(2,1)S(1)} custom-call(s32[2]{0:T(128)S(1)} %copy-done.19, bf16[4,576,128]{2,1,0:T(8,128)(2,1)S(1)} %copy-done.9, bf16[4,576,128]{2,1,0:T(8,128)(2,1)S(1)} %copy-done.14, bf16[4,576,128]{2,1,0:T(8,128)(2,1)S(1)} %bitcast.36, bf16[2,512,512]{2,1,0:T(8,128)(2,1)S(1)} %copy-done.20, bf16[2,512,512]{2,1,0:T(8,128)(2,1)S(1)} %copy-done.22), custom_call_target="tpu_custom_call" | custom-call | flops 1207959552 | bytes 6291456 | tf_op jit(solution)/shard_map/mix_first/pallas_call | solution.py:292
  96.9 0.8 copy-done.11
  97.7 30.1 %all_to_all.40.refs_0_ = bf16[4,576,128]{2,1,0:T(8,128)(2,1)S(1)} all-to-all(bf16[4,576,128]{2,1,0:T(8,128)(2,1)S(1)} %mix_first.1), channel_id=1, replica_groups=mesh['row'=32,'col'=4,'rep'=4] {'col'}, dimensions={0} | all-to-all | bytes 1179648 | tf_op jit(solution)/shard_map/all_to_all | solution.py:697
  127.8 1.3 inverse_rows_512_256.1
  129.2 9.0 %all-to-all-start.3 = ((bf16[32,72,128]{2,1,0:T(8,128)(2,1)}), bf16[32,72,128]{2,1,0:T(8,128)(2,1)S(1)}, u32[]{:S(2)}, u32[]{:S(2)}) async-start(bf16[32,72,128]{2,1,0:T(8,128)(2,1)} %inverse_rows_512_256.1), calls=%async_computation.3 | async-start | bytes 1179648 | tf_op jit(solution)/shard_map/all_to_all | solution.py:697
  138.4 0.1 copy.33
  138.5 0.1 reshape.170
  138.8 13.7 %all-to-all-done.3.m_ref = bf16[32,72,128]{2,1,0:T(8,128)(2,1)S(1)} async-done(((bf16[32,72,128]{2,1,0:T(8,128)(2,1)}), bf16[32,72,128]{2,1,0:T(8,128)(2,1)S(1)}, u32[]{:S(2)}, u32[]{:S(2)}) %all-to-all-start.3) | async-done | bytes 589856 | tf_op jit(solution)/shard_map/all_to_all | solution.py:697
  152.6 4.5 %token_step.1 = bf16[32,72,128]{2,1,0:T(8,128)(2,1)S(1)} custom-call(bf16[96,16,128]{2,1,0:T(8,128)(2,1)S(1)} %bitcast.29, bf16[32,72,128]{2,1,0:T(8,128)(2,1)S(1)} %all-to-all-done.3.m_ref, bf16[192,8,64]{2,1,0:T(8,128)(2,1)S(1)} %bitcast.32, bf16[192,384]{1,0:T(8,128)(2,1)S(1)} %bitcast.34, bf16[384,192]{1,0:T(8,128)(2,1)S(1)} %bitcast.35, ...), custom_call_target="tpu_custom_call" | custom-call | flops 301989888 | bytes 4194304 | tf_op jit(solution)/shard_map/token_step/pallas_call | solution.py:666
  157.1 21.9 %all_to_all.41.refs_0_ = bf16[32,72,128]{2,1,0:T(8,128)(2,1)S(1)} all-to-all(bf16[32,72,128]{2,1,0:T(8,128)(2,1)S(1)} %token_step.1), channel_id=1, replica_groups=mesh['row'=32,'col'=4,'rep'=4] {'row'}, dimensions={0} | all-to-all | bytes 1179648 | tf_op jit(solution)/shard_map/all_to_all | solution.py:697
  179.0 0.5 forward_rows_512_256.3
  179.5 33.5 %all_to_all.42.y_ref = bf16[4,576,128]{2,1,0:T(8,128)(2,1)S(1)} all-to-all(bf16[4,576,128]{2,1,0:T(8,128)(2,1)S(1)} %forward_rows_512_256.3), channel_id=1, replica_groups=mesh['row'=32,'col'=4,'rep'=4] {'col'}, dimensions={0} | all-to-all | bytes 1179648 | tf_op jit(solution)/shard_map/all_to_all | solution.py:697
  213.1 4.6 %mix_last.1 = (bf16[4,384,128]{2,1,0:T(8,128)(2,1)}, bf16[4,1152,128]{2,1,0:T(8,128)(2,1)S(1)}) custom-call(s32[2]{0:T(128)S(1)} %copy-done.19, bf16[4,576,128]{2,1,0:T(8,128)(2,1)S(1)} %copy-done.10, bf16[4,576,128]{2,1,0:T(8,128)(2,1)S(1)} %all_to_all.42.y_ref, bf16[4,576,128]{2,1,0:T(8,128)(2,1)S(1)} %copy-done.15, bf16[4,576,128]{2,1,0:T(8,128)(2,1)S(1)} %bitcast.37, ...), custom_call_target="tpu_custom_call" | custom-call | flops 1811939328 | bytes 8388608 | tf_op jit(solution)/shard_map/mix_last/pallas_call | solution.py:303
  217.7 1.0 copy-done.7
  218.8 6.4 %all-to-all-start.6 = ((bf16[4,384,128]{2,1,0:T(8,128)(2,1)}), bf16[4,384,128]{2,1,0:T(8,128)(2,1)S(1)}, u32[]{:S(2)}, u32[]{:S(2)}) async-start(bf16[4,384,128]{2,1,0:T(8,128)(2,1)} %get-tuple-element.19), calls=%async_computation.6 | async-start | bytes 786432 | tf_op jit(solution)/shard_map/all_to_all | solution.py:697
  225.3 13.8 %all-to-all-done.6.refs_0_ = bf16[4,384,128]{2,1,0:T(8,128)(2,1)S(1)} async-done(((bf16[4,384,128]{2,1,0:T(8,128)(2,1)}), bf16[4,384,128]{2,1,0:T(8,128)(2,1)S(1)}, u32[]{:S(2)}, u32[]{:S(2)}) %all-to-all-start.6) | async-done | bytes 393248 | tf_op jit(solution)/shard_map/all_to_all | solution.py:697
  239.0 8.5 %reduce-scatter.2.cloned.1.call-done = bf16[1,1152,128]{2,1,0:T(8,128)(2,1)} async-done(((bf16[4,1152,128]{2,1,0:T(8,128)(2,1)}), bf16[1,1152,128]{2,1,0:T(8,128)(2,1)}) %reduce-scatter.2.cloned.1.call-update) | async-done | bytes 294928 | tf_op jit(solution)/shard_map/reduce_scatter | solution.py:483
  247.5 1.2 inverse_rows_512.1
  248.7 12.3 %all-to-all-start.7 = ((bf16[32,48,128]{2,1,0:T(8,128)(2,1)}), bf16[32,48,128]{2,1,0:T(8,128)(2,1)S(1)}, u32[]{:S(2)}, u32[]{:S(2)}) async-start(bf16[32,48,128]{2,1,0:T(8,128)(2,1)} %inverse_rows_512.1), calls=%async_computation.8 | async-start | bytes 786432 | tf_op jit(solution)/shard_map/all_to_all | solution.py:697
  261.3 6.8 %collective-permute-start.2 = (bf16[16,128]{1,0:T(8,128)(2,1)S(1)}, bf16[16,128]{1,0:T(8,128)(2,1)S(1)}, u32[]{:S(2)}, u32[]{:S(2)}) collective-permute-start(bf16[16,128]{1,0:T(8,128)(2,1)S(1)} %maximum_maximum_fusion), channel_id=1, source_target_pairs={{0,8},{4,12},{1,9},{5,13},{2,10},{6,14},{3,11},{7,15},{16,24},{20,... | collective-permute-start | bytes 12296 | tf_op jit(solution)/shard_map/ppermute | solution.py:496
  268.4 2.1 collective-permute-start.3
  270.5 19.0 %collective-permute-done.3 = bf16[576,128]{1,0:T(8,128)(2,1)S(1)} collective-permute-done((bf16[576,128]{1,0:T(8,128)(2,1)S(1)}, bf16[576,128]{1,0:T(8,128)(2,1)S(1)}, u32[]{:S(2)}, u32[]{:S(2)}) %collective-permute-start.3) | collective-permute-done | bytes 147488 | tf_op jit(solution)/shard_map/ppermute | solution.py:496
  289.5 0.1 slice_select_fusion.recv_first
  289.8 2.3 place_grads.1
  292.0 0.2 fusion.3
  292.3 0.3 fusion.7
  292.6 1.1 fusion.6
  (90 shorter events, 1.3 us)
Async XLA Ops:
  11.5 24.0 %copy-start.5 = (bf16[512,512]{1,0:T(8,128)(2,1)S(1)}, bf16[512,512]{1,0:T(8,128)(2,1)}, u32[]{:S(2)}) copy-start(bf16[512,512]{1,0:T(8,128)(2,1)} %constant.38.clone.refs_1_) | copy-start | bytes 1572868
  11.5 24.0 %all-to-all-start = ((bf16[32,72,128]{2,1,0:T(8,128)(2,1)}), bf16[32,72,128]{2,1,0:T(8,128)(2,1)S(1)}, u32[]{:S(2)}, u32[]{:S(2)}) async-start(bf16[32,72,128]{2,1,0:T(8,128)(2,1)} %first_norm.1), calls=%async_computation | async-start | bytes 1179648 | tf_op jit(solution)/shard_map/all_to_all | solution.py:697
  20.8 37.2 %copy-start.19 = (s32[2]{0:T(128)S(1)}, s32[2]{0:T(128)}, u32[]{:S(2)}) copy-start(s32[2]{0:T(128)} %pad_add_fusion.place_ref) | copy-start | bytes 28
  24.6 33.4 %copy-start.1 = (f32[2,3,128,512]{3,2,1,0:T(8,128)S(1)}, f32[2,3,128,512]{3,2,1,0:T(8,128)}, u32[]{:S(2)}) copy-start(f32[2,3,128,512]{3,2,1,0:T(8,128)} %first_ref.3) | copy-start | bytes 4718596
  24.6 33.4 %copy-start.4 = (f32[2,6,64,256]{3,2,1,0:T(8,128)S(1)}, f32[2,6,64,256]{3,2,1,0:T(8,128)}, u32[]{:S(2)}) copy-start(f32[2,6,64,256]{3,2,1,0:T(8,128)} %second_ref.3) | copy-start | bytes 2359300
  24.6 22.9 %collective-permute-start = (bf16[576,128]{1,0:T(8,128)(2,1)}, bf16[576,128]{1,0:T(8,128)(2,1)}, u32[]{:S(2)}, u32[]{:S(2)}) collective-permute-start(bf16[576,128]{1,0:T(8,128)(2,1)} %get-tuple-element.14), channel_id=1, source_target_pairs={{0,12},{12,0},{4,8},{8,4},{1,13},{13,1},{5,9},{9,5},{2,14},{14,2},... | collective-permute-start | bytes 442376 | tf_op jit(solution)/shard_map/ppermute | solution.py:448
  34.2 13.4 %collective-permute-start.1 = (bf16[16,128]{1,0:T(8,128)(2,1)}, bf16[16,128]{1,0:T(8,128)(2,1)S(1)}, u32[]{:S(2)}, u32[]{:S(2)}) collective-permute-start(bf16[16,128]{1,0:T(8,128)(2,1)} %get-tuple-element.15), channel_id=1, source_target_pairs={{8,0},{12,4},{9,1},{13,5},{10,2},{14,6},{11,3},{15,7},{24,16},{28,... | collective-permute-start | bytes 12296 | tf_op jit(solution)/shard_map/ppermute | solution.py:448
  35.5 0.9 copy-start.16
  47.5 40.9 %all-to-all-start.1 = ((bf16[4,576,128]{2,1,0:T(8,128)(2,1)}), bf16[4,576,128]{2,1,0:T(8,128)(2,1)S(1)}, u32[]{:S(2)}, u32[]{:S(2)}) async-start(bf16[4,576,128]{2,1,0:T(8,128)(2,1)} %forward_rows_512_256.2), calls=%async_computation.1 | async-start | bytes 1179648 | tf_op jit(solution)/shard_map/all_to_all | solution.py:697
  60.0 2.0 copy-start.13
  88.4 0.9 copy-start.8
  89.3 1.1 copy-start.9
  90.3 1.1 copy-start.14
  91.4 1.2 copy-start.20
  92.6 1.2 copy-start.22
  93.9 33.9 %copy-start.6 = (bf16[512,512]{1,0:T(8,128)(2,1)S(1)}, bf16[512,512]{1,0:T(8,128)(2,1)}, u32[]{:S(2)}) copy-start(bf16[512,512]{1,0:T(8,128)(2,1)} %constant.42.clone.refs_1_) | copy-start | bytes 1572868
  93.9 33.9 %copy-start.18 = (bf16[256,256]{1,0:T(8,128)(2,1)S(1)}, bf16[256,256]{1,0:T(8,128)(2,1)}, u32[]{:S(2)}) copy-start(bf16[256,256]{1,0:T(8,128)(2,1)} %constant.43.clone.refs_2_) | copy-start | bytes 393220
  96.9 0.8 copy-start.11
  127.8 10.4 %copy-start.25 = (bf16[192,384]{1,0:T(8,128)(2,1)S(1)}, bf16[192,384]{1,0:T(8,128)(2,1)}, u32[]{:S(2)}) copy-start(bf16[192,384]{1,0:T(8,128)(2,1)} %param.21) | copy-start | bytes 442372
  127.8 10.7 %copy-start.27 = (f32[192]{0:T(256)S(1)}, f32[192]{0:T(256)}, u32[]{:S(2)}) copy-start(f32[192]{0:T(256)} %param.22) | copy-start | bytes 2308
  129.2 23.4 %copy-start = (bf16[1,96,16,128]{3,2,1,0:T(8,128)(2,1)S(1)}, bf16[1,96,16,128]{3,2,1,0:T(8,128)(2,1)}, u32[]{:S(2)}) copy-start(bf16[1,96,16,128]{3,2,1,0:T(8,128)(2,1)} %param.18) | copy-start | bytes 1179652
  129.2 23.4 %copy-start.3 = (bf16[1,192,8,64]{3,2,1,0:T(8,128)(2,1)S(1)}, bf16[1,192,8,64]{3,2,1,0:T(8,128)(2,1)}, u32[]{:S(2)}) copy-start(bf16[1,192,8,64]{3,2,1,0:T(8,128)(2,1)} %copy.31) | copy-start | bytes 589828
  129.2 23.4 %all-to-all-start.3 = ((bf16[32,72,128]{2,1,0:T(8,128)(2,1)}), bf16[32,72,128]{2,1,0:T(8,128)(2,1)S(1)}, u32[]{:S(2)}, u32[]{:S(2)}) async-start(bf16[32,72,128]{2,1,0:T(8,128)(2,1)} %inverse_rows_512_256.1), calls=%async_computation.3 | async-start | bytes 1179648 | tf_op jit(solution)/shard_map/all_to_all | solution.py:697
  138.2 109.3 %reduce-scatter.2.cloned.1.call-start = ((), (), s32[]{:S(2)}) async-start(), calls=%async_computation.9 | async-start | bytes 1474560 | tf_op jit(solution)/shard_map/reduce_scatter | solution.py:483
  152.6 26.4 %copy-start.17 = (bf16[256,256]{1,0:T(8,128)(2,1)S(1)}, bf16[256,256]{1,0:T(8,128)(2,1)}, u32[]{:S(2)}) copy-start(bf16[256,256]{1,0:T(8,128)(2,1)} %constant.39.clone.refs_2_) | copy-start | bytes 393220
  157.1 111.3 %copy-start.2 = (bf16[32,72,128]{2,1,0:T(8,128)(2,1)}, bf16[32,72,128]{2,1,0:T(8,128)(2,1)S(1)}, u32[]{:S(2)}) copy-start(bf16[32,72,128]{2,1,0:T(8,128)(2,1)S(1)} %token_step.1) | copy-start | bytes 1769476
  157.1 56.0 %copy-start.23 = (bf16[2,512,512]{2,1,0:T(8,128)(2,1)S(1)}, bf16[2,512,512]{2,1,0:T(8,128)(2,1)}, u32[]{:S(2)}) copy-start(bf16[2,512,512]{2,1,0:T(8,128)(2,1)} %constant.41.clone.second_tables) | copy-start | bytes 3145732
  179.0 34.1 %copy-start.10 = (bf16[4,576,128]{2,1,0:T(8,128)(2,1)S(1)}, bf16[4,576,128]{2,1,0:T(8,128)(2,1)}, u32[]{:S(2)}) copy-start(bf16[4,576,128]{2,1,0:T(8,128)(2,1)} %copy-done.8) | copy-start | bytes 1769476
  179.0 34.1 %copy-start.12 = (bf16[2304,128]{1,0:T(8,128)(2,1)S(1)}, bf16[2304,128]{1,0:T(8,128)(2,1)}, u32[]{:S(2)}) copy-start(bf16[2304,128]{1,0:T(8,128)(2,1)} %copy-done.11) | copy-start | bytes 1769476
  179.0 34.1 %copy-start.15 = (bf16[4,576,128]{2,1,0:T(8,128)(2,1)S(1)}, bf16[4,576,128]{2,1,0:T(8,128)(2,1)}, u32[]{:S(2)}) copy-start(bf16[4,576,128]{2,1,0:T(8,128)(2,1)} %copy-done.13) | copy-start | bytes 1769476
  179.0 34.1 %copy-start.21 = (bf16[2,512,512]{2,1,0:T(8,128)(2,1)S(1)}, bf16[2,512,512]{2,1,0:T(8,128)(2,1)}, u32[]{:S(2)}) copy-start(bf16[2,512,512]{2,1,0:T(8,128)(2,1)} %constant.40.clone.first_tables) | copy-start | bytes 3145732
  217.7 1.0 copy-start.7
  218.8 20.3 %all-to-all-start.6 = ((bf16[4,384,128]{2,1,0:T(8,128)(2,1)}), bf16[4,384,128]{2,1,0:T(8,128)(2,1)S(1)}, u32[]{:S(2)}, u32[]{:S(2)}) async-start(bf16[4,384,128]{2,1,0:T(8,128)(2,1)} %get-tuple-element.19), calls=%async_computation.6 | async-start | bytes 786432 | tf_op jit(solution)/shard_map/all_to_all | solution.py:697
  247.5 13.6 %copy-start.24 = (bf16[1,1152,128]{2,1,0:T(8,128)(2,1)S(1)}, bf16[1,1152,128]{2,1,0:T(8,128)(2,1)}, u32[]{:S(2)}) copy-start(bf16[1,1152,128]{2,1,0:T(8,128)(2,1)} %reduce-scatter.2.cloned.1.call-done) | copy-start | bytes 884740
  248.7 43.3 %copy-start.26 = (f32[96]{0:T(128)S(1)}, f32[96]{0:T(128)}, u32[]{:S(2)}) copy-start(f32[96]{0:T(128)} %gain_ref.1) | copy-start | bytes 1156
  248.7 43.3 %all-to-all-start.7 = ((bf16[32,48,128]{2,1,0:T(8,128)(2,1)}), bf16[32,48,128]{2,1,0:T(8,128)(2,1)S(1)}, u32[]{:S(2)}, u32[]{:S(2)}) async-start(bf16[32,48,128]{2,1,0:T(8,128)(2,1)} %inverse_rows_512.1), calls=%async_computation.8 | async-start | bytes 786432 | tf_op jit(solution)/shard_map/all_to_all | solution.py:697
  261.3 9.1 %collective-permute-start.2 = (bf16[16,128]{1,0:T(8,128)(2,1)S(1)}, bf16[16,128]{1,0:T(8,128)(2,1)S(1)}, u32[]{:S(2)}, u32[]{:S(2)}) collective-permute-start(bf16[16,128]{1,0:T(8,128)(2,1)S(1)} %maximum_maximum_fusion), channel_id=1, source_target_pairs={{0,8},{4,12},{1,9},{5,13},{2,10},{6,14},{3,11},{7,15},{16,24},{20,... | collective-permute-start | bytes 12296 | tf_op jit(solution)/shard_map/ppermute | solution.py:496
  268.4 24.2 %slice-start = ((bf16[32,72,128]{2,1,0:T(8,128)(2,1)}), bf16[32,48,128]{2,1,0:T(8,128)(2,1)S(1)}, s32[]{:S(2)}) async-start(bf16[32,72,128]{2,1,0:T(8,128)(2,1)} %copy-done.2), calls=%async_computation.10 | async-start | bytes 786432 | tf_op jit(solution)/shard_map/slice | solution.py:727
  268.4 21.1 %collective-permute-start.3 = (bf16[576,128]{1,0:T(8,128)(2,1)S(1)}, bf16[576,128]{1,0:T(8,128)(2,1)S(1)}, u32[]{:S(2)}, u32[]{:S(2)}) collective-permute-start(bf16[576,128]{1,0:T(8,128)(2,1)S(1)} %slice.64), channel_id=1, source_target_pairs={{0,12},{12,0},{4,8},{8,4},{1,13},{13,1},{5,9},{9,5},{2,14},{14,2},... | collective-permute-start | bytes 442376 | tf_op jit(solution)/shard_map/ppermute | solution.py:496
Sparse Core Ops, SparseCore 0:
  218.9 28.5 reduce-scatter.1

commit v6 on v5

--- a/solution.py
+++ b/solution.py
@@ -281,7 +281,7 @@
 
 
 def vmem(count):
-    return [pl.BlockSpec(memory_space=pltpu.VMEM)] * count
+    return [pl.BlockSpec()] * count
 
 
 def both_tables():
@@ -533,15 +533,24 @@
 
 
 def pack_pairs(block):
-    fields = block.astype(jnp.float32).reshape(96, 2, 8, 64)
-    at, lane = grid_of(64, LANES)
-    return sum(
-        dot(fields[:, i].reshape(768, 64).astype(jnp.bfloat16), ones_at(lane == at + 64 * i))
-        for i in range(2)
-    )
-
-
-def first_norm_kernel(x_ref, g_ref, gain_ref, out_ref, x_buf, g_buf, gain_buf, sems):
+    at, lane = grid_of(LANES, 192)
+    mine = lax.rem(lane, 2) == lax.div(at, 64)
+    fields = []
+    for i in range(8):
+        field = block[i].astype(jnp.float32)
+        fields.append(jnp.where(mine, jnp.concatenate([field, field], axis=0), 0.0))
+    at, lane = grid_of(96, 192)
+    return lax.dot_general(
+        ones_at(lax.div(lane, 2) == at),
+        jnp.concatenate(fields, axis=0).astype(jnp.bfloat16),
+        (((1,), (1,)), ((), ())),
+        preferred_element_type=jnp.float32,
+    )
+
+
+def first_norm_kernel(
+    x_ref, g_ref, gain_ref, out_ref, x_buf, g_buf, gain_buf, pack_buf, sems
+):
     copies = [
         pltpu.make_async_copy(source, target, sems.at[i])
         for i, (source, target) in enumerate(
@@ -561,7 +570,10 @@
             jnp.bfloat16
         )
     copies[2].wait()
-    packed = pack_pairs(g_buf[...]).reshape(ROWS, GROUPS * 8, LANES)
+    packed = pack_pairs(g_buf[...])
+    for i in range(8):
+        pack_buf[pl.ds(i, 96, stride=8), :] = packed[:, i * LANES : (i + 1) * LANES]
+    packed = pack_buf[...].reshape(ROWS, GROUPS * 8, LANES)
     out_ref[:, GROUPS * 16 :, :] = packed.astype(jnp.bfloat16)
 
 
@@ -572,8 +584,9 @@
         in_specs=hbm(3),
         scratch_shapes=[
             pltpu.VMEM((96, 16, LANES), jnp.bfloat16),
-            pltpu.VMEM((192, 8, 64), jnp.bfloat16),
+            pltpu.VMEM((8, 64, 192), jnp.bfloat16),
             pltpu.SMEM((96,), jnp.float32),
+            pltpu.VMEM((768, LANES), jnp.float32),
             pltpu.SemaphoreType.DMA((3,)),
         ],
         name="first_norm",
@@ -587,7 +600,7 @@
 
 def token_kernel(
     x_hbm, m_ref, g_hbm, w_hbm, wt_hbm, gain_ref, out_ref,
-    x_ref, g_ref, w_ref, wt_ref, s_ref, n_ref, back_ref, grad_ref, o_ref, sems,
+    x_ref, g_ref, w_ref, wt_ref, s_ref, n_ref, back_ref, o_ref, sems,
 ):
     copies = [
         pltpu.make_async_copy(source, target, sems.at[i])
@@ -612,7 +625,7 @@
     low = low_half()
     for copy in copies[1:]:
         copy.wait()
-    grad_ref[...] = pack_pairs(g_ref[...])
+    packed = pack_pairs(g_ref[...])
     for first in range(0, 8, 2):
         patches = [
             jnp.concatenate(
@@ -635,7 +648,8 @@
             n_ref[rows, :] = normed * gain_ref[...]
             upstream = back_ref[rows, :] * gain_ref[...]
             step = upstream - fold(upstream) / 192.0 - normed * (fold(upstream * normed) / 192.0)
-            total = grad_ref[rows, :] + scale * step
+            at = (first + i) * LANES
+            total = packed[:, at : at + LANES] + scale * step
             total = total.astype(jnp.bfloat16).astype(jnp.float32)
             grads.append((total, pltpu.roll(total, LANES // 2, 1)))
         even = jnp.where(low, grads[0][0], grads[1][1])
@@ -669,11 +683,10 @@
         in_specs=hbm(1) + vmem(1) + hbm(3) + vmem(1),
         scratch_shapes=[
             pltpu.VMEM((96, 16, LANES), jnp.bfloat16),
-            pltpu.VMEM((192, 8, 64), jnp.bfloat16),
+            pltpu.VMEM((8, 64, 192), jnp.bfloat16),
             pltpu.VMEM((192, 384), jnp.bfloat16),
             pltpu.VMEM((384, 192), jnp.bfloat16),
             pltpu.VMEM((2, 1536, LANES), jnp.float32),
-            pltpu.VMEM((768, LANES), jnp.float32),
             pltpu.VMEM((768, LANES), jnp.float32),
             pltpu.VMEM((768, LANES), jnp.float32),
             pltpu.VMEM((1536, LANES), jnp.float32),
@@ -701,7 +714,7 @@
     col = lax.axis_index("col")
     place = jnp.stack([col, lax.axis_index("rep")]).astype(jnp.int32)
     pixels = images.reshape(96, 16, LANES)
-    upstream = grad_out.reshape(192, 8, 64)
+    upstream = grad_out.transpose(0, 2, 3, 1).reshape(8, 64, 192)
     weight = reduce_weight.reshape(96, 2, 384).transpose(1, 0, 2).reshape(192, 384)
     gains = jnp.repeat(gain_second.reshape(96, 2), 64, axis=1)
 

time: 302 us -> 297 us (0.983)
  local copies, waits for them, and re-layouts: 11.2 us -> 5.78 us
    unnamed x57 -> x52, local copies, waits for them, and re-layouts: 10.2 us -> 4.72 us
where the time goes in v6:
time: 297 us; the launch traced here: 296 us
  blocking collectives  95.8 us (32%)
  waiting for transfers between devices  78.8 us (27%)
  starting transfers between devices  68 us (23%)
  Pallas kernels  28.3 us (10%)
  between operations  14.5 us (5%)
  local copies, waits for them, and re-layouts  5.78 us (2%)
  other arithmetic  4.56 us (2%)
    all_to_all x3, blocking collectives, exchange(): return lax.all_to_all(blocks, axis, split_axis=0, concat_axis=0, tiled=True)  83.8 us
    all_to_all x5, starting transfers between devices, exchange(): return lax.all_to_all(blocks, axis, split_axis=0, concat_axis=0, tiled=True)  47.4 us
    all_to_all x5, waiting for transfers between devices, exchange(): return lax.all_to_all(blocks, axis, split_axis=0, concat_axis=0, tiled=True)  41.9 us
    ppermute x1, waiting for transfers between devices, swap_grads(): lax.ppermute(sent, 'col', SWAP)  19 us
    all_gather x1, blocking collectives, patch_filters(): return lax.all_gather(recv, 'rep', axis=0, tiled=False)  12 us
    ppermute x1, waiting for transfers between devices, swap_filters(): lax.ppermute(zero, 'col', ((2, 0), (3, 1)))  9.8 us
    ppermute x1, starting transfers between devices, swap_filters(): lax.ppermute(sent, 'col', SWAP)  9.54 us
    reduce_scatter x1, waiting for transfers between devices, summed(): return lax.psum_scatter(terms, 'rep', scatter_dimension=0, tiled=False)  8.09 us
  transfers between devices with their start and end apart: 10, of which 6 were waited for; matrix products, arithmetic and copies ran while one was open for 1% of the time, Pallas kernels for 3%

profile of v6, /device:TPU:105, one launch (start us, length us, event | category | flops | bytes accessed | tf_op | source)
XLA Modules:
  0.0 295.7 jit_solution(568100104212388285)
XLA Ops:
  7.2 2.5 first_norm.1
  9.7 8.6 %all-to-all-start = ((bf16[32,72,128]{2,1,0:T(8,128)(2,1)}), bf16[32,72,128]{2,1,0:T(8,128)(2,1)S(1)}, u32[]{:S(2)}, u32[]{:S(2)}) async-start(bf16[32,72,128]{2,1,0:T(8,128)(2,1)} %first_norm.1), calls=%async_computation | async-start | bytes 1179648 | tf_op jit(solution)/shard_map/all_to_all | solution.py:710
  18.3 0.6 pad_add_fusion.place_ref
  18.9 3.8 %send_filters.1 = (bf16[576,128]{1,0:T(8,128)(2,1)}, bf16[16,128]{1,0:T(8,128)(2,1)}) custom-call(s32[2]{0:T(128)} %pad_add_fusion.place_ref, f32[2,3,128,512]{3,2,1,0:T(8,128)} %first_ref.3, f32[2,6,64,256]{3,2,1,0:T(8,128)} %second_ref.3), custom_call_target="tpu_custom_call" | custom-call | flops 100663296 | bytes 2097152 | tf_op jit(solution)/shard_map/send_filters/pallas_call | solution.py:406
  22.7 9.5 %collective-permute-start = (bf16[576,128]{1,0:T(8,128)(2,1)}, bf16[576,128]{1,0:T(8,128)(2,1)}, u32[]{:S(2)}, u32[]{:S(2)}) collective-permute-start(bf16[576,128]{1,0:T(8,128)(2,1)} %get-tuple-element.14), channel_id=1, source_target_pairs={{0,12},{12,0},{4,8},{8,4},{1,13},{13,1},{5,9},{9,5},{2,14},{14,2},... | collective-permute-start | bytes 442376 | tf_op jit(solution)/shard_map/ppermute | solution.py:448
  32.2 1.3 collective-permute-start.1
  33.6 0.9 copy-done.14
  34.5 1.4 forward_rows_512_256.2
  35.8 9.8 %collective-permute-done.1 = bf16[16,128]{1,0:T(8,128)(2,1)S(1)} collective-permute-done((bf16[16,128]{1,0:T(8,128)(2,1)}, bf16[16,128]{1,0:T(8,128)(2,1)S(1)}, u32[]{:S(2)}, u32[]{:S(2)}) %collective-permute-start.1) | collective-permute-done | bytes 4128 | tf_op jit(solution)/shard_map/ppermute | solution.py:448
  45.6 10.3 %all-to-all-start.1 = ((bf16[4,576,128]{2,1,0:T(8,128)(2,1)}), bf16[4,576,128]{2,1,0:T(8,128)(2,1)S(1)}, u32[]{:S(2)}, u32[]{:S(2)}) async-start(bf16[4,576,128]{2,1,0:T(8,128)(2,1)} %forward_rows_512_256.2), calls=%async_computation.1 | async-start | bytes 1179648 | tf_op jit(solution)/shard_map/all_to_all | solution.py:710
  55.9 0.1 broadcast_in_dim.107
  56.1 2.0 keep_filters.1.kept_ref
  58.1 1.0 bitcast_select_fusion.1
  59.1 1.0 bitcast_select_fusion
  60.1 12.0 %all-gather = bf16[2304,128]{1,0:T(8,128)(2,1)S(1)} all-gather(bf16[576,128]{1,0:T(8,128)(2,1)S(1)} %pad_maximum_fusion), channel_id=2, replica_groups=mesh['row'=32,'col'=4,'rep'=4] {'rep'}, dimensions={0}, use_global_device_ids=true | all-gather | bytes 737280 | tf_op jit(solution)/shard_map/all_gather | solution.py:453
  72.1 14.5 %all-to-all-done.1.x_ref = bf16[4,576,128]{2,1,0:T(8,128)(2,1)S(1)} async-done(((bf16[4,576,128]{2,1,0:T(8,128)(2,1)}), bf16[4,576,128]{2,1,0:T(8,128)(2,1)S(1)}, u32[]{:S(2)}, u32[]{:S(2)}) %all-to-all-start.1) | async-done | bytes 589856 | tf_op jit(solution)/shard_map/all_to_all | solution.py:710
  86.6 1.3 copy-done.12
  87.9 1.2 copy-done.18
  89.1 1.2 copy-done.20
  90.3 3.1 %mix_first.1 = bf16[4,576,128]{2,1,0:T(8,128)(2,1)S(1)} custom-call(s32[2]{0:T(128)S(1)} %copy-done.17, bf16[4,576,128]{2,1,0:T(8,128)(2,1)S(1)} %all-to-all-done.1.x_ref, bf16[4,576,128]{2,1,0:T(8,128)(2,1)S(1)} %copy-done.12, bf16[4,576,128]{2,1,0:T(8,128)(2,1)S(1)} %bitcast.38, bf16[2,512,512]{2,1,0:T(8,128)(2,1)S(1)} %copy-done.18, ...), custom_call_target="tpu_custom_call" | custom-call | flops 1207959552 | bytes 6291456 | tf_op jit(solution)/shard_map/mix_first/pallas_call | solution.py:292
  93.4 28.0 %all_to_all.40.refs_0_ = bf16[4,576,128]{2,1,0:T(8,128)(2,1)S(1)} all-to-all(bf16[4,576,128]{2,1,0:T(8,128)(2,1)S(1)} %mix_first.1), channel_id=1, replica_groups=mesh['row'=32,'col'=4,'rep'=4] {'col'}, dimensions={0} | all-to-all | bytes 1179648 | tf_op jit(solution)/shard_map/all_to_all | solution.py:710
  121.4 1.4 inverse_rows_512_256.1
  122.8 10.6 %all-to-all-start.3 = ((bf16[32,72,128]{2,1,0:T(8,128)(2,1)}), bf16[32,72,128]{2,1,0:T(8,128)(2,1)S(1)}, u32[]{:S(2)}, u32[]{:S(2)}) async-start(bf16[32,72,128]{2,1,0:T(8,128)(2,1)} %inverse_rows_512_256.1), calls=%async_computation.3 | async-start | bytes 1179648 | tf_op jit(solution)/shard_map/all_to_all | solution.py:710
  133.5 0.1 copy.30
  133.6 0.1 reshape.170
  133.9 0.1 copy.32.gain_ref
  134.0 13.7 %all-to-all-done.3.m_ref = bf16[32,72,128]{2,1,0:T(8,128)(2,1)S(1)} async-done(((bf16[32,72,128]{2,1,0:T(8,128)(2,1)}), bf16[32,72,128]{2,1,0:T(8,128)(2,1)S(1)}, u32[]{:S(2)}, u32[]{:S(2)}) %all-to-all-start.3) | async-done | bytes 589856 | tf_op jit(solution)/shard_map/all_to_all | solution.py:710
  147.7 4.9 %token_step.1 = bf16[32,72,128]{2,1,0:T(8,128)(2,1)S(1)} custom-call(bf16[96,16,128]{2,1,0:T(8,128)(2,1)S(1)} %bitcast.31, bf16[32,72,128]{2,1,0:T(8,128)(2,1)S(1)} %all-to-all-done.3.m_ref, bf16[8,64,192]{2,1,0:T(8,128)(2,1)S(1)} %bitcast.36, bf16[192,384]{1,0:T(8,128)(2,1)S(1)} %bitcast.34, bf16[384,192]{1,0:T(8,128)(2,1)S(1)} %bitcast.37, ...), custom_call_target="tpu_custom_call" | custom-call | flops 301989888 | bytes 4194304 | tf_op jit(solution)/shard_map/token_step/pallas_call | solution.py:680
  152.7 21.9 %all_to_all.41.refs_0_ = bf16[32,72,128]{2,1,0:T(8,128)(2,1)S(1)} all-to-all(bf16[32,72,128]{2,1,0:T(8,128)(2,1)S(1)} %token_step.1), channel_id=1, replica_groups=mesh['row'=32,'col'=4,'rep'=4] {'row'}, dimensions={0} | all-to-all | bytes 1179648 | tf_op jit(solution)/shard_map/all_to_all | solution.py:710
  174.6 0.5 forward_rows_512_256.3
  175.1 34.0 %all_to_all.42.y_ref = bf16[4,576,128]{2,1,0:T(8,128)(2,1)S(1)} all-to-all(bf16[4,576,128]{2,1,0:T(8,128)(2,1)S(1)} %forward_rows_512_256.3), channel_id=1, replica_groups=mesh['row'=32,'col'=4,'rep'=4] {'col'}, dimensions={0} | all-to-all | bytes 1179648 | tf_op jit(solution)/shard_map/all_to_all | solution.py:710
  209.1 5.4 %mix_last.1 = (bf16[4,384,128]{2,1,0:T(8,128)(2,1)}, bf16[4,1152,128]{2,1,0:T(8,128)(2,1)}) custom-call(s32[2]{0:T(128)S(1)} %copy-done.17, bf16[4,576,128]{2,1,0:T(8,128)(2,1)S(1)} %copy-done.8, bf16[4,576,128]{2,1,0:T(8,128)(2,1)S(1)} %all_to_all.42.y_ref, bf16[4,576,128]{2,1,0:T(8,128)(2,1)S(1)} %copy-done.13, bf16[4,576,128]{2,1,0:T(8,128)(2,1)S(1)} %bitcast.39, ...), custom_call_target="tpu_custom_call" | custom-call | flops 1811939328 | bytes 8388608 | tf_op jit(solution)/shard_map/mix_last/pallas_call | solution.py:303
  214.5 6.4 %all-to-all-start.6 = ((bf16[4,384,128]{2,1,0:T(8,128)(2,1)}), bf16[4,384,128]{2,1,0:T(8,128)(2,1)S(1)}, u32[]{:S(2)}, u32[]{:S(2)}) async-start(bf16[4,384,128]{2,1,0:T(8,128)(2,1)} %get-tuple-element.19), calls=%async_computation.6 | async-start | bytes 786432 | tf_op jit(solution)/shard_map/all_to_all | solution.py:710
  220.9 0.1 convert_reduce_fusion
  221.0 13.7 %all-to-all-done.6.refs_0_ = bf16[4,384,128]{2,1,0:T(8,128)(2,1)S(1)} async-done(((bf16[4,384,128]{2,1,0:T(8,128)(2,1)}), bf16[4,384,128]{2,1,0:T(8,128)(2,1)S(1)}, u32[]{:S(2)}, u32[]{:S(2)}) %all-to-all-start.6) | async-done | bytes 393248 | tf_op jit(solution)/shard_map/all_to_all | solution.py:710
  234.7 8.1 %reduce-scatter.2.cloned.1.call-done = bf16[1,1152,128]{2,1,0:T(8,128)(2,1)} async-done(((bf16[4,1152,128]{2,1,0:T(8,128)(2,1)}), bf16[1,1152,128]{2,1,0:T(8,128)(2,1)}) %reduce-scatter.2.cloned.1.call-update) | async-done | bytes 294928 | tf_op jit(solution)/shard_map/reduce_scatter | solution.py:483
  242.8 1.2 inverse_rows_512.1
  243.9 11.6 %all-to-all-start.7 = ((bf16[32,48,128]{2,1,0:T(8,128)(2,1)}), bf16[32,48,128]{2,1,0:T(8,128)(2,1)S(1)}, u32[]{:S(2)}, u32[]{:S(2)}) async-start(bf16[32,48,128]{2,1,0:T(8,128)(2,1)} %inverse_rows_512.1), calls=%async_computation.8 | async-start | bytes 786432 | tf_op jit(solution)/shard_map/all_to_all | solution.py:710
  255.8 7.6 %collective-permute-start.2 = (bf16[16,128]{1,0:T(8,128)(2,1)S(1)}, bf16[16,128]{1,0:T(8,128)(2,1)S(1)}, u32[]{:S(2)}, u32[]{:S(2)}) collective-permute-start(bf16[16,128]{1,0:T(8,128)(2,1)S(1)} %maximum_maximum_fusion), channel_id=1, source_target_pairs={{0,8},{4,12},{1,9},{5,13},{2,10},{6,14},{3,11},{7,15},{16,24},{20,... | collective-permute-start | bytes 12296 | tf_op jit(solution)/shard_map/ppermute | solution.py:496
  263.5 0.1 broadcast_in_dim.121
  263.6 2.1 collective-permute-start.3
  265.7 19.0 %collective-permute-done.3 = bf16[576,128]{1,0:T(8,128)(2,1)S(1)} collective-permute-done((bf16[576,128]{1,0:T(8,128)(2,1)S(1)}, bf16[576,128]{1,0:T(8,128)(2,1)S(1)}, u32[]{:S(2)}, u32[]{:S(2)}) %collective-permute-start.3) | collective-permute-done | bytes 147488 | tf_op jit(solution)/shard_map/ppermute | solution.py:496
  284.8 0.1 slice_select_fusion.recv_first
  284.9 0.1 slice_select_fusion.1.recv_second
  285.0 2.3 place_grads.1
  287.3 0.2 fusion.3
  287.5 0.3 fusion.7
  287.8 1.1 fusion.6
  (85 shorter events, 0.8 us)
Async XLA Ops:
  9.7 23.9 %copy-start.4 = (bf16[512,512]{1,0:T(8,128)(2,1)S(1)}, bf16[512,512]{1,0:T(8,128)(2,1)}, u32[]{:S(2)}) copy-start(bf16[512,512]{1,0:T(8,128)(2,1)} %constant.38.clone.refs_1_) | copy-start | bytes 1572868
  9.7 23.9 %all-to-all-start = ((bf16[32,72,128]{2,1,0:T(8,128)(2,1)}), bf16[32,72,128]{2,1,0:T(8,128)(2,1)S(1)}, u32[]{:S(2)}, u32[]{:S(2)}) async-start(bf16[32,72,128]{2,1,0:T(8,128)(2,1)} %first_norm.1), calls=%async_computation | async-start | bytes 1179648 | tf_op jit(solution)/shard_map/all_to_all | solution.py:710
  18.9 37.2 %copy-start.17 = (s32[2]{0:T(128)S(1)}, s32[2]{0:T(128)}, u32[]{:S(2)}) copy-start(s32[2]{0:T(128)} %pad_add_fusion.place_ref) | copy-start | bytes 28
  22.7 33.4 %copy-start.1 = (f32[2,3,128,512]{3,2,1,0:T(8,128)S(1)}, f32[2,3,128,512]{3,2,1,0:T(8,128)}, u32[]{:S(2)}) copy-start(f32[2,3,128,512]{3,2,1,0:T(8,128)} %first_ref.3) | copy-start | bytes 4718596
  22.7 33.4 %copy-start.3 = (f32[2,6,64,256]{3,2,1,0:T(8,128)S(1)}, f32[2,6,64,256]{3,2,1,0:T(8,128)}, u32[]{:S(2)}) copy-start(f32[2,6,64,256]{3,2,1,0:T(8,128)} %second_ref.3) | copy-start | bytes 2359300
  22.7 22.9 %collective-permute-start = (bf16[576,128]{1,0:T(8,128)(2,1)}, bf16[576,128]{1,0:T(8,128)(2,1)}, u32[]{:S(2)}, u32[]{:S(2)}) collective-permute-start(bf16[576,128]{1,0:T(8,128)(2,1)} %get-tuple-element.14), channel_id=1, source_target_pairs={{0,12},{12,0},{4,8},{8,4},{1,13},{13,1},{5,9},{9,5},{2,14},{14,2},... | collective-permute-start | bytes 442376 | tf_op jit(solution)/shard_map/ppermute | solution.py:448
  32.2 13.4 %collective-permute-start.1 = (bf16[16,128]{1,0:T(8,128)(2,1)}, bf16[16,128]{1,0:T(8,128)(2,1)S(1)}, u32[]{:S(2)}, u32[]{:S(2)}) collective-permute-start(bf16[16,128]{1,0:T(8,128)(2,1)} %get-tuple-element.15), channel_id=1, source_target_pairs={{8,0},{12,4},{9,1},{13,5},{10,2},{14,6},{11,3},{15,7},{24,16},{28,... | collective-permute-start | bytes 12296 | tf_op jit(solution)/shard_map/ppermute | solution.py:448
  33.6 0.9 copy-start.14
  45.6 41.0 %all-to-all-start.1 = ((bf16[4,576,128]{2,1,0:T(8,128)(2,1)}), bf16[4,576,128]{2,1,0:T(8,128)(2,1)S(1)}, u32[]{:S(2)}, u32[]{:S(2)}) async-start(bf16[4,576,128]{2,1,0:T(8,128)(2,1)} %forward_rows_512_256.2), calls=%async_computation.1 | async-start | bytes 1179648 | tf_op jit(solution)/shard_map/all_to_all | solution.py:710
  58.1 2.0 copy-start.11
  72.1 21.3 %copy-start.9 = (bf16[2304,128]{1,0:T(8,128)(2,1)}, bf16[2304,128]{1,0:T(8,128)(2,1)S(1)}, u32[]{:S(2)}) copy-start(bf16[2304,128]{1,0:T(8,128)(2,1)S(1)} %all-gather) | copy-start | bytes 1769476
  86.6 6.8 %copy-start.7 = (bf16[4,576,128]{2,1,0:T(8,128)(2,1)}, bf16[4,576,128]{2,1,0:T(8,128)(2,1)S(1)}, u32[]{:S(2)}) copy-start(bf16[4,576,128]{2,1,0:T(8,128)(2,1)S(1)} %all-to-all-done.1.x_ref) | copy-start | bytes 1769476
  86.6 1.3 copy-start.12
  87.9 1.2 copy-start.18
  89.1 1.2 copy-start.20
  90.3 31.1 %copy-start.5 = (bf16[512,512]{1,0:T(8,128)(2,1)S(1)}, bf16[512,512]{1,0:T(8,128)(2,1)}, u32[]{:S(2)}) copy-start(bf16[512,512]{1,0:T(8,128)(2,1)} %constant.42.clone.refs_1_) | copy-start | bytes 1572868
  90.3 31.1 %copy-start.16 = (bf16[256,256]{1,0:T(8,128)(2,1)S(1)}, bf16[256,256]{1,0:T(8,128)(2,1)}, u32[]{:S(2)}) copy-start(bf16[256,256]{1,0:T(8,128)(2,1)} %constant.43.clone.refs_2_) | copy-start | bytes 393220
  121.4 12.0 %copy-start.23 = (bf16[192,384]{1,0:T(8,128)(2,1)S(1)}, bf16[192,384]{1,0:T(8,128)(2,1)}, u32[]{:S(2)}) copy-start(bf16[192,384]{1,0:T(8,128)(2,1)} %param.21) | copy-start | bytes 442372
  121.4 12.2 %copy-start.25 = (f32[192]{0:T(256)S(1)}, f32[192]{0:T(256)}, u32[]{:S(2)}) copy-start(f32[192]{0:T(256)} %param.22) | copy-start | bytes 2308
  122.8 25.0 %copy-start = (bf16[1,96,16,128]{3,2,1,0:T(8,128)(2,1)S(1)}, bf16[1,96,16,128]{3,2,1,0:T(8,128)(2,1)}, u32[]{:S(2)}) copy-start(bf16[1,96,16,128]{3,2,1,0:T(8,128)(2,1)} %param.18) | copy-start | bytes 1179652
  122.8 25.0 %copy-start.6 = (bf16[1,192,8,64]{1,3,2,0:T(8,128)(2,1)S(1)}, bf16[1,192,8,64]{1,3,2,0:T(8,128)(2,1)}, u32[]{:S(2)}) copy-start(bf16[1,192,8,64]{1,3,2,0:T(8,128)(2,1)} %param.24) | copy-start | bytes 589828
  122.8 25.0 %all-to-all-start.3 = ((bf16[32,72,128]{2,1,0:T(8,128)(2,1)}), bf16[32,72,128]{2,1,0:T(8,128)(2,1)S(1)}, u32[]{:S(2)}, u32[]{:S(2)}) async-start(bf16[32,72,128]{2,1,0:T(8,128)(2,1)} %inverse_rows_512_256.1), calls=%async_computation.3 | async-start | bytes 1179648 | tf_op jit(solution)/shard_map/all_to_all | solution.py:710
  133.3 109.4 %reduce-scatter.2.cloned.1.call-start = ((), (), s32[]{:S(2)}) async-start(), calls=%async_computation.9 | async-start | bytes 1474560 | tf_op jit(solution)/shard_map/reduce_scatter | solution.py:483
  147.7 26.9 %copy-start.15 = (bf16[256,256]{1,0:T(8,128)(2,1)S(1)}, bf16[256,256]{1,0:T(8,128)(2,1)}, u32[]{:S(2)}) copy-start(bf16[256,256]{1,0:T(8,128)(2,1)} %constant.39.clone.refs_2_) | copy-start | bytes 393220
  152.7 111.0 %copy-start.2 = (bf16[32,72,128]{2,1,0:T(8,128)(2,1)}, bf16[32,72,128]{2,1,0:T(8,128)(2,1)S(1)}, u32[]{:S(2)}) copy-start(bf16[32,72,128]{2,1,0:T(8,128)(2,1)S(1)} %token_step.1) | copy-start | bytes 1769476
  152.7 56.4 %copy-start.21 = (bf16[2,512,512]{2,1,0:T(8,128)(2,1)S(1)}, bf16[2,512,512]{2,1,0:T(8,128)(2,1)}, u32[]{:S(2)}) copy-start(bf16[2,512,512]{2,1,0:T(8,128)(2,1)} %constant.41.clone.second_tables) | copy-start | bytes 3145732
  174.6 34.5 %copy-start.8 = (bf16[4,576,128]{2,1,0:T(8,128)(2,1)S(1)}, bf16[4,576,128]{2,1,0:T(8,128)(2,1)}, u32[]{:S(2)}) copy-start(bf16[4,576,128]{2,1,0:T(8,128)(2,1)} %copy-done.7) | copy-start | bytes 1769476
  174.6 34.5 %copy-start.10 = (bf16[2304,128]{1,0:T(8,128)(2,1)S(1)}, bf16[2304,128]{1,0:T(8,128)(2,1)}, u32[]{:S(2)}) copy-start(bf16[2304,128]{1,0:T(8,128)(2,1)} %copy-done.9) | copy-start | bytes 1769476
  174.6 34.5 %copy-start.13 = (bf16[4,576,128]{2,1,0:T(8,128)(2,1)S(1)}, bf16[4,576,128]{2,1,0:T(8,128)(2,1)}, u32[]{:S(2)}) copy-start(bf16[4,576,128]{2,1,0:T(8,128)(2,1)} %copy-done.11) | copy-start | bytes 1769476
  174.6 34.5 %copy-start.19 = (bf16[2,512,512]{2,1,0:T(8,128)(2,1)S(1)}, bf16[2,512,512]{2,1,0:T(8,128)(2,1)}, u32[]{:S(2)}) copy-start(bf16[2,512,512]{2,1,0:T(8,128)(2,1)} %constant.40.clone.first_tables) | copy-start | bytes 3145732
  214.5 20.2 %all-to-all-start.6 = ((bf16[4,384,128]{2,1,0:T(8,128)(2,1)}), bf16[4,384,128]{2,1,0:T(8,128)(2,1)S(1)}, u32[]{:S(2)}, u32[]{:S(2)}) async-start(bf16[4,384,128]{2,1,0:T(8,128)(2,1)} %get-tuple-element.19), calls=%async_computation.6 | async-start | bytes 786432 | tf_op jit(solution)/shard_map/all_to_all | solution.py:710
  242.8 12.9 %copy-start.22 = (bf16[1,1152,128]{2,1,0:T(8,128)(2,1)S(1)}, bf16[1,1152,128]{2,1,0:T(8,128)(2,1)}, u32[]{:S(2)}) copy-start(bf16[1,1152,128]{2,1,0:T(8,128)(2,1)} %reduce-scatter.2.cloned.1.call-done) | copy-start | bytes 884740
  243.9 43.3 %copy-start.24 = (f32[96]{0:T(128)S(1)}, f32[96]{0:T(128)}, u32[]{:S(2)}) copy-start(f32[96]{0:T(128)} %gain_ref.1) | copy-start | bytes 1156
  243.9 43.3 %all-to-all-start.7 = ((bf16[32,48,128]{2,1,0:T(8,128)(2,1)}), bf16[32,48,128]{2,1,0:T(8,128)(2,1)S(1)}, u32[]{:S(2)}, u32[]{:S(2)}) async-start(bf16[32,48,128]{2,1,0:T(8,128)(2,1)} %inverse_rows_512.1), calls=%async_computation.8 | async-start | bytes 786432 | tf_op jit(solution)/shard_map/all_to_all | solution.py:710
  255.8 9.9 %collective-permute-start.2 = (bf16[16,128]{1,0:T(8,128)(2,1)S(1)}, bf16[16,128]{1,0:T(8,128)(2,1)S(1)}, u32[]{:S(2)}, u32[]{:S(2)}) collective-permute-start(bf16[16,128]{1,0:T(8,128)(2,1)S(1)} %maximum_maximum_fusion), channel_id=1, source_target_pairs={{0,8},{4,12},{1,9},{5,13},{2,10},{6,14},{3,11},{7,15},{16,24},{20,... | collective-permute-start | bytes 12296 | tf_op jit(solution)/shard_map/ppermute | solution.py:496
  263.6 24.2 %slice-start = ((bf16[32,72,128]{2,1,0:T(8,128)(2,1)}), bf16[32,48,128]{2,1,0:T(8,128)(2,1)S(1)}, s32[]{:S(2)}) async-start(bf16[32,72,128]{2,1,0:T(8,128)(2,1)} %copy-done.2), calls=%async_computation.10 | async-start | bytes 786432 | tf_op jit(solution)/shard_map/slice | solution.py:740
  263.6 21.1 %collective-permute-start.3 = (bf16[576,128]{1,0:T(8,128)(2,1)S(1)}, bf16[576,128]{1,0:T(8,128)(2,1)S(1)}, u32[]{:S(2)}, u32[]{:S(2)}) collective-permute-start(bf16[576,128]{1,0:T(8,128)(2,1)S(1)} %slice.64), channel_id=1, source_target_pairs={{0,12},{12,0},{4,8},{8,4},{1,13},{13,1},{5,9},{9,5},{2,14},{14,2},... | collective-permute-start | bytes 442376 | tf_op jit(solution)/shard_map/ppermute | solution.py:496
Sparse Core Ops, SparseCore 0:
  214.6 28.0 reduce-scatter.1

commit v7 on v6

--- a/solution.py
+++ b/solution.py
@@ -17,6 +17,7 @@
 LANES = 128
 SECOND_SLOT = 2 * GROUPS * H1 // 8
 FILTER_ROWS = 2 * GROUPS * (H1 + H2) // 8
+EDGE_ROWS = 16
 
 epsilon = 1e-06
 
@@ -42,6 +43,14 @@
             imag[0] = cos[n // 2]
         parts += [real, imag]
     return np.concatenate(parts, axis=0)
+
+
+def edge_table(n):
+    cos, sin = cos_sin(n)
+    table = np.zeros((EDGE_ROWS, n))
+    table[4] = cos[n // 2]
+    table[6], table[7] = cos[n // 4], -sin[n // 4]
+    return table
 
 
 def col_tables(n):
@@ -87,16 +96,28 @@
 
 def forward_rows_kernel(layout, *refs):
     x_ref, tables, out_ref = refs[0], refs[1:-1], refs[-1]
-    for (n, first_in, first_out), table in zip(layout, tables):
+    edges = []
+    for i, (n, first_in, first_out) in enumerate(layout):
         rows = n // ROWS
         slots = n // 8
         block = x_ref[:, first_in : first_in + GROUPS * rows, :]
-        half = dot(table[...], gather_rows(block, rows)).astype(jnp.bfloat16)
+        gathered = gather_rows(block, rows)
+        half = dot(tables[2 * i][...], gathered).astype(jnp.bfloat16)
+        edges.append(dot(tables[2 * i + 1][...], gathered))
         half = half.reshape(COLS, 2, slots, GROUPS * LANES)
         for part in range(2):
             for g in range(GROUPS):
                 at = first_out + (part * GROUPS + g) * slots
                 out_ref[:, at : at + slots, :] = half[:, part, :, g * LANES : (g + 1) * LANES]
+    for c in range(COLS):
+        pieces = [
+            edge[2 * c + part : 2 * c + part + 1, g * LANES : (g + 1) * LANES]
+            for edge in edges
+            for part in range(2)
+            for g in range(GROUPS)
+        ]
+        pieces.append(jnp.zeros((EDGE_ROWS - len(pieces), LANES), jnp.float32))
+        out_ref[c, FILTER_ROWS:, :] = jnp.concatenate(pieces, axis=0).astype(jnp.bfloat16)
 
 
 def forward_rows(entries, sizes):
@@ -104,10 +125,10 @@
     flops = sum(2 * n * n * GROUPS * LANES for n in sizes)
     return pl.pallas_call(
         functools.partial(forward_rows_kernel, layout),
-        out_shape=jax.ShapeDtypeStruct((COLS, slots, LANES), jnp.bfloat16),
+        out_shape=jax.ShapeDtypeStruct((COLS, slots + EDGE_ROWS, LANES), jnp.bfloat16),
         name="forward_rows_" + "_".join(str(n) for n in sizes),
         **params(flops, 2 << 20),
-    )(entries, *[constant(row_table(n)) for n in sizes])
+    )(entries, *[constant(table(n)) for n in sizes for table in (row_table, edge_table)])
 
 
 def inverse_rows_kernel(layout, *refs):
@@ -248,6 +269,18 @@
             out_ref[q, FILTER_ROWS + at : FILTER_ROWS + at + count, :] = sent[:, lanes]
 
 
+def edge_spectrum(ref, first, tables):
+    edges = wide(ref, FILTER_ROWS, EDGE_ROWS)
+    with_cos, with_sin = dot(edges, tables[0]), dot(edges, tables[1])
+    real, imag = slice(first, first + GROUPS), slice(first + GROUPS, first + 2 * GROUPS)
+    return with_cos[real] - with_sin[imag], -with_cos[imag] - with_sin[real]
+
+
+def edge_terms(field, grad):
+    (s_r, s_i), (g_r, g_i) = field, grad
+    return [g_r * s_r + g_i * s_i, g_i * s_r - g_r * s_i]
+
+
 def mix_last_kernel(
     place_ref, x_ref, y_ref, kept_ref, recv_ref, first_tables, second_tables,
     out_ref, total_ref, terms_ref, sem,
@@ -258,12 +291,21 @@
     grad = spectrum(x_ref, SECOND_SLOT, slots, special, *tables)
     field = spectrum(y_ref, SECOND_SLOT, slots, special, *tables)
     put_terms(terms_ref, SECOND_SLOT, slots, near, field, grad)
+    at = 2 * GROUPS
+    second_edges = edge_terms(
+        edge_spectrum(y_ref, at, tables), edge_spectrum(x_ref, at, tables)
+    )
     slots = H1 // 8
     special, near = masks(place_ref, slots)
     tables = first_tables[0], first_tables[1]
     field = spectrum(x_ref, 0, slots, special, *tables)
     grad = spectrum(y_ref, 0, slots, special, *tables)
     put_terms(terms_ref, 0, slots, near, field, grad)
+    edges = edge_terms(edge_spectrum(x_ref, 0, tables), edge_spectrum(y_ref, 0, tables))
+    filled = jnp.zeros((EDGE_ROWS - 4 * GROUPS, 512), jnp.float32)
+    edges = jnp.concatenate(edges + second_edges + [filled], axis=0).astype(jnp.bfloat16)
+    for q in range(COLS):
+        terms_ref[q, 2 * FILTER_ROWS :, :] = edges[:, q * LANES : (q + 1) * LANES]
     copy = pltpu.make_async_copy(terms_ref, total_ref, sem)
     copy.start()
     real, imag = filters(near, kept_ref, recv_ref, 0, slots)
@@ -299,7 +341,7 @@
 
 
 def mix_last(place, entries, later, kept, recv):
-    total = (COLS, 2 * FILTER_ROWS, LANES)
+    total = (COLS, 2 * FILTER_ROWS + EDGE_ROWS, LANES)
     return pl.pallas_call(
         mix_last_kernel,
         out_shape=(
@@ -483,21 +525,8 @@
     return lax.psum_scatter(terms, "rep", scatter_dimension=0, tiled=False)
 
 
-def swap_grads(sent):
-    groups = 2 * GROUPS
-    zero = jnp.concatenate(
-        [
-            sent[:SECOND_SLOT].reshape(groups, H1 // 8, LANES)[:, 0],
-            sent[SECOND_SLOT:].reshape(groups, H2 // 8, LANES)[:, 0],
-            jnp.zeros((4, LANES), jnp.bfloat16),
-        ],
-        axis=0,
-    )
-    return lax.ppermute(sent, "col", SWAP), lax.ppermute(zero, "col", ((0, 2), (1, 3)))
-
-
-def place_grads(place, kept, swapped, col):
-    recv_first, recv_second = put_slots_zero(*swapped, col >= 2)
+def place_grads(place, kept, recv, edges, col):
+    recv_first, recv_second = put_slots_zero(recv, edges, col >= 2)
     return pl.pallas_call(
         place_grads_kernel,
         out_shape=(
@@ -734,13 +763,16 @@
     terms = summed(terms)
     rot_one = exchange(dspec_one, "col")
     rot_one, terms = lax.optimization_barrier((rot_one, terms))
-    swapped = swap_grads(terms[FILTER_ROWS:])
+    swapped = lax.ppermute(terms[FILTER_ROWS : 2 * FILTER_ROWS], "col", SWAP)
     grad_norm_one = unpack_first(exchange(inverse_rows(rot_one, (H1,)), "row"))
     grad_images = (
         unpack_first(tokens[:, : GROUPS * 16]).astype(jnp.float32)
         + norm_pullback_step(images.astype(jnp.float32), gain_first, grad_norm_one)
     ).astype(jnp.bfloat16)
-    grad_first, grad_second = place_grads(place, terms[:FILTER_ROWS], swapped, col)
+    grad_images, swapped = lax.optimization_barrier((grad_images, swapped))
+    grad_first, grad_second = place_grads(
+        place, terms[:FILTER_ROWS], swapped, terms[2 * FILTER_ROWS :], col
+    )
     return (grad_images, grad_first, grad_second)
 
 

time: 297 us -> 292 us (0.983)
  blocking collectives: 95.8 us -> 122 us
  waiting for transfers between devices: 78.8 us -> 59.1 us
  starting transfers between devices: 68 us -> 53.2 us
  local copies, waits for them, and re-layouts: 5.78 us -> 11.1 us
    all_to_all x3 -> x4, blocking collectives: 83.8 us -> 110 us  [exchange(): return lax.all_to_all(blocks, axis, split_axis=0, concat_axis=0, tiled=True)]
    ppermute x2 -> x1, waiting for transfers between devices: 19 us -> 9.2 us  [shards(): swapped = lax.ppermute(terms[FILTER_ROWS:2 * FILTER_ROWS], 'col', SWAP)]
    all_to_all x5 -> x4, starting transfers between devices: 47.4 us -> 39.6 us  [exchange(): return lax.all_to_all(blocks, axis, split_axis=0, concat_axis=0, tiled=True)]
    all_to_all x5 -> x4, waiting for transfers between devices: 41.9 us -> 34.2 us  [exchange(): return lax.all_to_all(blocks, axis, split_axis=0, concat_axis=0, tiled=True)]
    ppermute x2 -> x1, starting transfers between devices: 9.66 us -> 2.77 us  [shards(): swapped = lax.ppermute(terms[FILTER_ROWS:2 * FILTER_ROWS], 'col', SWAP)]
    unnamed x52 -> x68, local copies, waits for them, and re-layouts: 4.72 us -> 8.46 us
  transfers between devices with their start and end apart: 10 -> 8, of which waited for: 6 -> 6; matrix products, arithmetic and copies ran while one was open for 1% -> 2% of each run, Pallas kernels for 3% -> 2%
where the time goes in v7:
time: 292 us; the launch traced here: 291 us
  blocking collectives  122 us (42%)
  waiting for transfers between devices  59.1 us (20%)
  starting transfers between devices  53.2 us (18%)
  Pallas kernels  27.1 us (9%)
  between operations  14.5 us (5%)
  local copies, waits for them, and re-layouts  11.1 us (4%)
  other arithmetic  4.51 us (2%)
    all_to_all x4, blocking collectives, exchange(): return lax.all_to_all(blocks, axis, split_axis=0, concat_axis=0, tiled=True)  110 us
    all_to_all x4, starting transfers between devices, exchange(): return lax.all_to_all(blocks, axis, split_axis=0, concat_axis=0, tiled=True)  39.6 us
    all_to_all x4, waiting for transfers between devices, exchange(): return lax.all_to_all(blocks, axis, split_axis=0, concat_axis=0, tiled=True)  34.2 us
    all_gather x1, blocking collectives, patch_filters(): return lax.all_gather(recv, 'rep', axis=0, tiled=False)  12 us
    ppermute x1, waiting for transfers between devices, swap_filters(): lax.ppermute(zero, 'col', ((2, 0), (3, 1)))  9.71 us
    ppermute x1, starting transfers between devices, swap_filters(): lax.ppermute(sent, 'col', SWAP)  9.54 us
    ppermute x1, waiting for transfers between devices, shards(): swapped = lax.ppermute(terms[FILTER_ROWS:2 * FILTER_ROWS], 'col', SWAP)  9.2 us
    unnamed x68, local copies, waits for them, and re-layouts  8.46 us
  transfers between devices with their start and end apart: 8, of which 6 were waited for; matrix products, arithmetic and copies ran while one was open for 2% of the time, Pallas kernels for 2%

profile of v7, /device:TPU:105, one launch (start us, length us, event | category | flops | bytes accessed | tf_op | source)
XLA Modules:
  0.0 291.4 jit_solution(14162502129426348584)
XLA Ops:
  7.2 2.5 first_norm.1
  9.7 8.6 %all-to-all-start = ((bf16[32,72,128]{2,1,0:T(8,128)(2,1)}), bf16[32,72,128]{2,1,0:T(8,128)(2,1)S(1)}, u32[]{:S(2)}, u32[]{:S(2)}) async-start(bf16[32,72,128]{2,1,0:T(8,128)(2,1)} %first_norm.1), calls=%async_computation | async-start | bytes 1179648 | tf_op jit(solution)/shard_map/all_to_all | solution.py:739
  18.3 0.7 pad_add_fusion.place_ref
  19.0 3.6 %send_filters.1 = (bf16[576,128]{1,0:T(8,128)(2,1)}, bf16[16,128]{1,0:T(8,128)(2,1)}) custom-call(s32[2]{0:T(128)} %pad_add_fusion.place_ref, f32[2,3,128,512]{3,2,1,0:T(8,128)} %first_ref.3, f32[2,6,64,256]{3,2,1,0:T(8,128)} %second_ref.3), custom_call_target="tpu_custom_call" | custom-call | flops 100663296 | bytes 2097152 | tf_op jit(solution)/shard_map/send_filters/pallas_call | solution.py:448
  22.7 9.5 %collective-permute-start = (bf16[576,128]{1,0:T(8,128)(2,1)}, bf16[576,128]{1,0:T(8,128)(2,1)}, u32[]{:S(2)}, u32[]{:S(2)}) collective-permute-start(bf16[576,128]{1,0:T(8,128)(2,1)} %get-tuple-element.16), channel_id=1, source_target_pairs={{0,12},{12,0},{4,8},{8,4},{1,13},{13,1},{5,9},{9,5},{2,14},{14,2},... | collective-permute-start | bytes 442376 | tf_op jit(solution)/shard_map/ppermute | solution.py:490
  32.2 1.3 collective-permute-start.1
  33.6 0.9 copy-done.15
  34.5 1.4 forward_rows_512_256.2
  35.9 9.7 %collective-permute-done.1 = bf16[16,128]{1,0:T(8,128)(2,1)S(1)} collective-permute-done((bf16[16,128]{1,0:T(8,128)(2,1)}, bf16[16,128]{1,0:T(8,128)(2,1)S(1)}, u32[]{:S(2)}, u32[]{:S(2)}) %collective-permute-start.1) | collective-permute-done | bytes 4128 | tf_op jit(solution)/shard_map/ppermute | solution.py:490
  45.6 10.2 %all-to-all-start.1 = ((bf16[4,592,128]{2,1,0:T(8,128)(2,1)}), bf16[4,592,128]{2,1,0:T(8,128)(2,1)S(1)}, u32[]{:S(2)}, u32[]{:S(2)}) async-start(bf16[4,592,128]{2,1,0:T(8,128)(2,1)} %forward_rows_512_256.2), calls=%async_computation.1 | async-start | bytes 1212416 | tf_op jit(solution)/shard_map/all_to_all | solution.py:739
  55.9 0.6 broadcast_in_dim.104
  56.5 0.6 broadcast_in_dim.99
  57.1 0.7 copy-done.23
  57.8 2.0 keep_filters.1.kept_ref
  59.8 0.9 bitcast_select_fusion.3
  60.7 1.0 bitcast_select_fusion.1
  61.7 12.0 %all-gather = bf16[2304,128]{1,0:T(8,128)(2,1)S(1)} all-gather(bf16[576,128]{1,0:T(8,128)(2,1)S(1)} %pad_maximum_fusion), channel_id=2, replica_groups=mesh['row'=32,'col'=4,'rep'=4] {'rep'}, dimensions={0}, use_global_device_ids=true | all-gather | bytes 737280 | tf_op jit(solution)/shard_map/all_gather | solution.py:495
  73.7 13.7 %all-to-all-done.1.x_ref = bf16[4,592,128]{2,1,0:T(8,128)(2,1)S(1)} async-done(((bf16[4,592,128]{2,1,0:T(8,128)(2,1)}), bf16[4,592,128]{2,1,0:T(8,128)(2,1)S(1)}, u32[]{:S(2)}, u32[]{:S(2)}) %all-to-all-start.1) | async-done | bytes 606240 | tf_op jit(solution)/shard_map/all_to_all | solution.py:739
  87.4 1.2 copy-done.9
  88.7 1.2 copy-done.11
  89.9 0.7 copy-done.24
  90.5 2.9 mix_first.1
  93.4 28.4 %all_to_all.40.refs_0_ = bf16[4,576,128]{2,1,0:T(8,128)(2,1)S(1)} all-to-all(bf16[4,576,128]{2,1,0:T(8,128)(2,1)S(1)} %mix_first.1), channel_id=1, replica_groups=mesh['row'=32,'col'=4,'rep'=4] {'col'}, dimensions={0} | all-to-all | bytes 1179648 | tf_op jit(solution)/shard_map/all_to_all | solution.py:739
  121.9 1.3 inverse_rows_512_256.1
  123.2 7.7 %all-to-all-start.3 = ((bf16[32,72,128]{2,1,0:T(8,128)(2,1)}), bf16[32,72,128]{2,1,0:T(8,128)(2,1)S(1)}, u32[]{:S(2)}, u32[]{:S(2)}) async-start(bf16[32,72,128]{2,1,0:T(8,128)(2,1)} %inverse_rows_512_256.1), calls=%async_computation.3 | async-start | bytes 1179648 | tf_op jit(solution)/shard_map/all_to_all | solution.py:739
  131.1 0.8 copy.31
  132.0 0.1 reshape.164
  132.3 13.0 %all-to-all-done.3.m_ref = bf16[32,72,128]{2,1,0:T(8,128)(2,1)S(1)} async-done(((bf16[32,72,128]{2,1,0:T(8,128)(2,1)}), bf16[32,72,128]{2,1,0:T(8,128)(2,1)S(1)}, u32[]{:S(2)}, u32[]{:S(2)}) %all-to-all-start.3) | async-done | bytes 589856 | tf_op jit(solution)/shard_map/all_to_all | solution.py:739
  145.3 0.9 copy-done.13
  146.2 0.9 copy-done.14
  147.2 4.9 %token_step.1 = bf16[32,72,128]{2,1,0:T(8,128)(2,1)S(1)} custom-call(bf16[96,16,128]{2,1,0:T(8,128)(2,1)S(1)} %bitcast.25, bf16[32,72,128]{2,1,0:T(8,128)(2,1)S(1)} %all-to-all-done.3.m_ref, bf16[8,64,192]{2,1,0:T(8,128)(2,1)S(1)} %bitcast.32, bf16[192,384]{1,0:T(8,128)(2,1)S(1)} %bitcast.30, bf16[384,192]{1,0:T(8,128)(2,1)S(1)} %bitcast.33, ...), custom_call_target="tpu_custom_call" | custom-call | flops 301989888 | bytes 4194304 | tf_op jit(solution)/shard_map/token_step/pallas_call | solution.py:709
  152.1 21.7 %all_to_all.41.refs_0_ = bf16[32,72,128]{2,1,0:T(8,128)(2,1)S(1)} all-to-all(bf16[32,72,128]{2,1,0:T(8,128)(2,1)S(1)} %token_step.1), channel_id=1, replica_groups=mesh['row'=32,'col'=4,'rep'=4] {'row'}, dimensions={0} | all-to-all | bytes 1179648 | tf_op jit(solution)/shard_map/all_to_all | solution.py:739
  173.9 0.6 forward_rows_512_256.3
  174.5 37.4 %all_to_all.42.y_ref = bf16[4,592,128]{2,1,0:T(8,128)(2,1)S(1)} all-to-all(bf16[4,592,128]{2,1,0:T(8,128)(2,1)S(1)} %forward_rows_512_256.3), channel_id=1, replica_groups=mesh['row'=32,'col'=4,'rep'=4] {'col'}, dimensions={0} | all-to-all | bytes 1212416 | tf_op jit(solution)/shard_map/all_to_all | solution.py:739
  212.0 4.4 %mix_last.1 = (bf16[4,384,128]{2,1,0:T(8,128)(2,1)S(1)}, bf16[4,1168,128]{2,1,0:T(8,128)(2,1)S(1)}) custom-call(s32[2]{0:T(128)S(1)} %copy-done.25, bf16[4,592,128]{2,1,0:T(8,128)(2,1)S(1)} %all-to-all-done.1.x_ref, bf16[4,592,128]{2,1,0:T(8,128)(2,1)S(1)} %all_to_all.42.y_ref, bf16[4,576,128]{2,1,0:T(8,128)(2,1)S(1)} %keep_filters.1.kept_ref, ...), custom_call_target="tpu_custom_call" | custom-call | flops 1811939328 | bytes 8388608 | tf_op jit(solution)/shard_map/mix_last/pallas_call | solution.py:345
  216.4 1.0 copy-done.8
  217.4 0.7 copy-done.17
  218.2 22.2 %all_to_all.43.refs_0_ = bf16[4,384,128]{2,1,0:T(8,128)(2,1)S(1)} all-to-all(bf16[4,384,128]{2,1,0:T(8,128)(2,1)} %copy-done.17), channel_id=1, replica_groups=mesh['row'=32,'col'=4,'rep'=4] {'col'}, dimensions={0} | all-to-all | bytes 786432 | tf_op jit(solution)/shard_map/all_to_all | solution.py:739
  240.4 6.0 %reduce-scatter.2.cloned.1.call-done = bf16[1,1168,128]{2,1,0:T(8,128)(2,1)} async-done(((bf16[4,1168,128]{2,1,0:T(8,128)(2,1)}), bf16[1,1168,128]{2,1,0:T(8,128)(2,1)}) %reduce-scatter.2.cloned.1.call-update) | async-done | bytes 299024 | tf_op jit(solution)/shard_map/reduce_scatter | solution.py:525
  246.3 1.2 inverse_rows_512.1
  247.5 13.0 %all-to-all-start.7 = ((bf16[32,48,128]{2,1,0:T(8,128)(2,1)}), bf16[32,48,128]{2,1,0:T(8,128)(2,1)S(1)}, u32[]{:S(2)}, u32[]{:S(2)}) async-start(bf16[32,48,128]{2,1,0:T(8,128)(2,1)} %inverse_rows_512.1), calls=%async_computation.8 | async-start | bytes 786432 | tf_op jit(solution)/shard_map/all_to_all | solution.py:739
  260.9 2.8 collective-permute-start.2
  263.7 7.5 %all-to-all-done.7 = bf16[32,48,128]{2,1,0:T(8,128)(2,1)S(1)} async-done(((bf16[32,48,128]{2,1,0:T(8,128)(2,1)}), bf16[32,48,128]{2,1,0:T(8,128)(2,1)S(1)}, u32[]{:S(2)}, u32[]{:S(2)}) %all-to-all-start.7) | async-done | bytes 393248 | tf_op jit(solution)/shard_map/all_to_all | solution.py:739
  271.2 0.2 fusion.3
  271.4 0.3 fusion.7
  271.7 1.1 fusion.6
  272.8 9.2 %collective-permute-done.2 = bf16[576,128]{1,0:T(8,128)(2,1)S(1)} collective-permute-done((bf16[576,128]{1,0:T(8,128)(2,1)S(1)}, bf16[576,128]{1,0:T(8,128)(2,1)S(1)}, u32[]{:S(2)}, u32[]{:S(2)}) %collective-permute-start.2) | collective-permute-done | bytes 147488 | tf_op jit(solution)/shard_map/ppermute | solution.py:766
  282.3 2.3 place_grads.1
  (92 shorter events, 1.1 us)
Async XLA Ops:
  9.7 23.9 %copy-start.4 = (bf16[512,512]{1,0:T(8,128)(2,1)S(1)}, bf16[512,512]{1,0:T(8,128)(2,1)}, u32[]{:S(2)}) copy-start(bf16[512,512]{1,0:T(8,128)(2,1)} %constant.40.clone.refs_1_) | copy-start | bytes 1572868
  9.7 23.9 %copy-start.19 = (bf16[16,512]{1,0:T(8,128)(2,1)S(1)}, bf16[16,512]{1,0:T(8,128)(2,1)}, u32[]{:S(2)}) copy-start(bf16[16,512]{1,0:T(8,128)(2,1)} %constant.41.clone.refs_2_) | copy-start | bytes 49156
  9.7 23.9 %copy-start.21 = (bf16[16,256]{1,0:T(8,128)(2,1)S(1)}, bf16[16,256]{1,0:T(8,128)(2,1)}, u32[]{:S(2)}) copy-start(bf16[16,256]{1,0:T(8,128)(2,1)} %constant.43.clone.refs_4_) | copy-start | bytes 24580
  9.7 23.8 %all-to-all-start = ((bf16[32,72,128]{2,1,0:T(8,128)(2,1)}), bf16[32,72,128]{2,1,0:T(8,128)(2,1)S(1)}, u32[]{:S(2)}, u32[]{:S(2)}) async-start(bf16[32,72,128]{2,1,0:T(8,128)(2,1)} %first_norm.1), calls=%async_computation | async-start | bytes 1179648 | tf_op jit(solution)/shard_map/all_to_all | solution.py:739
  22.6 34.5 %copy-start.1 = (f32[2,3,128,512]{3,2,1,0:T(8,128)S(1)}, f32[2,3,128,512]{3,2,1,0:T(8,128)}, u32[]{:S(2)}) copy-start(f32[2,3,128,512]{3,2,1,0:T(8,128)} %first_ref.3) | copy-start | bytes 4718596
  22.7 34.4 %copy-start.3 = (f32[2,6,64,256]{3,2,1,0:T(8,128)S(1)}, f32[2,6,64,256]{3,2,1,0:T(8,128)}, u32[]{:S(2)}) copy-start(f32[2,6,64,256]{3,2,1,0:T(8,128)} %second_ref.3) | copy-start | bytes 2359300
  22.7 22.9 %collective-permute-start = (bf16[576,128]{1,0:T(8,128)(2,1)}, bf16[576,128]{1,0:T(8,128)(2,1)}, u32[]{:S(2)}, u32[]{:S(2)}) collective-permute-start(bf16[576,128]{1,0:T(8,128)(2,1)} %get-tuple-element.16), channel_id=1, source_target_pairs={{0,12},{12,0},{4,8},{8,4},{1,13},{13,1},{5,9},{9,5},{2,14},{14,2},... | collective-permute-start | bytes 442376 | tf_op jit(solution)/shard_map/ppermute | solution.py:490
  32.2 13.4 %collective-permute-start.1 = (bf16[16,128]{1,0:T(8,128)(2,1)}, bf16[16,128]{1,0:T(8,128)(2,1)S(1)}, u32[]{:S(2)}, u32[]{:S(2)}) collective-permute-start(bf16[16,128]{1,0:T(8,128)(2,1)} %get-tuple-element.17), channel_id=1, source_target_pairs={{8,0},{12,4},{9,1},{13,5},{10,2},{14,6},{11,3},{15,7},{24,16},{28,... | collective-permute-start | bytes 12296 | tf_op jit(solution)/shard_map/ppermute | solution.py:490
  33.6 0.9 copy-start.15
  45.6 10.9 %copy-start.29 = (bf16[16,128]{1,0:T(8,128)(2,1)}, bf16[16,128]{1,0:T(8,128)(2,1)S(1)}, u32[]{:S(2)}) copy-start(bf16[16,128]{1,0:T(8,128)(2,1)S(1)} %collective-permute-done.1) | copy-start | bytes 12292
  45.6 41.8 %all-to-all-start.1 = ((bf16[4,592,128]{2,1,0:T(8,128)(2,1)}), bf16[4,592,128]{2,1,0:T(8,128)(2,1)S(1)}, u32[]{:S(2)}, u32[]{:S(2)}) async-start(bf16[4,592,128]{2,1,0:T(8,128)(2,1)} %forward_rows_512_256.2), calls=%async_computation.1 | async-start | bytes 1212416 | tf_op jit(solution)/shard_map/all_to_all | solution.py:739
  57.1 0.7 copy-start.23
  57.8 2.0 copy-start.30
  57.8 2.0 copy-start.32
  57.8 2.9 %copy-start.33 = (pred[384]{0:T(512)(128)(4,1)S(1)}, pred[384]{0:T(512)(128)(4,1)}, u32[]{:S(2)}) copy-start(pred[384]{0:T(512)(128)(4,1)} %broadcast_in_dim.99) | copy-start | bytes 1156
  87.4 1.2 copy-start.9
  88.7 1.2 copy-start.11
  89.9 0.7 copy-start.24
  90.5 31.3 %copy-start.6 = (bf16[512,512]{1,0:T(8,128)(2,1)S(1)}, bf16[512,512]{1,0:T(8,128)(2,1)}, u32[]{:S(2)}) copy-start(bf16[512,512]{1,0:T(8,128)(2,1)} %constant.46.clone.refs_1_) | copy-start | bytes 1572868
  90.5 31.3 %copy-start.18 = (bf16[256,256]{1,0:T(8,128)(2,1)S(1)}, bf16[256,256]{1,0:T(8,128)(2,1)}, u32[]{:S(2)}) copy-start(bf16[256,256]{1,0:T(8,128)(2,1)} %constant.47.clone.refs_2_) | copy-start | bytes 393220
  121.9 9.2 %copy-start.27 = (bf16[192,384]{1,0:T(8,128)(2,1)S(1)}, bf16[192,384]{1,0:T(8,128)(2,1)}, u32[]{:S(2)}) copy-start(bf16[192,384]{1,0:T(8,128)(2,1)} %param.25) | copy-start | bytes 442372
  121.9 10.1 %copy-start.31 = (f32[192]{0:T(256)S(1)}, f32[192]{0:T(256)}, u32[]{:S(2)}) copy-start(f32[192]{0:T(256)} %param.26) | copy-start | bytes 2308
  123.2 22.1 %copy-start = (bf16[1,96,16,128]{3,2,1,0:T(8,128)(2,1)S(1)}, bf16[1,96,16,128]{3,2,1,0:T(8,128)(2,1)}, u32[]{:S(2)}) copy-start(bf16[1,96,16,128]{3,2,1,0:T(8,128)(2,1)} %param.22) | copy-start | bytes 1179652
  123.2 22.0 %all-to-all-start.3 = ((bf16[32,72,128]{2,1,0:T(8,128)(2,1)}), bf16[32,72,128]{2,1,0:T(8,128)(2,1)S(1)}, u32[]{:S(2)}, u32[]{:S(2)}) async-start(bf16[32,72,128]{2,1,0:T(8,128)(2,1)} %inverse_rows_512_256.1), calls=%async_computation.3 | async-start | bytes 1179648 | tf_op jit(solution)/shard_map/all_to_all | solution.py:739
  131.0 115.4 %reduce-scatter.2.cloned.1.call-start = ((), (), s32[]{:S(2)}) async-start(), calls=%async_computation.9 | async-start | bytes 1495040 | tf_op jit(solution)/shard_map/reduce_scatter | solution.py:525
  145.3 1.0 copy-start.13
  146.2 0.9 copy-start.14
  147.2 26.7 %copy-start.5 = (bf16[512,512]{1,0:T(8,128)(2,1)S(1)}, bf16[512,512]{1,0:T(8,128)(2,1)}, u32[]{:S(2)}) copy-start(bf16[512,512]{1,0:T(8,128)(2,1)} %constant.40.clone.refs_1_) | copy-start | bytes 1572868
  147.2 26.7 %copy-start.16 = (bf16[256,256]{1,0:T(8,128)(2,1)S(1)}, bf16[256,256]{1,0:T(8,128)(2,1)}, u32[]{:S(2)}) copy-start(bf16[256,256]{1,0:T(8,128)(2,1)} %constant.42.clone.refs_3_) | copy-start | bytes 393220
  147.2 26.7 %copy-start.20 = (bf16[16,512]{1,0:T(8,128)(2,1)S(1)}, bf16[16,512]{1,0:T(8,128)(2,1)}, u32[]{:S(2)}) copy-start(bf16[16,512]{1,0:T(8,128)(2,1)} %constant.41.clone.refs_2_) | copy-start | bytes 49156
  147.2 26.7 %copy-start.22 = (bf16[16,256]{1,0:T(8,128)(2,1)S(1)}, bf16[16,256]{1,0:T(8,128)(2,1)}, u32[]{:S(2)}) copy-start(bf16[16,256]{1,0:T(8,128)(2,1)} %constant.43.clone.refs_4_) | copy-start | bytes 24580
  152.1 108.7 %copy-start.2 = (bf16[32,72,128]{2,1,0:T(8,128)(2,1)}, bf16[32,72,128]{2,1,0:T(8,128)(2,1)S(1)}, u32[]{:S(2)}) copy-start(bf16[32,72,128]{2,1,0:T(8,128)(2,1)S(1)} %token_step.1) | copy-start | bytes 1769476
  173.9 38.1 %copy-start.10 = (bf16[2,512,512]{2,1,0:T(8,128)(2,1)S(1)}, bf16[2,512,512]{2,1,0:T(8,128)(2,1)}, u32[]{:S(2)}) copy-start(bf16[2,512,512]{2,1,0:T(8,128)(2,1)} %constant.44.clone.first_tables) | copy-start | bytes 3145732
  173.9 38.1 %copy-start.12 = (bf16[2,512,512]{2,1,0:T(8,128)(2,1)S(1)}, bf16[2,512,512]{2,1,0:T(8,128)(2,1)}, u32[]{:S(2)}) copy-start(bf16[2,512,512]{2,1,0:T(8,128)(2,1)} %constant.45.clone.second_tables) | copy-start | bytes 3145732
  173.9 38.1 %copy-start.25 = (s32[2]{0:T(128)S(1)}, s32[2]{0:T(128)}, u32[]{:S(2)}) copy-start(s32[2]{0:T(128)} %pad_add_fusion.place_ref) | copy-start | bytes 28
  216.4 1.0 copy-start.8
  217.4 0.7 copy-start.17
  218.2 28.2 %copy-start.7 = (bf16[512,512]{1,0:T(8,128)(2,1)S(1)}, bf16[512,512]{1,0:T(8,128)(2,1)}, u32[]{:S(2)}) copy-start(bf16[512,512]{1,0:T(8,128)(2,1)} %constant.46.clone.refs_1_) | copy-start | bytes 1572868
  246.3 14.5 %copy-start.26 = (bf16[1,1168,128]{2,1,0:T(8,128)(2,1)S(1)}, bf16[1,1168,128]{2,1,0:T(8,128)(2,1)}, u32[]{:S(2)}) copy-start(bf16[1,1168,128]{2,1,0:T(8,128)(2,1)} %reduce-scatter.2.cloned.1.call-done) | copy-start | bytes 897028
  247.5 23.7 %copy-start.28 = (f32[96]{0:T(128)S(1)}, f32[96]{0:T(128)}, u32[]{:S(2)}) copy-start(f32[96]{0:T(128)} %gain_ref.1) | copy-start | bytes 1156
  247.5 23.7 %all-to-all-start.7 = ((bf16[32,48,128]{2,1,0:T(8,128)(2,1)}), bf16[32,48,128]{2,1,0:T(8,128)(2,1)S(1)}, u32[]{:S(2)}, u32[]{:S(2)}) async-start(bf16[32,48,128]{2,1,0:T(8,128)(2,1)} %inverse_rows_512.1), calls=%async_computation.8 | async-start | bytes 786432 | tf_op jit(solution)/shard_map/all_to_all | solution.py:739
  260.9 10.9 %slice-start = ((bf16[32,72,128]{2,1,0:T(8,128)(2,1)}), bf16[32,48,128]{2,1,0:T(8,128)(2,1)S(1)}, s32[]{:S(2)}) async-start(bf16[32,72,128]{2,1,0:T(8,128)(2,1)} %copy-done.2), calls=%async_computation.10 | async-start | bytes 786432 | tf_op jit(solution)/shard_map/slice | solution.py:769
  260.9 21.1 %collective-permute-start.2 = (bf16[576,128]{1,0:T(8,128)(2,1)S(1)}, bf16[576,128]{1,0:T(8,128)(2,1)S(1)}, u32[]{:S(2)}, u32[]{:S(2)}) collective-permute-start(bf16[576,128]{1,0:T(8,128)(2,1)S(1)} %slice.47), channel_id=1, source_target_pairs={{0,12},{12,0},{4,8},{8,4},{1,13},{13,1},{5,9},{9,5},{2,14},{14,2},... | collective-permute-start | bytes 442376 | tf_op jit(solution)/shard_map/ppermute | solution.py:766
Sparse Core Ops, SparseCore 0:
  218.3 27.9 reduce-scatter.1

commit v8 on v7

--- a/solution.py
+++ b/solution.py
@@ -102,8 +102,9 @@
         slots = n // 8
         block = x_ref[:, first_in : first_in + GROUPS * rows, :]
         gathered = gather_rows(block, rows)
-        half = dot(tables[2 * i][...], gathered).astype(jnp.bfloat16)
-        edges.append(dot(tables[2 * i + 1][...], gathered))
+        result = dot(tables[i][...], gathered)
+        half = result[:n].astype(jnp.bfloat16)
+        edges.append(result[n:])
         half = half.reshape(COLS, 2, slots, GROUPS * LANES)
         for part in range(2):
             for g in range(GROUPS):
@@ -128,7 +129,7 @@
         out_shape=jax.ShapeDtypeStruct((COLS, slots + EDGE_ROWS, LANES), jnp.bfloat16),
         name="forward_rows_" + "_".join(str(n) for n in sizes),
         **params(flops, 2 << 20),
-    )(entries, *[constant(table(n)) for n in sizes for table in (row_table, edge_table)])
+    )(entries, *[constant(np.concatenate([row_table(n), edge_table(n)])) for n in sizes])
 
 
 def inverse_rows_kernel(layout, *refs):
@@ -232,10 +233,10 @@
     ]
 
 
-def mix_first_kernel(place_ref, x_ref, kept_ref, recv_ref, first_tables, second_tables, out_ref):
+def mix_first_kernel(place_ref, x_ref, kept_ref, recv_ref, tables, out_ref):
     slots = H1 // 8
     special, near = masks(place_ref, slots)
-    cos, sin = first_tables[0], first_tables[1]
+    cos, sin = tables[0], tables[1]
     up_r, up_i, down_r, down_i = spectrum(x_ref, 0, slots, special, cos, sin)
     real, imag = filters(near, kept_ref, recv_ref, 0, slots)
     up = (real[0] * up_r - imag[0] * up_i, real[0] * up_i + imag[0] * up_r)
@@ -244,7 +245,7 @@
 
     first, slots = SECOND_SLOT, H2 // 8
     special, near = masks(place_ref, slots)
-    cos, sin = second_tables[0], second_tables[1]
+    cos, sin = tables[2], tables[3]
     grad = spectrum(x_ref, first, slots, special, cos, sin)
     real, imag = filters(near, kept_ref, recv_ref, first, slots)
     up, down = apply_back(real, imag, grad)
@@ -282,12 +283,12 @@
 
 
 def mix_last_kernel(
-    place_ref, x_ref, y_ref, kept_ref, recv_ref, first_tables, second_tables,
+    place_ref, x_ref, y_ref, kept_ref, recv_ref, tables_ref,
     out_ref, total_ref, terms_ref, sem,
 ):
     slots = H2 // 8
     special, near = masks(place_ref, slots)
-    tables = second_tables[0], second_tables[1]
+    tables = tables_ref[2], tables_ref[3]
     grad = spectrum(x_ref, SECOND_SLOT, slots, special, *tables)
     field = spectrum(y_ref, SECOND_SLOT, slots, special, *tables)
     put_terms(terms_ref, SECOND_SLOT, slots, near, field, grad)
@@ -297,7 +298,7 @@
     )
     slots = H1 // 8
     special, near = masks(place_ref, slots)
-    tables = first_tables[0], first_tables[1]
+    tables = tables_ref[0], tables_ref[1]
     field = spectrum(x_ref, 0, slots, special, *tables)
     grad = spectrum(y_ref, 0, slots, special, *tables)
     put_terms(terms_ref, 0, slots, near, field, grad)
@@ -327,17 +328,17 @@
 
 
 def both_tables():
-    return [constant(np.stack(col_tables(n))) for n in (H1, H2)]
+    return constant(np.stack(col_tables(H1) + col_tables(H2)))
 
 
 def mix_first(place, entries, kept, recv):
     return pl.pallas_call(
         mix_first_kernel,
         out_shape=jax.ShapeDtypeStruct((COLS, FILTER_ROWS, LANES), jnp.bfloat16),
-        in_specs=[smem()] + vmem(5),
+        in_specs=[smem()] + vmem(4),
         name="mix_first",
         **params(8 * FILTER_ROWS * 512 * 512, 6 << 20),
-    )(place, entries, kept, recv, *both_tables())
+    )(place, entries, kept, recv, both_tables())
 
 
 def mix_last(place, entries, later, kept, recv):
@@ -348,12 +349,12 @@
             jax.ShapeDtypeStruct((COLS, SECOND_SLOT, LANES), jnp.bfloat16),
             jax.ShapeDtypeStruct(total, jnp.bfloat16),
         ),
-        in_specs=[smem()] + vmem(6),
+        in_specs=[smem()] + vmem(5),
         out_specs=tuple(vmem(1) + hbm(1)),
         scratch_shapes=[pltpu.VMEM(total, jnp.bfloat16), pltpu.SemaphoreType.DMA],
         name="mix_last",
         **params(12 * FILTER_ROWS * 512 * 512, 8 << 20),
-    )(place, entries, later, kept, recv, *both_tables())
+    )(place, entries, later, kept, recv, both_tables())
 
 
 def grid_of(rows, columns):
@@ -388,35 +389,35 @@
 
 
 def send_filters_kernel(
-    place_ref, first_ref, second_ref, sent_ref, zero_ref, first_buf, second_buf, sems
+    place_ref, quarter_ref, first_ref, second_ref, sent_ref, zero_ref, first_buf, second_buf, sems
 ):
-    quarter = place_ref[1]
+    quarter = quarter_ref[0]
     at = pl.ds(pl.multiple_of(quarter * LANES, LANES), LANES)
     first_copy = pltpu.make_async_copy(first_ref.at[:, :, :, at], first_buf, sems.at[0])
     second_copy = pltpu.make_async_copy(second_ref, second_buf, sems.at[1])
     first_copy.start()
     second_copy.start()
     near = place_ref[0] < 2
+    lanes = quarter_lanes(quarter)
+    groups = [(part, g) for part in range(2) for g in range(GROUPS)]
     zeros = []
+    first = 0
     for n in (H1, H2):
         slots = n // 8
-        first = 0 if n == H1 else 2 * GROUPS * H1 // 8
-        pick = sent_rows(near, slots)
         if n == H1:
             first_copy.wait()
+            rows = [first_buf[part, g].astype(jnp.bfloat16) for part, g in groups]
         else:
             second_copy.wait()
-            lanes = quarter_lanes(quarter)
-        for part in range(2):
-            for g in range(GROUPS):
-                if n == H1:
-                    rows = first_buf[part, g].astype(jnp.bfloat16)
-                else:
-                    rows = dot(second_pair(second_buf, part, g), lanes).astype(jnp.bfloat16)
-                rows = dot(pick, rows)
-                zeros.append(rows[:1])
-                sent_ref[first : first + slots, :] = rows.astype(jnp.bfloat16)
-                first += slots
+            rows = [second_pair(second_buf, part, g) for part, g in groups]
+            rows = dot(jnp.concatenate(rows, axis=0), lanes).astype(jnp.bfloat16)
+            rows = [rows[2 * slots * i : 2 * slots * (i + 1)] for i in range(len(groups))]
+        rows = dot(sent_rows(near, slots), jnp.concatenate(rows, axis=1))
+        for i in range(len(groups)):
+            picked = rows[:, i * LANES : (i + 1) * LANES]
+            zeros.append(picked[:1])
+            sent_ref[first : first + slots, :] = picked.astype(jnp.bfloat16)
+            first += slots
     zeros.append(jnp.zeros((4, LANES), jnp.float32))
     zero_ref[...] = jnp.concatenate(zeros, axis=0).astype(jnp.bfloat16)
 
@@ -444,14 +445,14 @@
                 first += slots
 
 
-def send_filters(place, filter_first, filter_second):
+def send_filters(place, quarter, filter_first, filter_second):
     return pl.pallas_call(
         send_filters_kernel,
         out_shape=(
             jax.ShapeDtypeStruct((FILTER_ROWS, LANES), jnp.bfloat16),
             jax.ShapeDtypeStruct((16, LANES), jnp.bfloat16),
         ),
-        in_specs=[smem()] + hbm(2),
+        in_specs=[smem()] * 2 + hbm(2),
         scratch_shapes=[
             pltpu.VMEM((2, GROUPS, H1 // 4, LANES), jnp.float32),
             pltpu.VMEM((2, 2 * GROUPS, H2 // 4, H2), jnp.float32),
@@ -459,7 +460,7 @@
         ],
         name="send_filters",
         **params(12 * 64 * 512 * 128 * 2, 2 << 20, 60),
-    )(place, filter_first, filter_second)
+    )(place, quarter, filter_first, filter_second)
 
 
 def keep_filters(place, filter_first, filter_second):
@@ -501,24 +502,28 @@
     near = place_ref[0] < 2
     wide_at, narrow_at = grid_of(LANES, LANES // 2)
     lanes = [ones_at(wide_at == narrow_at + 64 * i) for i in range(2)]
+    groups = [(part, g) for part in range(2) for g in range(GROUPS)]
     for n, kept, recv in ((H1, kept_first, recv_first), (H2, kept_second, recv_second)):
         slots = n // 8
         local, slot = grid_of(2 * slots, slots)
         mirror = lax.rem(2 * slots - slot, 2 * slots)
         pick_kept = ones_at(local == jnp.where(near, slot, slots - slot))
         pick_recv = ones_at(local == jnp.where(near, slots + slot, mirror))
-        for part in range(2):
-            for g in range(GROUPS):
-                at = (part * GROUPS + g) * slots
-                rows = dot(pick_kept, kept[at : at + slots]) + dot(
-                    pick_recv, recv[at : at + slots]
-                )
-                if n == H1:
-                    first_ref[part, g] = rows
-                else:
-                    rows = rows.astype(jnp.bfloat16)
-                    for i in range(2):
-                        second_ref[part, 2 * g + i] = dot(rows, lanes[i])
+        kept, recv = [
+            jnp.concatenate([ref[i * slots : (i + 1) * slots] for i in range(len(groups))], axis=1)
+            for ref in (kept, recv)
+        ]
+        rows = dot(pick_kept, kept) + dot(pick_recv, recv)
+        rows = [rows[:, i * LANES : (i + 1) * LANES] for i in range(len(groups))]
+        if n == H1:
+            for (part, g), block in zip(groups, rows):
+                first_ref[part, g] = block
+        else:
+            rows = jnp.concatenate(rows, axis=0).astype(jnp.bfloat16)
+            for i in range(2):
+                half = dot(rows, lanes[i])
+                for at, (part, g) in enumerate(groups):
+                    second_ref[part, 2 * g + i] = half[at * 2 * slots : (at + 1) * 2 * slots]
 
 
 def summed(terms):
@@ -741,13 +746,14 @@
 
 def shards(images, gain_first, filter_first, reduce_weight, gain_second, filter_second, grad_out):
     col = lax.axis_index("col")
-    place = jnp.stack([col, lax.axis_index("rep")]).astype(jnp.int32)
+    place = col.astype(jnp.int32).reshape(1)
     pixels = images.reshape(96, 16, LANES)
     upstream = grad_out.transpose(0, 2, 3, 1).reshape(8, 64, 192)
     weight = reduce_weight.reshape(96, 2, 384).transpose(1, 0, 2).reshape(192, 384)
     gains = jnp.repeat(gain_second.reshape(96, 2), 64, axis=1)
 
-    sent, zero = send_filters(place, filter_first, filter_second)
+    quarter = lax.axis_index("rep").astype(jnp.int32).reshape(1)
+    sent, zero = send_filters(place, quarter, filter_first, filter_second)
     swapped = swap_filters(sent, zero)
     kept = keep_filters(place, filter_first, filter_second)
     both = exchange(first_norm(pixels, upstream, gain_first), "row")

time: 292 us -> 291 us (level)
  the two profiles are of different devices: /device:TPU:105 before, /device:TPU:99 now
where the time goes in v8:
time: 291 us; the launch traced here: 290 us
  blocking collectives  135 us (46%)
  waiting for transfers between devices  56.8 us (20%)
  starting transfers between devices  47.8 us (16%)
  Pallas kernels  23.3 us (8%)
  between operations  14.4 us (5%)
  local copies, waits for them, and re-layouts  8.89 us (3%)
  other arithmetic  3.85 us (1%)
    all_to_all x4, blocking collectives, exchange(): return lax.all_to_all(blocks, axis, split_axis=0, concat_axis=0, tiled=True)  124 us
    all_to_all x4, waiting for transfers between devices, exchange(): return lax.all_to_all(blocks, axis, split_axis=0, concat_axis=0, tiled=True)  41.8 us
    all_to_all x4, starting transfers between devices, exchange(): return lax.all_to_all(blocks, axis, split_axis=0, concat_axis=0, tiled=True)  34.3 us
    all_gather x1, blocking collectives, patch_filters(): return lax.all_gather(recv, 'rep', axis=0, tiled=False)  10.7 us
    ppermute x1, starting transfers between devices, swap_filters(): lax.ppermute(sent, 'col', SWAP)  9.89 us
    ppermute x1, waiting for transfers between devices, shards(): swapped = lax.ppermute(terms[FILTER_ROWS:2 * FILTER_ROWS], 'col', SWAP)  7.66 us
    ppermute x1, waiting for transfers between devices, swap_filters(): lax.ppermute(zero, 'col', ((2, 0), (3, 1)))  7.32 us
    unnamed x50, local copies, waits for them, and re-layouts  6.23 us
  transfers between devices with their start and end apart: 8, of which 6 were waited for; matrix products, arithmetic and copies ran while one was open for 2% of the time, Pallas kernels for 2%

profile of v8, /device:TPU:99, one launch (start us, length us, event | category | flops | bytes accessed | tf_op | source)
XLA Modules:
  0.0 289.9 jit_solution(16196182203458998691)
XLA Ops:
  7.2 2.5 first_norm.1
  9.7 8.4 %all-to-all-start = ((bf16[32,72,128]{2,1,0:T(8,128)(2,1)}), bf16[32,72,128]{2,1,0:T(8,128)(2,1)S(1)}, u32[]{:S(2)}, u32[]{:S(2)}) async-start(bf16[32,72,128]{2,1,0:T(8,128)(2,1)} %first_norm.1), calls=%async_computation | async-start | bytes 1179648 | tf_op jit(solution)/shard_map/all_to_all | solution.py:744
  18.1 2.3 send_filters.1
  20.4 9.9 %collective-permute-start = (bf16[576,128]{1,0:T(8,128)(2,1)}, bf16[576,128]{1,0:T(8,128)(2,1)}, u32[]{:S(2)}, u32[]{:S(2)}) collective-permute-start(bf16[576,128]{1,0:T(8,128)(2,1)} %get-tuple-element.16), channel_id=1, source_target_pairs={{0,12},{12,0},{4,8},{8,4},{1,13},{13,1},{5,9},{9,5},{2,14},{14,2},... | collective-permute-start | bytes 442376 | tf_op jit(solution)/shard_map/ppermute | solution.py:491
  30.3 1.3 collective-permute-start.1
  31.6 2.5 all-to-all-done.refs_0_
  34.1 0.9 copy-done.13
  35.0 1.3 forward_rows_512_256.2
  36.4 7.3 %collective-permute-done.1 = bf16[16,128]{1,0:T(8,128)(2,1)S(1)} collective-permute-done((bf16[16,128]{1,0:T(8,128)(2,1)}, bf16[16,128]{1,0:T(8,128)(2,1)S(1)}, u32[]{:S(2)}, u32[]{:S(2)}) %collective-permute-start.1) | collective-permute-done | bytes 4128 | tf_op jit(solution)/shard_map/ppermute | solution.py:491
  43.7 10.3 %all-to-all-start.1 = ((bf16[4,592,128]{2,1,0:T(8,128)(2,1)}), bf16[4,592,128]{2,1,0:T(8,128)(2,1)S(1)}, u32[]{:S(2)}, u32[]{:S(2)}) async-start(bf16[4,592,128]{2,1,0:T(8,128)(2,1)} %forward_rows_512_256.2), calls=%async_computation.1 | async-start | bytes 1212416 | tf_op jit(solution)/shard_map/all_to_all | solution.py:744
  54.1 0.6 broadcast_in_dim.104
  54.7 0.6 broadcast_in_dim.99
  55.3 1.4 keep_filters.1.kept_ref
  56.8 0.9 bitcast_select_fusion.3
  57.7 1.0 bitcast_select_fusion.1
  58.7 10.7 %all-gather = bf16[2304,128]{1,0:T(8,128)(2,1)S(1)} all-gather(bf16[576,128]{1,0:T(8,128)(2,1)S(1)} %pad_maximum_fusion), channel_id=2, replica_groups=mesh['row'=32,'col'=4,'rep'=4] {'rep'}, dimensions={0}, use_global_device_ids=true | all-gather | bytes 737280 | tf_op jit(solution)/shard_map/all_gather | solution.py:496
  69.4 15.5 %all-to-all-done.1.x_ref = bf16[4,592,128]{2,1,0:T(8,128)(2,1)S(1)} async-done(((bf16[4,592,128]{2,1,0:T(8,128)(2,1)}), bf16[4,592,128]{2,1,0:T(8,128)(2,1)S(1)}, u32[]{:S(2)}, u32[]{:S(2)}) %all-to-all-start.1) | async-done | bytes 606240 | tf_op jit(solution)/shard_map/all_to_all | solution.py:744
  84.9 1.6 copy-done.6
  86.5 2.6 mix_first.1
  89.1 33.2 %all_to_all.40.refs_0_ = bf16[4,576,128]{2,1,0:T(8,128)(2,1)S(1)} all-to-all(bf16[4,576,128]{2,1,0:T(8,128)(2,1)S(1)} %mix_first.1), channel_id=1, replica_groups=mesh['row'=32,'col'=4,'rep'=4] {'col'}, dimensions={0} | all-to-all | bytes 1179648 | tf_op jit(solution)/shard_map/all_to_all | solution.py:744
  122.3 1.3 inverse_rows_512_256.1
  123.7 10.4 %all-to-all-start.3 = ((bf16[32,72,128]{2,1,0:T(8,128)(2,1)}), bf16[32,72,128]{2,1,0:T(8,128)(2,1)S(1)}, u32[]{:S(2)}, u32[]{:S(2)}) async-start(bf16[32,72,128]{2,1,0:T(8,128)(2,1)} %inverse_rows_512_256.1), calls=%async_computation.3 | async-start | bytes 1179648 | tf_op jit(solution)/shard_map/all_to_all | solution.py:744
  134.2 0.8 copy.25
  135.1 0.1 reshape.172
  135.3 0.1 copy.27.gain_ref
  135.4 14.4 %all-to-all-done.3.m_ref = bf16[32,72,128]{2,1,0:T(8,128)(2,1)S(1)} async-done(((bf16[32,72,128]{2,1,0:T(8,128)(2,1)}), bf16[32,72,128]{2,1,0:T(8,128)(2,1)S(1)}, u32[]{:S(2)}, u32[]{:S(2)}) %all-to-all-start.3) | async-done | bytes 589856 | tf_op jit(solution)/shard_map/all_to_all | solution.py:744
  149.8 0.9 copy-done.11
  150.7 0.9 copy-done.12
  151.7 4.9 %token_step.1 = bf16[32,72,128]{2,1,0:T(8,128)(2,1)S(1)} custom-call(bf16[96,16,128]{2,1,0:T(8,128)(2,1)S(1)} %bitcast.25, bf16[32,72,128]{2,1,0:T(8,128)(2,1)S(1)} %all-to-all-done.3.m_ref, bf16[8,64,192]{2,1,0:T(8,128)(2,1)S(1)} %bitcast.32, bf16[192,384]{1,0:T(8,128)(2,1)S(1)} %bitcast.30, bf16[384,192]{1,0:T(8,128)(2,1)S(1)} %bitcast.33, ...), custom_call_target="tpu_custom_call" | custom-call | flops 301989888 | bytes 4194304 | tf_op jit(solution)/shard_map/token_step/pallas_call | solution.py:714
  156.6 21.8 %all_to_all.41.refs_0_ = bf16[32,72,128]{2,1,0:T(8,128)(2,1)S(1)} all-to-all(bf16[32,72,128]{2,1,0:T(8,128)(2,1)S(1)} %token_step.1), channel_id=1, replica_groups=mesh['row'=32,'col'=4,'rep'=4] {'row'}, dimensions={0} | all-to-all | bytes 1179648 | tf_op jit(solution)/shard_map/all_to_all | solution.py:744
  178.4 0.5 forward_rows_512_256.3
  178.9 37.7 %all_to_all.42.y_ref = bf16[4,592,128]{2,1,0:T(8,128)(2,1)S(1)} all-to-all(bf16[4,592,128]{2,1,0:T(8,128)(2,1)S(1)} %forward_rows_512_256.3), channel_id=1, replica_groups=mesh['row'=32,'col'=4,'rep'=4] {'col'}, dimensions={0} | all-to-all | bytes 1212416 | tf_op jit(solution)/shard_map/all_to_all | solution.py:744
  216.6 4.0 %mix_last.1 = (bf16[4,384,128]{2,1,0:T(8,128)(2,1)S(1)}, bf16[4,1168,128]{2,1,0:T(8,128)(2,1)S(1)}) custom-call(s32[1]{0:T(128)} %bitcast.1.place_ref, bf16[4,592,128]{2,1,0:T(8,128)(2,1)S(1)} %all-to-all-done.1.x_ref, bf16[4,592,128]{2,1,0:T(8,128)(2,1)S(1)} %all_to_all.42.y_ref, bf16[4,576,128]{2,1,0:T(8,128)(2,1)S(1)} %keep_filters.1.kept_ref, ...), custom_call_target="tpu_custom_call" | custom-call | flops 1811939328 | bytes 8388608 | tf_op jit(solution)/shard_map/mix_last/pallas_call | solution.py:346
  220.6 1.0 copy-done.10
  221.6 0.7 copy-done.15
  222.4 31.3 %all_to_all.43.refs_0_ = bf16[4,384,128]{2,1,0:T(8,128)(2,1)S(1)} all-to-all(bf16[4,384,128]{2,1,0:T(8,128)(2,1)} %copy-done.15), channel_id=1, replica_groups=mesh['row'=32,'col'=4,'rep'=4] {'col'}, dimensions={0} | all-to-all | bytes 786432 | tf_op jit(solution)/shard_map/all_to_all | solution.py:744
  253.7 1.2 inverse_rows_512.1
  254.9 5.2 %all-to-all-start.7 = ((bf16[32,48,128]{2,1,0:T(8,128)(2,1)}), bf16[32,48,128]{2,1,0:T(8,128)(2,1)S(1)}, u32[]{:S(2)}, u32[]{:S(2)}) async-start(bf16[32,48,128]{2,1,0:T(8,128)(2,1)} %inverse_rows_512.1), calls=%async_computation.8 | async-start | bytes 786432 | tf_op jit(solution)/shard_map/all_to_all | solution.py:744
  260.3 0.1 convert_reduce_fusion
  260.5 2.3 collective-permute-start.2
  262.9 9.4 %all-to-all-done.7 = bf16[32,48,128]{2,1,0:T(8,128)(2,1)S(1)} async-done(((bf16[32,48,128]{2,1,0:T(8,128)(2,1)}), bf16[32,48,128]{2,1,0:T(8,128)(2,1)S(1)}, u32[]{:S(2)}, u32[]{:S(2)}) %all-to-all-start.7) | async-done | bytes 393248 | tf_op jit(solution)/shard_map/all_to_all | solution.py:744
  272.3 0.2 fusion.3
  272.5 0.3 fusion.7
  272.8 1.1 fusion.6
  273.9 7.7 %collective-permute-done.2 = bf16[576,128]{1,0:T(8,128)(2,1)S(1)} collective-permute-done((bf16[576,128]{1,0:T(8,128)(2,1)S(1)}, bf16[576,128]{1,0:T(8,128)(2,1)S(1)}, u32[]{:S(2)}, u32[]{:S(2)}) %collective-permute-start.2) | collective-permute-done | bytes 147488 | tf_op jit(solution)/shard_map/ppermute | solution.py:772
  281.6 0.1 bitcast_select_fusion.recv_first
  281.7 0.1 bitcast_select_fusion.2.recv_second
  281.8 1.2 place_grads.1
  (73 shorter events, 0.6 us)
Async XLA Ops:
  9.6 24.5 %copy-start.4 = (bf16[528,512]{1,0:T(8,128)(2,1)S(1)}, bf16[528,512]{1,0:T(8,128)(2,1)}, u32[]{:S(2)}) copy-start(bf16[528,512]{1,0:T(8,128)(2,1)} %constant.34.clone.refs_1_) | copy-start | bytes 1622020
  9.7 24.5 %all-to-all-start = ((bf16[32,72,128]{2,1,0:T(8,128)(2,1)}), bf16[32,72,128]{2,1,0:T(8,128)(2,1)S(1)}, u32[]{:S(2)}, u32[]{:S(2)}) async-start(bf16[32,72,128]{2,1,0:T(8,128)(2,1)} %first_norm.1), calls=%async_computation | async-start | bytes 1179648 | tf_op jit(solution)/shard_map/all_to_all | solution.py:744
  20.4 34.9 %copy-start.1 = (f32[2,3,128,512]{3,2,1,0:T(8,128)S(1)}, f32[2,3,128,512]{3,2,1,0:T(8,128)}, u32[]{:S(2)}) copy-start(f32[2,3,128,512]{3,2,1,0:T(8,128)} %first_ref.3) | copy-start | bytes 4718596
  20.4 34.9 %copy-start.3 = (f32[2,6,64,256]{3,2,1,0:T(8,128)S(1)}, f32[2,6,64,256]{3,2,1,0:T(8,128)}, u32[]{:S(2)}) copy-start(f32[2,6,64,256]{3,2,1,0:T(8,128)} %second_ref.3) | copy-start | bytes 2359300
  20.4 23.3 %collective-permute-start = (bf16[576,128]{1,0:T(8,128)(2,1)}, bf16[576,128]{1,0:T(8,128)(2,1)}, u32[]{:S(2)}, u32[]{:S(2)}) collective-permute-start(bf16[576,128]{1,0:T(8,128)(2,1)} %get-tuple-element.16), channel_id=1, source_target_pairs={{0,12},{12,0},{4,8},{8,4},{1,13},{13,1},{5,9},{9,5},{2,14},{14,2},... | collective-permute-start | bytes 442376 | tf_op jit(solution)/shard_map/ppermute | solution.py:491
  30.3 13.4 %collective-permute-start.1 = (bf16[16,128]{1,0:T(8,128)(2,1)}, bf16[16,128]{1,0:T(8,128)(2,1)S(1)}, u32[]{:S(2)}, u32[]{:S(2)}) collective-permute-start(bf16[16,128]{1,0:T(8,128)(2,1)} %get-tuple-element.17), channel_id=1, source_target_pairs={{8,0},{12,4},{9,1},{13,5},{10,2},{14,6},{11,3},{15,7},{24,16},{28,... | collective-permute-start | bytes 12296 | tf_op jit(solution)/shard_map/ppermute | solution.py:491
  34.1 0.9 copy-start.13
  43.7 11.0 %copy-start.20 = (bf16[16,128]{1,0:T(8,128)(2,1)}, bf16[16,128]{1,0:T(8,128)(2,1)S(1)}, u32[]{:S(2)}) copy-start(bf16[16,128]{1,0:T(8,128)(2,1)S(1)} %collective-permute-done.1) | copy-start | bytes 12292
  43.7 41.2 %all-to-all-start.1 = ((bf16[4,592,128]{2,1,0:T(8,128)(2,1)}), bf16[4,592,128]{2,1,0:T(8,128)(2,1)S(1)}, u32[]{:S(2)}, u32[]{:S(2)}) async-start(bf16[4,592,128]{2,1,0:T(8,128)(2,1)} %forward_rows_512_256.2), calls=%async_computation.1 | async-start | bytes 1212416 | tf_op jit(solution)/shard_map/all_to_all | solution.py:744
  55.3 1.5 copy-start.21
  55.3 1.5 copy-start.23
  55.3 2.4 copy-start.24
  84.9 1.6 copy-start.6
  86.5 35.8 %copy-start.8 = (bf16[512,512]{1,0:T(8,128)(2,1)S(1)}, bf16[512,512]{1,0:T(8,128)(2,1)}, u32[]{:S(2)}) copy-start(bf16[512,512]{1,0:T(8,128)(2,1)} %constant.37.clone.refs_1_) | copy-start | bytes 1572868
  86.5 35.8 %copy-start.16 = (bf16[256,256]{1,0:T(8,128)(2,1)S(1)}, bf16[256,256]{1,0:T(8,128)(2,1)}, u32[]{:S(2)}) copy-start(bf16[256,256]{1,0:T(8,128)(2,1)} %constant.38.clone.refs_2_) | copy-start | bytes 393220
  122.3 11.8 %copy-start.18 = (bf16[192,384]{1,0:T(8,128)(2,1)S(1)}, bf16[192,384]{1,0:T(8,128)(2,1)}, u32[]{:S(2)}) copy-start(bf16[192,384]{1,0:T(8,128)(2,1)} %param.19) | copy-start | bytes 442372
  122.3 12.7 %copy-start.22 = (f32[192]{0:T(256)S(1)}, f32[192]{0:T(256)}, u32[]{:S(2)}) copy-start(f32[192]{0:T(256)} %param.20) | copy-start | bytes 2308
  123.7 26.1 %copy-start = (bf16[1,96,16,128]{3,2,1,0:T(8,128)(2,1)S(1)}, bf16[1,96,16,128]{3,2,1,0:T(8,128)(2,1)}, u32[]{:S(2)}) copy-start(bf16[1,96,16,128]{3,2,1,0:T(8,128)(2,1)} %param.16) | copy-start | bytes 1179652
  123.7 26.1 %all-to-all-start.3 = ((bf16[32,72,128]{2,1,0:T(8,128)(2,1)}), bf16[32,72,128]{2,1,0:T(8,128)(2,1)S(1)}, u32[]{:S(2)}, u32[]{:S(2)}) async-start(bf16[32,72,128]{2,1,0:T(8,128)(2,1)} %inverse_rows_512_256.1), calls=%async_computation.3 | async-start | bytes 1179648 | tf_op jit(solution)/shard_map/all_to_all | solution.py:744
  134.1 119.6 %reduce-scatter.2.cloned.1.call-start = ((), (), s32[]{:S(2)}) async-start(), calls=%async_computation.9 | async-start | bytes 1495040 | tf_op jit(solution)/shard_map/reduce_scatter | solution.py:530
  149.8 1.0 copy-start.11
  150.7 0.9 copy-start.12
  151.7 26.7 %copy-start.5 = (bf16[528,512]{1,0:T(8,128)(2,1)S(1)}, bf16[528,512]{1,0:T(8,128)(2,1)}, u32[]{:S(2)}) copy-start(bf16[528,512]{1,0:T(8,128)(2,1)} %constant.34.clone.refs_1_) | copy-start | bytes 1622020
  151.7 26.7 %copy-start.14 = (bf16[272,256]{1,0:T(8,128)(2,1)S(1)}, bf16[272,256]{1,0:T(8,128)(2,1)}, u32[]{:S(2)}) copy-start(bf16[272,256]{1,0:T(8,128)(2,1)} %constant.35.clone.refs_2_) | copy-start | bytes 417796
  156.6 103.9 %copy-start.2 = (bf16[32,72,128]{2,1,0:T(8,128)(2,1)}, bf16[32,72,128]{2,1,0:T(8,128)(2,1)S(1)}, u32[]{:S(2)}) copy-start(bf16[32,72,128]{2,1,0:T(8,128)(2,1)S(1)} %token_step.1) | copy-start | bytes 1769476
  178.4 38.2 %copy-start.7 = (bf16[4,512,512]{2,1,0:T(8,128)(2,1)S(1)}, bf16[4,512,512]{2,1,0:T(8,128)(2,1)}, u32[]{:S(2)}) copy-start(bf16[4,512,512]{2,1,0:T(8,128)(2,1)} %constant.36.clone.tables.tables_ref) | copy-start | bytes 6291460
  220.6 1.0 copy-start.10
  221.6 0.7 copy-start.15
  222.4 31.4 %copy-start.9 = (bf16[512,512]{1,0:T(8,128)(2,1)S(1)}, bf16[512,512]{1,0:T(8,128)(2,1)}, u32[]{:S(2)}) copy-start(bf16[512,512]{1,0:T(8,128)(2,1)} %constant.37.clone.refs_1_) | copy-start | bytes 1572868
  253.7 6.7 %copy-start.17 = (bf16[1,1168,128]{2,1,0:T(8,128)(2,1)S(1)}, bf16[1,1168,128]{2,1,0:T(8,128)(2,1)}, u32[]{:S(2)}) copy-start(bf16[1,1168,128]{2,1,0:T(8,128)(2,1)} %reduce-scatter.2.cloned.1.call-done) | copy-start | bytes 897028
  254.9 17.4 %copy-start.19 = (f32[96]{0:T(128)S(1)}, f32[96]{0:T(128)}, u32[]{:S(2)}) copy-start(f32[96]{0:T(128)} %gain_ref.1) | copy-start | bytes 1156
  254.9 17.4 %all-to-all-start.7 = ((bf16[32,48,128]{2,1,0:T(8,128)(2,1)}), bf16[32,48,128]{2,1,0:T(8,128)(2,1)S(1)}, u32[]{:S(2)}, u32[]{:S(2)}) async-start(bf16[32,48,128]{2,1,0:T(8,128)(2,1)} %inverse_rows_512.1), calls=%async_computation.8 | async-start | bytes 786432 | tf_op jit(solution)/shard_map/all_to_all | solution.py:744
  260.5 12.4 %slice-start = ((bf16[32,72,128]{2,1,0:T(8,128)(2,1)}), bf16[32,48,128]{2,1,0:T(8,128)(2,1)S(1)}, s32[]{:S(2)}) async-start(bf16[32,72,128]{2,1,0:T(8,128)(2,1)} %copy-done.2), calls=%async_computation.10 | async-start | bytes 786432 | tf_op jit(solution)/shard_map/slice | solution.py:775
  260.5 21.1 %collective-permute-start.2 = (bf16[576,128]{1,0:T(8,128)(2,1)S(1)}, bf16[576,128]{1,0:T(8,128)(2,1)S(1)}, u32[]{:S(2)}, u32[]{:S(2)}) collective-permute-start(bf16[576,128]{1,0:T(8,128)(2,1)S(1)} %slice.47), channel_id=1, source_target_pairs={{0,12},{12,0},{4,8},{8,4},{1,13},{13,1},{5,9},{9,5},{2,14},{14,2},... | collective-permute-start | bytes 442376 | tf_op jit(solution)/shard_map/ppermute | solution.py:772
Sparse Core Ops, SparseCore 0:
  222.5 21.7 reduce-scatter.1

commit v9 on v8

--- a/solution.py
+++ b/solution.py
@@ -633,17 +633,8 @@
 
 
 def token_kernel(
-    x_hbm, m_ref, g_hbm, w_hbm, wt_hbm, gain_ref, out_ref,
-    x_ref, g_ref, w_ref, wt_ref, s_ref, n_ref, back_ref, o_ref, sems,
+    x_ref, m_ref, g_ref, w_ref, wt_ref, gain_ref, out_ref, s_ref, n_ref, back_ref, o_ref
 ):
-    copies = [
-        pltpu.make_async_copy(source, target, sems.at[i])
-        for i, (source, target) in enumerate(
-            ((x_hbm, x_ref), (w_hbm, w_ref), (g_hbm, g_ref), (wt_hbm, wt_ref))
-        )
-    ]
-    for copy in copies:
-        copy.start()
     at, lane = grid_of(LANES, 2 * LANES)
     spread_at = ones_at(at == 2 * lax.rem(lane, 64) + lax.div(lane, LANES))
     at, lane = grid_of(2 * LANES, 2 * LANES)
@@ -651,14 +642,11 @@
     merge_at = ones_at(lane == here)
     mixed = m_ref[:, : GROUPS * 16, :].astype(jnp.float32).reshape(1536, LANES)
     back_ref[...] = m_ref[:, GROUPS * 16 :, :].astype(jnp.float32).reshape(768, LANES)
-    copies[0].wait()
     section = x_ref[...].astype(jnp.float32).reshape(1536, LANES) + mixed
     spread = dot(section.astype(jnp.bfloat16), spread_at)
     for e in range(2):
         s_ref[e] = spread[:, e * LANES : (e + 1) * LANES]
     low = low_half()
-    for copy in copies[1:]:
-        copy.wait()
     packed = pack_pairs(g_ref[...])
     for first in range(0, 8, 2):
         patches = [
@@ -714,17 +702,12 @@
     return pl.pallas_call(
         token_kernel,
         out_shape=jax.ShapeDtypeStruct((ROWS, GROUPS * 24, LANES), jnp.bfloat16),
-        in_specs=hbm(1) + vmem(1) + hbm(3) + vmem(1),
+        in_specs=vmem(6),
         scratch_shapes=[
-            pltpu.VMEM((96, 16, LANES), jnp.bfloat16),
-            pltpu.VMEM((8, 64, 192), jnp.bfloat16),
-            pltpu.VMEM((192, 384), jnp.bfloat16),
-            pltpu.VMEM((384, 192), jnp.bfloat16),
             pltpu.VMEM((2, 1536, LANES), jnp.float32),
             pltpu.VMEM((768, LANES), jnp.float32),
             pltpu.VMEM((768, LANES), jnp.float32),
             pltpu.VMEM((1536, LANES), jnp.float32),
-            pltpu.SemaphoreType.DMA((4,)),
         ],
         name="token_step",
         **params(8 * 2 * 192 * 384 * 256, 4 << 20),

time: 291 us -> 290 us (level)
  no operation moved by 1% of the time
where the time goes in v9:
time: 290 us; the launch traced here: 289 us
  blocking collectives  135 us (47%)
  waiting for transfers between devices  56.8 us (20%)
  starting transfers between devices  47.8 us (16%)
  Pallas kernels  22.3 us (8%)
  between operations  14.4 us (5%)
  local copies, waits for them, and re-layouts  8.89 us (3%)
  other arithmetic  3.85 us (1%)
    all_to_all x4, blocking collectives, exchange(): return lax.all_to_all(blocks, axis, split_axis=0, concat_axis=0, tiled=True)  124 us
    all_to_all x4, waiting for transfers between devices, exchange(): return lax.all_to_all(blocks, axis, split_axis=0, concat_axis=0, tiled=True)  41.8 us
    all_to_all x4, starting transfers between devices, exchange(): return lax.all_to_all(blocks, axis, split_axis=0, concat_axis=0, tiled=True)  34.3 us
    all_gather x1, blocking collectives, patch_filters(): return lax.all_gather(recv, 'rep', axis=0, tiled=False)  10.7 us
    ppermute x1, starting transfers between devices, swap_filters(): lax.ppermute(sent, 'col', SWAP)  9.89 us
    ppermute x1, waiting for transfers between devices, shards(): swapped = lax.ppermute(terms[FILTER_ROWS:2 * FILTER_ROWS], 'col', SWAP)  7.66 us
    ppermute x1, waiting for transfers between devices, swap_filters(): lax.ppermute(zero, 'col', ((2, 0), (3, 1)))  7.32 us
    unnamed x50, local copies, waits for them, and re-layouts  6.23 us
  transfers between devices with their start and end apart: 8, of which 6 were waited for; matrix products, arithmetic and copies ran while one was open for 2% of the time, Pallas kernels for 2%

profile of v9, /device:TPU:99, one launch (start us, length us, event | category | flops | bytes accessed | tf_op | source)
XLA Modules:
  0.0 288.8 jit_solution(12609692298548787691)
XLA Ops:
  7.2 2.5 first_norm.1
  9.7 8.4 %all-to-all-start = ((bf16[32,72,128]{2,1,0:T(8,128)(2,1)}), bf16[32,72,128]{2,1,0:T(8,128)(2,1)S(1)}, u32[]{:S(2)}, u32[]{:S(2)}) async-start(bf16[32,72,128]{2,1,0:T(8,128)(2,1)} %first_norm.1), calls=%async_computation | async-start | bytes 1179648 | tf_op jit(solution)/shard_map/all_to_all | solution.py:727
  18.1 2.3 send_filters.1
  20.4 9.9 %collective-permute-start = (bf16[576,128]{1,0:T(8,128)(2,1)}, bf16[576,128]{1,0:T(8,128)(2,1)}, u32[]{:S(2)}, u32[]{:S(2)}) collective-permute-start(bf16[576,128]{1,0:T(8,128)(2,1)} %get-tuple-element.16), channel_id=1, source_target_pairs={{0,12},{12,0},{4,8},{8,4},{1,13},{13,1},{5,9},{9,5},{2,14},{14,2},... | collective-permute-start | bytes 442376 | tf_op jit(solution)/shard_map/ppermute | solution.py:491
  30.3 1.3 collective-permute-start.1
  31.6 2.5 all-to-all-done.refs_0_
  34.1 0.9 copy-done.13
  35.0 1.3 forward_rows_512_256.2
  36.4 7.3 %collective-permute-done.1 = bf16[16,128]{1,0:T(8,128)(2,1)S(1)} collective-permute-done((bf16[16,128]{1,0:T(8,128)(2,1)}, bf16[16,128]{1,0:T(8,128)(2,1)S(1)}, u32[]{:S(2)}, u32[]{:S(2)}) %collective-permute-start.1) | collective-permute-done | bytes 4128 | tf_op jit(solution)/shard_map/ppermute | solution.py:491
  43.7 10.3 %all-to-all-start.1 = ((bf16[4,592,128]{2,1,0:T(8,128)(2,1)}), bf16[4,592,128]{2,1,0:T(8,128)(2,1)S(1)}, u32[]{:S(2)}, u32[]{:S(2)}) async-start(bf16[4,592,128]{2,1,0:T(8,128)(2,1)} %forward_rows_512_256.2), calls=%async_computation.1 | async-start | bytes 1212416 | tf_op jit(solution)/shard_map/all_to_all | solution.py:727
  54.1 0.6 broadcast_in_dim.104
  54.7 0.6 broadcast_in_dim.99
  55.3 1.4 keep_filters.1.kept_ref
  56.8 0.9 bitcast_select_fusion.3
  57.7 1.0 bitcast_select_fusion.1
  58.7 10.7 %all-gather = bf16[2304,128]{1,0:T(8,128)(2,1)S(1)} all-gather(bf16[576,128]{1,0:T(8,128)(2,1)S(1)} %pad_maximum_fusion), channel_id=2, replica_groups=mesh['row'=32,'col'=4,'rep'=4] {'rep'}, dimensions={0}, use_global_device_ids=true | all-gather | bytes 737280 | tf_op jit(solution)/shard_map/all_gather | solution.py:496
  69.4 15.5 %all-to-all-done.1.x_ref = bf16[4,592,128]{2,1,0:T(8,128)(2,1)S(1)} async-done(((bf16[4,592,128]{2,1,0:T(8,128)(2,1)}), bf16[4,592,128]{2,1,0:T(8,128)(2,1)S(1)}, u32[]{:S(2)}, u32[]{:S(2)}) %all-to-all-start.1) | async-done | bytes 606240 | tf_op jit(solution)/shard_map/all_to_all | solution.py:727
  84.9 1.6 copy-done.6
  86.5 2.6 mix_first.1
  89.1 33.2 %all_to_all.40.refs_0_ = bf16[4,576,128]{2,1,0:T(8,128)(2,1)S(1)} all-to-all(bf16[4,576,128]{2,1,0:T(8,128)(2,1)S(1)} %mix_first.1), channel_id=1, replica_groups=mesh['row'=32,'col'=4,'rep'=4] {'col'}, dimensions={0} | all-to-all | bytes 1179648 | tf_op jit(solution)/shard_map/all_to_all | solution.py:727
  122.3 1.3 inverse_rows_512_256.1
  123.7 10.4 %all-to-all-start.3 = ((bf16[32,72,128]{2,1,0:T(8,128)(2,1)}), bf16[32,72,128]{2,1,0:T(8,128)(2,1)S(1)}, u32[]{:S(2)}, u32[]{:S(2)}) async-start(bf16[32,72,128]{2,1,0:T(8,128)(2,1)} %inverse_rows_512_256.1), calls=%async_computation.3 | async-start | bytes 1179648 | tf_op jit(solution)/shard_map/all_to_all | solution.py:727
  134.2 0.8 copy.25
  135.1 0.1 reshape.172
  135.3 0.1 copy.27.gain_ref
  135.4 14.4 %all-to-all-done.3.m_ref = bf16[32,72,128]{2,1,0:T(8,128)(2,1)S(1)} async-done(((bf16[32,72,128]{2,1,0:T(8,128)(2,1)}), bf16[32,72,128]{2,1,0:T(8,128)(2,1)S(1)}, u32[]{:S(2)}, u32[]{:S(2)}) %all-to-all-start.3) | async-done | bytes 589856 | tf_op jit(solution)/shard_map/all_to_all | solution.py:727
  149.8 0.9 copy-done.11
  150.7 0.9 copy-done.12
  151.7 3.9 %token_step.1 = bf16[32,72,128]{2,1,0:T(8,128)(2,1)S(1)} custom-call(bf16[96,16,128]{2,1,0:T(8,128)(2,1)S(1)} %bitcast.25, bf16[32,72,128]{2,1,0:T(8,128)(2,1)S(1)} %all-to-all-done.3.m_ref, bf16[8,64,192]{2,1,0:T(8,128)(2,1)S(1)} %bitcast.32, bf16[192,384]{1,0:T(8,128)(2,1)S(1)} %bitcast.30, bf16[384,192]{1,0:T(8,128)(2,1)S(1)} %bitcast.33, ...), custom_call_target="tpu_custom_call" | custom-call | flops 301989888 | bytes 4194304 | tf_op jit(solution)/shard_map/token_step/pallas_call | solution.py:702
  155.6 21.8 %all_to_all.41.refs_0_ = bf16[32,72,128]{2,1,0:T(8,128)(2,1)S(1)} all-to-all(bf16[32,72,128]{2,1,0:T(8,128)(2,1)S(1)} %token_step.1), channel_id=1, replica_groups=mesh['row'=32,'col'=4,'rep'=4] {'row'}, dimensions={0} | all-to-all | bytes 1179648 | tf_op jit(solution)/shard_map/all_to_all | solution.py:727
  177.4 0.5 forward_rows_512_256.3
  177.9 37.7 %all_to_all.42.y_ref = bf16[4,592,128]{2,1,0:T(8,128)(2,1)S(1)} all-to-all(bf16[4,592,128]{2,1,0:T(8,128)(2,1)S(1)} %forward_rows_512_256.3), channel_id=1, replica_groups=mesh['row'=32,'col'=4,'rep'=4] {'col'}, dimensions={0} | all-to-all | bytes 1212416 | tf_op jit(solution)/shard_map/all_to_all | solution.py:727
  215.6 4.0 %mix_last.1 = (bf16[4,384,128]{2,1,0:T(8,128)(2,1)S(1)}, bf16[4,1168,128]{2,1,0:T(8,128)(2,1)S(1)}) custom-call(s32[1]{0:T(128)} %bitcast.1.place_ref, bf16[4,592,128]{2,1,0:T(8,128)(2,1)S(1)} %all-to-all-done.1.x_ref, bf16[4,592,128]{2,1,0:T(8,128)(2,1)S(1)} %all_to_all.42.y_ref, bf16[4,576,128]{2,1,0:T(8,128)(2,1)S(1)} %keep_filters.1.kept_ref, ...), custom_call_target="tpu_custom_call" | custom-call | flops 1811939328 | bytes 8388608 | tf_op jit(solution)/shard_map/mix_last/pallas_call | solution.py:346
  219.6 1.0 copy-done.10
  220.6 0.7 copy-done.15
  221.4 31.3 %all_to_all.43.refs_0_ = bf16[4,384,128]{2,1,0:T(8,128)(2,1)S(1)} all-to-all(bf16[4,384,128]{2,1,0:T(8,128)(2,1)} %copy-done.15), channel_id=1, replica_groups=mesh['row'=32,'col'=4,'rep'=4] {'col'}, dimensions={0} | all-to-all | bytes 786432 | tf_op jit(solution)/shard_map/all_to_all | solution.py:727
  252.7 1.2 inverse_rows_512.1
  253.9 5.2 %all-to-all-start.7 = ((bf16[32,48,128]{2,1,0:T(8,128)(2,1)}), bf16[32,48,128]{2,1,0:T(8,128)(2,1)S(1)}, u32[]{:S(2)}, u32[]{:S(2)}) async-start(bf16[32,48,128]{2,1,0:T(8,128)(2,1)} %inverse_rows_512.1), calls=%async_computation.8 | async-start | bytes 786432 | tf_op jit(solution)/shard_map/all_to_all | solution.py:727
  259.3 0.1 convert_reduce_fusion
  259.5 2.3 collective-permute-start.2
  261.9 9.4 %all-to-all-done.7 = bf16[32,48,128]{2,1,0:T(8,128)(2,1)S(1)} async-done(((bf16[32,48,128]{2,1,0:T(8,128)(2,1)}), bf16[32,48,128]{2,1,0:T(8,128)(2,1)S(1)}, u32[]{:S(2)}, u32[]{:S(2)}) %all-to-all-start.7) | async-done | bytes 393248 | tf_op jit(solution)/shard_map/all_to_all | solution.py:727
  271.3 0.2 fusion.3
  271.5 0.3 fusion.7
  271.8 1.1 fusion.6
  272.9 7.7 %collective-permute-done.2 = bf16[576,128]{1,0:T(8,128)(2,1)S(1)} collective-permute-done((bf16[576,128]{1,0:T(8,128)(2,1)S(1)}, bf16[576,128]{1,0:T(8,128)(2,1)S(1)}, u32[]{:S(2)}, u32[]{:S(2)}) %collective-permute-start.2) | collective-permute-done | bytes 147488 | tf_op jit(solution)/shard_map/ppermute | solution.py:755
  280.6 0.1 bitcast_select_fusion.recv_first
  280.7 0.1 bitcast_select_fusion.2.recv_second
  280.8 1.2 place_grads.1
  (73 shorter events, 0.6 us)
Async XLA Ops:
  9.6 24.5 %copy-start.4 = (bf16[528,512]{1,0:T(8,128)(2,1)S(1)}, bf16[528,512]{1,0:T(8,128)(2,1)}, u32[]{:S(2)}) copy-start(bf16[528,512]{1,0:T(8,128)(2,1)} %constant.34.clone.refs_1_) | copy-start | bytes 1622020
  9.7 24.5 %all-to-all-start = ((bf16[32,72,128]{2,1,0:T(8,128)(2,1)}), bf16[32,72,128]{2,1,0:T(8,128)(2,1)S(1)}, u32[]{:S(2)}, u32[]{:S(2)}) async-start(bf16[32,72,128]{2,1,0:T(8,128)(2,1)} %first_norm.1), calls=%async_computation | async-start | bytes 1179648 | tf_op jit(solution)/shard_map/all_to_all | solution.py:727
  20.4 34.9 %copy-start.1 = (f32[2,3,128,512]{3,2,1,0:T(8,128)S(1)}, f32[2,3,128,512]{3,2,1,0:T(8,128)}, u32[]{:S(2)}) copy-start(f32[2,3,128,512]{3,2,1,0:T(8,128)} %first_ref.3) | copy-start | bytes 4718596
  20.4 34.9 %copy-start.3 = (f32[2,6,64,256]{3,2,1,0:T(8,128)S(1)}, f32[2,6,64,256]{3,2,1,0:T(8,128)}, u32[]{:S(2)}) copy-start(f32[2,6,64,256]{3,2,1,0:T(8,128)} %second_ref.3) | copy-start | bytes 2359300
  20.4 23.3 %collective-permute-start = (bf16[576,128]{1,0:T(8,128)(2,1)}, bf16[576,128]{1,0:T(8,128)(2,1)}, u32[]{:S(2)}, u32[]{:S(2)}) collective-permute-start(bf16[576,128]{1,0:T(8,128)(2,1)} %get-tuple-element.16), channel_id=1, source_target_pairs={{0,12},{12,0},{4,8},{8,4},{1,13},{13,1},{5,9},{9,5},{2,14},{14,2},... | collective-permute-start | bytes 442376 | tf_op jit(solution)/shard_map/ppermute | solution.py:491
  30.3 13.4 %collective-permute-start.1 = (bf16[16,128]{1,0:T(8,128)(2,1)}, bf16[16,128]{1,0:T(8,128)(2,1)S(1)}, u32[]{:S(2)}, u32[]{:S(2)}) collective-permute-start(bf16[16,128]{1,0:T(8,128)(2,1)} %get-tuple-element.17), channel_id=1, source_target_pairs={{8,0},{12,4},{9,1},{13,5},{10,2},{14,6},{11,3},{15,7},{24,16},{28,... | collective-permute-start | bytes 12296 | tf_op jit(solution)/shard_map/ppermute | solution.py:491
  34.1 0.9 copy-start.13
  43.7 11.0 %copy-start.20 = (bf16[16,128]{1,0:T(8,128)(2,1)}, bf16[16,128]{1,0:T(8,128)(2,1)S(1)}, u32[]{:S(2)}) copy-start(bf16[16,128]{1,0:T(8,128)(2,1)S(1)} %collective-permute-done.1) | copy-start | bytes 12292
  43.7 41.2 %all-to-all-start.1 = ((bf16[4,592,128]{2,1,0:T(8,128)(2,1)}), bf16[4,592,128]{2,1,0:T(8,128)(2,1)S(1)}, u32[]{:S(2)}, u32[]{:S(2)}) async-start(bf16[4,592,128]{2,1,0:T(8,128)(2,1)} %forward_rows_512_256.2), calls=%async_computation.1 | async-start | bytes 1212416 | tf_op jit(solution)/shard_map/all_to_all | solution.py:727
  55.3 1.5 copy-start.21
  55.3 1.5 copy-start.23
  55.3 2.4 copy-start.24
  84.9 1.6 copy-start.6
  86.5 35.8 %copy-start.8 = (bf16[512,512]{1,0:T(8,128)(2,1)S(1)}, bf16[512,512]{1,0:T(8,128)(2,1)}, u32[]{:S(2)}) copy-start(bf16[512,512]{1,0:T(8,128)(2,1)} %constant.37.clone.refs_1_) | copy-start | bytes 1572868
  86.5 35.8 %copy-start.16 = (bf16[256,256]{1,0:T(8,128)(2,1)S(1)}, bf16[256,256]{1,0:T(8,128)(2,1)}, u32[]{:S(2)}) copy-start(bf16[256,256]{1,0:T(8,128)(2,1)} %constant.38.clone.refs_2_) | copy-start | bytes 393220
  122.3 11.8 %copy-start.18 = (bf16[192,384]{1,0:T(8,128)(2,1)S(1)}, bf16[192,384]{1,0:T(8,128)(2,1)}, u32[]{:S(2)}) copy-start(bf16[192,384]{1,0:T(8,128)(2,1)} %param.19) | copy-start | bytes 442372
  122.3 12.7 %copy-start.22 = (f32[192]{0:T(256)S(1)}, f32[192]{0:T(256)}, u32[]{:S(2)}) copy-start(f32[192]{0:T(256)} %param.20) | copy-start | bytes 2308
  123.7 26.1 %copy-start = (bf16[1,96,16,128]{3,2,1,0:T(8,128)(2,1)S(1)}, bf16[1,96,16,128]{3,2,1,0:T(8,128)(2,1)}, u32[]{:S(2)}) copy-start(bf16[1,96,16,128]{3,2,1,0:T(8,128)(2,1)} %param.16) | copy-start | bytes 1179652
  123.7 26.1 %all-to-all-start.3 = ((bf16[32,72,128]{2,1,0:T(8,128)(2,1)}), bf16[32,72,128]{2,1,0:T(8,128)(2,1)S(1)}, u32[]{:S(2)}, u32[]{:S(2)}) async-start(bf16[32,72,128]{2,1,0:T(8,128)(2,1)} %inverse_rows_512_256.1), calls=%async_computation.3 | async-start | bytes 1179648 | tf_op jit(solution)/shard_map/all_to_all | solution.py:727
  134.1 118.6 %reduce-scatter.2.cloned.1.call-start = ((), (), s32[]{:S(2)}) async-start(), calls=%async_computation.9 | async-start | bytes 1495040 | tf_op jit(solution)/shard_map/reduce_scatter | solution.py:530
  149.8 1.0 copy-start.11
  150.7 0.9 copy-start.12
  151.7 25.7 %copy-start.5 = (bf16[528,512]{1,0:T(8,128)(2,1)S(1)}, bf16[528,512]{1,0:T(8,128)(2,1)}, u32[]{:S(2)}) copy-start(bf16[528,512]{1,0:T(8,128)(2,1)} %constant.34.clone.refs_1_) | copy-start | bytes 1622020
  151.7 25.7 %copy-start.14 = (bf16[272,256]{1,0:T(8,128)(2,1)S(1)}, bf16[272,256]{1,0:T(8,128)(2,1)}, u32[]{:S(2)}) copy-start(bf16[272,256]{1,0:T(8,128)(2,1)} %constant.35.clone.refs_2_) | copy-start | bytes 417796
  155.6 103.8 %copy-start.2 = (bf16[32,72,128]{2,1,0:T(8,128)(2,1)}, bf16[32,72,128]{2,1,0:T(8,128)(2,1)S(1)}, u32[]{:S(2)}) copy-start(bf16[32,72,128]{2,1,0:T(8,128)(2,1)S(1)} %token_step.1) | copy-start | bytes 1769476
  177.4 38.2 %copy-start.7 = (bf16[4,512,512]{2,1,0:T(8,128)(2,1)S(1)}, bf16[4,512,512]{2,1,0:T(8,128)(2,1)}, u32[]{:S(2)}) copy-start(bf16[4,512,512]{2,1,0:T(8,128)(2,1)} %constant.36.clone.tables.tables_ref) | copy-start | bytes 6291460
  219.6 1.0 copy-start.10
  220.6 0.7 copy-start.15
  221.4 31.4 %copy-start.9 = (bf16[512,512]{1,0:T(8,128)(2,1)S(1)}, bf16[512,512]{1,0:T(8,128)(2,1)}, u32[]{:S(2)}) copy-start(bf16[512,512]{1,0:T(8,128)(2,1)} %constant.37.clone.refs_1_) | copy-start | bytes 1572868
  252.7 6.7 %copy-start.17 = (bf16[1,1168,128]{2,1,0:T(8,128)(2,1)S(1)}, bf16[1,1168,128]{2,1,0:T(8,128)(2,1)}, u32[]{:S(2)}) copy-start(bf16[1,1168,128]{2,1,0:T(8,128)(2,1)} %reduce-scatter.2.cloned.1.call-done) | copy-start | bytes 897028
  253.9 17.4 %copy-start.19 = (f32[96]{0:T(128)S(1)}, f32[96]{0:T(128)}, u32[]{:S(2)}) copy-start(f32[96]{0:T(128)} %gain_ref.1) | copy-start | bytes 1156
  253.9 17.4 %all-to-all-start.7 = ((bf16[32,48,128]{2,1,0:T(8,128)(2,1)}), bf16[32,48,128]{2,1,0:T(8,128)(2,1)S(1)}, u32[]{:S(2)}, u32[]{:S(2)}) async-start(bf16[32,48,128]{2,1,0:T(8,128)(2,1)} %inverse_rows_512.1), calls=%async_computation.8 | async-start | bytes 786432 | tf_op jit(solution)/shard_map/all_to_all | solution.py:727
  259.5 12.3 %slice-start = ((bf16[32,72,128]{2,1,0:T(8,128)(2,1)}), bf16[32,48,128]{2,1,0:T(8,128)(2,1)S(1)}, s32[]{:S(2)}) async-start(bf16[32,72,128]{2,1,0:T(8,128)(2,1)} %copy-done.2), calls=%async_computation.10 | async-start | bytes 786432 | tf_op jit(solution)/shard_map/slice | solution.py:758
  259.5 21.1 %collective-permute-start.2 = (bf16[576,128]{1,0:T(8,128)(2,1)S(1)}, bf16[576,128]{1,0:T(8,128)(2,1)S(1)}, u32[]{:S(2)}, u32[]{:S(2)}) collective-permute-start(bf16[576,128]{1,0:T(8,128)(2,1)S(1)} %slice.47), channel_id=1, source_target_pairs={{0,12},{12,0},{4,8},{8,4},{1,13},{13,1},{5,9},{9,5},{2,14},{14,2},... | collective-permute-start | bytes 442376 | tf_op jit(solution)/shard_map/ppermute | solution.py:755
Sparse Core Ops, SparseCore 0:
  221.5 21.8 reduce-scatter.1
